TPU v7x, 32 devices: a whole 2x2x4 slice. The times are simulated.
32 devices in a mesh: dp: 8 (over z, x), row: 2 (over y), col: 2 (over core).
Axes of the slice: x: 2, y: 2, z: 4, core: 2. Of those that a mesh axis runs over, the one named last changes fastest.
Arguments:
- tokens: bfloat16 [4096, 768], P(('dp', 'col'), 'row'), may hold values from -6 to 6
- out_grad: bfloat16 [4096, 768], P(('dp', 'col'), 'row'), may hold values from -6 to 6
- seq_lengths: int32 [8, 2], P('dp'), may hold values from 0 to 512, as said below
- w_query: bfloat16 [768, 768], P('row', 'col'), may hold values from -0.21875 to 0.21875
- w_key: bfloat16 [768, 768], P('row', 'col'), may hold values from -0.21875 to 0.21875
- w_value: bfloat16 [768, 768], P('row', 'col'), may hold values from -0.21875 to 0.21875
- w_out: bfloat16 [768, 768], P('col', 'row'), may hold values from -1.75 to 1.75
- w_up: bfloat16 [768, 3072], P('row', 'col'), may hold values from -0.21875 to 0.21875
- w_down: bfloat16 [3072, 768], P('col', 'row'), may hold values from -0.109375 to 0.109375
- b_query: bfloat16 [768], P(('col', 'row')), may hold values from -3 to 3
- b_value: bfloat16 [768], P(('col', 'row')), may hold values from -3 to 3
- b_out: bfloat16 [768], P('row'), may hold values from -3 to 3
- b_up: bfloat16 [3072], P(('col', 'row')), may hold values from -3 to 3
- b_down: bfloat16 [768], P('row'), may hold values from -3 to 3
- gain_attn: bfloat16 [768], P('row'), may hold values from 0.25 to 1.75
- shift_attn: bfloat16 [768], P('row'), may hold values from -2 to 2
- gain_mlp: bfloat16 [768], P('row'), may hold values from 0.25 to 1.75
- shift_mlp: bfloat16 [768], P('row'), may hold values from -2 to 2
Outputs:
- output: bfloat16 [4096, 768], P(('dp', 'col'), 'row')
- input_grad: bfloat16 [4096, 768], P(('dp', 'col'), 'row')
- grad_query: float32 [768, 768], P('row', 'col')
- grad_key: float32 [768, 768], P('row', 'col')
- grad_value: float32 [768, 768], P('row', 'col')
- grad_out: float32 [768, 768], P('col', 'row')
- grad_up: float32 [768, 3072], P('row', 'col')
- grad_down: float32 [3072, 768], P('col', 'row')
- grad_b_query: float32 [768], P(('col', 'row'))
- grad_b_value: float32 [768], P(('col', 'row'))
- grad_b_out: float32 [768], P('row')
- grad_b_up: float32 [3072], P(('col', 'row'))
- grad_b_down: float32 [768], P('row')
- grad_gain_attn: float32 [768], P('row')
- grad_shift_attn: float32 [768], P('row')
- grad_gain_mlp: float32 [768], P('row')
- grad_shift_mlp: float32 [768], P('row')
Inputs may be any that keep to these rules, and one draw needn't show every extreme that they name: `seq_lengths`: row g: the first sequence has 128 or more tokens, the two lengths sum to at most 512, the rest of the group's slots is padding; in some row the first length is 512 and the second 0.
All inputs are finite; a program needn't handle non-finite values.
Results may differ from a plain program's by a relative error of at most 0.014.
Values may be sent and summed in bfloat16 or wider, within the bound.
No kernel may reach another device: no remote copies, remote signals or barrier semaphores. Data moves between devices by JAX's collectives and lax.ppermute only.
A program may use at most 128 MiB of HBM per device.

v0:
```python
from functools import partial

import jax
import jax.numpy as jnp
from jax import lax
from jax.sharding import PartitionSpec as P

D = 768
HEAD_DIM = 64


EPSILON = 1e-05
MASKED = -1e30


def product(left, right):
    return jnp.dot(left, right, preferred_element_type=jnp.float32)


def product_nt(left, right):
    return lax.dot_general(
        left, right, (((1,), (1,)), ((), ())), preferred_element_type=jnp.float32
    )


def product_tn(left, right):
    return lax.dot_general(
        left, right, (((0,), (0,)), ((), ())), preferred_element_type=jnp.float32
    )


def row_total(values):
    return lax.psum(values, "row")


def norm_forward(residual, gain_vec, shift_vec):
    row_mean = row_total(jnp.sum(residual, axis=1)) / D
    centered = residual - row_mean[:, None]
    variance = row_total(jnp.sum(centered * centered, axis=1)) / D
    inverse = lax.rsqrt(variance + EPSILON)[:, None]
    unit_rows = centered * inverse
    return ((unit_rows * gain_vec + shift_vec).astype(jnp.bfloat16), unit_rows, inverse)


def norm_backward(grad_rows, unit_rows, inverse, gain_vec):
    scaled = grad_rows * gain_vec
    sum_plain, sum_unit = lax.psum(
        (jnp.sum(scaled, axis=1), jnp.sum(scaled * unit_rows, axis=1)), "row"
    )
    grad_input = inverse * (scaled - sum_plain[:, None] / D - unit_rows * (sum_unit[:, None] / D))
    return (grad_input, jnp.sum(grad_rows * unit_rows, axis=0), jnp.sum(grad_rows, axis=0))


def token_gather(pieces):
    return lax.all_gather(pieces, "col", axis=0, tiled=True)


def rows_term(lefts, weights, flipped):

    def row_term(begin_row, row_count):
        accumulated = None
        for left_rows, weight in zip(lefts, weights):
            value_part = product_nt(left_rows, weight) if flipped else product(left_rows, weight)
            accumulated = value_part if accumulated is None else accumulated + value_part
        return accumulated

    return row_term


def token_sum(row_term, own_rows):
    return lax.psum_scatter(
        row_term(jnp.int32(0), own_rows * lax.axis_size("col")),
        "col",
        scatter_dimension=0,
        tiled=True,
    )


def wide_sum(partial_sum):
    return lax.psum_scatter(
        partial_sum.astype(jnp.bfloat16), "row", scatter_dimension=1, tiled=True
    ).astype(jnp.float32)


def wide_gather(pieces):
    return lax.all_gather(pieces, "row", axis=1, tiled=True)


def block_scores(query_rows, key_rows, allowed, score_scale):
    raw_scores = jnp.einsum(
        "qhd,khd->hqk", query_rows, key_rows, preferred_element_type=jnp.float32
    )
    return jnp.where(allowed[None], raw_scores * score_scale, MASKED)


def block_mask(documents, positions, start_row, stop_row):
    same_doc = documents[start_row:stop_row, None] == documents[None, :stop_row]
    return same_doc & (positions[None, :stop_row] <= positions[start_row:stop_row, None])


def attention_forward(query, keys_all, values_all, documents, positions, block_rows, score_scale):
    allowed = block_mask(documents, positions, 0, block_rows)
    scores = block_scores(query, keys_all, allowed, score_scale)
    largest = jnp.max(scores, axis=-1, keepdims=True)
    weights = jnp.exp(scores - largest)
    summed = jnp.sum(weights, axis=-1, keepdims=True)
    probs = (weights / summed).astype(jnp.bfloat16)
    outputs = jnp.einsum("hqk,khd->qhd", probs, values_all, preferred_element_type=jnp.float32)
    log_totals = [largest + jnp.log(summed)]
    return (outputs, log_totals)


def attention_backward(
    query,
    keys_all,
    values_all,
    grad_mixed,
    documents,
    positions,
    log_totals,
    block_rows,
    score_scale,
):
    group_rows = query.shape[0]
    grad_query = []
    grad_keys = jnp.zeros(keys_all.shape, jnp.float32)
    grad_values = jnp.zeros(values_all.shape, jnp.float32)
    for block_index, start_row in enumerate(range(0, group_rows, block_rows)):
        stop_row = start_row + block_rows
        allowed = block_mask(documents, positions, start_row, stop_row)
        scores = block_scores(query, keys_all, allowed, score_scale)
        probs = jnp.exp(scores - log_totals[block_index])
        grad_probs = jnp.einsum(
            "qhd,khd->hqk", grad_mixed, values_all, preferred_element_type=jnp.float32
        )
        inner = jnp.sum(probs * grad_probs, axis=-1, keepdims=True)
        grad_raw = (probs * (grad_probs - inner) * score_scale).astype(jnp.bfloat16)
        grad_query.append(
            jnp.einsum("hqk,khd->qhd", grad_raw, keys_all, preferred_element_type=jnp.float32)
        )
        grad_keys = grad_keys.at[:stop_row].add(
            jnp.einsum("hqk,qhd->khd", grad_raw, query, preferred_element_type=jnp.float32)
        )
        grad_values = grad_values.at[:stop_row].add(
            jnp.einsum(
                "hqk,qhd->khd",
                probs.astype(jnp.bfloat16),
                grad_mixed,
                preferred_element_type=jnp.float32,
            )
        )
    return (grad_query[0], grad_keys, grad_values)


def body(
    tokens,
    out_grad,
    seq_lengths,
    w_query,
    w_key,
    w_value,
    w_out,
    w_up,
    w_down,
    b_query,
    b_value,
    b_out,
    b_up,
    b_down,
    gain_attn,
    shift_attn,
    gain_mlp,
    shift_mlp,
):
    own_rows = tokens.shape[0]
    group_rows = own_rows * lax.axis_size("col")
    block_rows = min(512, group_rows)
    score_scale = HEAD_DIM ** (-0.5)
    positions = jnp.arange(group_rows, dtype=jnp.int32)
    lengths = seq_lengths[0]
    live_total = lengths[0] + lengths[1]
    documents = (positions >= lengths[0]).astype(jnp.int32) + (positions >= live_total).astype(
        jnp.int32
    )
    own_positions = lax.dynamic_slice_in_dim(positions, lax.axis_index("col") * own_rows, own_rows)
    live_rows = (own_positions < live_total).astype(jnp.float32)[:, None]
    residual = tokens.astype(jnp.float32)
    normed, unit_attn, inverse_attn = norm_forward(residual, gain_attn, shift_attn)
    normed_all = token_gather(normed)
    query, keys_all, values_all = (
        lax.psum_scatter(product(normed_all, w_query), "row", scatter_dimension=1, tiled=True),
        lax.psum_scatter(product(normed_all, w_key), "row", scatter_dimension=1, tiled=True),
        lax.psum_scatter(product(normed_all, w_value), "row", scatter_dimension=1, tiled=True),
    )
    query = (query + b_query).astype(jnp.bfloat16)
    keys_all = keys_all.astype(jnp.bfloat16)
    values_all = (values_all + b_value).astype(jnp.bfloat16)
    query_heads = query.reshape(group_rows, -1, HEAD_DIM)
    key_heads = keys_all.reshape(group_rows, -1, HEAD_DIM)
    value_heads = values_all.reshape(group_rows, -1, HEAD_DIM)
    mixed, log_totals = attention_forward(
        query_heads, key_heads, value_heads, documents, positions, block_rows, score_scale
    )
    mixed = mixed.reshape(group_rows, -1).astype(jnp.bfloat16)
    mixed_all = lax.all_gather(mixed, "row", axis=1, tiled=True)
    middle = residual + (token_sum(rows_term((mixed_all,), (w_out,), False), own_rows) + b_out)
    normed_mlp, unit_mlp, inverse_mlp = norm_forward(middle, gain_mlp, shift_mlp)
    normed_mlp_all = token_gather(normed_mlp)
    pre_act = wide_sum(product(normed_mlp_all, w_up)) + b_up
    hidden = jax.nn.gelu(pre_act, approximate=True).astype(jnp.bfloat16)
    hidden_all = wide_gather(hidden)
    output = middle + (token_sum(rows_term((hidden_all,), (w_down,), False), own_rows) + b_down)
    grad_top = out_grad.astype(jnp.float32) * live_rows
    grad_top_all = token_gather(grad_top.astype(jnp.bfloat16))
    grad_down = product_tn(hidden_all, grad_top_all)
    grad_b_down = jnp.sum(grad_top_all.astype(jnp.float32), axis=0)
    _, gelu_pullback = jax.vjp(partial(jax.nn.gelu, approximate=True), pre_act)
    grad_hidden = wide_sum(product_nt(grad_top_all, w_down))
    grad_pre = gelu_pullback(grad_hidden)[0].astype(jnp.bfloat16)
    grad_b_up = jnp.sum(grad_pre.astype(jnp.float32), axis=0)
    grad_pre_all = wide_gather(grad_pre)
    grad_up = product_tn(normed_mlp_all, grad_pre_all)
    grad_normed_mlp = token_sum(rows_term((grad_pre_all,), (w_up,), True), own_rows)
    grad_mid_norm, grad_gain_mlp, grad_shift_mlp = norm_backward(
        grad_normed_mlp, unit_mlp, inverse_mlp, gain_mlp
    )
    grad_middle = grad_top + grad_mid_norm
    grad_branch_all = token_gather(grad_middle.astype(jnp.bfloat16))
    grad_out = product_tn(mixed_all, grad_branch_all)
    grad_b_out = jnp.sum(grad_branch_all.astype(jnp.float32), axis=0)
    grad_mixed = lax.psum_scatter(
        product_nt(grad_branch_all, w_out), "row", scatter_dimension=1, tiled=True
    )
    grad_mixed = grad_mixed.astype(jnp.bfloat16).reshape(group_rows, -1, HEAD_DIM)
    grad_q, grad_k, grad_v = attention_backward(
        query_heads,
        key_heads,
        value_heads,
        grad_mixed,
        documents,
        positions,
        log_totals,
        block_rows,
        score_scale,
    )
    grad_q = grad_q.reshape(group_rows, -1).astype(jnp.bfloat16)
    grad_k = grad_k.reshape(group_rows, -1).astype(jnp.bfloat16)
    grad_v = grad_v.reshape(group_rows, -1).astype(jnp.bfloat16)
    grad_b_query = jnp.sum(grad_q.astype(jnp.float32), axis=0)
    grad_b_value = jnp.sum(grad_v.astype(jnp.float32), axis=0)
    grad_q_all, grad_k_all, grad_v_all = (
        lax.all_gather(grad_q, "row", axis=1, tiled=True),
        lax.all_gather(grad_k, "row", axis=1, tiled=True),
        lax.all_gather(grad_v, "row", axis=1, tiled=True),
    )
    grad_query = product_tn(normed_all, grad_q_all)
    grad_key = product_tn(normed_all, grad_k_all)
    grad_value = product_tn(normed_all, grad_v_all)
    grad_normed = token_sum(
        rows_term((grad_q_all, grad_k_all, grad_v_all), (w_query, w_key, w_value), True), own_rows
    )
    grad_in_norm, grad_gain_attn, grad_shift_attn = norm_backward(
        grad_normed, unit_attn, inverse_attn, gain_attn
    )
    input_grad = (grad_middle + grad_in_norm).astype(jnp.bfloat16)
    grad_gain_attn, grad_shift_attn, grad_gain_mlp, grad_shift_mlp = lax.psum(
        (grad_gain_attn, grad_shift_attn, grad_gain_mlp, grad_shift_mlp), "col"
    )
    (
        grad_query,
        grad_key,
        grad_value,
        grad_out,
        grad_up,
        grad_down,
        grad_b_query,
        grad_b_value,
        grad_b_out,
        grad_b_up,
        grad_b_down,
        grad_gain_attn,
        grad_shift_attn,
        grad_gain_mlp,
        grad_shift_mlp,
    ) = lax.psum(
        (
            grad_query,
            grad_key,
            grad_value,
            grad_out,
            grad_up,
            grad_down,
            grad_b_query,
            grad_b_value,
            grad_b_out,
            grad_b_up,
            grad_b_down,
            grad_gain_attn,
            grad_shift_attn,
            grad_gain_mlp,
            grad_shift_mlp,
        ),
        "dp",
    )
    return (
        output.astype(jnp.bfloat16),
        input_grad,
        grad_query,
        grad_key,
        grad_value,
        grad_out,
        grad_up,
        grad_down,
        grad_b_query,
        grad_b_value,
        grad_b_out,
        grad_b_up,
        grad_b_down,
        grad_gain_attn,
        grad_shift_attn,
        grad_gain_mlp,
        grad_shift_mlp,
    )


def solution(mesh):
    return jax.shard_map(
        body,
        mesh=mesh,
        in_specs=(
            P(("dp", "col"), "row"),
            P(("dp", "col"), "row"),
            P("dp", None),
            P("row", "col"),
            P("row", "col"),
            P("row", "col"),
            P("col", "row"),
            P("row", "col"),
            P("col", "row"),
            P(("col", "row")),
            P(("col", "row")),
            P("row"),
            P(("col", "row")),
            P("row"),
            P("row"),
            P("row"),
            P("row"),
            P("row"),
        ),
        out_specs=(
            P(("dp", "col"), "row"),
            P(("dp", "col"), "row"),
            P("row", "col"),
            P("row", "col"),
            P("row", "col"),
            P("col", "row"),
            P("row", "col"),
            P("col", "row"),
            P(("col", "row")),
            P(("col", "row")),
            P("row"),
            P(("col", "row")),
            P("row"),
            P("row"),
            P("row"),
            P("row"),
            P("row"),
        ),
        check_vma=False,
    )
```

profile of v0, /device:TPU:0, one launch (start us, length us, event | category | flops | bytes accessed | tf_op | source)
XLA Modules:
  0.0 588.9 jit_solution(11267299855931884981)
XLA Ops:
  8.4 5.9 psum.189
  15.4 4.9 psum.190
  32.9 13.7 %reduce-scatter.15.cloned.1.call-done = f32[512,192]{0,1:T(8,128)} async-done(((f32[512,384]{0,1:T(8,128)}), f32[512,192]{0,1:T(8,128)}) %reduce-scatter.15.cloned.1.call-update) | async-done | bytes 393232 | tf_op jit(solution)/shard_map/reduce_scatter | solution.py:192
  47.7 19.3 %reduce-scatter.13.cloned.1.call-done = f32[512,192]{0,1:T(8,128)} async-done(((f32[512,384]{0,1:T(8,128)}), f32[512,192]{0,1:T(8,128)}) %reduce-scatter.13.cloned.1.call-update) | async-done | bytes 393232 | tf_op jit(solution)/shard_map/reduce_scatter | solution.py:191
  71.0 16.3 %reduce-scatter.11.cloned.1.call-done = f32[512,192]{0,1:T(8,128)} async-done(((f32[512,384]{0,1:T(8,128)}), f32[512,192]{0,1:T(8,128)}) %reduce-scatter.11.cloned.1.call-update) | async-done | bytes 393232 | tf_op jit(solution)/shard_map/reduce_scatter | solution.py:193
  88.4 2.6 fusion.34
  91.0 7.4 %all_gather.31 = bf16[512,384]{0,1:T(8,128)(2,1)S(1)} all-gather(bf16[512,192]{0,1:T(8,128)(2,1)S(1)} %bitcast.73), channel_id=1, replica_groups=mesh['dp'=8,'row'=2,'col'=2] {'row'}, dimensions={1}, use_global_device_ids=true | all-gather | bytes 589824 | tf_op jit(solution)/shard_map/all_gather | solution.py:205
  102.8 3.5 convolution_convert_fusion
  109.4 4.9 psum.191
  114.5 4.9 psum.192
  125.7 12.4 %reduce-scatter.23.cloned.1.call-done = bf16[512,768]{1,0:T(8,128)(2,1)} async-done(((bf16[512,1536]{1,0:T(8,128)(2,1)}), bf16[512,768]{1,0:T(8,128)(2,1)}) %reduce-scatter.23.cloned.1.call-update) | async-done | bytes 786448 | tf_op jit(solution)/shard_map/reduce_scatter | solution.py:80
  138.2 28.9 %reduce-scatter.19.cloned.1.call-done = bf16[512,768]{1,0:T(8,128)(2,1)} async-done(((bf16[512,1536]{1,0:T(8,128)(2,1)}), bf16[512,768]{1,0:T(8,128)(2,1)}) %reduce-scatter.19.cloned.1.call-update) | async-done | bytes 786448 | tf_op jit(solution)/shard_map/reduce_scatter | solution.py:80
  167.1 4.5 convert_reduce_fusion
  172.3 26.6 %all-gather.5.cloned.1.call-done = bf16[512,1536]{1,0:T(8,128)(2,1)} async-done(((bf16[512,768]{1,0:T(8,128)(2,1)}), bf16[512,1536]{1,0:T(8,128)(2,1)}) %all-gather.5.cloned.1.call-update) | async-done | bytes 1572880 | tf_op jit(solution)/shard_map/all_gather | solution.py:86
  198.9 3.3 fusion.77
  202.3 26.0 %all-gather.3.cloned.1.call-done = bf16[512,1536]{1,0:T(8,128)(2,1)} async-done(((bf16[512,768]{1,0:T(8,128)(2,1)}), bf16[512,1536]{1,0:T(8,128)(2,1)}) %all-gather.3.cloned.1.call-update) | async-done | bytes 1572880 | tf_op jit(solution)/shard_map/all_gather | solution.py:86
  228.3 3.6 fusion.76
  233.2 6.2 %reduce-scatter.25.cloned.1.call-done = f32[256,384]{1,0:T(8,128)} async-done(((f32[512,384]{1,0:T(8,128)}), f32[256,384]{1,0:T(8,128)}) %reduce-scatter.25.cloned.1.call-update) | async-done | bytes 393232 | tf_op jit(solution)/shard_map/reduce_scatter | solution.py:71
  241.2 5.6 all-reduce.4
  248.1 3.5 reduce-scatter.21.cloned.1.call-done
  258.8 17.2 %reduce-scatter.27.cloned.1.call-done = f32[512,192]{0,1:T(8,128)} async-done(((f32[512,384]{0,1:T(8,128)}), f32[512,192]{0,1:T(8,128)}) %reduce-scatter.27.cloned.1.call-update) | async-done | bytes 393232 | tf_op jit(solution)/shard_map/reduce_scatter | solution.py:231
  280.3 7.0 %fusion.41 = bf16[3,64,512]{2,1,0:T(8,128)(2,1)} fusion(bf16[512,3,64]{0,2,1:T(8,128)(2,1)} %bitcast.70, f32[3,512,512]{1,2,0:T(8,128)} %fusion.79, f32[3,512,512]{1,2,0:T(8,128)} %copy-done.1, f32[3,512]{1,0:T(4,128)S(1)} %copy-done.26), kind=kOutput, calls=%fused_computation.45 | convolution fusion | flops 106268672 | bytes 6690816 | tf_op jit(solution)/shard_map/hqk,qhd->khd/dot_general | solution.py:142
  287.2 7.5 %convert_reduce_fusion.5 = (f32[3,64]{1,0:T(4,128)}, bf16[3,64,512]{2,1,0:T(8,128)(2,1)}) fusion(bf16[512,3,64]{0,2,1:T(8,128)(2,1)} %bitcast.68, f32[3,512,512]{1,2,0:T(8,128)} %fusion.79, f32[3,512,512]{1,2,0:T(8,128)} %copy-done.1, f32[3,512]{1,0:T(4,128)S(1)} %copy-done.26), kind=kOutput, calls=%fused_computation.70 | convolution fusion | flops 106465088 | bytes 6691584 | tf_op jit(solution)/shard_map/hqk,khd->qhd/dot_general | solution.py:139
  294.7 7.4 %all_gather.39 = bf16[512,384]{0,1:T(8,128)(2,1)S(1)} all-gather(bf16[512,192]{0,1:T(8,128)(2,1)S(1)} %bitcast.66), channel_id=1, replica_groups=mesh['dp'=8,'row'=2,'col'=2] {'row'}, dimensions={1}, use_global_device_ids=true | all-gather | bytes 589824 | tf_op jit(solution)/shard_map/all_gather | solution.py:254
  302.2 6.8 %all_gather.38 = bf16[512,384]{0,1:T(8,128)(2,1)S(1)} all-gather(bf16[512,192]{0,1:T(8,128)(2,1)} %bitcast.71), channel_id=1, replica_groups=mesh['dp'=8,'row'=2,'col'=2] {'row'}, dimensions={1}, use_global_device_ids=true | all-gather | bytes 589824 | tf_op jit(solution)/shard_map/all_gather | solution.py:253
  309.0 6.5 %all_gather.37 = bf16[512,384]{0,1:T(8,128)(2,1)S(1)} all-gather(bf16[512,192]{0,1:T(8,128)(2,1)} %bitcast.72), channel_id=1, replica_groups=mesh['dp'=8,'row'=2,'col'=2] {'row'}, dimensions={1}, use_global_device_ids=true | all-gather | bytes 589824 | tf_op jit(solution)/shard_map/all_gather | solution.py:252
  319.7 3.7 fusion.85
  323.4 2.4 fusion.86
  332.8 2.5 all-reduce.2
  335.3 39.6 %all-reduce = (f32[192]{0:T(256)}, f32[192]{0:T(256)}, f32[384]{0:T(512)}, f32[768]{0:T(1024)}, f32[384]{0:T(512)}, /*index=5*/f32[384]{0:T(512)}, f32[384]{0:T(512)}, f32[384]{0:T(512)}, f32[384]{0:T(512)}) all-reduce(f32[192]{0:T(256)S(1)} %reduce_sum.186, ...), channel_id=1, replica_groups=mesh['dp'=8,'row'=2,'col'=2] {'dp'}, use_global_device_ids=true, to_apply=%region_36.37 | all-reduce | flops 3456 | bytes 27648 | tf_op jit(solution)/shard_map/psum | solution.py:285
  374.8 4.9 all-reduce.3
  381.7 191.2 %all-reduce.7.cloned.1.call-done = (f32[384,384]{1,0:T(8,128)}, f32[384,384]{1,0:T(8,128)}, f32[384,384]{1,0:T(8,128)}, f32[384,384]{1,0:T(8,128)}, f32[384,1536]{1,0:T(8,128)}, /*index=5*/f32[1536,384]{1,0:T(8,128)}) async-done(((f32[384,384]{1,0:T(8,128)}, f32[384,384]{1,0:T(8,128)}, f32[384,384]{1,0:T(8,128)}, f32[384,384]{1,0:T(8,128)}, f32[384,1536]{1,0:T(8,128)}, /*index=5*/f32[1536,384]{1,0:T(8,128)}), ...) | async-done | bytes 7077904 | tf_op jit(solution)/shard_map/psum | solution.py:285
  (184 shorter events, 72.4 us)
Async XLA Ops:
  7.2 115.1 %copy-start = (bf16[384,1536]{1,0:T(8,128)(2,1)S(1)}, bf16[384,1536]{1,0:T(8,128)(2,1)}, u32[]{:S(2)}) copy-start(bf16[384,1536]{1,0:T(8,128)(2,1)} %param.33) | copy-start | bytes 3538948
  7.2 20.2 %copy-start.19 = (bf16[384,384]{1,0:T(8,128)(2,1)S(1)}, bf16[384,384]{1,0:T(8,128)(2,1)}, u32[]{:S(2)}) copy-start(bf16[384,384]{1,0:T(8,128)(2,1)} %param.29) | copy-start | bytes 884740
  7.2 39.4 %reduce-scatter.15.cloned.1.call-start = ((), (), s32[]{:S(2)}) async-start(), calls=%async_computation.12 | async-start | bytes 1179648 | tf_op jit(solution)/shard_map/reduce_scatter | solution.py:192
  14.3 8.5 %copy-start.27 = (f32[256]{0:T(256)}, f32[256]{0:T(256)S(1)}, u32[]{:S(2)}) copy-start(f32[256]{0:T(256)S(1)} %broadcast_multiply_fusion.5) | copy-start | bytes 3076
  27.3 39.7 %reduce-scatter.13.cloned.1.call-start = ((), (), s32[]{:S(2)}) async-start(), calls=%async_computation.11 | async-start | bytes 1179648 | tf_op jit(solution)/shard_map/reduce_scatter | solution.py:191
  28.7 58.6 %reduce-scatter.11.cloned.1.call-start = ((), (), s32[]{:S(2)}) async-start(), calls=%async_computation.10 | async-start | bytes 1179648 | tf_op jit(solution)/shard_map/reduce_scatter | solution.py:193
  30.1 78.1 %reduce-scatter.17.cloned.1.call-start = ((), (), s32[]{:S(2)}) async-start(), calls=%async_computation.13 | async-start | bytes 1179648 | tf_op jit(solution)/shard_map/reduce_scatter | solution.py:71
  47.7 23.3 %copy-start.21 = (bf16[512,192]{0,1:T(8,128)(2,1)}, bf16[512,192]{0,1:T(8,128)(2,1)S(1)}, u32[]{:S(2)}) copy-start(bf16[512,192]{0,1:T(8,128)(2,1)S(1)} %convert_element_type.186) | copy-start | bytes 589828
  71.0 17.4 %copy-start.25 = (f32[3,512]{1,0:T(4,128)}, f32[3,512]{1,0:T(4,128)S(1)}, u32[]{:S(2)}) copy-start(f32[3,512]{1,0:T(4,128)S(1)} %fusion.2) | copy-start | bytes 18436
  88.4 10.1 %copy-start.17 = (bf16[384,384]{1,0:T(8,128)(2,1)S(1)}, bf16[384,384]{1,0:T(8,128)(2,1)}, u32[]{:S(2)}) copy-start(bf16[384,384]{1,0:T(8,128)(2,1)} %param.32) | copy-start | bytes 884740
  91.0 9.5 %copy-start.20 = (bf16[256,384]{1,0:T(8,128)(2,1)S(1)}, bf16[256,384]{1,0:T(8,128)(2,1)}, u32[]{:S(2)}) copy-start(bf16[256,384]{1,0:T(8,128)(2,1)} %param.27) | copy-start | bytes 589828
  99.8 38.3 %reduce-scatter.23.cloned.1.call-start = ((), (), s32[]{:S(2)}) async-start(), calls=%async_computation.17 | async-start | bytes 2359296 | tf_op jit(solution)/shard_map/reduce_scatter | solution.py:80
  102.8 5.5 copy-start.3
  106.3 60.8 %reduce-scatter.19.cloned.1.call-start = ((), (), s32[]{:S(2)}) async-start(), calls=%async_computation.14 | async-start | bytes 2359296 | tf_op jit(solution)/shard_map/reduce_scatter | solution.py:80
  114.3 5.1 copy-start.29
  124.4 74.5 %all-gather.5.cloned.1.call-start = ((), (), s32[]{:S(2)}) async-start(), calls=%async_computation.18 | async-start | bytes 2359296 | tf_op jit(solution)/shard_map/all_gather | solution.py:86
  171.5 56.7 %all-gather.3.cloned.1.call-start = ((), (), s32[]{:S(2)}) async-start(), calls=%async_computation.15 | async-start | bytes 2359296 | tf_op jit(solution)/shard_map/all_gather | solution.py:86
  172.3 67.1 %reduce-scatter.25.cloned.1.call-start = ((), (), s32[]{:S(2)}) async-start(), calls=%async_computation.19 | async-start | bytes 1179648 | tf_op jit(solution)/shard_map/reduce_scatter | solution.py:71
  202.2 49.4 %reduce-scatter.21.cloned.1.call-start = ((), (), s32[]{:S(2)}) async-start(), calls=%async_computation.16 | async-start | bytes 1179648 | tf_op jit(solution)/shard_map/reduce_scatter | solution.py:71
  231.9 44.1 %reduce-scatter.27.cloned.1.call-start = ((), (), s32[]{:S(2)}) async-start(), calls=%async_computation.20 | async-start | bytes 1179648 | tf_op jit(solution)/shard_map/reduce_scatter | solution.py:231
  251.6 4.4 copy-start.18
  257.3 74.2 %reduce-scatter.29.cloned.1.call-start = ((), (), s32[]{:S(2)}) async-start(), calls=%async_computation.21 | async-start | bytes 1179648 | tf_op jit(solution)/shard_map/reduce_scatter | solution.py:71
  258.8 20.7 %copy-start.26 = (f32[3,512]{1,0:T(4,128)S(1)}, f32[3,512]{1,0:T(4,128)}, u32[]{:S(2)}) copy-start(f32[3,512]{1,0:T(4,128)} %log_add_fusion) | copy-start | bytes 18436
  294.7 23.0 %copy-start.14 = (bf16[384,384]{1,0:T(8,128)(2,1)S(1)}, bf16[384,384]{1,0:T(8,128)(2,1)}, u32[]{:S(2)}) copy-start(bf16[384,384]{1,0:T(8,128)(2,1)} %param.30) | copy-start | bytes 884740
  302.2 16.0 %copy-start.7 = (bf16[512,384]{0,1:T(8,128)(2,1)}, bf16[512,384]{0,1:T(8,128)(2,1)S(1)}, u32[]{:S(2)}) copy-start(bf16[512,384]{0,1:T(8,128)(2,1)S(1)} %all_gather.39) | copy-start | bytes 1179652
  302.2 16.0 %copy-start.16 = (bf16[384,384]{1,0:T(8,128)(2,1)S(1)}, bf16[384,384]{1,0:T(8,128)(2,1)}, u32[]{:S(2)}) copy-start(bf16[384,384]{1,0:T(8,128)(2,1)} %param.31) | copy-start | bytes 884740
  309.0 8.7 %copy-start.9 = (bf16[512,384]{0,1:T(8,128)(2,1)}, bf16[512,384]{0,1:T(8,128)(2,1)S(1)}, u32[]{:S(2)}) copy-start(bf16[512,384]{0,1:T(8,128)(2,1)S(1)} %all_gather.38) | copy-start | bytes 1179652
  319.6 253.2 %all-reduce.7.cloned.1.call-start = ((), (), s32[]{:S(2)}) async-start(), calls=%async_computation.22 | async-start | bytes 14155776 | tf_op jit(solution)/shard_map/psum | solution.py:285
  330.7 4.5 copy-start.33
  330.8 49.0 %copy-start.13 = (f32[256,384]{1,0:T(8,128)S(1)}, f32[256,384]{1,0:T(8,128)}, u32[]{:S(2)}) copy-start(f32[256,384]{1,0:T(8,128)} %get-tuple-element.91) | copy-start | bytes 1179652
  572.8 4.8 copy-start.23
  572.8 5.6 copy-start.12
  (25 other events, 59.7 us)
Sparse Core Ops, SparseCore 0:
  27.4 19.2 reduce-scatter.14
  49.6 17.4 reduce-scatter.12
  69.8 17.4 reduce-scatter.10
  100.0 8.2 reduce-scatter.16
  110.9 27.2 reduce-scatter.22
  140.9 26.0 reduce-scatter.18
  171.7 27.2 all-gather.4
  201.0 27.1 all-gather.2
  231.1 8.2 reduce-scatter.24
  242.1 9.3 reduce-scatter.20
  257.4 18.5 reduce-scatter.26
  319.7 8.2 reduce-scatter.28
  333.7 239.0 all-reduce.6
where the time goes:
time: 590 us; the launch traced here: 589 us
  waiting for transfers between devices  364 us (62%)
  blocking collectives  110 us (19%)
  matrix products  55.2 us (9%)
  other arithmetic  29.1 us (5%)
  between operations  15.7 us (3%)
  local copies, waits for them, and re-layouts  14.3 us (2%)
    psum x1, waiting for transfers between devices, body(): lax.psum((grad_query, grad_key, grad_value, grad_out, grad_up, grad_down,...  191 us
    all_gather x2, waiting for transfers between devices, wide_gather(): return lax.all_gather(pieces, 'row', axis=1, tiled=True)  52.6 us
    reduce_scatter x2, waiting for transfers between devices, wide_sum(): lax.psum_scatter(partial_sum.astype(jnp.bfloat16), 'row', scatter_dimensi...  41.3 us
    psum x1, blocking collectives, body(): lax.psum((grad_query, grad_key, grad_value, grad_out, grad_up, grad_down,...  39.6 us
    psum x4, blocking collectives, row_total(): return lax.psum(values, 'row')  20.7 us
    reduce_scatter x1, waiting for transfers between devices, body(): lax.psum_scatter(product(normed_all, w_query), 'row', scatter_dimension=1...  19.3 us
    reduce_scatter x1, waiting for transfers between devices, body(): lax.psum_scatter(product_nt(grad_branch_all, w_out), 'row', scatter_dimen...  17.2 us
    reduce_scatter x1, waiting for transfers between devices, body(): lax.psum_scatter(product(normed_all, w_value), 'row', scatter_dimension=1...  16.3 us
  transfers between devices with their start and end apart: 13, of which 12 were waited for; matrix products, arithmetic and copies ran while one was open for 7% of the time, Pallas kernels for 0%

commit v1 on v0

v1 whole, which is shorter than its diff:
```python
import jax
import jax.numpy as jnp
from jax import lax
from jax.sharding import PartitionSpec as P

HEAD_DIM = 64
EPSILON = 1e-05
MASKED = -1e30
F32 = jnp.float32
BF16 = jnp.bfloat16
SWAP = ((0, 1), (1, 0))


def dot(left, right):
    return jnp.dot(left, right, preferred_element_type=F32)


def dot_nt(left, right):
    return lax.dot_general(left, right, (((1,), (1,)), ((), ())), preferred_element_type=F32)


def dot_tn(left, right):
    return lax.dot_general(left, right, (((0,), (0,)), ((), ())), preferred_element_type=F32)


def from_row(values):
    return lax.ppermute(values, "row", SWAP)


def from_col(values):
    return lax.ppermute(values, "col", SWAP)


def pick(first, values, axis):
    size = values.shape[axis] // 2
    low = lax.slice_in_dim(values, 0, size, axis=axis)
    high = lax.slice_in_dim(values, size, 2 * size, axis=axis)
    return jnp.where(first == 0, low, high), jnp.where(first == 0, high, low)


def ordered(index, mine, other, axis):
    return jnp.where(
        index == 0,
        jnp.concatenate([mine, other], axis=axis),
        jnp.concatenate([other, mine], axis=axis),
    )


def both_tokens(col, own):
    return ordered(col, own, from_col(own), 0)


def swap_halves(values):
    half = values.shape[1] // 2
    return jnp.concatenate([values[:, half:], values[:, :half]], axis=1)


def own_token_sum(col, partial_sum):
    keep, send = pick(col, partial_sum, 0)
    return keep + from_col(send.astype(BF16)).astype(F32)


def dp_pairs(bit):
    count = lax.axis_size("dp")
    return [(i, i ^ (1 << bit)) for i in range(count)]


def halving(values, axis, bits):
    index = lax.axis_index("dp")
    for bit in bits:
        own = (index >> bit) & 1
        half = values.shape[axis] // 2
        send = lax.dynamic_slice_in_dim(values, (1 - own) * half, half, axis)
        keep = lax.dynamic_slice_in_dim(values, own * half, half, axis)
        received = lax.ppermute(send, "dp", dp_pairs(bit))
        values = (keep.astype(F32) + received.astype(F32)).astype(BF16)
    return values


def doubling(values, axis, bits):
    index = lax.axis_index("dp")
    for bit in reversed(bits):
        received = lax.ppermute(values, "dp", dp_pairs(bit))
        values = ordered((index >> bit) & 1, values, received, axis)
    return values


def bit_orders():
    count = lax.axis_size("dp").bit_length() - 1
    first = list(range(count))
    second = [1, 0] + first[2:] if count > 1 else first
    return first, second


def parts_of(values, axis):
    size = values.shape[axis]
    cut = size * 2 // 3
    orders = bit_orders()
    return (
        (lax.slice_in_dim(values, 0, cut, axis=axis), orders[0]),
        (lax.slice_in_dim(values, cut, size, axis=axis), orders[1]),
    )


def reduce_rows_first(values):
    done = []
    for part, order in parts_of(values, 1):
        reduced = halving(part, 1, order)
        both = jnp.stack([reduced[0], from_row(reduced[1])])
        done.append(doubling(both, 1, order))
    return jnp.concatenate(done, axis=1)


def reduce_columns(values):
    half = values.shape[1] // 2
    done = []
    for part, order in parts_of(values, 0):
        reduced = halving(part, 0, order)
        both = jnp.stack([reduced[:, :half], from_row(reduced[:, half:])])
        done.append(doubling(both, 1, order))
    return jnp.concatenate(done, axis=1)


def reduce_small(values):
    for bit in bit_orders()[0]:
        values = values + lax.ppermute(values, "dp", dp_pairs(bit))
    return values


def norm_forward(values, gain_vec, shift_vec):
    mean = jnp.mean(values, axis=1, keepdims=True)
    centered = values - mean
    variance = jnp.mean(centered * centered, axis=1, keepdims=True)
    inverse = lax.rsqrt(variance + EPSILON)
    unit = centered * inverse
    return (unit * gain_vec + shift_vec).astype(BF16), unit, inverse


def heads_of(values):
    return values.reshape(values.shape[0], -1, HEAD_DIM)


def scores_of(query, keys_all, allowed):
    raw = jnp.einsum("qhd,khd->hqk", query, keys_all, preferred_element_type=F32)
    return jnp.where(allowed[None], raw * HEAD_DIM ** (-0.5), MASKED)


def attention_forward(query, keys_all, values_all, allowed):
    scores = scores_of(query, keys_all, allowed)
    largest = jnp.max(scores, axis=-1, keepdims=True)
    weights = jnp.exp(scores - largest)
    summed = jnp.sum(weights, axis=-1, keepdims=True)
    probs = (weights / summed).astype(BF16)
    mixed = jnp.einsum("hqk,khd->qhd", probs, values_all, preferred_element_type=F32)
    return mixed, largest + jnp.log(summed)


def attention_backward(query, keys_all, values_all, grad_mixed, allowed, log_totals):
    scores = scores_of(query, keys_all, allowed)
    probs = jnp.exp(scores - log_totals)
    grad_probs = jnp.einsum("qhd,khd->hqk", grad_mixed, values_all, preferred_element_type=F32)
    inner = jnp.sum(probs * grad_probs, axis=-1, keepdims=True)
    grad_raw = (probs * (grad_probs - inner) * HEAD_DIM ** (-0.5)).astype(BF16)
    grad_q = jnp.einsum("hqk,khd->qhd", grad_raw, keys_all, preferred_element_type=F32)
    grad_k = jnp.einsum("hqk,qhd->khd", grad_raw, query, preferred_element_type=F32)
    grad_v = jnp.einsum(
        "hqk,qhd->khd", probs.astype(BF16), grad_mixed, preferred_element_type=F32
    )
    return grad_q, grad_k, grad_v


def body(
    tokens,
    out_grad,
    seq_lengths,
    w_query,
    w_key,
    w_value,
    w_out,
    w_up,
    w_down,
    b_query,
    b_value,
    b_out,
    b_up,
    b_down,
    gain_attn,
    shift_attn,
    gain_mlp,
    shift_mlp,
):
    row = lax.axis_index("row")
    col = lax.axis_index("col")
    own_rows, half = tokens.shape
    width = 2 * half
    group_rows = 2 * own_rows

    positions = jnp.arange(group_rows, dtype=jnp.int32)
    lengths = seq_lengths[0]
    live_total = lengths[0] + lengths[1]
    documents = (positions >= lengths[0]).astype(jnp.int32) + (positions >= live_total).astype(
        jnp.int32
    )
    allowed = (documents[:, None] == documents[None, :]) & (
        positions[None, :] <= positions[:, None]
    )
    own_positions = col * own_rows + jnp.arange(own_rows, dtype=jnp.int32)
    live_rows = (own_positions < live_total)[:, None]

    vectors = jnp.stack([gain_attn, shift_attn, b_out, gain_mlp, shift_mlp])
    tokens_other = from_row(tokens)
    vectors = jnp.concatenate([vectors, from_row(vectors)], axis=1).astype(F32)
    gain_a, shift_a, bias_o, gain_m, shift_m = [vectors[i : i + 1] for i in range(5)]

    kept, sent = zip(*[pick(row, w, 1) for w in (w_query, w_key, w_value)])
    kept, sent = jnp.concatenate(kept, axis=1), jnp.concatenate(sent, axis=1)
    w_qkv = jnp.concatenate([kept, from_row(sent)], axis=0)
    kept, sent = pick(row, w_out, 0)
    w_o = jnp.concatenate([kept, from_row(sent)], axis=1)
    kept, sent = pick(row, w_up, 1)
    w_u = jnp.concatenate([kept, from_row(sent)], axis=0)
    grad_other = from_row(out_grad)
    kept, sent = pick(row, w_down, 0)
    w_d = jnp.concatenate([kept, from_row(sent)], axis=1)

    residual = jnp.concatenate([tokens, tokens_other], axis=1).astype(F32)
    normed, unit_attn, inverse_attn = norm_forward(residual, gain_a, shift_a)
    normed_all = both_tokens(col, normed)

    third = w_query.shape[1] // 2
    zeros = jnp.zeros_like(b_query)
    projected = dot(normed_all, w_qkv) + jnp.concatenate([b_query, zeros, b_value]).astype(F32)
    projected = projected.astype(BF16)
    query, keys_all, values_all = [
        heads_of(projected[:, i * third : (i + 1) * third]) for i in range(3)
    ]
    mixed, log_totals = attention_forward(query, keys_all, values_all, allowed)
    mixed = mixed.astype(BF16).reshape(group_rows, -1)

    branch = own_token_sum(col, dot(mixed, w_o))
    middle = residual + (branch + swap_halves(from_row(branch.astype(BF16))).astype(F32) + bias_o)
    normed_mlp, unit_mlp, inverse_mlp = norm_forward(middle, gain_m, shift_m)
    normed_mlp_all = both_tokens(col, normed_mlp)
    pre_act = dot(normed_mlp_all, w_u) + b_up.astype(F32)
    hidden_wide, gelu_pullback = jax.vjp(lambda u: jax.nn.gelu(u, approximate=True), pre_act)
    hidden = hidden_wide.astype(BF16)

    top = jnp.where(live_rows, jnp.concatenate([out_grad, grad_other], axis=1), 0)
    top_all = both_tokens(col, top)
    grad_down = reduce_columns(dot_tn(hidden, top_all).astype(BF16))

    grad_pre = gelu_pullback(dot_nt(top_all, w_d))[0].astype(BF16)
    grad_up = dot_tn(normed_mlp_all, grad_pre).astype(BF16)
    grad_up = reduce_rows_first(grad_up.reshape(2, half, -1))

    grad_normed = own_token_sum(col, dot_nt(grad_pre, w_u))
    grad_normed = grad_normed + swap_halves(from_row(grad_normed.astype(BF16))).astype(F32)
    scaled = grad_normed * gain_m
    mean_plain = jnp.mean(scaled, axis=1, keepdims=True)
    mean_unit = jnp.mean(scaled * unit_mlp, axis=1, keepdims=True)
    grad_middle = top.astype(F32) + inverse_mlp * (scaled - mean_plain - unit_mlp * mean_unit)
    grad_gain_mlp = jnp.sum((grad_normed * unit_mlp)[:, :half], axis=0)
    grad_shift_mlp = jnp.sum(grad_normed[:, :half], axis=0)

    branch_grad = grad_middle.astype(BF16)
    branch_all = both_tokens(col, branch_grad)
    grad_out = dot_tn(branch_all, mixed)
    grad_mixed = heads_of(dot_nt(branch_all, w_o).astype(BF16))
    grad_q, grad_k, grad_v = attention_backward(
        query, keys_all, values_all, grad_mixed, allowed, log_totals
    )
    grad_qkv = jnp.concatenate(
        [part.astype(BF16).reshape(group_rows, -1) for part in (grad_q, grad_k, grad_v)], axis=1
    )
    attention_grads = jnp.concatenate([dot_tn(normed_all, grad_qkv), grad_out], axis=1)
    attention_grads = reduce_rows_first(attention_grads.astype(BF16).reshape(2, half, -1))

    grad_normed = own_token_sum(col, dot_nt(grad_qkv, w_qkv))
    scaled = grad_normed * gain_a
    sums = jnp.stack([jnp.sum(scaled, axis=1), jnp.sum(scaled * unit_attn, axis=1)])
    sums = (sums + from_row(sums)) / width
    grad_normed = grad_normed[:, :half] + from_row(grad_normed[:, half:].astype(BF16)).astype(F32)
    unit_own = unit_attn[:, :half]
    grad_in = inverse_attn * (
        grad_normed * gain_a[:, :half] - sums[0][:, None] - unit_own * sums[1][:, None]
    )
    input_grad = (grad_middle[:, :half] + grad_in).astype(BF16)
    grad_gain_attn = jnp.sum(grad_normed * unit_own, axis=0)
    grad_shift_attn = jnp.sum(grad_normed, axis=0)

    raised = own_token_sum(col, dot(hidden, w_d))
    raised = raised[:, :half] + from_row(raised[:, half:].astype(BF16)).astype(F32)
    output = (middle[:, :half] + raised + b_down.astype(F32)).astype(BF16)

    halves = jnp.concatenate([grad_gain_attn, grad_shift_attn, grad_gain_mlp, grad_shift_mlp])
    halves = halves + from_col(halves)
    wide_sums = jnp.sum(grad_qkv.astype(F32), axis=0)
    small = jnp.concatenate(
        [
            halves,
            wide_sums[:third],
            wide_sums[2 * third :],
            jnp.sum(branch_all[:, :half].astype(F32), axis=0),
            jnp.sum(grad_pre.astype(F32), axis=0),
            jnp.sum(top_all[:, :half].astype(F32), axis=0),
        ]
    )
    small = reduce_small(small)
    sizes = [half] * 4 + [third, third, half, b_up.shape[0], half]
    vectors, begin = [], 0
    for size in sizes:
        vectors.append(small[begin : begin + size])
        begin += size
    g_gain_a, g_shift_a, g_gain_m, g_shift_m, g_b_query, g_b_value, g_b_out, g_b_up, g_b_down = (
        vectors
    )

    def side_by_side(values):
        return ordered(row, values[0], values[1], 1).astype(F32)

    grad_query, grad_key, grad_value, grad_out = [
        side_by_side(attention_grads[:, :, i * third : (i + 1) * third]) for i in range(4)
    ]
    return (
        output,
        input_grad,
        grad_query,
        grad_key,
        grad_value,
        grad_out.T,
        side_by_side(grad_up),
        ordered(row, grad_down[0], grad_down[1], 0).astype(F32),
        g_b_query,
        g_b_value,
        g_b_out,
        g_b_up,
        g_b_down,
        g_gain_a,
        g_shift_a,
        g_gain_m,
        g_shift_m,
    )


def solution(mesh):
    return jax.shard_map(
        body,
        mesh=mesh,
        in_specs=(
            P(("dp", "col"), "row"),
            P(("dp", "col"), "row"),
            P("dp", None),
            P("row", "col"),
            P("row", "col"),
            P("row", "col"),
            P("col", "row"),
            P("row", "col"),
            P("col", "row"),
            P(("col", "row")),
            P(("col", "row")),
            P("row"),
            P(("col", "row")),
            P("row"),
            P("row"),
            P("row"),
            P("row"),
            P("row"),
        ),
        out_specs=(
            P(("dp", "col"), "row"),
            P(("dp", "col"), "row"),
            P("row", "col"),
            P("row", "col"),
            P("row", "col"),
            P("col", "row"),
            P("row", "col"),
            P("col", "row"),
            P(("col", "row")),
            P(("col", "row")),
            P("row"),
            P(("col", "row")),
            P("row"),
            P("row"),
            P("row"),
            P("row"),
            P("row"),
        ),
        check_vma=False,
    )
```

time: 590 us -> 281 us (0.48)
  waiting for transfers between devices: 364 us -> 126 us
  blocking collectives: 110 us -> 0 us
  starting transfers between devices: 0.72 us -> 65.3 us
  matrix products: 55.2 us -> 31.9 us
  between operations: 15.7 us -> 3.57 us
  other arithmetic: 29.1 us -> 40.4 us
    psum x1 -> x0, waiting for transfers between devices: 191 us -> none  [body(): lax.psum((grad_query, grad_key, grad_value, grad_out, grad_up, grad_down,...]
    ppermute x0 -> x66, waiting for transfers between devices: none -> 126 us  [the longest x18 55 us: halving(): received = lax.ppermute(send, 'dp', dp_pairs(bit))]
    reduce_scatter x10 -> x0, waiting for transfers between devices: 119 us -> none  [the longest x2 41.3 us: wide_sum(): lax.psum_scatter(partial_sum.astype(jnp.bfloat16), 'row', scatter_dimensi...]
    psum x8 -> x0, blocking collectives: 73.3 us -> none  [the longest x1 39.6 us: body(): lax.psum((grad_query, grad_key, grad_value, grad_out, grad_up, grad_down,...]
    ppermute x0 -> x66, starting transfers between devices: none -> 65.3 us  [the longest x18 24.6 us: halving(): received = lax.ppermute(send, 'dp', dp_pairs(bit))]
    all_gather x2 -> x0, waiting for transfers between devices: 52.6 us -> none  [wide_gather(): return lax.all_gather(pieces, 'row', axis=1, tiled=True)]
    all_gather x8 -> x0, blocking collectives: 36.5 us -> none  [the longest x4 8.34 us: token_gather(): return lax.all_gather(pieces, 'col', axis=0, tiled=True)]
    dot_general x23 -> x17, matrix products: 52.8 us -> 29.7 us  [the longest x4 7.39 us: dot_nt(): lax.dot_general(left, right, (((1,), (1,)), ((), ())), preferred_element_...]
  transfers between devices with their start and end apart: 13 -> 66, of which waited for: 12 -> 29; matrix products, arithmetic and copies ran while one was open for 7% -> 25% of each run, Pallas kernels for 0% -> 0%
where the time goes in v1:
time: 281 us; the launch traced here: 280 us
  waiting for transfers between devices  126 us (45%)
  starting transfers between devices  65.3 us (23%)
  other arithmetic  40.4 us (14%)
  matrix products  31.9 us (11%)
  local copies, waits for them, and re-layouts  12.5 us (4%)
  between operations  3.57 us (1%)
    ppermute x18, waiting for transfers between devices, halving(): received = lax.ppermute(send, 'dp', dp_pairs(bit))  55 us
    ppermute x18, waiting for transfers between devices, from_row(): return lax.ppermute(values, 'row', SWAP)  45.6 us
    ppermute x18, starting transfers between devices, halving(): received = lax.ppermute(send, 'dp', dp_pairs(bit))  24.6 us
    ppermute x18, waiting for transfers between devices, doubling(): received = lax.ppermute(values, 'dp', dp_pairs(bit))  21 us
    ppermute x18, starting transfers between devices, doubling(): received = lax.ppermute(values, 'dp', dp_pairs(bit))  18.7 us
    ppermute x18, starting transfers between devices, from_row(): return lax.ppermute(values, 'row', SWAP)  17.5 us
    select_n x20, other arithmetic, ordered(): jnp.where(index == 0, jnp.concatenate([mine, other], axis=axis), jnp.conc...  8.8 us
    dot_general x4, matrix products, dot_nt(): lax.dot_general(left, right, (((1,), (1,)), ((), ())), preferred_element_...  7.39 us
  transfers between devices with their start and end apart: 66, of which 29 were waited for; matrix products, arithmetic and copies ran while one was open for 25% of the time, Pallas kernels for 0%

profile of v1, /device:TPU:0, one launch (start us, length us, event | category | flops | bytes accessed | tf_op | source)
XLA Modules:
  0.0 280.0 jit_solution(5799285130754878203)
XLA Ops:
  4.2 3.0 %collective-permute-start.1 = (bf16[5,384]{1,0:T(8,128)(2,1)S(1)}, bf16[5,384]{1,0:T(8,128)(2,1)S(1)}, u32[]{:S(2)}, u32[]{:S(2)}) collective-permute-start(bf16[5,384]{1,0:T(8,128)(2,1)S(1)} %stack.74), channel_id=1, source_target_pairs={{0,2},{2,0},{1,3},{3,1},{4,6},{6,4},{5,7},{7,5},{8,10},{10,8},{9,1... | collective-permute-start | bytes 11528 | tf_op jit(solution)/shard_map/ppermute | solution.py:27
  17.2 10.3 %collective-permute-done.3 = bf16[384,576]{1,0:T(8,128)(2,1)S(1)} collective-permute-done((bf16[384,576]{1,0:T(8,128)(2,1)S(1)}, bf16[384,576]{1,0:T(8,128)(2,1)S(1)}, u32[]{:S(2)}, u32[]{:S(2)}) %collective-permute-start.3) | collective-permute-done | bytes 442400 | tf_op jit(solution)/shard_map/ppermute | solution.py:27
  44.7 16.7 %collective-permute-done.6 = bf16[256,768]{1,0:T(8,128)(2,1)} collective-permute-done((bf16[256,768]{1,0:T(8,128)(2,1)}, bf16[256,768]{1,0:T(8,128)(2,1)}, u32[]{:S(2)}, u32[]{:S(2)}) %collective-permute-start.6) | collective-permute-done | bytes 393248 | tf_op jit(solution)/shard_map/ppermute | solution.py:27
  68.1 5.5 %collective-permute-done.9 = bf16[768,384]{1,0:T(8,128)(2,1)} collective-permute-done((bf16[768,384]{1,0:T(8,128)(2,1)}, bf16[768,384]{1,0:T(8,128)(2,1)}, u32[]{:S(2)}, u32[]{:S(2)}) %collective-permute-start.9) | collective-permute-done | bytes 589856 | tf_op jit(solution)/shard_map/ppermute | solution.py:27
  73.6 3.3 %convert_reduce_fusion = (f32[768]{0:T(1024)}, bf16[512,768]{1,0:T(8,128)(2,1)S(1)}) fusion(f32[512,768]{1,0:T(8,128)S(1)} %convolution_add_fusion, bf16[512,768]{1,0:T(8,128)(2,1)S(1)} %maximum_select_fusion.4, bf16[768,384]{1,0:T(8,128)(2,1)} %collective-permute-done.9, bf16[768,384]{1,0:T(8,128)(2,1)S(1)} %copy-done.19), kind=kOutput, calls=%fused_computation.29 | convolution fusion | flops 614989056 | bytes 4328448 | tf_op jit(solution)/shard_map/dot_general | solution.py:19
  81.1 2.3 fusion.48
  91.2 16.5 %collective-permute-done.42 = bf16[2,32,768]{2,1,0:T(8,128)(2,1)S(1)} collective-permute-done((bf16[2,32,768]{2,1,0:T(8,128)(2,1)S(1)}, bf16[2,32,768]{2,1,0:T(8,128)(2,1)S(1)}, u32[]{:S(2)}, u32[]{:S(2)}) %collective-permute-start.42) | collective-permute-done | bytes 98336 | tf_op jit(solution)/shard_map/ppermute | solution.py:75
  109.2 3.1 %collective-permute-done.56 = bf16[64,768]{1,0:T(8,128)(2,1)S(1)} collective-permute-done((bf16[64,768]{1,0:T(8,128)(2,1)S(1)}, bf16[64,768]{1,0:T(8,128)(2,1)S(1)}, u32[]{:S(2)}, u32[]{:S(2)}) %collective-permute-start.56) | collective-permute-done | bytes 98336 | tf_op jit(solution)/shard_map/ppermute | solution.py:75
  112.3 2.6 collective-permute-start.43
  114.9 2.3 collective-permute-done.43
  117.3 2.6 collective-permute-start.57
  119.9 2.3 collective-permute-done.57
  122.7 3.4 %collective-permute-done.44 = bf16[16,768]{1,0:T(8,128)(2,1)S(1)} collective-permute-done((bf16[16,768]{1,0:T(8,128)(2,1)S(1)}, bf16[16,768]{1,0:T(8,128)(2,1)S(1)}, u32[]{:S(2)}, u32[]{:S(2)}) %collective-permute-start.44) | collective-permute-done | bytes 24608 | tf_op jit(solution)/shard_map/ppermute | solution.py:27
  126.5 3.6 %collective-permute-done.58 = bf16[32,384]{1,0:T(8,128)(2,1)S(1)} collective-permute-done((bf16[32,384]{1,0:T(8,128)(2,1)S(1)}, bf16[32,384]{1,0:T(8,128)(2,1)S(1)}, u32[]{:S(2)}, u32[]{:S(2)}) %collective-permute-start.58) | collective-permute-done | bytes 24608 | tf_op jit(solution)/shard_map/ppermute | solution.py:27
  130.1 2.7 collective-permute-start.45
  139.6 3.1 %collective-permute-done.46 = bf16[2,32,768]{2,1,0:T(8,128)(2,1)S(1)} collective-permute-done((bf16[2,32,768]{2,1,0:T(8,128)(2,1)S(1)}, bf16[2,32,768]{2,1,0:T(8,128)(2,1)S(1)}, u32[]{:S(2)}, u32[]{:S(2)}) %collective-permute-start.46) | collective-permute-done | bytes 98336 | tf_op jit(solution)/shard_map/ppermute | solution.py:83
  144.3 3.1 %collective-permute-done.60 = bf16[2,64,384]{2,1,0:T(8,128)(2,1)S(1)} collective-permute-done((bf16[2,64,384]{2,1,0:T(8,128)(2,1)S(1)}, bf16[2,64,384]{2,1,0:T(8,128)(2,1)S(1)}, u32[]{:S(2)}, u32[]{:S(2)}) %collective-permute-start.60) | collective-permute-done | bytes 98336 | tf_op jit(solution)/shard_map/ppermute | solution.py:83
  149.6 2.7 collective-permute-start.36
  153.5 3.5 %collective-permute-done.36 = bf16[2,32,768]{2,1,0:T(8,128)(2,1)S(1)} collective-permute-done((bf16[2,32,768]{2,1,0:T(8,128)(2,1)S(1)}, bf16[2,32,768]{2,1,0:T(8,128)(2,1)S(1)}, u32[]{:S(2)}, u32[]{:S(2)}) %collective-permute-start.36) | collective-permute-done | bytes 98336 | tf_op jit(solution)/shard_map/ppermute | solution.py:75
  157.4 5.7 %collective-permute-done.50 = bf16[64,768]{1,0:T(8,128)(2,1)S(1)} collective-permute-done((bf16[64,768]{1,0:T(8,128)(2,1)S(1)}, bf16[64,768]{1,0:T(8,128)(2,1)S(1)}, u32[]{:S(2)}, u32[]{:S(2)}) %collective-permute-start.50) | collective-permute-done | bytes 98336 | tf_op jit(solution)/shard_map/ppermute | solution.py:75
  175.5 4.3 %collective-permute-done.39 = bf16[2,64,768]{2,1,0:T(8,128)(2,1)S(1)} collective-permute-done((bf16[2,64,768]{2,1,0:T(8,128)(2,1)S(1)}, bf16[2,64,768]{2,1,0:T(8,128)(2,1)S(1)}, u32[]{:S(2)}, u32[]{:S(2)}) %collective-permute-start.39) | collective-permute-done | bytes 196640 | tf_op jit(solution)/shard_map/ppermute | solution.py:83
  190.3 5.1 %fusion.36 = bf16[3,64,512]{2,1,0:T(8,128)(2,1)} fusion(bf16[512,3,64]{0,2,1:T(8,128)(2,1)} %bitcast.105, f32[3,512,512]{1,2,0:T(8,128)} %fusion.118, f32[3,512,512]{1,2,0:T(8,128)S(1)} %get-tuple-element.115, f32[3,512]{1,0:T(4,128)} %copy-done.41), kind=kOutput, calls=%fused_computation.69 | convolution fusion | flops 106268672 | bytes 6690816 | tf_op jit(solution)/shard_map/hqk,khd->qhd/dot_general | solution.py:164
  195.4 5.1 %fusion.39 = bf16[3,64,512]{2,1,0:T(8,128)(2,1)} fusion(bf16[512,3,64]{0,2,1:T(8,128)(2,1)} %bitcast.103, f32[3,512,512]{1,2,0:T(8,128)} %fusion.118, f32[3,512,512]{1,2,0:T(8,128)S(1)} %get-tuple-element.115, f32[3,512]{1,0:T(4,128)S(1)} %copy-done.42), kind=kOutput, calls=%fused_computation.70 | convolution fusion | flops 106268672 | bytes 6690816 | tf_op jit(solution)/shard_map/hqk,qhd->khd/dot_general | solution.py:165
  208.9 2.6 collective-permute-done.27
  215.4 6.5 %collective-permute-done.28 = bf16[2,32,768]{2,1,0:T(8,128)(2,1)S(1)} collective-permute-done((bf16[2,32,768]{2,1,0:T(8,128)(2,1)S(1)}, bf16[2,32,768]{2,1,0:T(8,128)(2,1)S(1)}, u32[]{:S(2)}, u32[]{:S(2)}) %collective-permute-start.28) | collective-permute-done | bytes 98336 | tf_op jit(solution)/shard_map/ppermute | solution.py:75
  237.9 5.1 %collective-permute-done.21 = bf16[2,64,768]{2,1,0:T(8,128)(2,1)S(1)} collective-permute-done((bf16[2,64,768]{2,1,0:T(8,128)(2,1)S(1)}, bf16[2,64,768]{2,1,0:T(8,128)(2,1)S(1)}, u32[]{:S(2)}, u32[]{:S(2)}) %collective-permute-start.21) | collective-permute-done | bytes 196640 | tf_op jit(solution)/shard_map/ppermute | solution.py:75
  244.3 4.3 %collective-permute-done.22 = bf16[2,32,768]{2,1,0:T(8,128)(2,1)S(1)} collective-permute-done((bf16[2,32,768]{2,1,0:T(8,128)(2,1)S(1)}, bf16[2,32,768]{2,1,0:T(8,128)(2,1)S(1)}, u32[]{:S(2)}, u32[]{:S(2)}) %collective-permute-start.22) | collective-permute-done | bytes 98336 | tf_op jit(solution)/shard_map/ppermute | solution.py:75
  250.6 2.3 collective-permute-done.23
  254.7 2.5 collective-permute-start.64
  258.6 2.5 collective-permute-start.25
  263.7 4.0 %collective-permute-done.65 = f32[3456]{0:T(1024)S(1)} collective-permute-done((f32[3456]{0:T(1024)S(1)}, f32[3456]{0:T(1024)S(1)}, u32[]{:S(2)}, u32[]{:S(2)}) %collective-permute-start.65) | collective-permute-done | bytes 13856 | tf_op jit(solution)/shard_map/ppermute | solution.py:126
  270.5 5.1 %collective-permute-done.26 = bf16[2,128,768]{2,1,0:T(8,128)(2,1)S(1)} collective-permute-done((bf16[2,128,768]{2,1,0:T(8,128)(2,1)S(1)}, bf16[2,128,768]{2,1,0:T(8,128)(2,1)S(1)}, u32[]{:S(2)}, u32[]{:S(2)}) %collective-permute-start.26) | collective-permute-done | bytes 393248 | tf_op jit(solution)/shard_map/ppermute | solution.py:83
  (410 shorter events, 128.6 us)
Async XLA Ops:
  4.2 10.5 %collective-permute-start.1 = (bf16[5,384]{1,0:T(8,128)(2,1)S(1)}, bf16[5,384]{1,0:T(8,128)(2,1)S(1)}, u32[]{:S(2)}, u32[]{:S(2)}) collective-permute-start(bf16[5,384]{1,0:T(8,128)(2,1)S(1)} %stack.74), channel_id=1, source_target_pairs={{0,2},{2,0},{1,3},{3,1},{4,6},{6,4},{5,7},{7,5},{8,10},{10,8},{9,1... | collective-permute-start | bytes 11528 | tf_op jit(solution)/shard_map/ppermute | solution.py:27
  9.0 21.4 %collective-permute-start.4 = (bf16[192,384]{1,0:T(8,128)(2,1)}, bf16[192,384]{1,0:T(8,128)(2,1)}, u32[]{:S(2)}, u32[]{:S(2)}) collective-permute-start(bf16[192,384]{1,0:T(8,128)(2,1)} %get-tuple-element.81), channel_id=1, source_target_pairs={{0,2},{2,0},{1,3},{3,1},{4,6},{6,4},{5,7},{7,5},{8,10},{10,8},{9,1... | collective-permute-start | bytes 442376 | tf_op jit(solution)/shard_map/ppermute | solution.py:27
  12.6 14.9 %collective-permute-start.3 = (bf16[384,576]{1,0:T(8,128)(2,1)S(1)}, bf16[384,576]{1,0:T(8,128)(2,1)S(1)}, u32[]{:S(2)}, u32[]{:S(2)}) collective-permute-start(bf16[384,576]{1,0:T(8,128)(2,1)S(1)} %pad_maximum_fusion.12), channel_id=1, source_target_pairs={{0,2},{2,0},{1,3},{3,1},{4,6},{6,4},{5,7},{7,5},{8,10},{10,8},{9,1... | collective-permute-start | bytes 1327112 | tf_op jit(solution)/shard_map/ppermute | solution.py:27
  16.1 11.4 %collective-permute-start.2 = (bf16[256,768]{1,0:T(8,128)(2,1)S(1)}, bf16[256,768]{1,0:T(8,128)(2,1)S(1)}, u32[]{:S(2)}, u32[]{:S(2)}) collective-permute-start(bf16[256,768]{1,0:T(8,128)(2,1)S(1)} %add_convert_fusion.4), channel_id=1, source_target_pairs={{0,1},{1,0},{2,3},{3,2},{4,5},{5,4},{6,7},{7,6},{8,9},{9,8},{10,11... | collective-permute-start | bytes 1179656 | tf_op jit(solution)/shard_map/ppermute | solution.py:31
  32.3 11.2 %collective-permute-start.12 = (bf16[256,384]{1,0:T(8,128)(2,1)}, bf16[256,384]{1,0:T(8,128)(2,1)}, u32[]{:S(2)}, u32[]{:S(2)}) collective-permute-start(bf16[256,384]{1,0:T(8,128)(2,1)} %param.19), channel_id=1, source_target_pairs={{0,2},{2,0},{1,3},{3,1},{4,6},{6,4},{5,7},{7,5},{8,10},{10,8},{9,1... | collective-permute-start | bytes 589832 | tf_op jit(solution)/shard_map/ppermute | solution.py:27
  33.9 31.6 %collective-permute-start.8 = (bf16[384,768]{1,0:T(8,128)(2,1)}, bf16[384,768]{1,0:T(8,128)(2,1)}, u32[]{:S(2)}, u32[]{:S(2)}) collective-permute-start(bf16[384,768]{1,0:T(8,128)(2,1)} %get-tuple-element.69), channel_id=1, source_target_pairs={{0,2},{2,0},{1,3},{3,1},{4,6},{6,4},{5,7},{7,5},{8,10},{10,8},{9,1... | collective-permute-start | bytes 1769480 | tf_op jit(solution)/shard_map/ppermute | solution.py:27
  36.4 25.1 %collective-permute-start.6 = (bf16[256,768]{1,0:T(8,128)(2,1)}, bf16[256,768]{1,0:T(8,128)(2,1)}, u32[]{:S(2)}, u32[]{:S(2)}) collective-permute-start(bf16[256,768]{1,0:T(8,128)(2,1)} %fusion.84), channel_id=1, source_target_pairs={{0,2},{2,0},{1,3},{3,1},{4,6},{6,4},{5,7},{7,5},{8,10},{10,8},{9,1... | collective-permute-start | bytes 1179656 | tf_op jit(solution)/shard_map/ppermute | solution.py:27
  37.9 35.7 %collective-permute-start.9 = (bf16[768,384]{1,0:T(8,128)(2,1)}, bf16[768,384]{1,0:T(8,128)(2,1)}, u32[]{:S(2)}, u32[]{:S(2)}) collective-permute-start(bf16[768,384]{1,0:T(8,128)(2,1)} %get-tuple-element.71), channel_id=1, source_target_pairs={{0,2},{2,0},{1,3},{3,1},{4,6},{6,4},{5,7},{7,5},{8,10},{10,8},{9,1... | collective-permute-start | bytes 1769480 | tf_op jit(solution)/shard_map/ppermute | solution.py:27
  44.6 19.8 %collective-permute-start.13 = (bf16[256,768]{1,0:T(8,128)(2,1)S(1)}, bf16[256,768]{1,0:T(8,128)(2,1)S(1)}, u32[]{:S(2)}, u32[]{:S(2)}) collective-permute-start(bf16[256,768]{1,0:T(8,128)(2,1)S(1)} %maximum_select_fusion.9), channel_id=1, source_target_pairs={{0,1},{1,0},{2,3},{3,2},{4,5},{5,4},{6,7},{7,6},{8,9},{9,8},{10,11... | collective-permute-start | bytes 1179656 | tf_op jit(solution)/shard_map/ppermute | solution.py:31
  78.9 8.5 %collective-permute-start.41 = (bf16[2,64,768]{2,1,0:T(8,128)(2,1)S(1)}, bf16[2,64,768]{2,1,0:T(8,128)(2,1)S(1)}, u32[]{:S(2)}, u32[]{:S(2)}) collective-permute-start(bf16[2,64,768]{2,1,0:T(8,128)(2,1)S(1)} %constant_dynamic-slice_fusion.8), channel_id=1, source_target_pairs={{0,8},{4,12},{8,0},{12,4},{16,24},{20,28},{24,16},{28,20},{1,9},{5... | collective-permute-start | bytes 589832 | tf_op jit(solution)/shard_map/ppermute | solution.py:75
  80.5 9.1 %collective-permute-start.55 = (bf16[128,768]{1,0:T(8,128)(2,1)S(1)}, bf16[128,768]{1,0:T(8,128)(2,1)S(1)}, u32[]{:S(2)}, u32[]{:S(2)}) collective-permute-start(bf16[128,768]{1,0:T(8,128)(2,1)S(1)} %constant_dynamic-slice_fusion.2), channel_id=1, source_target_pairs={{0,8},{4,12},{8,0},{12,4},{16,24},{20,28},{24,16},{28,20},{1,9},{5... | collective-permute-start | bytes 589832 | tf_op jit(solution)/shard_map/ppermute | solution.py:75
  85.4 47.3 %collective-permute-start.14 = (bf16[256,768]{1,0:T(8,128)(2,1)S(1)}, bf16[256,768]{1,0:T(8,128)(2,1)S(1)}, u32[]{:S(2)}, u32[]{:S(2)}) collective-permute-start(bf16[256,768]{1,0:T(8,128)(2,1)S(1)} %select_convert_fusion.1), channel_id=1, source_target_pairs={{0,1},{1,0},{2,3},{3,2},{4,5},{5,4},{6,7},{7,6},{8,9},{9,8},{10,11... | collective-permute-start | bytes 1179656 | tf_op jit(solution)/shard_map/ppermute | solution.py:31
  85.6 47.7 %collective-permute-start.34 = (bf16[2,128,768]{2,1,0:T(8,128)(2,1)S(1)}, bf16[2,128,768]{2,1,0:T(8,128)(2,1)S(1)}, u32[]{:S(2)}, u32[]{:S(2)}) collective-permute-start(bf16[2,128,768]{2,1,0:T(8,128)(2,1)S(1)} %constant_dynamic-slice_fusion.11), channel_id=1, source_target_pairs={{0,4},{4,0},{8,12},{12,8},{16,20},{20,16},{24,28},{28,24},{1,5},{5... | collective-permute-start | bytes 1179656 | tf_op jit(solution)/shard_map/ppermute | solution.py:75
  87.1 46.8 %collective-permute-start.10 = (bf16[256,768]{1,0:T(8,128)(2,1)S(1)}, bf16[256,768]{1,0:T(8,128)(2,1)S(1)}, u32[]{:S(2)}, u32[]{:S(2)}) collective-permute-start(bf16[256,768]{1,0:T(8,128)(2,1)S(1)} %select_convert_fusion.2), channel_id=1, source_target_pairs={{0,1},{1,0},{2,3},{3,2},{4,5},{5,4},{6,7},{7,6},{8,9},{9,8},{10,11... | collective-permute-start | bytes 1179656 | tf_op jit(solution)/shard_map/ppermute | solution.py:31
  87.4 48.6 %collective-permute-start.48 = (bf16[256,768]{1,0:T(8,128)(2,1)S(1)}, bf16[256,768]{1,0:T(8,128)(2,1)S(1)}, u32[]{:S(2)}, u32[]{:S(2)}) collective-permute-start(bf16[256,768]{1,0:T(8,128)(2,1)S(1)} %constant_dynamic-slice_fusion.5), channel_id=1, source_target_pairs={{0,4},{4,0},{8,12},{12,8},{16,20},{20,16},{24,28},{28,24},{1,5},{5... | collective-permute-start | bytes 1179656 | tf_op jit(solution)/shard_map/ppermute | solution.py:75
  89.6 18.0 %collective-permute-start.42 = (bf16[2,32,768]{2,1,0:T(8,128)(2,1)S(1)}, bf16[2,32,768]{2,1,0:T(8,128)(2,1)S(1)}, u32[]{:S(2)}, u32[]{:S(2)}) collective-permute-start(bf16[2,32,768]{2,1,0:T(8,128)(2,1)S(1)} %constant_dynamic-slice_fusion.7), channel_id=1, source_target_pairs={{0,4},{4,0},{8,12},{12,8},{16,20},{20,16},{24,28},{28,24},{1,5},{5... | collective-permute-start | bytes 294920 | tf_op jit(solution)/shard_map/ppermute | solution.py:75
  133.2 35.3 %collective-permute-start.15 = (bf16[256,768]{1,0:T(8,128)(2,1)S(1)}, bf16[256,768]{1,0:T(8,128)(2,1)S(1)}, u32[]{:S(2)}, u32[]{:S(2)}) collective-permute-start(bf16[256,768]{1,0:T(8,128)(2,1)S(1)} %fusion.85), channel_id=1, source_target_pairs={{0,2},{2,0},{1,3},{3,1},{4,6},{6,4},{5,7},{7,5},{8,10},{10,8},{9,1... | collective-permute-start | bytes 1179656 | tf_op jit(solution)/shard_map/ppermute | solution.py:27
  134.0 15.2 %collective-permute-start.35 = (bf16[2,64,768]{2,1,0:T(8,128)(2,1)S(1)}, bf16[2,64,768]{2,1,0:T(8,128)(2,1)S(1)}, u32[]{:S(2)}, u32[]{:S(2)}) collective-permute-start(bf16[2,64,768]{2,1,0:T(8,128)(2,1)S(1)} %constant_dynamic-slice_fusion.10), channel_id=1, source_target_pairs={{0,8},{4,12},{8,0},{12,4},{16,24},{20,28},{24,16},{28,20},{1,9},{5... | collective-permute-start | bytes 589832 | tf_op jit(solution)/shard_map/ppermute | solution.py:75
  136.0 16.4 %collective-permute-start.11 = (bf16[256,384]{1,0:T(8,128)(2,1)S(1)}, bf16[256,384]{1,0:T(8,128)(2,1)S(1)}, u32[]{:S(2)}, u32[]{:S(2)}) collective-permute-start(bf16[256,384]{1,0:T(8,128)(2,1)S(1)} %slice.618), channel_id=1, source_target_pairs={{0,2},{2,0},{1,3},{3,1},{4,6},{6,4},{5,7},{7,5},{8,10},{10,8},{9,1... | collective-permute-start | bytes 589832 | tf_op jit(solution)/shard_map/ppermute | solution.py:27
  137.7 11.9 %collective-permute-start.49 = (bf16[128,768]{1,0:T(8,128)(2,1)S(1)}, bf16[128,768]{1,0:T(8,128)(2,1)S(1)}, u32[]{:S(2)}, u32[]{:S(2)}) collective-permute-start(bf16[128,768]{1,0:T(8,128)(2,1)S(1)} %constant_dynamic-slice_fusion.4), channel_id=1, source_target_pairs={{0,8},{4,12},{8,0},{12,4},{16,24},{20,28},{24,16},{28,20},{1,9},{5... | collective-permute-start | bytes 589832 | tf_op jit(solution)/shard_map/ppermute | solution.py:75
  147.4 16.3 %collective-permute-start.47 = (bf16[2,64,768]{2,1,0:T(8,128)(2,1)S(1)}, bf16[2,64,768]{2,1,0:T(8,128)(2,1)S(1)}, u32[]{:S(2)}, u32[]{:S(2)}) collective-permute-start(bf16[2,64,768]{2,1,0:T(8,128)(2,1)S(1)} %maximum_select_fusion.23), channel_id=1, source_target_pairs={{0,8},{4,12},{8,0},{12,4},{16,24},{20,28},{24,16},{28,20},{1,9},{5... | collective-permute-start | bytes 589832 | tf_op jit(solution)/shard_map/ppermute | solution.py:83
  149.2 15.4 %collective-permute-start.61 = (bf16[2,128,384]{2,1,0:T(8,128)(2,1)S(1)}, bf16[2,128,384]{2,1,0:T(8,128)(2,1)S(1)}, u32[]{:S(2)}, u32[]{:S(2)}) collective-permute-start(bf16[2,128,384]{2,1,0:T(8,128)(2,1)S(1)} %maximum_select_fusion.25), channel_id=1, source_target_pairs={{0,8},{4,12},{8,0},{12,4},{16,24},{20,28},{24,16},{28,20},{1,9},{5... | collective-permute-start | bytes 589832 | tf_op jit(solution)/shard_map/ppermute | solution.py:83
  152.4 10.7 %collective-permute-start.50 = (bf16[64,768]{1,0:T(8,128)(2,1)S(1)}, bf16[64,768]{1,0:T(8,128)(2,1)S(1)}, u32[]{:S(2)}, u32[]{:S(2)}) collective-permute-start(bf16[64,768]{1,0:T(8,128)(2,1)S(1)} %constant_dynamic-slice_fusion.3), channel_id=1, source_target_pairs={{0,16},{4,20},{8,24},{12,28},{16,0},{20,4},{24,8},{28,12},{1,17},{... | collective-permute-start | bytes 294920 | tf_op jit(solution)/shard_map/ppermute | solution.py:75
  170.1 14.2 %collective-permute-start.16 = (bf16[256,768]{1,0:T(8,128)(2,1)S(1)}, bf16[256,768]{1,0:T(8,128)(2,1)S(1)}, u32[]{:S(2)}, u32[]{:S(2)}) collective-permute-start(bf16[256,768]{1,0:T(8,128)(2,1)S(1)} %get-tuple-element.48), channel_id=1, source_target_pairs={{0,1},{1,0},{2,3},{3,2},{4,5},{5,4},{6,7},{7,6},{8,9},{9,8},{10,11... | collective-permute-start | bytes 1179656 | tf_op jit(solution)/shard_map/ppermute | solution.py:31
  180.7 42.9 %collective-permute-start.40 = (bf16[2,128,768]{2,1,0:T(8,128)(2,1)}, bf16[2,128,768]{2,1,0:T(8,128)(2,1)}, u32[]{:S(2)}, u32[]{:S(2)}) collective-permute-start(bf16[2,128,768]{2,1,0:T(8,128)(2,1)} %maximum_select_fusion.12), channel_id=1, source_target_pairs={{0,4},{4,0},{8,12},{12,8},{16,20},{20,16},{24,28},{28,24},{1,5},{5... | collective-permute-start | bytes 1179656 | tf_op jit(solution)/shard_map/ppermute | solution.py:83
  183.0 29.1 %collective-permute-start.54 = (bf16[2,256,384]{2,1,0:T(8,128)(2,1)}, bf16[2,256,384]{2,1,0:T(8,128)(2,1)}, u32[]{:S(2)}, u32[]{:S(2)}) collective-permute-start(bf16[2,256,384]{2,1,0:T(8,128)(2,1)} %maximum_select_fusion.14), channel_id=1, source_target_pairs={{0,4},{4,0},{8,12},{12,8},{16,20},{20,16},{24,28},{28,24},{1,5},{5... | collective-permute-start | bytes 1179656 | tf_op jit(solution)/shard_map/ppermute | solution.py:83
  208.2 25.1 %collective-permute-start.17 = (bf16[256,768]{1,0:T(8,128)(2,1)S(1)}, bf16[256,768]{1,0:T(8,128)(2,1)S(1)}, u32[]{:S(2)}, u32[]{:S(2)}) collective-permute-start(bf16[256,768]{1,0:T(8,128)(2,1)S(1)} %select_convert_fusion), channel_id=1, source_target_pairs={{0,1},{1,0},{2,3},{3,2},{4,5},{5,4},{6,7},{7,6},{8,9},{9,8},{10,11... | collective-permute-start | bytes 1179656 | tf_op jit(solution)/shard_map/ppermute | solution.py:31
  208.3 27.7 %collective-permute-start.20 = (bf16[2,128,768]{2,1,0:T(8,128)(2,1)S(1)}, bf16[2,128,768]{2,1,0:T(8,128)(2,1)S(1)}, u32[]{:S(2)}, u32[]{:S(2)}) collective-permute-start(bf16[2,128,768]{2,1,0:T(8,128)(2,1)S(1)} %constant_dynamic-slice_fusion.16), channel_id=1, source_target_pairs={{0,4},{4,0},{8,12},{12,8},{16,20},{20,16},{24,28},{28,24},{1,5},{5... | collective-permute-start | bytes 1179656 | tf_op jit(solution)/shard_map/ppermute | solution.py:75
  211.5 10.3 %collective-permute-start.28 = (bf16[2,32,768]{2,1,0:T(8,128)(2,1)S(1)}, bf16[2,32,768]{2,1,0:T(8,128)(2,1)S(1)}, u32[]{:S(2)}, u32[]{:S(2)}) collective-permute-start(bf16[2,32,768]{2,1,0:T(8,128)(2,1)S(1)} %constant_dynamic-slice_fusion.13), channel_id=1, source_target_pairs={{0,4},{4,0},{8,12},{12,8},{16,20},{20,16},{24,28},{28,24},{1,5},{5... | collective-permute-start | bytes 294920 | tf_op jit(solution)/shard_map/ppermute | solution.py:75
  231.6 21.6 %collective-permute-start.31 = (bf16[2,16,768]{2,1,0:T(8,128)(2,1)}, bf16[2,16,768]{2,1,0:T(8,128)(2,1)}, u32[]{:S(2)}, u32[]{:S(2)}) collective-permute-start(bf16[2,16,768]{2,1,0:T(8,128)(2,1)} %pad_maximum_fusion.23), channel_id=1, source_target_pairs={{0,16},{4,20},{8,24},{12,28},{16,0},{20,4},{24,8},{28,12},{1,17},{... | collective-permute-start | bytes 147464 | tf_op jit(solution)/shard_map/ppermute | solution.py:83
  254.1 9.5 %collective-permute-start.32 = (bf16[2,32,768]{2,1,0:T(8,128)(2,1)S(1)}, bf16[2,32,768]{2,1,0:T(8,128)(2,1)S(1)}, u32[]{:S(2)}, u32[]{:S(2)}) collective-permute-start(bf16[2,32,768]{2,1,0:T(8,128)(2,1)S(1)} %maximum_select_fusion.30), channel_id=1, source_target_pairs={{0,4},{4,0},{8,12},{12,8},{16,20},{20,16},{24,28},{28,24},{1,5},{5... | collective-permute-start | bytes 294920 | tf_op jit(solution)/shard_map/ppermute | solution.py:83
  258.6 9.1 %collective-permute-start.25 = (bf16[2,64,768]{2,1,0:T(8,128)(2,1)S(1)}, bf16[2,64,768]{2,1,0:T(8,128)(2,1)S(1)}, u32[]{:S(2)}, u32[]{:S(2)}) collective-permute-start(bf16[2,64,768]{2,1,0:T(8,128)(2,1)S(1)} %maximum_select_fusion.20), channel_id=1, source_target_pairs={{0,8},{4,12},{8,0},{12,4},{16,24},{20,28},{24,16},{28,20},{1,9},{5... | collective-permute-start | bytes 589832 | tf_op jit(solution)/shard_map/ppermute | solution.py:83
  (102 other events, 771.8 us)

commit v2 on v1

v2 whole, which is shorter than its diff:
```python
import jax
import jax.numpy as jnp
from jax import lax
from jax.experimental import pallas as pl
from jax.experimental.pallas import tpu as pltpu
from jax.sharding import PartitionSpec as P

HEAD_DIM = 64
EPSILON = 1e-05
MASKED = -1e30
F32 = jnp.float32
BF16 = jnp.bfloat16
SWAP = ((0, 1), (1, 0))
CUBIC = 0.044715
ROOT = 0.7978845608028654
MIB = 1024 * 1024


def dot(left, right):
    return jnp.dot(left, right, preferred_element_type=F32)


def dot_nt(left, right):
    return lax.dot_general(left, right, (((1,), (1,)), ((), ())), preferred_element_type=F32)


def dot_tn(left, right):
    return lax.dot_general(left, right, (((0,), (0,)), ((), ())), preferred_element_type=F32)


def from_row(values):
    return lax.ppermute(values, "row", SWAP)


def from_col(values):
    return lax.ppermute(values, "col", SWAP)


def dp_pairs(bit):
    count = lax.axis_size("dp")
    return [(i, i ^ (1 << bit)) for i in range(count)]


def from_dp(values, bit):
    return lax.ppermute(values, "dp", dp_pairs(bit))


def hold(*values):
    return lax.optimization_barrier(values)


def shape(dims, kind):
    return jax.ShapeDtypeStruct(tuple(dims), kind)


def call(kernel, out_shape, *operands, flops=0, scratch=(), smem=(), vmem=16):
    spaces = [pltpu.SMEM if i in smem else pltpu.VMEM for i in range(len(operands))]
    moved = sum(x.size * x.dtype.itemsize for x in operands)
    return pl.pallas_call(
        kernel,
        out_shape=out_shape,
        in_specs=[pl.BlockSpec(memory_space=space) for space in spaces],
        scratch_shapes=list(scratch),
        compiler_params=pltpu.CompilerParams(vmem_limit_bytes=vmem * MIB),
        cost_estimate=pl.CostEstimate(flops=flops, bytes_accessed=moved, transcendentals=0),
    )(*operands)


def half_rows(index, size):
    return pl.ds(pl.multiple_of(index * size, size), size)


def pack_kernel(gain_a, shift_a, bias, gain_m, shift_m, w_q, w_k, w_v, b_q, b_v, b_u, b_d, vec, loc, kept, sent):
    vec[...] = jnp.zeros_like(vec)
    loc[...] = jnp.zeros_like(loc)
    for i, ref in enumerate((gain_a, shift_a, bias, gain_m, shift_m)):
        vec[i : i + 1] = ref[...].astype(F32).reshape(1, -1)
    third = w_q.shape[1] // 2
    loc[0:1, :third] = b_q[...].astype(F32).reshape(1, -1)
    loc[0:1, 2 * third : 3 * third] = b_v[...].astype(F32).reshape(1, -1)
    loc[1:2, : b_u.shape[0]] = b_u[...].astype(F32).reshape(1, -1)
    loc[2:3, : b_d.shape[0]] = b_d[...].astype(F32).reshape(1, -1)
    first = lax.axis_index("row") == 0
    keeps, sends = [], []
    for ref in (w_q, w_k, w_v):
        low, high = ref[:, :third], ref[:, third:]
        keeps.append(jnp.where(first, low, high))
        sends.append(jnp.where(first, high, low))
    kept[...] = jnp.concatenate(keeps, axis=1)
    sent[...] = jnp.concatenate(sends, axis=1)


def normed_parts(values):
    mean = jnp.mean(values, axis=1, keepdims=True)
    centered = values - mean
    variance = jnp.mean(centered * centered, axis=1, keepdims=True)
    inverse = lax.rsqrt(variance + EPSILON)
    return centered * inverse, inverse


def wide_vector(vec, vec_other, i):
    return jnp.concatenate([vec[i : i + 1], vec_other[i : i + 1]], axis=1)


def first_norm_kernel(tokens, tokens_other, vec, vec_other, normed, unit_out, inverse_out):
    values = jnp.concatenate([tokens[...], tokens_other[...]], axis=1).astype(F32)
    unit, inverse = normed_parts(values)
    gain, shift = wide_vector(vec, vec_other, 0), wide_vector(vec, vec_other, 1)
    normed[...] = (unit * gain + shift).astype(BF16)
    unit_out[...] = unit
    inverse_out[...] = jnp.broadcast_to(inverse, inverse_out.shape)


def head_mask(width, head):
    lanes = lax.broadcasted_iota(jnp.int32, (1, width), 1)
    return lanes // HEAD_DIM == head


def allowed_block(lengths, keys, first_query, count):
    first, second = lengths[0, 0], lengths[0, 0] + lengths[0, 1]
    query = first_query + lax.broadcasted_iota(jnp.int32, (1, count), 1)
    begin = jnp.where(query >= second, second, jnp.where(query >= first, first, 0))
    key = lax.broadcasted_iota(jnp.int32, (keys, count), 0)
    return (key >= begin) & (key <= query)


def forward_kernel(lengths, own, other, w_kept, w_got, loc, norm_out, q_out, k_out, v_out, o_out, lse):
    own_rows, width = own.shape
    half = width // 2
    third = q_out.shape[1]
    col = lax.axis_index("col")
    for ref, at in ((own, col), (other, 1 - col)):
        where = half_rows(at, own_rows)
        values = ref[...]
        norm_out[where] = values
        total = dot(values[:, :half], w_kept[...]) + dot(values[:, half:], w_got[...])
        total = (total + loc[0:1, : 3 * third]).astype(BF16)
        q_out[where] = total[:, :third]
        k_out[where] = total[:, third : 2 * third]
        v_out[where] = total[:, 2 * third :]
    lse[...] = jnp.zeros_like(lse)
    values_t = v_out[...].T
    for begin in (0, own_rows):
        keys = begin + own_rows
        allowed = allowed_block(lengths, keys, begin, own_rows)
        query = q_out[begin:keys] * BF16(HEAD_DIM ** (-0.5))
        parts = []
        for head in range(third // HEAD_DIM):
            key = jnp.where(head_mask(third, head), k_out[:keys], BF16(0))
            scores = jnp.where(allowed, dot_nt(key, query), MASKED)
            largest = jnp.max(scores, axis=0, keepdims=True)
            weights = jnp.exp(scores - largest)
            summed = jnp.sum(weights, axis=0, keepdims=True)
            lse[head : head + 1, begin:keys] = largest + jnp.log(summed)
            mixed = dot(
                values_t[head * HEAD_DIM : (head + 1) * HEAD_DIM, :keys], weights.astype(BF16)
            )
            parts.append(mixed / summed)
        o_out[begin:keys] = jnp.concatenate(parts, axis=0).T.astype(BF16)


def split_tokens(total_of, keep, send, own_rows, col):
    keep[...] = total_of(half_rows(col, own_rows))
    send[...] = total_of(half_rows(1 - col, own_rows)).astype(BF16)


def branch_kernel(mixed, mixed_other, w_mine, w_other, keep, send):
    row, col = lax.axis_index("row"), lax.axis_index("col")
    third = mixed.shape[1]
    own, far = half_rows(row, third), half_rows(1 - row, third)

    def total_of(rows):
        near_rows, far_rows = mixed[rows], mixed_other[rows]
        return jnp.concatenate(
            [dot(near_rows, w[own]) + dot(far_rows, w[far]) for w in (w_mine, w_other)], axis=1
        )

    split_tokens(total_of, keep, send, keep.shape[0], col)


def second_norm_kernel(tokens, tokens_other, keep, got, vec, vec_other, middle, normed, unit_out, inverse_out):
    values = jnp.concatenate([tokens[...], tokens_other[...]], axis=1).astype(F32)
    values = values + (keep[...] + got[...].astype(F32) + wide_vector(vec, vec_other, 2))
    middle[...] = values[:, : middle.shape[1]]
    unit, inverse = normed_parts(values)
    gain, shift = wide_vector(vec, vec_other, 3), wide_vector(vec, vec_other, 4)
    normed[...] = (unit * gain + shift).astype(BF16)
    unit_out[...] = unit
    inverse_out[...] = jnp.broadcast_to(inverse, inverse_out.shape)


def both_sides(got, got_side, axis):
    first = lax.axis_index("dp") % 2 == 0
    low = jnp.where(first, got[...], got_side[...])
    high = jnp.where(first, got_side[...], got[...])
    return jnp.concatenate([low, high], axis=axis)


def up_kernel(own, other, w_up, got, got_side, loc, norm_out, hidden_out, slope_out, w_other_out):
    own_rows, width = own.shape
    half = width // 2
    units = got.shape[1]
    row, col = lax.axis_index("row"), lax.axis_index("col")
    w_mine = w_up[:, pl.ds(pl.multiple_of(row * units, units), units)]
    w_other = both_sides(got, got_side, 0)
    w_other_out[...] = w_other
    for ref, at in ((own, col), (other, 1 - col)):
        where = half_rows(at, own_rows)
        values = ref[...]
        norm_out[where] = values
        u = dot(values[:, :half], w_mine) + dot(values[:, half:], w_other) + loc[1:2, :units]
        squared = u * u
        bent = jnp.tanh(ROOT * (u + CUBIC * (squared * u)))
        raised = 0.5 * (1.0 + bent)
        hidden_out[where] = (u * raised).astype(BF16)
        slope_out[where] = raised + 0.5 * u * (1.0 - bent * bent) * (
            ROOT * (1.0 + (3.0 * CUBIC) * squared)
        )


def split_rows(total, keep, send, bit):
    own = (lax.axis_index("dp") // (1 << bit)) % 2 == 0
    half = keep.shape[-2]
    low, high = total[..., :half, :], total[..., half:, :]
    keep[...] = jnp.where(own, low, high)
    send[...] = jnp.where(own, high, low)


def masked_top(lengths, mine, far, at):
    live = lengths[0, 0] + lengths[0, 1]
    own_rows = mine.shape[0]
    position = at * own_rows + lax.broadcasted_iota(jnp.int32, (own_rows, 1), 0)
    values = jnp.concatenate([mine[...], far[...]], axis=1)
    return jnp.where(position < live, values, BF16(0))


def down_kernel(bit_down, bit_up, lengths, top, top_far, top_col, top_far_col, hidden, slope, normed, w_down, got, got_side,
                w_up, w_up_other, down_keep, down_send, up_keep, up_send, keep, send, sums, w_other_out, top_all, grad_pre):
    own_rows, half = top.shape
    units = hidden.shape[1]
    row, col = lax.axis_index("row"), lax.axis_index("col")
    top_all[half_rows(col, own_rows)] = masked_top(lengths, top, top_far, col)
    top_all[half_rows(1 - col, own_rows)] = masked_top(lengths, top_col, top_far_col, 1 - col)
    top_rows = top_all[...]
    split_rows(dot_tn(hidden[...], top_rows).astype(BF16), down_keep, down_send, bit_down)
    w_other = both_sides(got, got_side, 0)
    w_other_out[...] = w_other
    grad_hidden = dot_nt(top_rows[:, :half], w_down[half_rows(row, units)]) + dot_nt(
        top_rows[:, half:], w_other
    )
    grads = (grad_hidden * slope[...]).astype(BF16)
    grad_pre[...] = grads
    w_mine = w_up[:, pl.ds(pl.multiple_of(row * units, units), units)]

    def total_of(rows):
        values = grad_pre[rows]
        return jnp.concatenate([dot_nt(values, w_mine), dot_nt(values, w_up_other[...])], axis=1)

    split_tokens(total_of, keep, send, own_rows, col)
    total = dot_tn(normed[...], grads).astype(BF16)
    split_rows(total.reshape(2, half, units), up_keep, up_send, bit_up)
    sums[...] = jnp.zeros_like(sums)
    sums[0:1] = jnp.sum(grads.astype(F32), axis=0, keepdims=True)
    sums[1:2, :half] = jnp.sum(top_rows[:, :half].astype(F32), axis=0, keepdims=True)


def output_kernel(hidden, w_down, w_other, keep, send):
    units = hidden.shape[1]
    row, col = lax.axis_index("row"), lax.axis_index("col")
    w_mine = w_down[half_rows(row, units)]

    def total_of(rows):
        values = hidden[rows]
        return jnp.concatenate([dot(values, w_mine), dot(values, w_other[...])], axis=1)

    split_tokens(total_of, keep, send, keep.shape[0], col)


def second_back_kernel(lengths, total, total_far, unit_ref, inverse_ref, vec, vec_other, top, top_far, middle_out, datt, sums):
    half = top.shape[1]
    got = total_far[...].astype(F32)
    grads = total[...].astype(F32) + jnp.concatenate([got[:, half:], got[:, :half]], axis=1)
    unit = unit_ref[...]
    scaled = grads * wide_vector(vec, vec_other, 3)
    mean_plain = jnp.mean(scaled, axis=1, keepdims=True)
    mean_unit = jnp.mean(scaled * unit, axis=1, keepdims=True)
    own = masked_top(lengths, top, top_far, lax.axis_index("col")).astype(F32)
    result = own + inverse_ref[:, :1] * (scaled - mean_plain - unit * mean_unit)
    middle_out[...] = result[:, :half]
    datt[...] = result.astype(BF16)
    sums[...] = jnp.zeros_like(sums)
    sums[0:1] = jnp.sum((grads * unit)[:, :half], axis=0, keepdims=True)
    sums[1:2] = jnp.sum(grads[:, :half], axis=0, keepdims=True)


def backward_kernel(bit_first, bit_second, lengths, own, other, w_mine, w_other, q_ref, k_ref, v_ref, o_ref, lse, normed, w_kept, w_got,
                    first_keep, first_send, second_keep, second_send, keep, send, sums, datt, out, acc_k, acc_v, do_ref):
    own_rows, width = own.shape
    half = width // 2
    third = q_ref.shape[1]
    row, col = lax.axis_index("row"), lax.axis_index("col")
    quarter = half_rows(row, third)
    for ref, at in ((own, col), (other, 1 - col)):
        where = half_rows(at, own_rows)
        values = ref[...]
        datt[where] = values
        do_ref[where] = (
            dot_nt(values[:, :half], w_mine[quarter]) + dot_nt(values[:, half:], w_other[quarter])
        ).astype(BF16)
    keys_t = k_ref[...].T
    acc_k[...] = jnp.zeros_like(acc_k)
    acc_v[...] = jnp.zeros_like(acc_v)
    scale = BF16(HEAD_DIM ** (-0.5))
    for begin in (0, own_rows):
        keys = begin + own_rows
        allowed = allowed_block(lengths, keys, begin, own_rows)
        query = q_ref[begin:keys] * scale
        grad_mixed = do_ref[begin:keys]
        parts = []
        for head in range(third // HEAD_DIM):
            mask = head_mask(third, head)
            key = jnp.where(mask, k_ref[:keys], BF16(0))
            scores = jnp.where(allowed, dot_nt(key, query), MASKED)
            probs = jnp.exp(scores - lse[head : head + 1, begin:keys])
            value = jnp.where(mask, v_ref[:keys], BF16(0))
            grad_probs = dot_nt(value, grad_mixed)
            both = probs * grad_probs
            inner = jnp.sum(both, axis=0, keepdims=True)
            grad_raw = (both - probs * inner).astype(BF16) * scale
            acc_v[:keys] += jnp.where(mask, dot(probs.astype(BF16), grad_mixed), 0.0)
            acc_k[:keys] += jnp.where(mask, dot(grad_raw, q_ref[begin:keys]), 0.0)
            parts.append(dot(keys_t[head * HEAD_DIM : (head + 1) * HEAD_DIM, :keys], grad_raw))
        out[begin:keys, :third] = jnp.concatenate(parts, axis=0).T.astype(BF16)
    out[:, third : 2 * third] = acc_k[...].astype(BF16)
    out[:, 2 * third :] = acc_v[...].astype(BF16)
    grads = out[...]
    weights = dot_tn(normed[...], grads).astype(BF16)
    grad_out = dot_tn(datt[...], o_ref[...]).astype(BF16)
    split_rows(weights[:, : 2 * third].reshape(2, half, 2 * third), first_keep, first_send, bit_first)
    last = jnp.concatenate([weights[:, 2 * third :], grad_out], axis=1)
    split_rows(last.reshape(2, half, 2 * third), second_keep, second_send, bit_second)

    def total_of(rows):
        values = out[rows]
        return jnp.concatenate([dot_nt(values, w_kept[...]), dot_nt(values, w_got[...])], axis=1)

    split_tokens(total_of, keep, send, own_rows, col)
    sums[...] = jnp.zeros_like(sums)
    sums[0:1, : 3 * third] = jnp.sum(grads.astype(F32), axis=0, keepdims=True)
    sums[1:2, :half] = jnp.sum(datt[:, :half].astype(F32), axis=0, keepdims=True)


def first_back_kernel(keep, got, unit_ref, vec, vec_other, mine, far, stats):
    half = mine.shape[1]
    grads = keep[...] + got[...].astype(F32)
    mine[...] = grads[:, :half]
    far[...] = grads[:, half:].astype(BF16)
    scaled = grads * wide_vector(vec, vec_other, 0)
    plain = jnp.sum(scaled, axis=1, keepdims=True)
    crossed = jnp.sum(scaled * unit_ref[...], axis=1, keepdims=True)
    lanes = lax.broadcasted_iota(jnp.int32, (1, 128), 1)
    both = jnp.where(lanes == 0, plain, jnp.where(lanes == 1, crossed, 0.0))
    stats[...] = both.T[:8]


def last_kernel(mine, got, stats, stats_far, unit_ref, inverse_ref, vec, middle, result, sums):
    half = mine.shape[1]
    unit = unit_ref[:, :half]
    grads = mine[...] + got[...].astype(F32)
    total = (stats[...] + stats_far[...]) / (2 * half)
    columns = jnp.concatenate([total, jnp.zeros((120, total.shape[1]), F32)], axis=0).T
    grad_in = inverse_ref[:, :1] * (
        grads * vec[0:1] - columns[:, 0:1] - unit * columns[:, 1:2]
    )
    result[...] = (middle[...] + grad_in).astype(BF16)
    sums[...] = jnp.zeros_like(sums)
    sums[0:1] = jnp.sum(grads * unit, axis=0, keepdims=True)
    sums[1:2] = jnp.sum(grads, axis=0, keepdims=True)


def halve_kernel(bit, kept, got, keep, send):
    total = (kept[...].astype(F32) + got[...].astype(F32)).astype(BF16)
    split_rows(total, keep, send, bit)


def turn_kernel(stacked, kept, got, keep, send):
    total = (kept[...].astype(F32) + got[...].astype(F32)).astype(BF16)
    if stacked:
        keep[...], send[...] = total[0], total[1]
    else:
        half = keep.shape[1]
        keep[...], send[...] = total[:, :half], total[:, half:]


def stack_kernel(mine, got, out):
    out[0], out[1] = mine[...], got[...]


def double_kernel(bit, mine, got, out):
    own = (lax.axis_index("dp") // (1 << bit)) % 2 == 0
    half = mine.shape[1]
    out[:, :half] = jnp.where(own, mine[...], got[...])
    out[:, half:] = jnp.where(own, got[...], mine[...])


class Chain:
    def __init__(self, keep, send, bits, stacked):
        self.keep, self.bits, self.stacked = keep, bits, stacked
        self.stage = 0
        self.steps = 2 * len(bits) + 1
        self.got = from_dp(send, bits[0])

    def step(self):
        self.stage += 1
        count, stage = len(self.bits), self.stage
        if stage < count:
            bit = self.bits[stage]
            dims = self.keep.shape[:-2] + (self.keep.shape[-2] // 2, self.keep.shape[-1])
            self.keep, send = call(
                lambda *refs: halve_kernel(bit, *refs), (shape(dims, BF16),) * 2, self.keep, self.got
            )
            self.got = from_dp(send, bit)
        elif stage == count:
            rows, width = self.keep.shape[-2:]
            dims = (rows, width) if self.stacked else (rows, width // 2)
            stacked = self.stacked
            self.keep, send = call(
                lambda *refs: turn_kernel(stacked, *refs),
                (shape(dims, BF16),) * 2,
                self.keep,
                self.got,
            )
            self.got = from_row(send)
        elif stage < self.steps:
            self.gather()
            self.got = from_dp(self.keep, self.bits[2 * count - stage])

    def gather(self):
        count, stage = len(self.bits), self.stage
        if stage == count + 1:
            dims = (2,) + self.keep.shape
            self.keep = call(stack_kernel, shape(dims, BF16), self.keep, self.got)
        else:
            bit = self.bits[2 * count - stage + 1]
            pair, rows, width = self.keep.shape
            self.keep = call(
                lambda *refs: double_kernel(bit, *refs),
                shape((pair, 2 * rows, width), BF16),
                self.keep,
                self.got,
            )

    @property
    def last_bit(self):
        return self.bits[0]


def arrived(chains, *others):
    flat = [(chain.keep, chain.got) for chain in chains]
    flat, others = lax.optimization_barrier((flat, others))
    for chain, (keep, got) in zip(chains, flat):
        chain.keep, chain.got = keep, got
    return others


def advance(chains):
    for chain in chains:
        chain.step()


def ordered_halves(bit, mine, got):
    own = (lax.axis_index("dp") // (1 << bit)) % 2 == 0
    return jnp.concatenate(
        [jnp.where(own, mine, got), jnp.where(own, got, mine)], axis=0
    )


def by_row(mine, far, axis):
    first = lax.axis_index("row") == 0
    return jnp.concatenate(
        [jnp.where(first, mine, far), jnp.where(first, far, mine)], axis=axis
    )


def up_end_kernel(bit, mine, got, out):
    own = (lax.axis_index("dp") // (1 << bit)) % 2
    here = pl.program_id(0) == own
    near = jnp.where(here, mine[0], got[0])
    far = jnp.where(here, mine[1], got[1])
    out[...] = by_row(near, far, 1).astype(F32)


def down_end_kernel(bit, mine, got, out):
    own = (lax.axis_index("dp") // (1 << bit)) % 2
    here = pl.program_id(1) == own
    near = pl.program_id(0) == lax.axis_index("row")
    part = jnp.where(near, jnp.where(here, mine[0], got[0]), jnp.where(here, mine[1], got[1]))
    out[...] = part.astype(F32)


def attention_end_kernel(bit, flip, mine, got, left, right):
    near = ordered_halves(bit, mine[0], got[0])
    far = ordered_halves(bit, mine[1], got[1])
    third = near.shape[1] // 2
    left[...] = by_row(near[:, :third], far[:, :third], 1).astype(F32)
    last = by_row(near[:, third:], far[:, third:], 1).astype(F32)
    right[...] = last.T if flip else last


def end_call(kernel, grid, out_shape, block, index, mine, got):
    whole = pl.BlockSpec(memory_space=pltpu.VMEM)
    return pl.pallas_call(
        kernel,
        grid=grid,
        out_shape=out_shape,
        in_specs=[whole, whole],
        out_specs=pl.BlockSpec(block, index),
        compiler_params=pltpu.CompilerParams(vmem_limit_bytes=16 * MIB),
    )(mine, got)


def body(
    tokens,
    out_grad,
    seq_lengths,
    w_query,
    w_key,
    w_value,
    w_out,
    w_up,
    w_down,
    b_query,
    b_value,
    b_out,
    b_up,
    b_down,
    gain_attn,
    shift_attn,
    gain_mlp,
    shift_mlp,
):
    row = lax.axis_index("row")
    own_rows, half = tokens.shape
    width = 2 * half
    rows = 2 * own_rows
    third = w_query.shape[1] // 2
    units = w_up.shape[1] // 2
    side = lax.axis_index("dp") % 2
    count = lax.axis_size("dp").bit_length() - 1
    bits = list(range(count))
    turned = [1, 0] + bits[2:] if count > 1 else bits
    tall = shape((own_rows, width), F32)
    tall_low = shape((own_rows, width), BF16)
    column = shape((own_rows, 128), F32)
    pair_sums = shape((8, half), F32)

    tokens_far = from_row(tokens)
    operands = (
        gain_attn, shift_attn, b_out, gain_mlp, shift_mlp, w_query, w_key, w_value,
        b_query, b_value, b_up, b_down,
    )
    out_shape = (
        shape((8, half), F32),
        shape((8, units), F32),
        shape((half, 3 * third), BF16),
        shape((half, 3 * third), BF16),
    )
    whole = lambda x: pl.BlockSpec(x.shape, lambda i: (0,) * len(x.shape))
    vec, loc, w_kept, sent = pl.pallas_call(
        pack_kernel,
        grid=(1,),
        out_shape=out_shape,
        in_specs=[whole(x) for x in operands],
        out_specs=tuple(pl.BlockSpec(memory_space=pltpu.VMEM) for _ in out_shape),
        compiler_params=pltpu.CompilerParams(vmem_limit_bytes=16 * MIB),
    )(*operands)
    vec_far = from_row(vec)
    w_got = from_row(sent)
    top_col = from_col(out_grad)
    sent_up = lax.dynamic_slice(
        w_up, (side * (half // 2), (1 - row) * units), (half // 2, units)
    )
    sent_down = lax.dynamic_slice(
        w_down, ((1 - row) * units + side * (units // 2), 0), (units // 2, half)
    )
    tokens_far, vec_far, w_out_send, sent_up = hold(tokens_far, vec_far, w_out, sent_up)

    normed, unit_attn, inverse_attn = call(
        first_norm_kernel, (tall_low, tall, column), tokens, tokens_far, vec, vec_far
    )
    normed_col = from_col(normed)
    w_out_far = from_row(w_out_send)
    up_got = from_row(sent_up)
    normed_col, w_got = hold(normed_col, w_got)

    like = shape((rows, third), BF16)
    normed_all, query, key, value, mixed, lse = call(
        forward_kernel,
        (shape((rows, width), BF16), like, like, like, like, shape((8, rows), F32)),
        seq_lengths,
        normed,
        normed_col,
        w_kept,
        w_got,
        loc,
        flops=2 * rows * third * (3 * width + 2 * rows),
        smem=(0,),
    )
    mixed_far = from_row(mixed)
    mixed_far, w_out_far, out_grad_send, sent_down, up_got = hold(
        mixed_far, w_out_far, out_grad, sent_down, up_got
    )

    keep, send = call(
        branch_kernel, (tall, tall_low), mixed, mixed_far, w_out, w_out_far,
        flops=2 * rows * width * half,
    )
    got = from_col(send)
    up_side = from_dp(up_got, 0)
    top_far = from_row(out_grad_send)
    down_got = from_row(sent_down)
    (got,) = hold(got)

    middle, normed_mlp, unit_mlp, inverse_mlp = call(
        second_norm_kernel,
        (shape((own_rows, half), F32), tall_low, tall, column),
        tokens, tokens_far, keep, got, vec, vec_far,
    )
    normed_mlp_col = from_col(normed_mlp)
    normed_mlp_col, up_side, top_far = hold(normed_mlp_col, up_side, top_far)

    normed_mlp_all, hidden, slope, w_up_far = call(
        up_kernel,
        (
            shape((rows, width), BF16),
            shape((rows, units), BF16),
            shape((rows, units), F32),
            shape((half, units), BF16),
        ),
        normed_mlp, normed_mlp_col, w_up, up_got, up_side, loc,
        flops=2 * rows * width * units,
    )
    top_far_col = from_col(top_far)
    down_side = from_dp(down_got, 0)
    hidden, top_far_col, down_side = hold(hidden, top_far_col, down_side)

    split_down = shape((units // 2, width), BF16)
    split_up = shape((2, half // 2, units), BF16)
    down_keep, down_send, up_keep, up_send, keep, send, mlp_sums, w_down_far = call(
        lambda *refs: down_kernel(bits[0], turned[0], *refs),
        (
            split_down, split_down, split_up, split_up, tall, tall_low,
            shape((8, units), F32), shape((units, half), BF16),
        ),
        seq_lengths, out_grad, top_far, top_col, top_far_col, hidden, slope, normed_mlp_all,
        w_down, down_got, down_side, w_up, w_up_far,
        flops=8 * rows * width * units,
        scratch=[pltpu.VMEM((rows, width), BF16), pltpu.VMEM((rows, units), BF16)],
        smem=(0,),
    )
    got = from_col(send)
    down = Chain(down_keep, down_send, bits, False)
    up = Chain(up_keep, up_send, turned, True)
    (got,) = hold(got)

    total = (keep + got.astype(F32)).astype(BF16)
    total_far = from_row(total)
    keep, send = call(
        output_kernel, (tall, tall_low), hidden, w_down, w_down_far,
        flops=2 * rows * width * units,
    )
    got = from_col(send)
    total_far, got = hold(total_far, got)

    grad_middle, datt, mid_sums = call(
        second_back_kernel,
        (shape((own_rows, half), F32), tall_low, pair_sums),
        seq_lengths, total, total_far, unit_mlp, inverse_mlp, vec, vec_far, out_grad, top_far,
        smem=(0,),
    )
    datt_col = from_col(datt)
    raised = keep + got.astype(F32)
    raised_far = from_row(raised[:, half:].astype(BF16))
    (datt_col,) = arrived([down, up], datt_col)
    advance([down, up])

    split_pair = shape((2, half // 2, 2 * third), BF16)
    first_keep, first_send, second_keep, second_send, keep, send, attn_sums = call(
        lambda *refs: backward_kernel(bits[0], turned[0], *refs),
        (split_pair,) * 4 + (tall, tall_low, shape((8, width), F32)),
        seq_lengths, datt, datt_col, w_out, w_out_far, query, key, value, mixed, lse,
        normed_all, w_kept, w_got,
        flops=2 * rows * third * (5 * width + 5 * rows),
        scratch=[
            pltpu.VMEM((rows, width), BF16),
            pltpu.VMEM((rows, 3 * third), BF16),
            pltpu.VMEM((rows, third), F32),
            pltpu.VMEM((rows, third), F32),
            pltpu.VMEM((rows, third), BF16),
        ],
        smem=(0,),
    )
    keep, send, raised_far = arrived([down, up], keep, send, raised_far)
    got = from_col(send)
    first = Chain(first_keep, first_send, bits, True)
    second = Chain(second_keep, second_send, turned, True)
    advance([down, up])
    output = (middle + raised[:, :half] + raised_far.astype(F32) + loc[2:3, :half]).astype(BF16)
    (got,) = hold(got)

    mine, far, stats = call(
        first_back_kernel,
        (shape((own_rows, half), F32), shape((own_rows, half), BF16), shape((8, own_rows), F32)),
        keep, got, unit_attn, vec, vec_far,
    )
    got = from_row(far)
    stats_far = from_row(stats)
    got, stats_far = arrived([down, up, first, second], got, stats_far)
    advance([down, up, first, second])
    input_grad, in_sums = call(
        last_kernel,
        (shape((own_rows, half), BF16), pair_sums),
        mine, got, stats, stats_far, unit_attn, inverse_attn, vec, grad_middle,
    )

    halves = jnp.concatenate([in_sums, mid_sums], axis=1)
    halves = halves + from_col(halves)
    small = jnp.concatenate(
        [halves[:2], mlp_sums[:2, :width], attn_sums[:2], jnp.zeros((2, width), F32)]
    )
    for bit in bits:
        (small,) = arrived([down, up, first, second], small)
        if first.stage < first.steps - 1:
            advance([down, up, first, second])
        small = small + from_dp(small, bit)
    for chain in (first, second):
        while chain.stage < chain.steps - 1:
            chain.step()
    for chain in (down, up):
        while chain.stage < chain.steps - 1:
            chain.step()

    wide = w_query.shape[1]
    outs = (shape((half, wide), F32),) * 2
    grad_query, grad_key = call(
        lambda *refs: attention_end_kernel(first.last_bit, False, *refs), outs, first.keep, first.got
    )
    grad_value, grad_out = call(
        lambda *refs: attention_end_kernel(second.last_bit, True, *refs), outs, second.keep, second.got
    )
    grad_down = end_call(
        lambda *refs: down_end_kernel(down.last_bit, *refs),
        (2, 2),
        shape((2 * units, half), F32),
        (units // 2, half),
        lambda i, j: (2 * i + j, 0),
        down.keep,
        down.got,
    )
    grad_up = end_call(
        lambda *refs: up_end_kernel(up.last_bit, *refs),
        (2,),
        shape((half, 2 * units), F32),
        (half // 2, 2 * units),
        lambda i: (i, 0),
        up.keep,
        up.got,
    )
    return (
        output,
        input_grad,
        grad_query,
        grad_key,
        grad_value,
        grad_out,
        grad_up,
        grad_down,
        small[4, :third],
        small[4, 2 * third : 3 * third],
        small[5, :half],
        small[2, :units],
        small[3, :half],
        small[0, :half],
        small[1, :half],
        small[0, half:],
        small[1, half:],
    )


def solution(mesh):
    return jax.shard_map(
        body,
        mesh=mesh,
        in_specs=(
            P(("dp", "col"), "row"),
            P(("dp", "col"), "row"),
            P("dp", None),
            P("row", "col"),
            P("row", "col"),
            P("row", "col"),
            P("col", "row"),
            P("row", "col"),
            P("col", "row"),
            P(("col", "row")),
            P(("col", "row")),
            P("row"),
            P(("col", "row")),
            P("row"),
            P("row"),
            P("row"),
            P("row"),
            P("row"),
        ),
        out_specs=(
            P(("dp", "col"), "row"),
            P(("dp", "col"), "row"),
            P("row", "col"),
            P("row", "col"),
            P("row", "col"),
            P("col", "row"),
            P("row", "col"),
            P("col", "row"),
            P(("col", "row")),
            P(("col", "row")),
            P("row"),
            P(("col", "row")),
            P("row"),
            P("row"),
            P("row"),
            P("row"),
            P("row"),
        ),
        check_vma=False,
    )
```

time: 281 us -> 204 us (0.73)
  other arithmetic: 40.4 us -> 1 us
  matrix products: 31.9 us -> 0 us
  Pallas kernels: 0 us -> 31.9 us
  waiting for transfers between devices: 126 us -> 96 us
  starting transfers between devices: 65.3 us -> 58 us
  local copies, waits for them, and re-layouts: 12.5 us -> 15.6 us
    dot_general x18 -> x0, matrix products: 31.9 us -> none  [the longest x4 7.39 us: dot_nt(): lax.dot_general(left, right, (((1,), (1,)), ((), ())), preferred_element_...]
    pallas_call x0 -> x40, Pallas kernels: none -> 31.9 us  [the longest x37 27 us: call(): pl.pallas_call(kernel, out_shape=out_shape, in_specs=[pl.BlockSpec(memory...]
    ppermute x39 -> x29, waiting for transfers between devices: 80 us -> 55.3 us  [from_dp(): return lax.ppermute(values, 'dp', dp_pairs(bit))]
    select_n x27 -> x0, other arithmetic: 15.3 us -> none  [the longest x20 8.8 us: ordered(): jnp.where(index == 0, jnp.concatenate([mine, other], axis=axis), jnp.conc...]
    convert_element_type x34 -> x2, other arithmetic: 11.9 us -> 0.84 us  [the longest x1 0.77 us: body(): (middle + raised[:, :half] + raised_far.astype(F32) + loc[2:3, :half]).as...]
    unnamed x137 -> x51, local copies, waits for them, and re-layouts: 1.6 us -> 12 us
    ppermute x39 -> x29, starting transfers between devices: 47.2 us -> 38.3 us  [from_dp(): return lax.ppermute(values, 'dp', dp_pairs(bit))]
    ppermute x18 -> x16, waiting for transfers between devices: 45.6 us -> 38.8 us  [from_row(): return lax.ppermute(values, 'row', SWAP)]
  transfers between devices with their start and end apart: 66 -> 55, of which waited for: 29 -> 25; matrix products, arithmetic and copies ran while one was open for 25% -> 2% of each run, Pallas kernels for 0% -> 11%
where the time goes in v2:
time: 204 us
  waiting for transfers between devices  96 us (47%)
  starting transfers between devices  58 us (28%)
  Pallas kernels  31.9 us (16%)
  local copies, waits for them, and re-layouts  15.6 us (8%)
    ppermute x29, waiting for transfers between devices, from_dp(): return lax.ppermute(values, 'dp', dp_pairs(bit))  55.3 us
    ppermute x16, waiting for transfers between devices, from_row(): return lax.ppermute(values, 'row', SWAP)  38.8 us
    ppermute x29, starting transfers between devices, from_dp(): return lax.ppermute(values, 'dp', dp_pairs(bit))  38.3 us
    pallas_call x37, Pallas kernels, call(): pl.pallas_call(kernel, out_shape=out_shape, in_specs=[pl.BlockSpec(memory...  27 us
    ppermute x16, starting transfers between devices, from_row(): return lax.ppermute(values, 'row', SWAP)  18 us
    unnamed x51, local copies, waits for them, and re-layouts  12 us
  transfers between devices with their start and end apart: 55, of which 25 were waited for; matrix products, arithmetic and copies ran while one was open for 2% of the time, Pallas kernels for 11%

profile of v2, /device:TPU:0, one launch (start us, length us, event | category | flops | bytes accessed | tf_op | source)
XLA Modules:
  0.0 203.6 jit_solution(5913942184757061419)
XLA Ops:
  0.7 3.0 %collective-permute-start = (bf16[256,384]{1,0:T(8,128)(2,1)}, bf16[256,384]{1,0:T(8,128)(2,1)S(1)}, u32[]{:S(2)}, u32[]{:S(2)}) collective-permute-start(bf16[256,384]{1,0:T(8,128)(2,1)} %tokens.3), channel_id=1, source_target_pairs={{0,2},{2,0},{1,3},{3,1},{4,6},{6,4},{5,7},{7,5},{8,10},{10,8},{9,1... | collective-permute-start | bytes 589832 | tf_op jit(solution)/shard_map/ppermute | solution.py:32
  14.0 2.0 collective-permute-start.1
  17.7 9.4 %collective-permute-done.1.vec_other = f32[8,384]{1,0:T(8,128)S(1)} collective-permute-done((f32[8,384]{1,0:T(8,128)S(1)}, f32[8,384]{1,0:T(8,128)S(1)}, u32[]{:S(2)}, u32[]{:S(2)}) %collective-permute-start.1) | collective-permute-done | bytes 12320 | tf_op jit(solution)/shard_map/ppermute | solution.py:32
  29.7 4.9 %shard_map.307 = (bf16[512,768]{1,0:T(8,128)(2,1)S(1)}, bf16[512,192]{1,0:T(8,128)(2,1)S(1)}, bf16[512,192]{1,0:T(8,128)(2,1)S(1)}, bf16[512,192]{1,0:T(8,128)(2...) custom-call(s32[1,2]{1,0:T(1,128)S(1)} %copy-done.16, bf16[256,768]{1,0:T(8,128)(2,1)S(1)} %get-tuple-element.164.own, ...), custom_call_target="tpu_custom_call" | custom-call | flops 654311424 | bytes 1695752 | tf_op jit(solution)/shard_map/pallas_call | solution.py:59
  37.9 6.0 %collective-permute-done.6.got = bf16[192,768]{1,0:T(8,128)(2,1)S(1)} collective-permute-done((bf16[192,768]{1,0:T(8,128)(2,1)}, bf16[192,768]{1,0:T(8,128)(2,1)S(1)}, u32[]{:S(2)}, u32[]{:S(2)}) %collective-permute-start.6) | collective-permute-done | bytes 294944 | tf_op jit(solution)/shard_map/ppermute | solution.py:32
  44.0 5.3 %collective-permute-done.4.mixed_other = bf16[512,192]{1,0:T(8,128)(2,1)} collective-permute-done((bf16[512,192]{1,0:T(8,128)(2,1)}, bf16[512,192]{1,0:T(8,128)(2,1)}, u32[]{:S(2)}, u32[]{:S(2)}) %collective-permute-start.4) | collective-permute-done | bytes 196640 | tf_op jit(solution)/shard_map/ppermute | solution.py:32
  49.2 1.9 shard_map.308
  57.1 6.3 %collective-permute-done.12.refs_9_ = bf16[384,384]{1,0:T(8,128)(2,1)S(1)} collective-permute-done((bf16[384,384]{1,0:T(8,128)(2,1)S(1)}, bf16[384,384]{1,0:T(8,128)(2,1)S(1)}, u32[]{:S(2)}, u32[]{:S(2)}) %collective-permute-start.12) | collective-permute-done | bytes 294944 | tf_op jit(solution)/shard_map/ppermute | solution.py:32
  64.9 2.2 %collective-permute-done.10.refs_2_.top_far = bf16[256,384]{1,0:T(8,128)(2,1)S(1)} collective-permute-done((bf16[256,384]{1,0:T(8,128)(2,1)S(1)}, bf16[256,384]{1,0:T(8,128)(2,1)S(1)}, u32[]{:S(2)}, u32[]{:S(2)}) %collective-permute-start.10) | collective-permute-done | bytes 196640 | tf_op jit(solution)/shard_map/ppermute | solution.py:32
  69.1 2.2 %collective-permute-done.13.refs_10_ = bf16[384,384]{1,0:T(8,128)(2,1)S(1)} collective-permute-done((bf16[384,384]{1,0:T(8,128)(2,1)S(1)}, bf16[384,384]{1,0:T(8,128)(2,1)S(1)}, u32[]{:S(2)}, u32[]{:S(2)}) %collective-permute-start.13) | collective-permute-done | bytes 294944 | tf_op jit(solution)/shard_map/ppermute | solution.py:45
  71.3 4.2 %shard_map.311 = (bf16[384,768]{1,0:T(8,128)(2,1)S(1)}, bf16[384,768]{1,0:T(8,128)(2,1)S(1)}, bf16[2,192,768]{2,1,0:T(8,128)(2,1)S(1)}, bf16[2,192,768]{2,1,0:T(...) custom-call(s32[1,2]{1,0:T(1,128)S(1)} %copy-done.16, ...), custom_call_target="tpu_custom_call" | custom-call | flops 2415919104 | bytes 7471112 | tf_op jit(solution)/shard_map/pallas_call | solution.py:59
  81.0 7.6 %collective-permute-done.16.total_far = bf16[256,768]{1,0:T(8,128)(2,1)S(1)} collective-permute-done((bf16[256,768]{1,0:T(8,128)(2,1)S(1)}, bf16[256,768]{1,0:T(8,128)(2,1)S(1)}, u32[]{:S(2)}, u32[]{:S(2)}) %collective-permute-start.16) | collective-permute-done | bytes 393248 | tf_op jit(solution)/shard_map/ppermute | solution.py:32
  90.0 2.9 %collective-permute-done.18.refs_1_ = bf16[384,768]{1,0:T(8,128)(2,1)S(1)} collective-permute-done((bf16[384,768]{1,0:T(8,128)(2,1)S(1)}, bf16[384,768]{1,0:T(8,128)(2,1)S(1)}, u32[]{:S(2)}, u32[]{:S(2)}) %collective-permute-start.18) | collective-permute-done | bytes 589856 | tf_op jit(solution)/shard_map/ppermute | solution.py:45
  98.6 6.4 %shard_map.316 = (bf16[2,192,384]{2,1,0:T(8,128)(2,1)S(1)}, bf16[2,192,384]{2,1,0:T(8,128)(2,1)S(1)}, bf16[2,192,384]{2,1,0:T(8,128)(2,1)S(1)}, bf16[2,192,384]{...) custom-call(s32[1,2]{1,0:T(1,128)S(1)} %copy-done.16, ...), custom_call_target="tpu_custom_call" | custom-call | flops 1258291200 | bytes 3850248 | tf_op jit(solution)/shard_map/pallas_call | solution.py:59
  108.1 2.6 %collective-permute-start.25 = (bf16[96,768]{1,0:T(8,128)(2,1)S(1)}, bf16[96,768]{1,0:T(8,128)(2,1)S(1)}, u32[]{:S(2)}, u32[]{:S(2)}) collective-permute-start(bf16[96,768]{1,0:T(8,128)(2,1)S(1)} %get-tuple-element.230), channel_id=1, source_target_pairs={{0,16},{4,20},{8,24},{12,28},{16,0},{20,4},{24,8},{28,12},{1,17},{... | collective-permute-start | bytes 442376 | tf_op jit(solution)/shard_map/ppermute | solution.py:45
  111.3 3.3 %collective-permute-done.27.refs_1_ = bf16[2,192,384]{2,1,0:T(8,128)(2,1)S(1)} collective-permute-done((bf16[2,192,384]{2,1,0:T(8,128)(2,1)S(1)}, bf16[2,192,384]{2,1,0:T(8,128)(2,1)S(1)}, u32[]{:S(2)}, u32[]{:S(2)}) %collective-permute-start.27) | collective-permute-done | bytes 294944 | tf_op jit(solution)/shard_map/ppermute | solution.py:45
  115.1 7.0 %collective-permute-done.28.refs_1_ = bf16[2,192,384]{2,1,0:T(8,128)(2,1)S(1)} collective-permute-done((bf16[2,192,384]{2,1,0:T(8,128)(2,1)S(1)}, bf16[2,192,384]{2,1,0:T(8,128)(2,1)S(1)}, u32[]{:S(2)}, u32[]{:S(2)}) %collective-permute-start.28) | collective-permute-done | bytes 294944 | tf_op jit(solution)/shard_map/ppermute | solution.py:45
  123.3 3.4 %collective-permute-start.31 = (bf16[96,384]{1,0:T(8,128)(2,1)S(1)}, bf16[96,384]{1,0:T(8,128)(2,1)S(1)}, u32[]{:S(2)}, u32[]{:S(2)}) collective-permute-start(bf16[96,384]{1,0:T(8,128)(2,1)S(1)} %get-tuple-element.249), channel_id=1, source_target_pairs={{0,2},{2,0},{1,3},{3,1},{4,6},{6,4},{5,7},{7,5},{8,10},{10,8},{9,1... | collective-permute-start | bytes 221192 | tf_op jit(solution)/shard_map/ppermute | solution.py:32
  131.3 1.7 collective-permute-done.33.refs_1_
  133.9 3.4 %collective-permute-start.37 = (bf16[2,48,768]{2,1,0:T(8,128)(2,1)S(1)}, bf16[2,48,768]{2,1,0:T(8,128)(2,1)S(1)}, u32[]{:S(2)}, u32[]{:S(2)}) collective-permute-start(bf16[2,48,768]{2,1,0:T(8,128)(2,1)S(1)} %shard_map.326.refs_0_), channel_id=1, source_target_pairs={{0,16},{4,20},{8,24},{12,28},{16,0},{20,4},{24,8},{28,12},{1,17},{... | collective-permute-start | bytes 442376 | tf_op jit(solution)/shard_map/ppermute | solution.py:45
  137.5 3.0 %collective-permute-start.38 = (bf16[2,48,384]{2,1,0:T(8,128)(2,1)S(1)}, bf16[2,48,384]{2,1,0:T(8,128)(2,1)S(1)}, u32[]{:S(2)}, u32[]{:S(2)}) collective-permute-start(bf16[2,48,384]{2,1,0:T(8,128)(2,1)S(1)} %get-tuple-element.273), channel_id=1, source_target_pairs={{0,16},{4,20},{8,24},{12,28},{16,0},{20,4},{24,8},{28,12},{1,17},{... | collective-permute-start | bytes 221192 | tf_op jit(solution)/shard_map/ppermute | solution.py:45
  141.2 3.3 %collective-permute-done.40 = f32[8,768]{1,0:T(8,128)S(1)} collective-permute-done((f32[8,768]{1,0:T(8,128)S(1)}, f32[8,768]{1,0:T(8,128)S(1)}, u32[]{:S(2)}, u32[]{:S(2)}) %collective-permute-start.40) | collective-permute-done | bytes 24608 | tf_op jit(solution)/shard_map/ppermute | solution.py:45
  144.5 10.3 %collective-permute-done.38.refs_1_ = bf16[2,48,384]{2,1,0:T(8,128)(2,1)S(1)} collective-permute-done((bf16[2,48,384]{2,1,0:T(8,128)(2,1)S(1)}, bf16[2,48,384]{2,1,0:T(8,128)(2,1)S(1)}, u32[]{:S(2)}, u32[]{:S(2)}) %collective-permute-start.38) | collective-permute-done | bytes 73760 | tf_op jit(solution)/shard_map/ppermute | solution.py:45
  158.9 2.0 collective-permute-start.45
  160.9 4.4 %collective-permute-done.45 = f32[8,768]{1,0:T(8,128)S(1)} collective-permute-done((f32[8,768]{1,0:T(8,128)S(1)}, f32[8,768]{1,0:T(8,128)S(1)}, u32[]{:S(2)}, u32[]{:S(2)}) %collective-permute-start.45) | collective-permute-done | bytes 24608 | tf_op jit(solution)/shard_map/ppermute | solution.py:45
  166.6 1.8 collective-permute-start.46
  171.4 1.8 collective-permute-start.52
  174.5 2.0 collective-permute-start.50
  178.0 7.6 %collective-permute-done.50.refs_1_ = bf16[2,96,384]{2,1,0:T(8,128)(2,1)S(1)} collective-permute-done((bf16[2,96,384]{2,1,0:T(8,128)(2,1)S(1)}, bf16[2,96,384]{2,1,0:T(8,128)(2,1)S(1)}, u32[]{:S(2)}, u32[]{:S(2)}) %collective-permute-start.50) | collective-permute-done | bytes 147488 | tf_op jit(solution)/shard_map/ppermute | solution.py:45
  187.2 3.7 %collective-permute-done.47.refs_1_ = bf16[2,96,384]{2,1,0:T(8,128)(2,1)S(1)} collective-permute-done((bf16[2,96,384]{2,1,0:T(8,128)(2,1)S(1)}, bf16[2,96,384]{2,1,0:T(8,128)(2,1)S(1)}, u32[]{:S(2)}, u32[]{:S(2)}) %collective-permute-start.47) | collective-permute-done | bytes 147488 | tf_op jit(solution)/shard_map/ppermute | solution.py:45
  193.6 4.2 %collective-permute-done.48.refs_1_ = bf16[2,192,384]{2,1,0:T(8,128)(2,1)S(1)} collective-permute-done((bf16[2,192,384]{2,1,0:T(8,128)(2,1)S(1)}, bf16[2,192,384]{2,1,0:T(8,128)(2,1)S(1)}, u32[]{:S(2)}, u32[]{:S(2)}) %collective-permute-start.48) | collective-permute-done | bytes 294944 | tf_op jit(solution)/shard_map/ppermute | solution.py:45
  201.6 2.0 shard_map.344
  (189 shorter events, 70.4 us)
Async XLA Ops:
  0.7 26.5 %collective-permute-start = (bf16[256,384]{1,0:T(8,128)(2,1)}, bf16[256,384]{1,0:T(8,128)(2,1)S(1)}, u32[]{:S(2)}, u32[]{:S(2)}) collective-permute-start(bf16[256,384]{1,0:T(8,128)(2,1)} %tokens.3), channel_id=1, source_target_pairs={{0,2},{2,0},{1,3},{3,1},{4,6},{6,4},{5,7},{7,5},{8,10},{10,8},{9,1... | collective-permute-start | bytes 589832 | tf_op jit(solution)/shard_map/ppermute | solution.py:32
  14.0 15.7 %collective-permute-start.3 = (bf16[384,576]{1,0:T(8,128)(2,1)}, bf16[384,576]{1,0:T(8,128)(2,1)}, u32[]{:S(2)}, u32[]{:S(2)}) collective-permute-start(bf16[384,576]{1,0:T(8,128)(2,1)} %get-tuple-element.165), channel_id=1, source_target_pairs={{0,2},{2,0},{1,3},{3,1},{4,6},{6,4},{5,7},{7,5},{8,10},{10,8},{9,1... | collective-permute-start | bytes 1327112 | tf_op jit(solution)/shard_map/ppermute | solution.py:32
  14.0 13.1 %collective-permute-start.1 = (f32[8,384]{1,0:T(8,128)S(1)}, f32[8,384]{1,0:T(8,128)S(1)}, u32[]{:S(2)}, u32[]{:S(2)}) collective-permute-start(f32[8,384]{1,0:T(8,128)S(1)} %get-tuple-element.161.vec), channel_id=1, source_target_pairs={{0,2},{2,0},{1,3},{3,1},{4,6},{6,4},{5,7},{7,5},{8,10},{10,8},{9,1... | collective-permute-start | bytes 36872 | tf_op jit(solution)/shard_map/ppermute | solution.py:32
  27.6 10.4 %collective-permute-start.5 = (bf16[384,384]{1,0:T(8,128)(2,1)}, bf16[384,384]{1,0:T(8,128)(2,1)}, u32[]{:S(2)}, u32[]{:S(2)}) collective-permute-start(bf16[384,384]{1,0:T(8,128)(2,1)} %refs_3_.1), channel_id=1, source_target_pairs={{0,2},{2,0},{1,3},{3,1},{4,6},{6,4},{5,7},{7,5},{8,10},{10,8},{9,1... | collective-permute-start | bytes 884744 | tf_op jit(solution)/shard_map/ppermute | solution.py:32
  27.9 16.0 %collective-permute-start.6 = (bf16[192,768]{1,0:T(8,128)(2,1)}, bf16[192,768]{1,0:T(8,128)(2,1)S(1)}, u32[]{:S(2)}, u32[]{:S(2)}) collective-permute-start(bf16[192,768]{1,0:T(8,128)(2,1)} %dynamic_slice.6), channel_id=1, source_target_pairs={{0,2},{2,0},{1,3},{3,1},{4,6},{6,4},{5,7},{7,5},{8,10},{10,8},{9,1... | collective-permute-start | bytes 884744 | tf_op jit(solution)/shard_map/ppermute | solution.py:32
  37.6 11.7 %collective-permute-start.4 = (bf16[512,192]{1,0:T(8,128)(2,1)}, bf16[512,192]{1,0:T(8,128)(2,1)}, u32[]{:S(2)}, u32[]{:S(2)}) collective-permute-start(bf16[512,192]{1,0:T(8,128)(2,1)} %get-tuple-element.170.mixed.refs_8_), channel_id=1, source_target_pairs={{0,2},{2,0},{1,3},{3,1},{4,6},{6,4},{5,7},{7,5},{8,10},{10,8},{9,1... | collective-permute-start | bytes 589832 | tf_op jit(solution)/shard_map/ppermute | solution.py:32
  53.4 13.7 %collective-permute-start.8 = (bf16[256,768]{1,0:T(8,128)(2,1)S(1)}, bf16[256,768]{1,0:T(8,128)(2,1)S(1)}, u32[]{:S(2)}, u32[]{:S(2)}) collective-permute-start(bf16[256,768]{1,0:T(8,128)(2,1)S(1)} %get-tuple-element.178.own), channel_id=1, source_target_pairs={{0,1},{1,0},{2,3},{3,2},{4,5},{5,4},{6,7},{7,6},{8,9},{9,8},{10,11... | collective-permute-start | bytes 1179656 | tf_op jit(solution)/shard_map/ppermute | solution.py:36
  53.6 9.8 %collective-permute-start.12 = (bf16[384,384]{1,0:T(8,128)(2,1)S(1)}, bf16[384,384]{1,0:T(8,128)(2,1)S(1)}, u32[]{:S(2)}, u32[]{:S(2)}) collective-permute-start(bf16[384,384]{1,0:T(8,128)(2,1)S(1)} %constant_dynamic-slice_fusion), channel_id=1, source_target_pairs={{0,2},{2,0},{1,3},{3,1},{4,6},{6,4},{5,7},{7,5},{8,10},{10,8},{9,1... | collective-permute-start | bytes 884744 | tf_op jit(solution)/shard_map/ppermute | solution.py:32
  53.9 13.2 %collective-permute-start.9 = (bf16[192,768]{1,0:T(8,128)(2,1)S(1)}, bf16[192,768]{1,0:T(8,128)(2,1)S(1)}, u32[]{:S(2)}, u32[]{:S(2)}) collective-permute-start(bf16[192,768]{1,0:T(8,128)(2,1)S(1)} %collective-permute-done.6.got), channel_id=1, source_target_pairs={{0,4},{4,0},{8,12},{12,8},{16,20},{20,16},{24,28},{28,24},{1,5},{5... | collective-permute-start | bytes 884744 | tf_op jit(solution)/shard_map/ppermute | solution.py:45
  55.6 11.5 %collective-permute-start.10 = (bf16[256,384]{1,0:T(8,128)(2,1)S(1)}, bf16[256,384]{1,0:T(8,128)(2,1)S(1)}, u32[]{:S(2)}, u32[]{:S(2)}) collective-permute-start(bf16[256,384]{1,0:T(8,128)(2,1)S(1)} %copy-done.6), channel_id=1, source_target_pairs={{0,2},{2,0},{1,3},{3,1},{4,6},{6,4},{5,7},{7,5},{8,10},{10,8},{9,1... | collective-permute-start | bytes 589832 | tf_op jit(solution)/shard_map/ppermute | solution.py:32
  77.4 11.2 %collective-permute-start.16 = (bf16[256,768]{1,0:T(8,128)(2,1)S(1)}, bf16[256,768]{1,0:T(8,128)(2,1)S(1)}, u32[]{:S(2)}, u32[]{:S(2)}) collective-permute-start(bf16[256,768]{1,0:T(8,128)(2,1)S(1)} %add_convert_fusion.total), channel_id=1, source_target_pairs={{0,2},{2,0},{1,3},{3,1},{4,6},{6,4},{5,7},{7,5},{8,10},{10,8},{9,1... | collective-permute-start | bytes 1179656 | tf_op jit(solution)/shard_map/ppermute | solution.py:32
  77.8 15.1 %collective-permute-start.18 = (bf16[384,768]{1,0:T(8,128)(2,1)S(1)}, bf16[384,768]{1,0:T(8,128)(2,1)S(1)}, u32[]{:S(2)}, u32[]{:S(2)}) collective-permute-start(bf16[384,768]{1,0:T(8,128)(2,1)S(1)} %get-tuple-element.199), channel_id=1, source_target_pairs={{0,4},{4,0},{8,12},{12,8},{16,20},{20,16},{24,28},{28,24},{1,5},{5... | collective-permute-start | bytes 1769480 | tf_op jit(solution)/shard_map/ppermute | solution.py:45
  79.5 14.8 %collective-permute-start.19 = (bf16[2,192,768]{2,1,0:T(8,128)(2,1)S(1)}, bf16[2,192,768]{2,1,0:T(8,128)(2,1)S(1)}, u32[]{:S(2)}, u32[]{:S(2)}) collective-permute-start(bf16[2,192,768]{2,1,0:T(8,128)(2,1)S(1)} %get-tuple-element.201), channel_id=1, source_target_pairs={{0,8},{4,12},{8,0},{12,4},{16,24},{20,28},{24,16},{28,20},{1,9},{5... | collective-permute-start | bytes 1769480 | tf_op jit(solution)/shard_map/ppermute | solution.py:45
  94.5 10.6 %collective-permute-start.21 = (bf16[192,768]{1,0:T(8,128)(2,1)S(1)}, bf16[192,768]{1,0:T(8,128)(2,1)S(1)}, u32[]{:S(2)}, u32[]{:S(2)}) collective-permute-start(bf16[192,768]{1,0:T(8,128)(2,1)S(1)} %get-tuple-element.209), channel_id=1, source_target_pairs={{0,8},{4,12},{8,0},{12,4},{16,24},{20,28},{24,16},{28,20},{1,9},{5... | collective-permute-start | bytes 884744 | tf_op jit(solution)/shard_map/ppermute | solution.py:45
  96.3 8.8 %collective-permute-start.22 = (bf16[2,96,768]{2,1,0:T(8,128)(2,1)S(1)}, bf16[2,96,768]{2,1,0:T(8,128)(2,1)S(1)}, u32[]{:S(2)}, u32[]{:S(2)}) collective-permute-start(bf16[2,96,768]{2,1,0:T(8,128)(2,1)S(1)} %get-tuple-element.213), channel_id=1, source_target_pairs={{0,4},{4,0},{8,12},{12,8},{16,20},{20,16},{24,28},{28,24},{1,5},{5... | collective-permute-start | bytes 884744 | tf_op jit(solution)/shard_map/ppermute | solution.py:45
  105.2 9.4 %collective-permute-start.27 = (bf16[2,192,384]{2,1,0:T(8,128)(2,1)S(1)}, bf16[2,192,384]{2,1,0:T(8,128)(2,1)S(1)}, u32[]{:S(2)}, u32[]{:S(2)}) collective-permute-start(bf16[2,192,384]{2,1,0:T(8,128)(2,1)S(1)} %get-tuple-element.236), channel_id=1, source_target_pairs={{0,4},{4,0},{8,12},{12,8},{16,20},{20,16},{24,28},{28,24},{1,5},{5... | collective-permute-start | bytes 884744 | tf_op jit(solution)/shard_map/ppermute | solution.py:45
  106.7 15.4 %collective-permute-start.28 = (bf16[2,192,384]{2,1,0:T(8,128)(2,1)S(1)}, bf16[2,192,384]{2,1,0:T(8,128)(2,1)S(1)}, u32[]{:S(2)}, u32[]{:S(2)}) collective-permute-start(bf16[2,192,384]{2,1,0:T(8,128)(2,1)S(1)} %get-tuple-element.238), channel_id=1, source_target_pairs={{0,8},{4,12},{8,0},{12,4},{16,24},{20,28},{24,16},{28,20},{1,9},{5... | collective-permute-start | bytes 884744 | tf_op jit(solution)/shard_map/ppermute | solution.py:45
  107.5 14.7 %collective-permute-start.29 = (bf16[256,384]{1,0:T(8,128)(2,1)S(1)}, bf16[256,384]{1,0:T(8,128)(2,1)S(1)}, u32[]{:S(2)}, u32[]{:S(2)}) collective-permute-start(bf16[256,384]{1,0:T(8,128)(2,1)S(1)} %get-tuple-element.239), channel_id=1, source_target_pairs={{0,2},{2,0},{1,3},{3,1},{4,6},{6,4},{5,7},{7,5},{8,10},{10,8},{9,1... | collective-permute-start | bytes 589832 | tf_op jit(solution)/shard_map/ppermute | solution.py:32
  108.1 14.0 %collective-permute-start.25 = (bf16[96,768]{1,0:T(8,128)(2,1)S(1)}, bf16[96,768]{1,0:T(8,128)(2,1)S(1)}, u32[]{:S(2)}, u32[]{:S(2)}) collective-permute-start(bf16[96,768]{1,0:T(8,128)(2,1)S(1)} %get-tuple-element.230), channel_id=1, source_target_pairs={{0,16},{4,20},{8,24},{12,28},{16,0},{20,4},{24,8},{28,12},{1,17},{... | collective-permute-start | bytes 442376 | tf_op jit(solution)/shard_map/ppermute | solution.py:45
  110.9 11.3 %collective-permute-start.26 = (bf16[2,48,768]{2,1,0:T(8,128)(2,1)S(1)}, bf16[2,48,768]{2,1,0:T(8,128)(2,1)S(1)}, u32[]{:S(2)}, u32[]{:S(2)}) collective-permute-start(bf16[2,48,768]{2,1,0:T(8,128)(2,1)S(1)} %get-tuple-element.234), channel_id=1, source_target_pairs={{0,16},{4,20},{8,24},{12,28},{16,0},{20,4},{24,8},{28,12},{1,17},{... | collective-permute-start | bytes 442376 | tf_op jit(solution)/shard_map/ppermute | solution.py:45
  133.9 22.0 %collective-permute-start.37 = (bf16[2,48,768]{2,1,0:T(8,128)(2,1)S(1)}, bf16[2,48,768]{2,1,0:T(8,128)(2,1)S(1)}, u32[]{:S(2)}, u32[]{:S(2)}) collective-permute-start(bf16[2,48,768]{2,1,0:T(8,128)(2,1)S(1)} %shard_map.326.refs_0_), channel_id=1, source_target_pairs={{0,16},{4,20},{8,24},{12,28},{16,0},{20,4},{24,8},{28,12},{1,17},{... | collective-permute-start | bytes 442376 | tf_op jit(solution)/shard_map/ppermute | solution.py:45
  137.4 18.6 %collective-permute-start.36 = (bf16[2,96,384]{2,1,0:T(8,128)(2,1)S(1)}, bf16[2,96,384]{2,1,0:T(8,128)(2,1)S(1)}, u32[]{:S(2)}, u32[]{:S(2)}) collective-permute-start(bf16[2,96,384]{2,1,0:T(8,128)(2,1)S(1)} %shard_map.325.refs_0_), channel_id=1, source_target_pairs={{0,16},{4,20},{8,24},{12,28},{16,0},{20,4},{24,8},{28,12},{1,17},{... | collective-permute-start | bytes 442376 | tf_op jit(solution)/shard_map/ppermute | solution.py:45
  137.5 17.3 %collective-permute-start.38 = (bf16[2,48,384]{2,1,0:T(8,128)(2,1)S(1)}, bf16[2,48,384]{2,1,0:T(8,128)(2,1)S(1)}, u32[]{:S(2)}, u32[]{:S(2)}) collective-permute-start(bf16[2,48,384]{2,1,0:T(8,128)(2,1)S(1)} %get-tuple-element.273), channel_id=1, source_target_pairs={{0,16},{4,20},{8,24},{12,28},{16,0},{20,4},{24,8},{28,12},{1,17},{... | collective-permute-start | bytes 221192 | tf_op jit(solution)/shard_map/ppermute | solution.py:45
  140.5 15.4 %collective-permute-start.39 = (bf16[2,48,384]{2,1,0:T(8,128)(2,1)S(1)}, bf16[2,48,384]{2,1,0:T(8,128)(2,1)S(1)}, u32[]{:S(2)}, u32[]{:S(2)}) collective-permute-start(bf16[2,48,384]{2,1,0:T(8,128)(2,1)S(1)} %get-tuple-element.277), channel_id=1, source_target_pairs={{0,16},{4,20},{8,24},{12,28},{16,0},{20,4},{24,8},{28,12},{1,17},{... | collective-permute-start | bytes 221192 | tf_op jit(solution)/shard_map/ppermute | solution.py:45
  156.0 9.4 %collective-permute-start.42 = (bf16[2,96,768]{2,1,0:T(8,128)(2,1)S(1)}, bf16[2,96,768]{2,1,0:T(8,128)(2,1)S(1)}, u32[]{:S(2)}, u32[]{:S(2)}) collective-permute-start(bf16[2,96,768]{2,1,0:T(8,128)(2,1)S(1)} %shard_map.330.refs_0_), channel_id=1, source_target_pairs={{0,4},{4,0},{8,12},{12,8},{16,20},{20,16},{24,28},{28,24},{1,5},{5... | collective-permute-start | bytes 884744 | tf_op jit(solution)/shard_map/ppermute | solution.py:45
  165.4 9.1 %collective-permute-start.49 = (bf16[2,48,384]{2,1,0:T(8,128)(2,1)S(1)}, bf16[2,48,384]{2,1,0:T(8,128)(2,1)S(1)}, u32[]{:S(2)}, u32[]{:S(2)}) collective-permute-start(bf16[2,48,384]{2,1,0:T(8,128)(2,1)S(1)} %shard_map.337.refs_0_), channel_id=1, source_target_pairs={{0,16},{4,20},{8,24},{12,28},{16,0},{20,4},{24,8},{28,12},{1,17},{... | collective-permute-start | bytes 221192 | tf_op jit(solution)/shard_map/ppermute | solution.py:45
  168.4 8.9 %collective-permute-start.54 = (f32[8,768]{1,0:T(8,128)S(1)}, f32[8,768]{1,0:T(8,128)S(1)}, u32[]{:S(2)}, u32[]{:S(2)}) collective-permute-start(f32[8,768]{1,0:T(8,128)S(1)} %add.64), channel_id=1, source_target_pairs={{0,16},{4,20},{8,24},{12,28},{16,0},{20,4},{24,8},{28,12},{1,17},{... | collective-permute-start | bytes 73736 | tf_op jit(solution)/shard_map/ppermute | solution.py:45
  169.8 31.8 %collective-permute-start.53 = (bf16[2,384,384]{2,1,0:T(8,128)(2,1)S(1)}, bf16[2,384,384]{2,1,0:T(8,128)(2,1)S(1)}, u32[]{:S(2)}, u32[]{:S(2)}) collective-permute-start(bf16[2,384,384]{2,1,0:T(8,128)(2,1)S(1)} %shard_map.343.refs_0_), channel_id=1, source_target_pairs={{0,4},{4,0},{8,12},{12,8},{16,20},{20,16},{24,28},{28,24},{1,5},{5... | collective-permute-start | bytes 1769480 | tf_op jit(solution)/shard_map/ppermute | solution.py:45
  171.4 28.7 %collective-permute-start.52 = (bf16[2,192,768]{2,1,0:T(8,128)(2,1)S(1)}, bf16[2,192,768]{2,1,0:T(8,128)(2,1)S(1)}, u32[]{:S(2)}, u32[]{:S(2)}) collective-permute-start(bf16[2,192,768]{2,1,0:T(8,128)(2,1)S(1)} %shard_map.341.refs_0_), channel_id=1, source_target_pairs={{0,8},{4,12},{8,0},{12,4},{16,24},{20,28},{24,16},{28,20},{1,9},{5... | collective-permute-start | bytes 1769480 | tf_op jit(solution)/shard_map/ppermute | solution.py:45
  174.4 16.5 %collective-permute-start.47 = (bf16[2,96,384]{2,1,0:T(8,128)(2,1)S(1)}, bf16[2,96,384]{2,1,0:T(8,128)(2,1)S(1)}, u32[]{:S(2)}, u32[]{:S(2)}) collective-permute-start(bf16[2,96,384]{2,1,0:T(8,128)(2,1)S(1)} %shard_map.334.refs_0_), channel_id=1, source_target_pairs={{0,8},{4,12},{8,0},{12,4},{16,24},{20,28},{24,16},{28,20},{1,9},{5... | collective-permute-start | bytes 442376 | tf_op jit(solution)/shard_map/ppermute | solution.py:45
  174.5 11.0 %collective-permute-start.50 = (bf16[2,96,384]{2,1,0:T(8,128)(2,1)S(1)}, bf16[2,96,384]{2,1,0:T(8,128)(2,1)S(1)}, u32[]{:S(2)}, u32[]{:S(2)}) collective-permute-start(bf16[2,96,384]{2,1,0:T(8,128)(2,1)S(1)} %shard_map.338.refs_0_), channel_id=1, source_target_pairs={{0,4},{4,0},{8,12},{12,8},{16,20},{20,16},{24,28},{28,24},{1,5},{5... | collective-permute-start | bytes 442376 | tf_op jit(solution)/shard_map/ppermute | solution.py:45
  185.6 13.3 %collective-permute-start.51 = (bf16[2,192,384]{2,1,0:T(8,128)(2,1)S(1)}, bf16[2,192,384]{2,1,0:T(8,128)(2,1)S(1)}, u32[]{:S(2)}, u32[]{:S(2)}) collective-permute-start(bf16[2,192,384]{2,1,0:T(8,128)(2,1)S(1)} %shard_map.339.refs_0_), channel_id=1, source_target_pairs={{0,8},{4,12},{8,0},{12,4},{16,24},{20,28},{24,16},{28,20},{1,9},{5... | collective-permute-start | bytes 884744 | tf_op jit(solution)/shard_map/ppermute | solution.py:45
  (48 other events, 265.5 us)

commit v3 on v2

--- a/solution.py
+++ b/solution.py
@@ -53,16 +53,25 @@
     return jax.ShapeDtypeStruct(tuple(dims), kind)
 
 
-def call(kernel, out_shape, *operands, flops=0, scratch=(), smem=(), vmem=16):
-    spaces = [pltpu.SMEM if i in smem else pltpu.VMEM for i in range(len(operands))]
-    moved = sum(x.size * x.dtype.itemsize for x in operands)
+def call(kernel, out_shape, *operands, scratch=(), smem=(), hbm=(), hbm_out=(), vmem=16):
+    spaces = [
+        pltpu.SMEM if i in smem else pltpu.HBM if i in hbm else pltpu.VMEM
+        for i in range(len(operands))
+    ]
+    out_specs = jax.tree.map(lambda _: pl.BlockSpec(memory_space=pltpu.VMEM), out_shape)
+    if hbm_out:
+        out_specs = tuple(
+            pl.BlockSpec(memory_space=pltpu.HBM if i in hbm_out else pltpu.VMEM)
+            for i in range(len(out_shape))
+        )
     return pl.pallas_call(
         kernel,
         out_shape=out_shape,
         in_specs=[pl.BlockSpec(memory_space=space) for space in spaces],
+        out_specs=out_specs,
         scratch_shapes=list(scratch),
         compiler_params=pltpu.CompilerParams(vmem_limit_bytes=vmem * MIB),
-        cost_estimate=pl.CostEstimate(flops=flops, bytes_accessed=moved, transcendentals=0),
+        cost_estimate=pl.CostEstimate(flops=0, bytes_accessed=0, transcendentals=0),
     )(*operands)
 
 
@@ -70,24 +79,61 @@
     return pl.ds(pl.multiple_of(index * size, size), size)
 
 
-def pack_kernel(gain_a, shift_a, bias, gain_m, shift_m, w_q, w_k, w_v, b_q, b_v, b_u, b_d, vec, loc, kept, sent):
+def start_copies(pairs, sems):
+    copies = [
+        pltpu.make_async_copy(source, target, sems.at[i]) for i, (source, target) in enumerate(pairs)
+    ]
+    for copy in copies:
+        copy.start()
+    return copies
+
+
+def vector_kernel(*refs):
+    sources, (vec, loc), held, sems = refs[:9], refs[9:11], refs[11:20], refs[20]
+    for copy in start_copies(list(zip(sources, held)), sems):
+        copy.wait()
     vec[...] = jnp.zeros_like(vec)
     loc[...] = jnp.zeros_like(loc)
-    for i, ref in enumerate((gain_a, shift_a, bias, gain_m, shift_m)):
+    for i, ref in enumerate(held[:5]):
         vec[i : i + 1] = ref[...].astype(F32).reshape(1, -1)
-    third = w_q.shape[1] // 2
+    b_q, b_v, b_u, b_d = held[5:]
+    third = b_q.shape[0]
     loc[0:1, :third] = b_q[...].astype(F32).reshape(1, -1)
     loc[0:1, 2 * third : 3 * third] = b_v[...].astype(F32).reshape(1, -1)
     loc[1:2, : b_u.shape[0]] = b_u[...].astype(F32).reshape(1, -1)
     loc[2:3, : b_d.shape[0]] = b_d[...].astype(F32).reshape(1, -1)
-    first = lax.axis_index("row") == 0
+
+
+def pack_kernel(w_q, w_k, w_v, w_out, w_up, w_down, loc, kept, sent, out_sent, up_sent, down_sent,
+                held_q, held_k, held_v, sems):
+    row, side = lax.axis_index("row"), lax.axis_index("dp") % 2
+    units = up_sent.shape[1]
+    sent_rows = sent.shape[0]
+    out_rows, up_rows, down_rows = out_sent.shape[0], up_sent.shape[0], down_sent.shape[0]
+    copies = start_copies(
+        [
+            (w_q, held_q),
+            (w_k, held_k),
+            (w_v, held_v),
+            (w_out.at[half_rows(side, out_rows)], out_sent),
+            (w_up.at[half_rows(side, up_rows), half_rows(1 - row, units)], up_sent),
+            (w_down.at[half_rows(2 * (1 - row) + side, down_rows)], down_sent),
+        ],
+        sems,
+    )
+    first = row == 0
+    third = w_q.shape[1] // 2
     keeps, sends = [], []
-    for ref in (w_q, w_k, w_v):
+    for ref, copy in zip((held_q, held_k, held_v), copies):
+        copy.wait()
         low, high = ref[:, :third], ref[:, third:]
         keeps.append(jnp.where(first, low, high))
         sends.append(jnp.where(first, high, low))
     kept[...] = jnp.concatenate(keeps, axis=1)
-    sent[...] = jnp.concatenate(sends, axis=1)
+    whole = jnp.concatenate(sends, axis=1)
+    sent[...] = jnp.where(side == 0, whole[:sent_rows], whole[sent_rows:])
+    for copy in copies[3:]:
+        copy.wait()
 
 
 def normed_parts(values):
@@ -124,20 +170,25 @@
     return (key >= begin) & (key <= query)
 
 
-def forward_kernel(lengths, own, other, w_kept, w_got, loc, norm_out, q_out, k_out, v_out, o_out, lse):
+def forward_kernel(lengths, own, other, w_kept, got, got_side, loc, norm_hbm, q_hbm, k_hbm, v_hbm, o_out, lse,
+                   norm_out, q_out, k_out, v_out, sems):
     own_rows, width = own.shape
     half = width // 2
     third = q_out.shape[1]
     col = lax.axis_index("col")
+    w_got = both_sides(got, got_side, 0)
     for ref, at in ((own, col), (other, 1 - col)):
         where = half_rows(at, own_rows)
         values = ref[...]
         norm_out[where] = values
-        total = dot(values[:, :half], w_kept[...]) + dot(values[:, half:], w_got[...])
+        total = dot(values[:, :half], w_kept[...]) + dot(values[:, half:], w_got)
         total = (total + loc[0:1, : 3 * third]).astype(BF16)
         q_out[where] = total[:, :third]
         k_out[where] = total[:, third : 2 * third]
         v_out[where] = total[:, 2 * third :]
+    copies = start_copies(
+        [(norm_out, norm_hbm), (q_out, q_hbm), (k_out, k_hbm), (v_out, v_hbm)], sems
+    )
     lse[...] = jnp.zeros_like(lse)
     values_t = v_out[...].T
     for begin in (0, own_rows):
@@ -157,6 +208,8 @@
             )
             parts.append(mixed / summed)
         o_out[begin:keys] = jnp.concatenate(parts, axis=0).T.astype(BF16)
+    for copy in copies:
+        copy.wait()
 
 
 def split_tokens(total_of, keep, send, own_rows, col):
@@ -164,7 +217,8 @@
     send[...] = total_of(half_rows(1 - col, own_rows)).astype(BF16)
 
 
-def branch_kernel(mixed, mixed_other, w_mine, w_other, keep, send):
+def branch_kernel(mixed, mixed_other, w_mine, got, got_side, keep, send, w_other):
+    w_other[...] = both_sides(got, got_side, 0)
     row, col = lax.axis_index("row"), lax.axis_index("col")
     third = mixed.shape[1]
     own, far = half_rows(row, third), half_rows(1 - row, third)
@@ -293,8 +347,12 @@
     sums[1:2] = jnp.sum(grads[:, :half], axis=0, keepdims=True)
 
 
-def backward_kernel(bit_first, bit_second, lengths, own, other, w_mine, w_other, q_ref, k_ref, v_ref, o_ref, lse, normed, w_kept, w_got,
-                    first_keep, first_send, second_keep, second_send, keep, send, sums, datt, out, acc_k, acc_v, do_ref):
+def backward_kernel(bit_first, bit_second, lengths, own, other, w_mine, w_other, q_hbm, k_hbm, v_hbm, o_ref, lse, normed_hbm, w_kept, got, got_side,
+                    first_keep, first_send, second_keep, second_send, keep, send, sums, datt, out, acc_k, acc_v, do_ref,
+                    q_ref, k_ref, v_ref, normed, sems):
+    copies = start_copies(
+        [(q_hbm, q_ref), (k_hbm, k_ref), (v_hbm, v_ref), (normed_hbm, normed)], sems
+    )
     own_rows, width = own.shape
     half = width // 2
     third = q_ref.shape[1]
@@ -307,6 +365,8 @@
         do_ref[where] = (
             dot_nt(values[:, :half], w_mine[quarter]) + dot_nt(values[:, half:], w_other[quarter])
         ).astype(BF16)
+    for copy in copies:
+        copy.wait()
     keys_t = k_ref[...].T
     acc_k[...] = jnp.zeros_like(acc_k)
     acc_v[...] = jnp.zeros_like(acc_v)
@@ -340,9 +400,11 @@
     last = jnp.concatenate([weights[:, 2 * third :], grad_out], axis=1)
     split_rows(last.reshape(2, half, 2 * third), second_keep, second_send, bit_second)
 
+    w_got = both_sides(got, got_side, 0)
+
     def total_of(rows):
         values = out[rows]
-        return jnp.concatenate([dot_nt(values, w_kept[...]), dot_nt(values, w_got[...])], axis=1)
+        return jnp.concatenate([dot_nt(values, w_kept[...]), dot_nt(values, w_got)], axis=1)
 
     split_tokens(total_of, keep, send, own_rows, col)
     sums[...] = jnp.zeros_like(sums)
@@ -555,43 +617,45 @@
     pair_sums = shape((8, half), F32)
 
     tokens_far = from_row(tokens)
-    operands = (
-        gain_attn, shift_attn, b_out, gain_mlp, shift_mlp, w_query, w_key, w_value,
-        b_query, b_value, b_up, b_down,
-    )
-    out_shape = (
-        shape((8, half), F32),
-        shape((8, units), F32),
-        shape((half, 3 * third), BF16),
-        shape((half, 3 * third), BF16),
-    )
-    whole = lambda x: pl.BlockSpec(x.shape, lambda i: (0,) * len(x.shape))
-    vec, loc, w_kept, sent = pl.pallas_call(
+    operands = (gain_attn, shift_attn, b_out, gain_mlp, shift_mlp, b_query, b_value, b_up, b_down)
+    vec, loc = call(
+        vector_kernel,
+        (shape((8, half), F32), shape((8, units), F32)),
+        *operands,
+        hbm=range(9),
+        vmem=60,
+        scratch=[pltpu.VMEM(x.shape, x.dtype) for x in operands] + [pltpu.SemaphoreType.DMA((9,))],
+    )
+    vec_far = from_row(vec)
+    block = pltpu.VMEM((half, 2 * third), BF16)
+    w_kept, sent, sent_out, sent_up, sent_down = call(
         pack_kernel,
-        grid=(1,),
-        out_shape=out_shape,
-        in_specs=[whole(x) for x in operands],
-        out_specs=tuple(pl.BlockSpec(memory_space=pltpu.VMEM) for _ in out_shape),
-        compiler_params=pltpu.CompilerParams(vmem_limit_bytes=16 * MIB),
-    )(*operands)
-    vec_far = from_row(vec)
+        (
+            shape((half, 3 * third), BF16),
+            shape((half // 2, 3 * third), BF16),
+            shape((w_out.shape[0] // 2, half), BF16),
+            shape((half // 2, units), BF16),
+            shape((units // 2, half), BF16),
+        ),
+        w_query, w_key, w_value, w_out, w_up, w_down, loc,
+        hbm=range(6),
+        vmem=60,
+        scratch=[block, block, block, pltpu.SemaphoreType.DMA((6,))],
+    )
+    top_col = from_col(out_grad)
+    tokens_far, vec_far, sent = hold(tokens_far, vec_far, sent)
     w_got = from_row(sent)
-    top_col = from_col(out_grad)
-    sent_up = lax.dynamic_slice(
-        w_up, (side * (half // 2), (1 - row) * units), (half // 2, units)
-    )
-    sent_down = lax.dynamic_slice(
-        w_down, ((1 - row) * units + side * (units // 2), 0), (units // 2, half)
-    )
-    tokens_far, vec_far, w_out_send, sent_up = hold(tokens_far, vec_far, w_out, sent_up)
-
     normed, unit_attn, inverse_attn = call(
         first_norm_kernel, (tall_low, tall, column), tokens, tokens_far, vec, vec_far
     )
+    normed, sent_out, sent_up, sent_down = hold(normed, sent_out, sent_up, sent_down)
     normed_col = from_col(normed)
-    w_out_far = from_row(w_out_send)
+    w_side = from_dp(w_got, 0)
+    out_got = from_row(sent_out)
     up_got = from_row(sent_up)
-    normed_col, w_got = hold(normed_col, w_got)
+    down_got = from_row(sent_down)
+    normed_col, w_got, w_side, out_got = hold(normed_col, w_got, w_side, out_got)
+    out_side = from_dp(out_got, 0)
 
     like = shape((rows, third), BF16)
     normed_all, query, key, value, mixed, lse = call(
@@ -602,23 +666,29 @@
         normed_col,
         w_kept,
         w_got,
+        w_side,
         loc,
-        flops=2 * rows * third * (3 * width + 2 * rows),
         smem=(0,),
-    )
+        hbm_out=range(4),
+        scratch=[pltpu.VMEM((rows, width), BF16)]
+        + [pltpu.VMEM((rows, third), BF16)] * 3
+        + [pltpu.SemaphoreType.DMA((4,))],
+    )
+    mixed, up_got = hold(mixed, up_got)
     mixed_far = from_row(mixed)
-    mixed_far, w_out_far, out_grad_send, sent_down, up_got = hold(
-        mixed_far, w_out_far, out_grad, sent_down, up_got
-    )
-
-    keep, send = call(
-        branch_kernel, (tall, tall_low), mixed, mixed_far, w_out, w_out_far,
-        flops=2 * rows * width * half,
+    up_side = from_dp(up_got, 0)
+    mixed_far, out_side, up_side, down_got, out_grad_send = hold(
+        mixed_far, out_side, up_side, down_got, out_grad
+    )
+
+    keep, send, w_out_far = call(
+        branch_kernel, (tall, tall_low, shape(w_out.shape, BF16)),
+        mixed, mixed_far, w_out, out_got, out_side,
     )
     got = from_col(send)
-    up_side = from_dp(up_got, 0)
     top_far = from_row(out_grad_send)
-    down_got = from_row(sent_down)
+    top_far_col = from_col(top_far)
+    down_side = from_dp(down_got, 0)
     (got,) = hold(got)
 
     middle, normed_mlp, unit_mlp, inverse_mlp = call(
@@ -627,7 +697,7 @@
         tokens, tokens_far, keep, got, vec, vec_far,
     )
     normed_mlp_col = from_col(normed_mlp)
-    normed_mlp_col, up_side, top_far = hold(normed_mlp_col, up_side, top_far)
+    normed_mlp_col, top_far, down_side = hold(normed_mlp_col, top_far, down_side)
 
     normed_mlp_all, hidden, slope, w_up_far = call(
         up_kernel,
@@ -638,11 +708,8 @@
             shape((half, units), BF16),
         ),
         normed_mlp, normed_mlp_col, w_up, up_got, up_side, loc,
-        flops=2 * rows * width * units,
-    )
-    top_far_col = from_col(top_far)
-    down_side = from_dp(down_got, 0)
-    hidden, top_far_col, down_side = hold(hidden, top_far_col, down_side)
+    )
+    hidden, top_far, top_far_col, down_side = hold(hidden, top_far, top_far_col, down_side)
 
     split_down = shape((units // 2, width), BF16)
     split_up = shape((2, half // 2, units), BF16)
@@ -654,7 +721,6 @@
         ),
         seq_lengths, out_grad, top_far, top_col, top_far_col, hidden, slope, normed_mlp_all,
         w_down, down_got, down_side, w_up, w_up_far,
-        flops=8 * rows * width * units,
         scratch=[pltpu.VMEM((rows, width), BF16), pltpu.VMEM((rows, units), BF16)],
         smem=(0,),
     )
@@ -667,7 +733,6 @@
     total_far = from_row(total)
     keep, send = call(
         output_kernel, (tall, tall_low), hidden, w_down, w_down_far,
-        flops=2 * rows * width * units,
     )
     got = from_col(send)
     total_far, got = hold(total_far, got)
@@ -689,16 +754,17 @@
         lambda *refs: backward_kernel(bits[0], turned[0], *refs),
         (split_pair,) * 4 + (tall, tall_low, shape((8, width), F32)),
         seq_lengths, datt, datt_col, w_out, w_out_far, query, key, value, mixed, lse,
-        normed_all, w_kept, w_got,
-        flops=2 * rows * third * (5 * width + 5 * rows),
+        normed_all, w_kept, w_got, w_side,
         scratch=[
             pltpu.VMEM((rows, width), BF16),
             pltpu.VMEM((rows, 3 * third), BF16),
             pltpu.VMEM((rows, third), F32),
             pltpu.VMEM((rows, third), F32),
-            pltpu.VMEM((rows, third), BF16),
-        ],
+        ]
+        + [pltpu.VMEM((rows, third), BF16)] * 4
+        + [pltpu.VMEM((rows, width), BF16), pltpu.SemaphoreType.DMA((4,))],
         smem=(0,),
+        hbm=(5, 6, 7, 10),
     )
     keep, send, raised_far = arrived([down, up], keep, send, raised_far)
     got = from_col(send)
@@ -715,8 +781,9 @@
     )
     got = from_row(far)
     stats_far = from_row(stats)
-    got, stats_far = arrived([down, up, first, second], got, stats_far)
-    advance([down, up, first, second])
+    pair, late = [first, second], [down, up]
+    got, stats_far = arrived(pair + late, got, stats_far)
+    advance(pair + late)
     input_grad, in_sums = call(
         last_kernel,
         (shape((own_rows, half), BF16), pair_sums),
@@ -724,21 +791,27 @@
     )
 
     halves = jnp.concatenate([in_sums, mid_sums], axis=1)
-    halves = halves + from_col(halves)
+    halves_col = from_col(halves)
+    (halves_col,) = arrived(pair + late, halves_col)
     small = jnp.concatenate(
-        [halves[:2], mlp_sums[:2, :width], attn_sums[:2], jnp.zeros((2, width), F32)]
-    )
-    for bit in bits:
-        (small,) = arrived([down, up, first, second], small)
-        if first.stage < first.steps - 1:
-            advance([down, up, first, second])
+        [
+            (halves + halves_col)[:2],
+            mlp_sums[:2, :width],
+            attn_sums[:2],
+            jnp.zeros((2, width), F32),
+        ]
+    )
+    waiting = list(bits)
+    while pair[0].stage < pair[0].steps - 1:
+        moving = [chain for chain in late + pair if chain.stage < chain.steps - 1]
+        advance(moving)
+        if waiting:
+            (small_far,) = arrived(moving, from_dp(small, waiting.pop(0)))
+            small = small + small_far
+        else:
+            arrived(moving)
+    for bit in waiting:
         small = small + from_dp(small, bit)
-    for chain in (first, second):
-        while chain.stage < chain.steps - 1:
-            chain.step()
-    for chain in (down, up):
-        while chain.stage < chain.steps - 1:
-            chain.step()
 
     wide = w_query.shape[1]
     outs = (shape((half, wide), F32),) * 2

time: 204 us -> 183 us (0.90)
  local copies, waits for them, and re-layouts: 15.6 us -> 3 us
  waiting for transfers between devices: 96 us -> 83.9 us
  starting transfers between devices: 58 us -> 60.8 us
    ppermute x16, waiting for transfers between devices: 38.8 us -> 27 us  [from_row(): return lax.ppermute(values, 'row', SWAP)]
    unnamed x51 -> x21, local copies, waits for them, and re-layouts: 12 us -> 1.08 us
    ppermute x29 -> x31, starting transfers between devices: 38.3 us -> 41.5 us  [from_dp(): return lax.ppermute(values, 'dp', dp_pairs(bit))]
    pallas_call x37 -> x39, Pallas kernels: 27 us -> 29.7 us  [call(): pl.pallas_call(kernel, out_shape=out_shape, in_specs=[pl.BlockSpec(memory...]
    ppermute x29 -> x31, waiting for transfers between devices: 55.3 us -> 54 us  [from_dp(): return lax.ppermute(values, 'dp', dp_pairs(bit))]
  transfers between devices with their start and end apart: 55 -> 57, of which waited for: 25 -> 28; matrix products, arithmetic and copies ran while one was open for 2% -> 2% of each run, Pallas kernels for 11% -> 14%
where the time goes in v3:
time: 183 us
  waiting for transfers between devices  83.9 us (46%)
  starting transfers between devices  60.8 us (33%)
  Pallas kernels  33.2 us (18%)
  local copies, waits for them, and re-layouts  3 us (2%)
    ppermute x31, waiting for transfers between devices, from_dp(): return lax.ppermute(values, 'dp', dp_pairs(bit))  54 us
    ppermute x31, starting transfers between devices, from_dp(): return lax.ppermute(values, 'dp', dp_pairs(bit))  41.5 us
    pallas_call x39, Pallas kernels, call(): pl.pallas_call(kernel, out_shape=out_shape, in_specs=[pl.BlockSpec(memory...  29.7 us
    ppermute x16, waiting for transfers between devices, from_row(): return lax.ppermute(values, 'row', SWAP)  27 us
    ppermute x16, starting transfers between devices, from_row(): return lax.ppermute(values, 'row', SWAP)  17.7 us
  transfers between devices with their start and end apart: 57, of which 28 were waited for; matrix products, arithmetic and copies ran while one was open for 2% of the time, Pallas kernels for 14%

profile of v3, /device:TPU:0, one launch (start us, length us, event | category | flops | bytes accessed | tf_op | source)
XLA Modules:
  0.0 183.2 jit_solution(9779407306557487849)
XLA Ops:
  0.7 3.0 %collective-permute-start = (bf16[256,384]{1,0:T(8,128)(2,1)}, bf16[256,384]{1,0:T(8,128)(2,1)S(1)}, u32[]{:S(2)}, u32[]{:S(2)}) collective-permute-start(bf16[256,384]{1,0:T(8,128)(2,1)} %tokens.3), channel_id=1, source_target_pairs={{0,2},{2,0},{1,3},{3,1},{4,6},{6,4},{5,7},{7,5},{8,10},{10,8},{9,1... | collective-permute-start | bytes 589832 | tf_op jit(solution)/shard_map/ppermute | solution.py:32
  5.3 3.6 %shard_map.306 = (bf16[384,576]{1,0:T(8,128)(2,1)}, bf16[192,576]{1,0:T(8,128)(2,1)}, bf16[192,384]{1,0:T(8,128)(2,1)}, bf16[192,768]{1,0:T(8,128)(2,1)}, bf16[384,384]{1,0:T(8,128)(2,1)}) custom-call(bf16[384,384]{1,0:T(8,128)(2,1)} %w_q.1, bf16[384,384]{1,0:T(8,128)(2,1)} %w_k.1, bf16[384,384]{1,0:T(8,128)(2,1)} %w_v.1, bf16[384,384]{1,0:T(8,128)(2,1)} %refs_3_.3, ...), custom_call_target="tpu_custom_call" | custom-call | tf_op jit(solution)/shard_map/pallas_call | solution.py:67
  11.7 6.6 %collective-permute-done.3.got.refs_12_ = bf16[192,576]{1,0:T(8,128)(2,1)S(1)} collective-permute-done((bf16[192,576]{1,0:T(8,128)(2,1)}, bf16[192,576]{1,0:T(8,128)(2,1)S(1)}, u32[]{:S(2)}, u32[]{:S(2)}) %collective-permute-start.3) | collective-permute-done | bytes 221216 | tf_op jit(solution)/shard_map/ppermute | solution.py:32
  22.1 5.7 %collective-permute-done.5.got = bf16[192,384]{1,0:T(8,128)(2,1)S(1)} collective-permute-done((bf16[192,384]{1,0:T(8,128)(2,1)}, bf16[192,384]{1,0:T(8,128)(2,1)S(1)}, u32[]{:S(2)}, u32[]{:S(2)}) %collective-permute-start.5) | collective-permute-done | bytes 147488 | tf_op jit(solution)/shard_map/ppermute | solution.py:32
  28.8 4.1 %shard_map.308 = (bf16[512,768]{1,0:T(8,128)(2,1)S(1)}, bf16[512,192]{1,0:T(8,128)(2,1)S(1)}, bf16[512,192]{1,0:T(8,128)(2,1)S(1)}, bf16[512,192]{1,0:T(8,128)(2...) custom-call(s32[1,2]{1,0:T(1,128)S(1)} %copy-done.9, bf16[256,768]{1,0:T(8,128)(2,1)S(1)} %get-tuple-element.199.own, ...), custom_call_target="tpu_custom_call" | custom-call | tf_op jit(solution)/shard_map/pallas_call | solution.py:67
  33.0 1.9 %collective-permute-start.9 = (bf16[192,768]{1,0:T(8,128)(2,1)S(1)}, bf16[192,768]{1,0:T(8,128)(2,1)S(1)}, u32[]{:S(2)}, u32[]{:S(2)}) collective-permute-start(bf16[192,768]{1,0:T(8,128)(2,1)S(1)} %collective-permute-done.6.got), channel_id=1, source_target_pairs={{0,4},{4,0},{8,12},{12,8},{16,20},{20,16},{24,28},{28,24},{1,5},{5... | collective-permute-start | bytes 884744 | tf_op jit(solution)/shard_map/ppermute | solution.py:45
  36.9 5.1 %collective-permute-done.8.got_side = bf16[192,384]{1,0:T(8,128)(2,1)S(1)} collective-permute-done((bf16[192,384]{1,0:T(8,128)(2,1)S(1)}, bf16[192,384]{1,0:T(8,128)(2,1)S(1)}, u32[]{:S(2)}, u32[]{:S(2)}) %collective-permute-start.8) | collective-permute-done | bytes 147488 | tf_op jit(solution)/shard_map/ppermute | solution.py:45
  48.2 4.2 %collective-permute-done.13.refs_2_.top_far = bf16[256,384]{1,0:T(8,128)(2,1)S(1)} collective-permute-done((bf16[256,384]{1,0:T(8,128)(2,1)S(1)}, bf16[256,384]{1,0:T(8,128)(2,1)S(1)}, u32[]{:S(2)}, u32[]{:S(2)}) %collective-permute-start.13) | collective-permute-done | bytes 196640 | tf_op jit(solution)/shard_map/ppermute | solution.py:32
  52.9 2.8 %collective-permute-done.14.refs_10_ = bf16[384,384]{1,0:T(8,128)(2,1)S(1)} collective-permute-done((bf16[384,384]{1,0:T(8,128)(2,1)S(1)}, bf16[384,384]{1,0:T(8,128)(2,1)S(1)}, u32[]{:S(2)}, u32[]{:S(2)}) %collective-permute-start.14) | collective-permute-done | bytes 294944 | tf_op jit(solution)/shard_map/ppermute | solution.py:45
  57.2 4.2 %shard_map.312 = (bf16[384,768]{1,0:T(8,128)(2,1)S(1)}, bf16[384,768]{1,0:T(8,128)(2,1)S(1)}, bf16[2,192,768]{2,1,0:T(8,128)(2,1)S(1)}, bf16[2,192,768]{2,1,0:T(...) custom-call(s32[1,2]{1,0:T(1,128)S(1)} %copy-done.9, ...), custom_call_target="tpu_custom_call" | custom-call | tf_op jit(solution)/shard_map/pallas_call | solution.py:67
  66.9 7.6 %collective-permute-done.18.total_far = bf16[256,768]{1,0:T(8,128)(2,1)S(1)} collective-permute-done((bf16[256,768]{1,0:T(8,128)(2,1)S(1)}, bf16[256,768]{1,0:T(8,128)(2,1)S(1)}, u32[]{:S(2)}, u32[]{:S(2)}) %collective-permute-start.18) | collective-permute-done | bytes 393248 | tf_op jit(solution)/shard_map/ppermute | solution.py:32
  75.8 3.2 %collective-permute-done.20.refs_1_ = bf16[384,768]{1,0:T(8,128)(2,1)S(1)} collective-permute-done((bf16[384,768]{1,0:T(8,128)(2,1)S(1)}, bf16[384,768]{1,0:T(8,128)(2,1)S(1)}, u32[]{:S(2)}, u32[]{:S(2)}) %collective-permute-start.20) | collective-permute-done | bytes 589856 | tf_op jit(solution)/shard_map/ppermute | solution.py:45
  84.5 6.1 %shard_map.317 = (bf16[2,192,384]{2,1,0:T(8,128)(2,1)S(1)}, bf16[2,192,384]{2,1,0:T(8,128)(2,1)S(1)}, bf16[2,192,384]{2,1,0:T(8,128)(2,1)S(1)}, bf16[2,192,384]{...) custom-call(s32[1,2]{1,0:T(1,128)S(1)} %copy-done.9, ...), custom_call_target="tpu_custom_call" | custom-call | tf_op jit(solution)/shard_map/pallas_call | solution.py:67
  93.6 2.7 %collective-permute-start.29 = (bf16[96,768]{1,0:T(8,128)(2,1)S(1)}, bf16[96,768]{1,0:T(8,128)(2,1)S(1)}, u32[]{:S(2)}, u32[]{:S(2)}) collective-permute-start(bf16[96,768]{1,0:T(8,128)(2,1)S(1)} %get-tuple-element.275), channel_id=1, source_target_pairs={{0,16},{4,20},{8,24},{12,28},{16,0},{20,4},{24,8},{28,12},{1,17},{... | collective-permute-start | bytes 442376 | tf_op jit(solution)/shard_map/ppermute | solution.py:45
  96.8 3.3 %collective-permute-done.27.refs_1_ = bf16[2,192,384]{2,1,0:T(8,128)(2,1)S(1)} collective-permute-done((bf16[2,192,384]{2,1,0:T(8,128)(2,1)S(1)}, bf16[2,192,384]{2,1,0:T(8,128)(2,1)S(1)}, u32[]{:S(2)}, u32[]{:S(2)}) %collective-permute-start.27) | collective-permute-done | bytes 294944 | tf_op jit(solution)/shard_map/ppermute | solution.py:45
  100.6 7.1 %collective-permute-done.28.refs_1_ = bf16[2,192,384]{2,1,0:T(8,128)(2,1)S(1)} collective-permute-done((bf16[2,192,384]{2,1,0:T(8,128)(2,1)S(1)}, bf16[2,192,384]{2,1,0:T(8,128)(2,1)S(1)}, u32[]{:S(2)}, u32[]{:S(2)}) %collective-permute-start.28) | collective-permute-done | bytes 294944 | tf_op jit(solution)/shard_map/ppermute | solution.py:45
  107.8 2.7 %collective-permute-start.33 = (bf16[2,96,384]{2,1,0:T(8,128)(2,1)S(1)}, bf16[2,96,384]{2,1,0:T(8,128)(2,1)S(1)}, u32[]{:S(2)}, u32[]{:S(2)}) collective-permute-start(bf16[2,96,384]{2,1,0:T(8,128)(2,1)S(1)} %get-tuple-element.290), channel_id=1, source_target_pairs={{0,8},{4,12},{8,0},{12,4},{16,24},{20,28},{24,16},{28,20},{1,9},{5... | collective-permute-start | bytes 442376 | tf_op jit(solution)/shard_map/ppermute | solution.py:45
  118.5 3.3 %collective-permute-start.40 = (bf16[2,48,384]{2,1,0:T(8,128)(2,1)S(1)}, bf16[2,48,384]{2,1,0:T(8,128)(2,1)S(1)}, u32[]{:S(2)}, u32[]{:S(2)}) collective-permute-start(bf16[2,48,384]{2,1,0:T(8,128)(2,1)S(1)} %get-tuple-element.312), channel_id=1, source_target_pairs={{0,16},{4,20},{8,24},{12,28},{16,0},{20,4},{24,8},{28,12},{1,17},{... | collective-permute-start | bytes 221192 | tf_op jit(solution)/shard_map/ppermute | solution.py:45
  122.0 3.0 %collective-permute-start.39 = (bf16[2,48,768]{2,1,0:T(8,128)(2,1)S(1)}, bf16[2,48,768]{2,1,0:T(8,128)(2,1)S(1)}, u32[]{:S(2)}, u32[]{:S(2)}) collective-permute-start(bf16[2,48,768]{2,1,0:T(8,128)(2,1)S(1)} %shard_map.327.refs_0_), channel_id=1, source_target_pairs={{0,16},{4,20},{8,24},{12,28},{16,0},{20,4},{24,8},{28,12},{1,17},{... | collective-permute-start | bytes 442376 | tf_op jit(solution)/shard_map/ppermute | solution.py:45
  126.6 2.3 %collective-permute-done.42 = f32[8,768]{1,0:T(8,128)S(1)} collective-permute-done((f32[8,768]{1,0:T(8,128)S(1)}, f32[8,768]{1,0:T(8,128)S(1)}, u32[]{:S(2)}, u32[]{:S(2)}) %collective-permute-start.42) | collective-permute-done | bytes 24608 | tf_op jit(solution)/shard_map/ppermute | solution.py:45
  129.0 3.8 %collective-permute-done.40.refs_1_ = bf16[2,48,384]{2,1,0:T(8,128)(2,1)S(1)} collective-permute-done((bf16[2,48,384]{2,1,0:T(8,128)(2,1)S(1)}, bf16[2,48,384]{2,1,0:T(8,128)(2,1)S(1)}, u32[]{:S(2)}, u32[]{:S(2)}) %collective-permute-start.40) | collective-permute-done | bytes 73760 | tf_op jit(solution)/shard_map/ppermute | solution.py:45
  134.4 3.2 %collective-permute-done.39.refs_1_ = bf16[2,48,768]{2,1,0:T(8,128)(2,1)S(1)} collective-permute-done((bf16[2,48,768]{2,1,0:T(8,128)(2,1)S(1)}, bf16[2,48,768]{2,1,0:T(8,128)(2,1)S(1)}, u32[]{:S(2)}, u32[]{:S(2)}) %collective-permute-start.39) | collective-permute-done | bytes 147488 | tf_op jit(solution)/shard_map/ppermute | solution.py:45
  137.6 2.0 %collective-permute-done.38.refs_1_ = bf16[2,96,384]{2,1,0:T(8,128)(2,1)S(1)} collective-permute-done((bf16[2,96,384]{2,1,0:T(8,128)(2,1)S(1)}, bf16[2,96,384]{2,1,0:T(8,128)(2,1)S(1)}, u32[]{:S(2)}, u32[]{:S(2)}) %collective-permute-start.38) | collective-permute-done | bytes 147488 | tf_op jit(solution)/shard_map/ppermute | solution.py:45
  143.5 2.0 %collective-permute-start.47 = (f32[8,768]{1,0:T(8,128)S(1)}, f32[8,768]{1,0:T(8,128)S(1)}, u32[]{:S(2)}, u32[]{:S(2)}) collective-permute-start(f32[8,768]{1,0:T(8,128)S(1)} %fusion.3), channel_id=1, source_target_pairs={{0,8},{4,12},{8,0},{12,4},{16,24},{20,28},{24,16},{28,20},{1,9},{5... | collective-permute-start | bytes 73736 | tf_op jit(solution)/shard_map/ppermute | solution.py:45
  145.5 4.1 %collective-permute-done.47 = f32[8,768]{1,0:T(8,128)S(1)} collective-permute-done((f32[8,768]{1,0:T(8,128)S(1)}, f32[8,768]{1,0:T(8,128)S(1)}, u32[]{:S(2)}, u32[]{:S(2)}) %collective-permute-start.47) | collective-permute-done | bytes 24608 | tf_op jit(solution)/shard_map/ppermute | solution.py:45
  150.6 2.5 %collective-permute-start.52 = (f32[8,768]{1,0:T(8,128)S(1)}, f32[8,768]{1,0:T(8,128)S(1)}, u32[]{:S(2)}, u32[]{:S(2)}) collective-permute-start(f32[8,768]{1,0:T(8,128)S(1)} %add.43), channel_id=1, source_target_pairs={{0,16},{4,20},{8,24},{12,28},{16,0},{20,4},{24,8},{28,12},{1,17},{... | collective-permute-start | bytes 73736 | tf_op jit(solution)/shard_map/ppermute | solution.py:45
  153.6 2.5 %collective-permute-start.50 = (bf16[2,48,384]{2,1,0:T(8,128)(2,1)S(1)}, bf16[2,48,384]{2,1,0:T(8,128)(2,1)S(1)}, u32[]{:S(2)}, u32[]{:S(2)}) collective-permute-start(bf16[2,48,384]{2,1,0:T(8,128)(2,1)S(1)} %shard_map.336.refs_0_), channel_id=1, source_target_pairs={{0,16},{4,20},{8,24},{12,28},{16,0},{20,4},{24,8},{28,12},{1,17},{... | collective-permute-start | bytes 221192 | tf_op jit(solution)/shard_map/ppermute | solution.py:45
  156.1 7.2 %collective-permute-done.52 = f32[8,768]{1,0:T(8,128)S(1)} collective-permute-done((f32[8,768]{1,0:T(8,128)S(1)}, f32[8,768]{1,0:T(8,128)S(1)}, u32[]{:S(2)}, u32[]{:S(2)}) %collective-permute-start.52) | collective-permute-done | bytes 24608 | tf_op jit(solution)/shard_map/ppermute | solution.py:45
  164.9 1.9 %collective-permute-done.49.refs_1_ = bf16[2,192,768]{2,1,0:T(8,128)(2,1)S(1)} collective-permute-done((bf16[2,192,768]{2,1,0:T(8,128)(2,1)S(1)}, bf16[2,192,768]{2,1,0:T(8,128)(2,1)S(1)}, u32[]{:S(2)}, u32[]{:S(2)}) %collective-permute-start.49) | collective-permute-done | bytes 589856 | tf_op jit(solution)/shard_map/ppermute | solution.py:45
  170.4 2.0 %shard_map.345 = f32[1536,384]{1,0:T(8,128)} custom-call(bf16[2,384,384]{2,1,0:T(8,128)(2,1)S(1)} %shard_map.334.refs_0_, bf16[2,384,384]{2,1,0:T(8,128)(2,1)S(1)} %collective-permute-done.48.refs_1_), custom_call_target="tpu_custom_call" | custom-call | tf_op jit(solution)/shard_map/pallas_call | solution.py:574
  174.1 2.1 %collective-permute-start.55 = (bf16[2,192,384]{2,1,0:T(8,128)(2,1)S(1)}, bf16[2,192,384]{2,1,0:T(8,128)(2,1)S(1)}, u32[]{:S(2)}, u32[]{:S(2)}) collective-permute-start(bf16[2,192,384]{2,1,0:T(8,128)(2,1)S(1)} %shard_map.340.refs_0_), channel_id=1, source_target_pairs={{0,4},{4,0},{8,12},{12,8},{16,20},{20,16},{24,28},{28,24},{1,5},{5... | collective-permute-start | bytes 884744 | tf_op jit(solution)/shard_map/ppermute | solution.py:45
  177.3 2.5 %collective-permute-done.56.refs_1_ = bf16[2,192,384]{2,1,0:T(8,128)(2,1)S(1)} collective-permute-done((bf16[2,192,384]{2,1,0:T(8,128)(2,1)S(1)}, bf16[2,192,384]{2,1,0:T(8,128)(2,1)S(1)}, u32[]{:S(2)}, u32[]{:S(2)}) %collective-permute-start.56) | collective-permute-done | bytes 294944 | tf_op jit(solution)/shard_map/ppermute | solution.py:45
  (162 shorter events, 64.0 us)
Async XLA Ops:
  0.7 8.5 %collective-permute-start = (bf16[256,384]{1,0:T(8,128)(2,1)}, bf16[256,384]{1,0:T(8,128)(2,1)S(1)}, u32[]{:S(2)}, u32[]{:S(2)}) collective-permute-start(bf16[256,384]{1,0:T(8,128)(2,1)} %tokens.3), channel_id=1, source_target_pairs={{0,2},{2,0},{1,3},{3,1},{4,6},{6,4},{5,7},{7,5},{8,10},{10,8},{9,1... | collective-permute-start | bytes 589832 | tf_op jit(solution)/shard_map/ppermute | solution.py:32
  9.2 9.1 %collective-permute-start.3 = (bf16[192,576]{1,0:T(8,128)(2,1)}, bf16[192,576]{1,0:T(8,128)(2,1)S(1)}, u32[]{:S(2)}, u32[]{:S(2)}) collective-permute-start(bf16[192,576]{1,0:T(8,128)(2,1)} %get-tuple-element.200), channel_id=1, source_target_pairs={{0,2},{2,0},{1,3},{3,1},{4,6},{6,4},{5,7},{7,5},{8,10},{10,8},{9,1... | collective-permute-start | bytes 663560 | tf_op jit(solution)/shard_map/ppermute | solution.py:32
  11.3 16.4 %collective-permute-start.2 = (bf16[256,768]{1,0:T(8,128)(2,1)S(1)}, bf16[256,768]{1,0:T(8,128)(2,1)S(1)}, u32[]{:S(2)}, u32[]{:S(2)}) collective-permute-start(bf16[256,768]{1,0:T(8,128)(2,1)S(1)} %get-tuple-element.199.own), channel_id=1, source_target_pairs={{0,1},{1,0},{2,3},{3,2},{4,5},{5,4},{6,7},{7,6},{8,9},{9,8},{10,11... | collective-permute-start | bytes 1179656 | tf_op jit(solution)/shard_map/ppermute | solution.py:36
  11.4 21.5 %collective-permute-start.6 = (bf16[192,768]{1,0:T(8,128)(2,1)}, bf16[192,768]{1,0:T(8,128)(2,1)S(1)}, u32[]{:S(2)}, u32[]{:S(2)}) collective-permute-start(bf16[192,768]{1,0:T(8,128)(2,1)} %get-tuple-element.207), channel_id=1, source_target_pairs={{0,2},{2,0},{1,3},{3,1},{4,6},{6,4},{5,7},{7,5},{8,10},{10,8},{9,1... | collective-permute-start | bytes 884744 | tf_op jit(solution)/shard_map/ppermute | solution.py:32
  18.3 9.5 %collective-permute-start.4 = (bf16[192,576]{1,0:T(8,128)(2,1)S(1)}, bf16[192,576]{1,0:T(8,128)(2,1)S(1)}, u32[]{:S(2)}, u32[]{:S(2)}) collective-permute-start(bf16[192,576]{1,0:T(8,128)(2,1)S(1)} %collective-permute-done.3.got.refs_12_), channel_id=1, source_target_pairs={{0,4},{4,0},{8,12},{12,8},{16,20},{20,16},{24,28},{28,24},{1,5},{5... | collective-permute-start | bytes 663560 | tf_op jit(solution)/shard_map/ppermute | solution.py:45
  21.6 15.3 %collective-permute-start.10 = (bf16[384,384]{1,0:T(8,128)(2,1)}, bf16[384,384]{1,0:T(8,128)(2,1)S(1)}, u32[]{:S(2)}, u32[]{:S(2)}) collective-permute-start(bf16[384,384]{1,0:T(8,128)(2,1)} %get-tuple-element.211), channel_id=1, source_target_pairs={{0,2},{2,0},{1,3},{3,1},{4,6},{6,4},{5,7},{7,5},{8,10},{10,8},{9,1... | collective-permute-start | bytes 884744 | tf_op jit(solution)/shard_map/ppermute | solution.py:32
  33.0 9.0 %collective-permute-start.9 = (bf16[192,768]{1,0:T(8,128)(2,1)S(1)}, bf16[192,768]{1,0:T(8,128)(2,1)S(1)}, u32[]{:S(2)}, u32[]{:S(2)}) collective-permute-start(bf16[192,768]{1,0:T(8,128)(2,1)S(1)} %collective-permute-done.6.got), channel_id=1, source_target_pairs={{0,4},{4,0},{8,12},{12,8},{16,20},{20,16},{24,28},{28,24},{1,5},{5... | collective-permute-start | bytes 884744 | tf_op jit(solution)/shard_map/ppermute | solution.py:45
  45.0 10.7 %collective-permute-start.12 = (bf16[256,768]{1,0:T(8,128)(2,1)S(1)}, bf16[256,768]{1,0:T(8,128)(2,1)S(1)}, u32[]{:S(2)}, u32[]{:S(2)}) collective-permute-start(bf16[256,768]{1,0:T(8,128)(2,1)S(1)} %get-tuple-element.217.own), channel_id=1, source_target_pairs={{0,1},{1,0},{2,3},{3,2},{4,5},{5,4},{6,7},{7,6},{8,9},{9,8},{10,11... | collective-permute-start | bytes 1179656 | tf_op jit(solution)/shard_map/ppermute | solution.py:36
  46.7 9.0 %collective-permute-start.14 = (bf16[384,384]{1,0:T(8,128)(2,1)S(1)}, bf16[384,384]{1,0:T(8,128)(2,1)S(1)}, u32[]{:S(2)}, u32[]{:S(2)}) collective-permute-start(bf16[384,384]{1,0:T(8,128)(2,1)S(1)} %collective-permute-done.10.refs_9_), channel_id=1, source_target_pairs={{0,4},{4,0},{8,12},{12,8},{16,20},{20,16},{24,28},{28,24},{1,5},{5... | collective-permute-start | bytes 884744 | tf_op jit(solution)/shard_map/ppermute | solution.py:45
  63.3 11.2 %collective-permute-start.18 = (bf16[256,768]{1,0:T(8,128)(2,1)S(1)}, bf16[256,768]{1,0:T(8,128)(2,1)S(1)}, u32[]{:S(2)}, u32[]{:S(2)}) collective-permute-start(bf16[256,768]{1,0:T(8,128)(2,1)S(1)} %add_convert_fusion.total), channel_id=1, source_target_pairs={{0,2},{2,0},{1,3},{3,1},{4,6},{6,4},{5,7},{7,5},{8,10},{10,8},{9,1... | collective-permute-start | bytes 1179656 | tf_op jit(solution)/shard_map/ppermute | solution.py:32
  63.9 15.1 %collective-permute-start.20 = (bf16[384,768]{1,0:T(8,128)(2,1)S(1)}, bf16[384,768]{1,0:T(8,128)(2,1)S(1)}, u32[]{:S(2)}, u32[]{:S(2)}) collective-permute-start(bf16[384,768]{1,0:T(8,128)(2,1)S(1)} %get-tuple-element.239), channel_id=1, source_target_pairs={{0,4},{4,0},{8,12},{12,8},{16,20},{20,16},{24,28},{28,24},{1,5},{5... | collective-permute-start | bytes 1769480 | tf_op jit(solution)/shard_map/ppermute | solution.py:45
  65.4 14.8 %collective-permute-start.21 = (bf16[2,192,768]{2,1,0:T(8,128)(2,1)S(1)}, bf16[2,192,768]{2,1,0:T(8,128)(2,1)S(1)}, u32[]{:S(2)}, u32[]{:S(2)}) collective-permute-start(bf16[2,192,768]{2,1,0:T(8,128)(2,1)S(1)} %get-tuple-element.241), channel_id=1, source_target_pairs={{0,8},{4,12},{8,0},{12,4},{16,24},{20,28},{24,16},{28,20},{1,9},{5... | collective-permute-start | bytes 1769480 | tf_op jit(solution)/shard_map/ppermute | solution.py:45
  80.4 10.2 %collective-permute-start.23 = (bf16[192,768]{1,0:T(8,128)(2,1)S(1)}, bf16[192,768]{1,0:T(8,128)(2,1)S(1)}, u32[]{:S(2)}, u32[]{:S(2)}) collective-permute-start(bf16[192,768]{1,0:T(8,128)(2,1)S(1)} %get-tuple-element.249), channel_id=1, source_target_pairs={{0,8},{4,12},{8,0},{12,4},{16,24},{20,28},{24,16},{28,20},{1,9},{5... | collective-permute-start | bytes 884744 | tf_op jit(solution)/shard_map/ppermute | solution.py:45
  82.2 8.4 %collective-permute-start.24 = (bf16[2,96,768]{2,1,0:T(8,128)(2,1)S(1)}, bf16[2,96,768]{2,1,0:T(8,128)(2,1)S(1)}, u32[]{:S(2)}, u32[]{:S(2)}) collective-permute-start(bf16[2,96,768]{2,1,0:T(8,128)(2,1)S(1)} %get-tuple-element.253), channel_id=1, source_target_pairs={{0,4},{4,0},{8,12},{12,8},{16,20},{20,16},{24,28},{28,24},{1,5},{5... | collective-permute-start | bytes 884744 | tf_op jit(solution)/shard_map/ppermute | solution.py:45
  90.7 9.4 %collective-permute-start.27 = (bf16[2,192,384]{2,1,0:T(8,128)(2,1)S(1)}, bf16[2,192,384]{2,1,0:T(8,128)(2,1)S(1)}, u32[]{:S(2)}, u32[]{:S(2)}) collective-permute-start(bf16[2,192,384]{2,1,0:T(8,128)(2,1)S(1)} %get-tuple-element.269), channel_id=1, source_target_pairs={{0,4},{4,0},{8,12},{12,8},{16,20},{20,16},{24,28},{28,24},{1,5},{5... | collective-permute-start | bytes 884744 | tf_op jit(solution)/shard_map/ppermute | solution.py:45
  92.3 15.4 %collective-permute-start.28 = (bf16[2,192,384]{2,1,0:T(8,128)(2,1)S(1)}, bf16[2,192,384]{2,1,0:T(8,128)(2,1)S(1)}, u32[]{:S(2)}, u32[]{:S(2)}) collective-permute-start(bf16[2,192,384]{2,1,0:T(8,128)(2,1)S(1)} %get-tuple-element.271), channel_id=1, source_target_pairs={{0,8},{4,12},{8,0},{12,4},{16,24},{20,28},{24,16},{28,20},{1,9},{5... | collective-permute-start | bytes 884744 | tf_op jit(solution)/shard_map/ppermute | solution.py:45
  93.0 14.6 %collective-permute-start.31 = (bf16[256,384]{1,0:T(8,128)(2,1)S(1)}, bf16[256,384]{1,0:T(8,128)(2,1)S(1)}, u32[]{:S(2)}, u32[]{:S(2)}) collective-permute-start(bf16[256,384]{1,0:T(8,128)(2,1)S(1)} %get-tuple-element.280), channel_id=1, source_target_pairs={{0,2},{2,0},{1,3},{3,1},{4,6},{6,4},{5,7},{7,5},{8,10},{10,8},{9,1... | collective-permute-start | bytes 589832 | tf_op jit(solution)/shard_map/ppermute | solution.py:32
  93.6 14.0 %collective-permute-start.29 = (bf16[96,768]{1,0:T(8,128)(2,1)S(1)}, bf16[96,768]{1,0:T(8,128)(2,1)S(1)}, u32[]{:S(2)}, u32[]{:S(2)}) collective-permute-start(bf16[96,768]{1,0:T(8,128)(2,1)S(1)} %get-tuple-element.275), channel_id=1, source_target_pairs={{0,16},{4,20},{8,24},{12,28},{16,0},{20,4},{24,8},{28,12},{1,17},{... | collective-permute-start | bytes 442376 | tf_op jit(solution)/shard_map/ppermute | solution.py:45
  96.4 11.3 %collective-permute-start.30 = (bf16[2,48,768]{2,1,0:T(8,128)(2,1)S(1)}, bf16[2,48,768]{2,1,0:T(8,128)(2,1)S(1)}, u32[]{:S(2)}, u32[]{:S(2)}) collective-permute-start(bf16[2,48,768]{2,1,0:T(8,128)(2,1)S(1)} %get-tuple-element.279), channel_id=1, source_target_pairs={{0,16},{4,20},{8,24},{12,28},{16,0},{20,4},{24,8},{28,12},{1,17},{... | collective-permute-start | bytes 442376 | tf_op jit(solution)/shard_map/ppermute | solution.py:45
  107.8 10.7 %collective-permute-start.33 = (bf16[2,96,384]{2,1,0:T(8,128)(2,1)S(1)}, bf16[2,96,384]{2,1,0:T(8,128)(2,1)S(1)}, u32[]{:S(2)}, u32[]{:S(2)}) collective-permute-start(bf16[2,96,384]{2,1,0:T(8,128)(2,1)S(1)} %get-tuple-element.290), channel_id=1, source_target_pairs={{0,8},{4,12},{8,0},{12,4},{16,24},{20,28},{24,16},{28,20},{1,9},{5... | collective-permute-start | bytes 442376 | tf_op jit(solution)/shard_map/ppermute | solution.py:45
  118.5 14.3 %collective-permute-start.40 = (bf16[2,48,384]{2,1,0:T(8,128)(2,1)S(1)}, bf16[2,48,384]{2,1,0:T(8,128)(2,1)S(1)}, u32[]{:S(2)}, u32[]{:S(2)}) collective-permute-start(bf16[2,48,384]{2,1,0:T(8,128)(2,1)S(1)} %get-tuple-element.312), channel_id=1, source_target_pairs={{0,16},{4,20},{8,24},{12,28},{16,0},{20,4},{24,8},{28,12},{1,17},{... | collective-permute-start | bytes 221192 | tf_op jit(solution)/shard_map/ppermute | solution.py:45
  121.9 12.5 %collective-permute-start.41 = (bf16[2,48,384]{2,1,0:T(8,128)(2,1)S(1)}, bf16[2,48,384]{2,1,0:T(8,128)(2,1)S(1)}, u32[]{:S(2)}, u32[]{:S(2)}) collective-permute-start(bf16[2,48,384]{2,1,0:T(8,128)(2,1)S(1)} %get-tuple-element.316), channel_id=1, source_target_pairs={{0,16},{4,20},{8,24},{12,28},{16,0},{20,4},{24,8},{28,12},{1,17},{... | collective-permute-start | bytes 221192 | tf_op jit(solution)/shard_map/ppermute | solution.py:45
  122.0 15.6 %collective-permute-start.39 = (bf16[2,48,768]{2,1,0:T(8,128)(2,1)S(1)}, bf16[2,48,768]{2,1,0:T(8,128)(2,1)S(1)}, u32[]{:S(2)}, u32[]{:S(2)}) collective-permute-start(bf16[2,48,768]{2,1,0:T(8,128)(2,1)S(1)} %shard_map.327.refs_0_), channel_id=1, source_target_pairs={{0,16},{4,20},{8,24},{12,28},{16,0},{20,4},{24,8},{28,12},{1,17},{... | collective-permute-start | bytes 442376 | tf_op jit(solution)/shard_map/ppermute | solution.py:45
  125.0 14.6 %collective-permute-start.38 = (bf16[2,96,384]{2,1,0:T(8,128)(2,1)S(1)}, bf16[2,96,384]{2,1,0:T(8,128)(2,1)S(1)}, u32[]{:S(2)}, u32[]{:S(2)}) collective-permute-start(bf16[2,96,384]{2,1,0:T(8,128)(2,1)S(1)} %shard_map.326.refs_0_), channel_id=1, source_target_pairs={{0,16},{4,20},{8,24},{12,28},{16,0},{20,4},{24,8},{28,12},{1,17},{... | collective-permute-start | bytes 442376 | tf_op jit(solution)/shard_map/ppermute | solution.py:45
  139.6 10.0 %collective-permute-start.44 = (bf16[2,96,768]{2,1,0:T(8,128)(2,1)S(1)}, bf16[2,96,768]{2,1,0:T(8,128)(2,1)S(1)}, u32[]{:S(2)}, u32[]{:S(2)}) collective-permute-start(bf16[2,96,768]{2,1,0:T(8,128)(2,1)S(1)} %shard_map.331.refs_0_), channel_id=1, source_target_pairs={{0,4},{4,0},{8,12},{12,8},{16,20},{20,16},{24,28},{28,24},{1,5},{5... | collective-permute-start | bytes 884744 | tf_op jit(solution)/shard_map/ppermute | solution.py:45
  141.2 8.5 %collective-permute-start.43 = (bf16[2,192,384]{2,1,0:T(8,128)(2,1)S(1)}, bf16[2,192,384]{2,1,0:T(8,128)(2,1)S(1)}, u32[]{:S(2)}, u32[]{:S(2)}) collective-permute-start(bf16[2,192,384]{2,1,0:T(8,128)(2,1)S(1)} %shard_map.330.refs_0_), channel_id=1, source_target_pairs={{0,8},{4,12},{8,0},{12,4},{16,24},{20,28},{24,16},{28,20},{1,9},{5... | collective-permute-start | bytes 884744 | tf_op jit(solution)/shard_map/ppermute | solution.py:45
  141.3 8.4 %collective-permute-start.45 = (bf16[48,384]{1,0:T(8,128)(2,1)S(1)}, bf16[48,384]{1,0:T(8,128)(2,1)S(1)}, u32[]{:S(2)}, u32[]{:S(2)}) collective-permute-start(bf16[48,384]{1,0:T(8,128)(2,1)S(1)} %get-tuple-element.327), channel_id=1, source_target_pairs={{0,2},{2,0},{1,3},{3,1},{4,6},{6,4},{5,7},{7,5},{8,10},{10,8},{9,1... | collective-permute-start | bytes 110600 | tf_op jit(solution)/shard_map/ppermute | solution.py:32
  149.7 17.0 %collective-permute-start.49 = (bf16[2,192,768]{2,1,0:T(8,128)(2,1)S(1)}, bf16[2,192,768]{2,1,0:T(8,128)(2,1)S(1)}, u32[]{:S(2)}, u32[]{:S(2)}) collective-permute-start(bf16[2,192,768]{2,1,0:T(8,128)(2,1)S(1)} %shard_map.335.refs_0_), channel_id=1, source_target_pairs={{0,8},{4,12},{8,0},{12,4},{16,24},{20,28},{24,16},{28,20},{1,9},{5... | collective-permute-start | bytes 1769480 | tf_op jit(solution)/shard_map/ppermute | solution.py:45
  150.2 16.6 %collective-permute-start.48 = (bf16[2,384,384]{2,1,0:T(8,128)(2,1)S(1)}, bf16[2,384,384]{2,1,0:T(8,128)(2,1)S(1)}, u32[]{:S(2)}, u32[]{:S(2)}) collective-permute-start(bf16[2,384,384]{2,1,0:T(8,128)(2,1)S(1)} %shard_map.334.refs_0_), channel_id=1, source_target_pairs={{0,4},{4,0},{8,12},{12,8},{16,20},{20,16},{24,28},{28,24},{1,5},{5... | collective-permute-start | bytes 1769480 | tf_op jit(solution)/shard_map/ppermute | solution.py:45
  150.6 12.7 %collective-permute-start.52 = (f32[8,768]{1,0:T(8,128)S(1)}, f32[8,768]{1,0:T(8,128)S(1)}, u32[]{:S(2)}, u32[]{:S(2)}) collective-permute-start(f32[8,768]{1,0:T(8,128)S(1)} %add.43), channel_id=1, source_target_pairs={{0,16},{4,20},{8,24},{12,28},{16,0},{20,4},{24,8},{28,12},{1,17},{... | collective-permute-start | bytes 73736 | tf_op jit(solution)/shard_map/ppermute | solution.py:45
  153.0 11.0 %collective-permute-start.51 = (bf16[2,48,384]{2,1,0:T(8,128)(2,1)S(1)}, bf16[2,48,384]{2,1,0:T(8,128)(2,1)S(1)}, u32[]{:S(2)}, u32[]{:S(2)}) collective-permute-start(bf16[2,48,384]{2,1,0:T(8,128)(2,1)S(1)} %shard_map.337.refs_0_), channel_id=1, source_target_pairs={{0,16},{4,20},{8,24},{12,28},{16,0},{20,4},{24,8},{28,12},{1,17},{... | collective-permute-start | bytes 221192 | tf_op jit(solution)/shard_map/ppermute | solution.py:45
  153.6 11.3 %collective-permute-start.50 = (bf16[2,48,384]{2,1,0:T(8,128)(2,1)S(1)}, bf16[2,48,384]{2,1,0:T(8,128)(2,1)S(1)}, u32[]{:S(2)}, u32[]{:S(2)}) collective-permute-start(bf16[2,48,384]{2,1,0:T(8,128)(2,1)S(1)} %shard_map.336.refs_0_), channel_id=1, source_target_pairs={{0,16},{4,20},{8,24},{12,28},{16,0},{20,4},{24,8},{28,12},{1,17},{... | collective-permute-start | bytes 221192 | tf_op jit(solution)/shard_map/ppermute | solution.py:45
  (35 other events, 273.8 us)

commit v4 on v3

v4 whole, which is shorter than its diff:
```python
import jax
import jax.numpy as jnp
from jax import lax
from jax.experimental import pallas as pl
from jax.experimental.pallas import tpu as pltpu
from jax.sharding import PartitionSpec as P

HEAD_DIM = 64
EPSILON = 1e-05
MASKED = -1e30
F32 = jnp.float32
BF16 = jnp.bfloat16
SWAP = ((0, 1), (1, 0))
CUBIC = 0.044715
ROOT = 0.7978845608028654
MIB = 1024 * 1024
VMEM_START = 54
EXTRA = 16


def dot(left, right):
    return jnp.dot(left, right, preferred_element_type=F32)


def dot_nt(left, right):
    return lax.dot_general(left, right, (((1,), (1,)), ((), ())), preferred_element_type=F32)


def dot_tn(left, right):
    return lax.dot_general(left, right, (((0,), (0,)), ((), ())), preferred_element_type=F32)


def from_row(values):
    return lax.ppermute(values, "row", SWAP)


def from_col(values):
    return lax.ppermute(values, "col", SWAP)


def dp_pairs(bit):
    count = lax.axis_size("dp")
    return [(i, i ^ (1 << bit)) for i in range(count)]


def from_dp(values, bit):
    return lax.ppermute(values, "dp", dp_pairs(bit))


def hold(*values):
    return lax.optimization_barrier(values)


def shape(dims, kind):
    return jax.ShapeDtypeStruct(tuple(dims), kind)


def call(kernel, out_shape, *operands, scratch=(), smem=(), hbm=(), hbm_out=(), vmem=16):
    spaces = [
        pltpu.SMEM if i in smem else pltpu.HBM if i in hbm else pltpu.VMEM
        for i in range(len(operands))
    ]
    out_specs = jax.tree.map(lambda _: pl.BlockSpec(memory_space=pltpu.VMEM), out_shape)
    if hbm_out:
        out_specs = tuple(
            pl.BlockSpec(memory_space=pltpu.HBM if i in hbm_out else pltpu.VMEM)
            for i in range(len(out_shape))
        )
    return pl.pallas_call(
        kernel,
        out_shape=out_shape,
        in_specs=[pl.BlockSpec(memory_space=space) for space in spaces],
        out_specs=out_specs,
        scratch_shapes=list(scratch),
        compiler_params=pltpu.CompilerParams(vmem_limit_bytes=vmem * MIB),
        cost_estimate=pl.CostEstimate(flops=0, bytes_accessed=0, transcendentals=0),
    )(*operands)


def half_rows(index, size):
    return pl.ds(pl.multiple_of(index * size, size), size)


def start_copies(pairs, sems):
    copies = [
        pltpu.make_async_copy(source, target, sems.at[i]) for i, (source, target) in enumerate(pairs)
    ]
    for copy in copies:
        copy.start()
    return copies


GAIN_A, SHIFT_A, BIAS_O, GAIN_M, SHIFT_M, BIAS_QKV, BIAS_UP, BIAS_DOWN = 0, 1, 2, 3, 4, 5, 6, 8


def start_kernel(*refs):
    vectors, (w_q, w_k, w_v, w_out, w_up, w_down) = refs[:9], refs[9:15]
    kept, sent, out_sent, up_sent, down_sent = refs[15:20]
    held, held_w, extra, sems = refs[20:29], refs[29:32], refs[32], refs[33]
    row, side = lax.axis_index("row"), lax.axis_index("dp") % 2
    other_side = (lax.axis_index("dp") // 2) % 2
    units = up_sent.shape[1]
    copies = start_copies(
        list(zip((w_q, w_k, w_v), held_w))
        + list(zip(vectors, held))
        + [
            (w_out.at[half_rows(side, out_sent.shape[0])], out_sent),
            (w_up.at[half_rows(side, up_sent.shape[0]), half_rows(1 - row, units)], up_sent),
            (w_down.at[half_rows(2 * (1 - row) + other_side, down_sent.shape[0])], down_sent),
        ],
        sems,
    )
    first = row == 0
    half, third = w_q.shape[0], w_q.shape[1] // 2
    keeps, sends = [], []
    for ref, copy in zip(held_w, copies):
        copy.wait()
        low, high = ref[:, :third], ref[:, third:]
        keeps.append(jnp.where(first, low, high))
        sends.append(jnp.where(first, high, low))
    kept[:half] = jnp.concatenate(keeps, axis=1)
    sent[:half] = jnp.concatenate(sends, axis=1)
    for copy in copies[3:]:
        copy.wait()
    extra[...] = jnp.zeros_like(extra)
    lines = [ref[...].astype(F32).reshape(1, -1) for ref in held]
    for i in range(5):
        extra[i : i + 1, :half] = lines[i]
    b_q, b_v, b_u, b_d = lines[5:]
    extra[BIAS_QKV : BIAS_QKV + 1, :third] = b_q
    extra[BIAS_QKV : BIAS_QKV + 1, 2 * third :] = b_v
    for i in range(2):
        extra[BIAS_UP + i : BIAS_UP + i + 1, :half] = b_u[:, i * half : (i + 1) * half]
    extra[BIAS_DOWN : BIAS_DOWN + 1, :half] = b_d
    kept[half:] = extra[...].astype(BF16)
    sent[half:] = extra[...].astype(BF16)


def normed_parts(values):
    mean = jnp.mean(values, axis=1, keepdims=True)
    centered = values - mean
    variance = jnp.mean(centered * centered, axis=1, keepdims=True)
    inverse = lax.rsqrt(variance + EPSILON)
    return centered * inverse, inverse


def both_halves(mine, far):
    return jnp.concatenate([mine[...], far[...]], axis=1).astype(F32)


def vector_of(kept, i):
    half = kept.shape[0] - EXTRA
    return kept[half:].astype(F32)[i : i + 1, :half]


def wide_vector(kept, got, i):
    return jnp.concatenate([vector_of(kept, i), vector_of(got, i)], axis=1)


def head_mask(width, head):
    lanes = lax.broadcasted_iota(jnp.int32, (1, width), 1)
    return lanes // HEAD_DIM == head


def allowed_block(lengths, keys, first_query, count):
    first, second = lengths[0, 0], lengths[0, 0] + lengths[0, 1]
    query = first_query + lax.broadcasted_iota(jnp.int32, (1, count), 1)
    begin = jnp.where(query >= second, second, jnp.where(query >= first, first, 0))
    key = lax.broadcasted_iota(jnp.int32, (keys, count), 0)
    return (key >= begin) & (key <= query)


def forward_kernel(lengths, own, own_far, col_own, col_far, w_kept, w_got, norm_hbm, q_hbm, k_hbm, v_hbm, o_out, lse,
                   norm_out, q_out, k_out, v_out, sems):
    own_rows, half = own.shape
    third = q_out.shape[1]
    col = lax.axis_index("col")
    gain, shift = wide_vector(w_kept, w_got, GAIN_A), wide_vector(w_kept, w_got, SHIFT_A)
    bias = w_kept[half:].astype(F32)[BIAS_QKV : BIAS_QKV + 1]
    for ref, far, at in ((own, own_far, col), (col_own, col_far, 1 - col)):
        where = half_rows(at, own_rows)
        unit, _ = normed_parts(both_halves(ref, far))
        values = (unit * gain + shift).astype(BF16)
        norm_out[where] = values
        total = dot(values[:, :half], w_kept[:half]) + dot(values[:, half:], w_got[:half])
        total = (total + bias).astype(BF16)
        q_out[where] = total[:, :third]
        k_out[where] = total[:, third : 2 * third]
        v_out[where] = total[:, 2 * third :]
    copies = start_copies(
        [(norm_out, norm_hbm), (q_out, q_hbm), (k_out, k_hbm), (v_out, v_hbm)], sems
    )
    lse[...] = jnp.zeros_like(lse)
    values_t = v_out[...].T
    for begin in (0, own_rows):
        keys = begin + own_rows
        allowed = allowed_block(lengths, keys, begin, own_rows)
        query = q_out[begin:keys] * BF16(HEAD_DIM ** (-0.5))
        parts = []
        for head in range(third // HEAD_DIM):
            key = jnp.where(head_mask(third, head), k_out[:keys], BF16(0))
            scores = jnp.where(allowed, dot_nt(key, query), MASKED)
            largest = jnp.max(scores, axis=0, keepdims=True)
            weights = jnp.exp(scores - largest)
            summed = jnp.sum(weights, axis=0, keepdims=True)
            lse[head : head + 1, begin:keys] = largest + jnp.log(summed)
            mixed = dot(
                values_t[head * HEAD_DIM : (head + 1) * HEAD_DIM, :keys], weights.astype(BF16)
            )
            parts.append(mixed / summed)
        o_out[begin:keys] = jnp.concatenate(parts, axis=0).T.astype(BF16)
    for copy in copies:
        copy.wait()


def split_tokens(total_of, keep, send, own_rows, col):
    keep[...] = total_of(half_rows(col, own_rows))
    send[...] = total_of(half_rows(1 - col, own_rows)).astype(BF16)


def branch_kernel(mixed, mixed_other, w_mine, got, got_side, keep, send, w_other):
    w_other[...] = both_sides(got, got_side, 0)
    row = lax.axis_index("row")
    third = mixed.shape[1]
    own, far = half_rows(row, third), half_rows(1 - row, third)

    for i, w in enumerate((w_mine, w_other)):
        lanes = slice(i * w.shape[1], (i + 1) * w.shape[1])
        part = dot(mixed[...], w[own]) + dot(mixed_other[...], w[far])
        keep[:, lanes] = part
        send[:, lanes] = part.astype(BF16)


def second_norm_kernel(own, own_far, col_own, col_far, keep, got, kept, sent, middle, normed, unit_out, inverse_out):
    own_rows = own.shape[0]
    col = lax.axis_index("col")
    bias, gain, shift = [wide_vector(kept, sent, i) for i in (BIAS_O, GAIN_M, SHIFT_M)]
    for ref, far, at in ((own, own_far, col), (col_own, col_far, 1 - col)):
        where = half_rows(at, own_rows)
        values = both_halves(ref, far) + (keep[where] + got[where].astype(F32) + bias)
        unit, inverse = normed_parts(values)
        normed[where] = (unit * gain + shift).astype(BF16)
        if ref is own:
            middle[...] = values[:, : middle.shape[1]]
            unit_out[...] = unit
            inverse_out[...] = jnp.broadcast_to(inverse, inverse_out.shape)


def both_sides(got, got_side, axis, bit=0):
    first = (lax.axis_index("dp") // (1 << bit)) % 2 == 0
    low = jnp.where(first, got[...], got_side[...])
    high = jnp.where(first, got_side[...], got[...])
    return jnp.concatenate([low, high], axis=axis)


def up_kernel(normed, w_up, got, got_side, kept, hidden_out, slope_out, w_other_out):
    rows, width = normed.shape
    half = width // 2
    units = got.shape[1]
    row = lax.axis_index("row")
    w_mine = w_up[:, pl.ds(pl.multiple_of(row * units, units), units)]
    w_other = both_sides(got, got_side, 0)
    w_other_out[...] = w_other
    bias = jnp.concatenate([vector_of(kept, BIAS_UP + i) for i in range(2)], axis=1)
    for begin in (0, rows // 2):
        where = slice(begin, begin + rows // 2)
        values = normed[where]
        u = dot(values[:, :half], w_mine) + dot(values[:, half:], w_other) + bias
        squared = u * u
        bent = jnp.tanh(ROOT * (u + CUBIC * (squared * u)))
        raised = 0.5 * (1.0 + bent)
        hidden_out[where] = (u * raised).astype(BF16)
        slope_out[where] = raised + 0.5 * u * (1.0 - bent * bent) * (
            ROOT * (1.0 + (3.0 * CUBIC) * squared)
        )


def split_rows(total, keep, send, bit):
    own = (lax.axis_index("dp") // (1 << bit)) % 2 == 0
    half = keep.shape[-2]
    low, high = total[..., :half, :], total[..., half:, :]
    keep[...] = jnp.where(own, low, high)
    send[...] = jnp.where(own, high, low)


def masked_top(lengths, mine, far, at):
    live = lengths[0, 0] + lengths[0, 1]
    own_rows = mine.shape[0]
    position = at * own_rows + lax.broadcasted_iota(jnp.int32, (own_rows, 1), 0)
    values = jnp.concatenate([mine[...], far[...]], axis=1)
    return jnp.where(position < live, values, BF16(0))


def down_kernel(bit_down, bit_up, lengths, top, top_far, top_col, top_far_col, hidden, slope, normed, w_down, got, got_side,
                w_up, w_up_other, down_keep, down_send, up_keep, up_send, keep, send, sums, w_other_out, top_all, grad_pre):
    own_rows, half = top.shape
    units = hidden.shape[1]
    row, col = lax.axis_index("row"), lax.axis_index("col")
    top_all[half_rows(col, own_rows)] = masked_top(lengths, top, top_far, col)
    top_all[half_rows(1 - col, own_rows)] = masked_top(lengths, top_col, top_far_col, 1 - col)
    top_rows = top_all[...]
    total = dot_tn(hidden[...], top_rows).astype(BF16)
    split_rows(jnp.stack([total[:, :half], total[:, half:]]), down_keep, down_send, bit_down)
    w_other = both_sides(got, got_side, 0, 1)
    w_other_out[...] = w_other
    grad_hidden = dot_nt(top_rows[:, :half], w_down[half_rows(row, units)]) + dot_nt(
        top_rows[:, half:], w_other
    )
    grads = (grad_hidden * slope[...]).astype(BF16)
    grad_pre[...] = grads
    w_mine = w_up[:, pl.ds(pl.multiple_of(row * units, units), units)]

    def total_of(rows):
        values = grad_pre[rows]
        return jnp.concatenate([dot_nt(values, w_mine), dot_nt(values, w_up_other[...])], axis=1)

    split_tokens(total_of, keep, send, own_rows, col)
    total = dot_tn(normed[...], grads).astype(BF16)
    total = total.reshape(2, half, units)
    total = jnp.concatenate([total[..., : units // 2], total[..., units // 2 :]], axis=1)
    split_rows(total, up_keep, up_send, bit_up)
    sums[...] = jnp.zeros_like(sums)
    sums[0:1] = jnp.sum(grads.astype(F32), axis=0, keepdims=True)
    sums[1:2, :half] = jnp.sum(top_rows[:, :half].astype(F32), axis=0, keepdims=True)


def output_kernel(hidden, w_down, w_other, keep, send):
    units = hidden.shape[1]
    row, col = lax.axis_index("row"), lax.axis_index("col")
    w_mine = w_down[half_rows(row, units)]

    def total_of(rows):
        values = hidden[rows]
        return jnp.concatenate([dot(values, w_mine), dot(values, w_other[...])], axis=1)

    split_tokens(total_of, keep, send, keep.shape[0], col)


def second_back_kernel(lengths, total, total_far, unit_ref, inverse_ref, kept, sent, top, top_far, middle_out, datt, sums):
    half = top.shape[1]
    got = total_far[...].astype(F32)
    grads = total[...].astype(F32) + jnp.concatenate([got[:, half:], got[:, :half]], axis=1)
    unit = unit_ref[...]
    scaled = grads * wide_vector(kept, sent, GAIN_M)
    mean_plain = jnp.mean(scaled, axis=1, keepdims=True)
    mean_unit = jnp.mean(scaled * unit, axis=1, keepdims=True)
    own = masked_top(lengths, top, top_far, lax.axis_index("col")).astype(F32)
    result = own + inverse_ref[:, :1] * (scaled - mean_plain - unit * mean_unit)
    middle_out[...] = result[:, :half]
    datt[...] = result.astype(BF16)
    sums[...] = jnp.zeros_like(sums)
    sums[0:1] = jnp.sum((grads * unit)[:, :half], axis=0, keepdims=True)
    sums[1:2] = jnp.sum(grads[:, :half], axis=0, keepdims=True)


def backward_kernel(bit_first, bit_second, lengths, own, other, w_mine, w_other, q_hbm, k_hbm, v_hbm, o_ref, lse, normed_hbm, w_kept, w_got,
                    first_keep, first_send, second_keep, second_send, keep, send, sums, datt, out, acc_k, acc_v, do_ref,
                    q_ref, k_ref, v_ref, normed, sems):
    copies = start_copies(
        [(q_hbm, q_ref), (k_hbm, k_ref), (v_hbm, v_ref), (normed_hbm, normed)], sems
    )
    own_rows, width = own.shape
    half = width // 2
    third = q_ref.shape[1]
    row, col = lax.axis_index("row"), lax.axis_index("col")
    quarter = half_rows(row, third)
    for ref, at in ((own, col), (other, 1 - col)):
        where = half_rows(at, own_rows)
        values = ref[...]
        datt[where] = values
        do_ref[where] = (
            dot_nt(values[:, :half], w_mine[quarter]) + dot_nt(values[:, half:], w_other[quarter])
        ).astype(BF16)
    for copy in copies:
        copy.wait()
    keys_t = k_ref[...].T
    acc_k[...] = jnp.zeros_like(acc_k)
    acc_v[...] = jnp.zeros_like(acc_v)
    scale = BF16(HEAD_DIM ** (-0.5))
    for begin in (0, own_rows):
        keys = begin + own_rows
        allowed = allowed_block(lengths, keys, begin, own_rows)
        query = q_ref[begin:keys] * scale
        grad_mixed = do_ref[begin:keys]
        parts = []
        for head in range(third // HEAD_DIM):
            mask = head_mask(third, head)
            key = jnp.where(mask, k_ref[:keys], BF16(0))
            scores = jnp.where(allowed, dot_nt(key, query), MASKED)
            probs = jnp.exp(scores - lse[head : head + 1, begin:keys])
            value = jnp.where(mask, v_ref[:keys], BF16(0))
            grad_probs = dot_nt(value, grad_mixed)
            both = probs * grad_probs
            inner = jnp.sum(both, axis=0, keepdims=True)
            grad_raw = (both - probs * inner).astype(BF16) * scale
            acc_v[:keys] += jnp.where(mask, dot(probs.astype(BF16), grad_mixed), 0.0)
            acc_k[:keys] += jnp.where(mask, dot(grad_raw, q_ref[begin:keys]), 0.0)
            parts.append(dot(keys_t[head * HEAD_DIM : (head + 1) * HEAD_DIM, :keys], grad_raw))
        out[begin:keys, :third] = jnp.concatenate(parts, axis=0).T.astype(BF16)
    out[:, third : 2 * third] = acc_k[...].astype(BF16)
    out[:, 2 * third :] = acc_v[...].astype(BF16)
    grads = out[...]
    weights = dot_tn(normed[...], grads).astype(BF16)
    grad_out = dot_tn(datt[...], o_ref[...]).astype(BF16)
    split_rows(weights[:, : 2 * third].reshape(2, half, 2 * third), first_keep, first_send, bit_first)
    last = jnp.concatenate([weights[:, 2 * third :], grad_out], axis=1)
    split_rows(last.reshape(2, half, 2 * third), second_keep, second_send, bit_second)

    def total_of(rows):
        values = out[rows]
        return jnp.concatenate([dot_nt(values, w_kept[:half]), dot_nt(values, w_got[:half])], axis=1)

    split_tokens(total_of, keep, send, own_rows, col)
    sums[...] = jnp.zeros_like(sums)
    sums[0:1, : 3 * third] = jnp.sum(grads.astype(F32), axis=0, keepdims=True)
    sums[1:2, :half] = jnp.sum(datt[:, :half].astype(F32), axis=0, keepdims=True)


def first_back_kernel(keep, got, raised_keep, raised_got, own, own_far, kept, sent, mine, raised, out, stats, unit_out, inverse_out):
    own_rows, half = mine.shape
    unit, inverse = normed_parts(both_halves(own, own_far))
    unit_out[...] = unit[:, :half]
    inverse_out[...] = jnp.broadcast_to(inverse, inverse_out.shape)
    grads = keep[...] + got[...].astype(F32)
    total = raised_keep[...] + raised_got[...].astype(F32)
    mine[...], raised[...] = grads[:, :half], total[:, :half]
    out[:own_rows] = grads[:, half:].astype(BF16)
    out[own_rows : 2 * own_rows] = total[:, half:].astype(BF16)
    scaled = grads * wide_vector(kept, sent, GAIN_A)
    plain = jnp.sum(scaled, axis=1, keepdims=True)
    crossed = jnp.sum(scaled * unit, axis=1, keepdims=True)
    lanes = lax.broadcasted_iota(jnp.int32, (1, 128), 1)
    both = jnp.where(lanes == 0, plain, jnp.where(lanes == 1, crossed, 0.0)).T[:8]
    stats[...] = both
    high = both.astype(BF16)
    low = (both - high.astype(F32)).astype(BF16)
    out[2 * own_rows :] = jnp.zeros((EXTRA, half), BF16)
    out[2 * own_rows :, :own_rows] = jnp.concatenate([high, low], axis=0)


def last_kernel(mine, raised, got, stats, unit_ref, inverse_ref, kept, middle, grad_middle, mid_sums, output, result, sums):
    own_rows, half = mine.shape
    unit = unit_ref[...]
    grads = mine[...] + got[:own_rows].astype(F32)
    pairs = got[2 * own_rows :, :own_rows].astype(F32)
    total = (stats[...] + (pairs[:8] + pairs[8:])) / (2 * half)
    columns = jnp.concatenate([total, jnp.zeros((120, total.shape[1]), F32)], axis=0).T
    grad_in = inverse_ref[:, :1] * (
        grads * vector_of(kept, GAIN_A) - columns[:, 0:1] - unit * columns[:, 1:2]
    )
    result[...] = (grad_middle[...] + grad_in).astype(BF16)
    far = got[own_rows : 2 * own_rows].astype(F32)
    output[...] = (middle[...] + (raised[...] + far) + vector_of(kept, BIAS_DOWN)).astype(BF16)
    sums[...] = jnp.zeros_like(sums)
    sums[0:1] = jnp.sum(grads * unit, axis=0, keepdims=True)
    sums[1:2] = jnp.sum(grads, axis=0, keepdims=True)
    sums[2:4] = mid_sums[0:2]


def bit_clear(bit):
    return (lax.axis_index("dp") // (1 << bit)) % 2 == 0


def total_of_pair(kept, got):
    return (kept[...].astype(F32) + got[...].astype(F32)).astype(BF16)


def halve_kernel(bit_a, bit_b, kept_a, got_a, kept_b, got_b, keep_a, send_a, keep_b, send_b):
    split_rows(total_of_pair(kept_a, got_a), keep_a, send_a, bit_a)
    split_rows(total_of_pair(kept_b, got_b), keep_b, send_b, bit_b)


def cross_kernel(bit, kept_a, got_a, kept_b, got_b, keep, to_dp, to_row, to_both):
    own = bit_clear(bit)
    half = keep.shape[1]
    for i, (kept, got) in enumerate(((kept_a, got_a), (kept_b, got_b))):
        total = total_of_pair(kept, got)
        low, high = total[:, :half], total[:, half:]
        here, there = jnp.where(own, low, high), jnp.where(own, high, low)
        keep[i], to_dp[i], to_row[i], to_both[i] = here[0], there[0], here[1], there[1]


def join_kernel(keep, from_dp_ref, from_row_ref, from_both_ref, out):
    mine = total_of_pair(keep, from_dp_ref)
    other = total_of_pair(from_row_ref, from_both_ref)
    for i in range(2):
        out[i, 0], out[i, 1] = mine[i], other[i]


def join_more_kernel(keep, from_dp_ref, from_row_ref, from_both_ref, halves, halves_col, mlp, attn, out):
    mine = total_of_pair(keep, from_dp_ref)
    other = total_of_pair(from_row_ref, from_both_ref)
    rows, half = mine.shape[1:]
    for i in range(2):
        out[2 * i * rows : (2 * i + 1) * rows] = mine[i]
        out[(2 * i + 1) * rows : (2 * i + 2) * rows] = other[i]
    third = half // 2
    lines = [
        (halves[...] + halves_col[...])[:4],
        jnp.concatenate([attn[0:1, :third], attn[0:1, 2 * third : 3 * third]], axis=1),
        attn[1:2, :half],
        mlp[0:1, :half],
        mlp[0:1, half : 2 * half],
        mlp[1:2, :half],
        jnp.zeros((EXTRA - 9, half), F32),
    ]
    out[4 * rows :] = jnp.concatenate(lines, axis=0).astype(BF16)


def extra_sum(mine, got):
    return mine[-EXTRA:].astype(F32) + got[-EXTRA:].astype(F32)


def ordered_rows(own, mine, got, begin, rows, out, at):
    low, high = mine[begin : begin + rows], got[begin : begin + rows]
    out[at : at + rows] = jnp.where(own, low, high)
    out[at + rows : at + 2 * rows] = jnp.where(own, high, low)


def part_more_kernel(bit, mine, got, out_a, out_b):
    own = bit_clear(bit)
    rows = out_b.shape[0] // 4
    for i, out in enumerate((out_a, out_b)):
        for p in range(2):
            ordered_rows(own, mine, got, (2 * i + p) * rows, rows, out, 2 * p * rows)
    out_a[4 * rows :] = extra_sum(mine, got).astype(BF16)


def double_more_kernel(bit_a, bit_b, mine_a, got_a, mine_b, got_b, out_a, out_b):
    rows = mine_b.shape[0] // 2
    for bit, mine, got, out in ((bit_a, mine_a, got_a, out_a), (bit_b, mine_b, got_b, out_b)):
        own = bit_clear(bit)
        for p in range(2):
            ordered_rows(own, mine, got, p * rows, rows, out, 2 * p * rows)
    out_a[4 * rows :] = extra_sum(mine_a, got_a).astype(BF16)


def doubled(bit, mine, got, out):
    own = bit_clear(bit)
    half = mine.shape[1]
    out[:, :half] = jnp.where(own, mine, got)
    out[:, half:] = jnp.where(own, got, mine)


def part_kernel(bit, mine, got, out_a, out_b):
    doubled(bit, mine[0], got[0], out_a)
    doubled(bit, mine[1], got[1], out_b)


def double_kernel(bit_a, bit_b, mine_a, got_a, mine_b, got_b, out_a, out_b):
    doubled(bit_a, mine_a[...], got_a[...], out_a)
    doubled(bit_b, mine_b[...], got_b[...], out_b)


def double_apart_kernel(bit_a, bit_b, mine_a, got_a, mine_b, got_b, *outs):
    for i in range(2):
        for bit, mine, got, out in ((bit_a, mine_a, got_a, outs[i]), (bit_b, mine_b, got_b, outs[2 + i])):
            own = bit_clear(bit)
            half = mine.shape[1]
            out[:half] = jnp.where(own, mine[i], got[i])
            out[half:] = jnp.where(own, got[i], mine[i])


def from_both(values, bit):
    count = lax.axis_size("dp")
    pairs = [(2 * i + r, 2 * (i ^ (1 << bit)) + 1 - r) for i in range(count) for r in range(2)]
    return lax.ppermute(values, ("dp", "row"), pairs)


class Pair:
    def __init__(self, keep_a, send_a, keep_b, send_b, bits_a, bits_b, apart):
        self.bits_a, self.bits_b = bits_a, bits_b
        self.apart = apart
        self.count = len(bits_a)
        self.stage = 0
        self.steps = 2 * self.count + apart
        self.state = (keep_a, from_dp(send_a, bits_a[0]), keep_b, from_dp(send_b, bits_b[0]))

    @property
    def on_last(self):
        return self.stage == self.steps - 1

    def step(self):
        self.stage += 1
        count, stage = self.count, self.stage
        last = self.bits_a[-1]
        if stage < count:
            rows, lanes = self.state[0].shape[1:]
            if stage < count - 1:
                bit_a, bit_b = self.bits_a[stage], self.bits_b[stage]
                keep_a, send_a, keep_b, send_b = call(
                    lambda *refs: halve_kernel(bit_a, bit_b, *refs),
                    (shape((2, rows // 2, lanes), BF16),) * 4,
                    *self.state,
                )
                self.state = (keep_a, from_dp(send_a, bit_a), keep_b, from_dp(send_b, bit_b))
            else:
                keep, to_dp, to_row, to_both = call(
                    lambda *refs: cross_kernel(last, *refs),
                    (shape((2, rows // 2, lanes), BF16),) * 4,
                    *self.state,
                )
                self.state = (keep, from_dp(to_dp, last), from_row(to_row), from_both(to_both, last))
        elif not self.apart:
            self.gather()
        elif stage == count:
            rows, lanes = self.state[0].shape[1:]
            mine = call(join_kernel, shape((2, 2, rows, lanes), BF16), *self.state)
            self.state = (mine, from_dp(mine, last))
        elif stage == 2 * count:
            mine_a, got_a, mine_b, got_b, next_a, next_b = self.state
            more_a, more_b = from_dp(next_a, self.bits_a[0]), from_dp(next_b, self.bits_b[0])
            self.state = (mine_a, got_a, mine_b, got_b, next_a, more_a, next_b, more_b)
        elif self.apart and stage == 2 * count - 1:
            rows, lanes = self.state[0].shape[-2:]
            before_a, before_b = self.bits_a[1], self.bits_b[1]
            a0, a1, b0, b1 = call(
                lambda *refs: double_apart_kernel(before_a, before_b, *refs),
                (shape((2 * rows, lanes), BF16),) * 4,
                *self.state,
            )
            self.state = (a0, from_dp(a0, self.bits_a[0]), b0, from_dp(b0, self.bits_b[0]), a1, b1)
        else:
            index = 2 * count - 1 - stage
            bit_a, bit_b = self.bits_a[index], self.bits_b[index]
            rows, lanes = self.state[0].shape[-2:]
            outs = (shape((2, 2 * rows, lanes), BF16),) * 2
            if stage == count + 1:
                mine_a, mine_b = call(lambda *refs: part_kernel(last, *refs), outs, *self.state)
            else:
                before_a, before_b = self.bits_a[index + 1], self.bits_b[index + 1]
                mine_a, mine_b = call(
                    lambda *refs: double_kernel(before_a, before_b, *refs), outs, *self.state
                )
            self.state = (mine_a, from_dp(mine_a, bit_a), mine_b, from_dp(mine_b, bit_b))


    def gather(self):
        count, stage = self.count, self.stage
        rows, lanes = self.state[0].shape[-2:]
        last = self.bits_a[-1]
        if stage == count:
            out = shape((4 * rows + EXTRA, lanes), BF16)
            mine = call(join_more_kernel, out, *self.state, *self.vectors)
            self.state = (mine, from_dp(mine, last))
            return
        index = 2 * count - 1 - stage
        if stage == count + 1:
            rows = rows - EXTRA
            kernel = lambda *refs: part_more_kernel(last, *refs)
        else:
            rows = 2 * (rows - EXTRA)
            before_a, before_b = self.bits_a[index + 1], self.bits_b[index + 1]
            kernel = lambda *refs: double_more_kernel(before_a, before_b, *refs)
        outs = (shape((rows + EXTRA, lanes), BF16), shape((rows, lanes), BF16))
        mine_a, mine_b = call(kernel, outs, *self.state)
        got_a, got_b = from_dp(mine_a, self.bits_a[index]), from_dp(mine_b, self.bits_b[index])
        self.state = (mine_a, got_a, mine_b, got_b)


def arrived(pairs, *others):
    states, others = lax.optimization_barrier(([pair.state for pair in pairs], others))
    for pair, state in zip(pairs, states):
        pair.state = state
    return others


def ordered_halves(bit, mine, got):
    own = (lax.axis_index("dp") // (1 << bit)) % 2 == 0
    return jnp.concatenate(
        [jnp.where(own, mine, got), jnp.where(own, got, mine)], axis=0
    )


def by_row(mine, far, axis):
    first = lax.axis_index("row") == 0
    return jnp.concatenate(
        [jnp.where(first, mine, far), jnp.where(first, far, mine)], axis=axis
    )


def feed_end_kernel(bit, mine_0, got_0, mine_1, got_1, out):
    own = (lax.axis_index("dp") // (1 << bit)) % 2
    here = pl.program_id(1) == own
    near = pl.program_id(0) == lax.axis_index("row")
    part = jnp.where(
        near,
        jnp.where(here, mine_0[...], got_0[...]),
        jnp.where(here, mine_1[...], got_1[...]),
    )
    out[...] = part.astype(F32)


def attention_end(bit, flip, mine, got, left, right):
    rows, half = left.shape[0], left.shape[1]
    own = bit_clear(bit)
    part = rows // 2
    sides = []
    for p in range(2):
        low, high = mine[p * part : (p + 1) * part], got[p * part : (p + 1) * part]
        sides.append(jnp.concatenate([jnp.where(own, low, high), jnp.where(own, high, low)], axis=0))
    near, far = sides
    third = half // 2
    left[...] = by_row(near[:, :third], far[:, :third], 1).astype(F32)
    last = by_row(near[:, third:], far[:, third:], 1).astype(F32)
    right[...] = last.T if flip else last


def first_end_kernel(bit, mine, got, left, right, small):
    attention_end(bit, False, mine, got, left, right)
    small[...] = extra_sum(mine, got)


def second_end_kernel(bit, mine, got, left, right):
    attention_end(bit, True, mine, got, left, right)


def end_call(kernel, grid, out_shape, block, index, *operands):
    whole = pl.BlockSpec(memory_space=pltpu.VMEM)
    return pl.pallas_call(
        kernel,
        grid=grid,
        out_shape=out_shape,
        in_specs=[whole] * len(operands),
        out_specs=pl.BlockSpec(block, index),
        compiler_params=pltpu.CompilerParams(vmem_limit_bytes=16 * MIB),
    )(*operands)


def body(
    tokens,
    out_grad,
    seq_lengths,
    w_query,
    w_key,
    w_value,
    w_out,
    w_up,
    w_down,
    b_query,
    b_value,
    b_out,
    b_up,
    b_down,
    gain_attn,
    shift_attn,
    gain_mlp,
    shift_mlp,
):
    row = lax.axis_index("row")
    own_rows, half = tokens.shape
    width = 2 * half
    rows = 2 * own_rows
    third = w_query.shape[1] // 2
    units = w_up.shape[1] // 2
    side = lax.axis_index("dp") % 2
    count = lax.axis_size("dp").bit_length() - 1
    bits = list(range(count))
    turned = [1, 0] + bits[2:] if count > 1 else bits
    tall = shape((own_rows, width), F32)
    tall_low = shape((own_rows, width), BF16)
    column = shape((own_rows, 128), F32)
    pair_sums = shape((8, half), F32)

    tokens_far = from_row(tokens)
    vectors = (gain_attn, shift_attn, b_out, gain_mlp, shift_mlp, b_query, b_value, b_up, b_down)
    block = pltpu.VMEM((half, 2 * third), BF16)
    w_kept, sent, sent_out, sent_up, sent_down = call(
        start_kernel,
        (
            shape((half + EXTRA, 3 * third), BF16),
            shape((half + EXTRA, 3 * third), BF16),
            shape((w_out.shape[0] // 2, half), BF16),
            shape((half // 2, units), BF16),
            shape((units // 2, half), BF16),
        ),
        *vectors, w_query, w_key, w_value, w_out, w_up, w_down,
        hbm=range(15),
        scratch=[pltpu.VMEM(x.shape, x.dtype) for x in vectors]
        + [block, block, block, pltpu.VMEM((EXTRA, 3 * third), F32), pltpu.SemaphoreType.DMA((15,))],
        vmem=VMEM_START,
    )
    tokens_far, sent, sent_out = hold(tokens_far, sent, sent_out)
    w_got = from_row(sent)
    out_got = from_row(sent_out)
    tokens_col = from_col(tokens)
    tokens_far_col = from_col(tokens_far)
    top_col = from_col(out_grad)
    tokens_far, tokens_col, tokens_far_col, w_got, out_got, sent_up, sent_down = hold(
        tokens_far, tokens_col, tokens_far_col, w_got, out_got, sent_up, sent_down
    )
    up_got = from_row(sent_up)
    down_got = from_row(sent_down)
    out_side = from_dp(out_got, 0)
    every_token = (tokens, tokens_far, tokens_col, tokens_far_col)

    like = shape((rows, third), BF16)
    normed_all, query, key, value, mixed, lse = call(
        forward_kernel,
        (shape((rows, width), BF16), like, like, like, like, shape((8, rows), F32)),
        seq_lengths,
        *every_token,
        w_kept,
        w_got,
        smem=(0,),
        hbm_out=range(4),
        scratch=[pltpu.VMEM((rows, width), BF16)]
        + [pltpu.VMEM((rows, third), BF16)] * 3
        + [pltpu.SemaphoreType.DMA((4,))],
    )
    mixed_far = from_row(mixed)
    mixed_gate, up_got = hold(mixed, up_got)
    up_side = from_dp(up_got, 0)
    mixed_far, out_side, up_side, down_got, out_grad_send = hold(
        mixed_far, out_side, up_side, down_got, out_grad
    )

    keep, send, w_out_far = call(
        branch_kernel,
        (shape((rows, width), F32), shape((rows, width), BF16), shape(w_out.shape, BF16)),
        mixed_gate, mixed_far, w_out, out_got, out_side,
    )
    got = from_col(send)
    top_far = from_row(out_grad_send)
    down_side = from_dp(down_got, 1)
    (got,) = hold(got)

    middle, normed_mlp_all, unit_mlp, inverse_mlp = call(
        second_norm_kernel,
        (shape((own_rows, half), F32), shape((rows, width), BF16), tall, column),
        *every_token, keep, got, w_kept, w_got,
    )
    hidden, slope, w_up_far = call(
        up_kernel,
        (shape((rows, units), BF16), shape((rows, units), F32), shape((half, units), BF16)),
        normed_mlp_all, w_up, up_got, up_side, w_kept,
    )
    hidden, top_far = hold(hidden, top_far)
    top_far_col = from_col(top_far)
    top_far_col, down_side = hold(top_far_col, down_side)

    split_down = shape((2, units // 2, half), BF16)
    split_up = shape((2, half, units // 2), BF16)
    down_keep, down_send, up_keep, up_send, keep, send, mlp_sums, w_down_far = call(
        lambda *refs: down_kernel(bits[0], turned[0], *refs),
        (
            split_down, split_down, split_up, split_up, tall, tall_low,
            shape((8, units), F32), shape((units, half), BF16),
        ),
        seq_lengths, out_grad, top_far, top_col, top_far_col, hidden, slope, normed_mlp_all,
        w_down, down_got, down_side, w_up, w_up_far,
        scratch=[pltpu.VMEM((rows, width), BF16), pltpu.VMEM((rows, units), BF16)],
        smem=(0,),
    )
    got = from_col(send)
    feed = Pair(down_keep, down_send, up_keep, up_send, bits, turned, True)
    (got,) = hold(got)

    total = (keep + got.astype(F32)).astype(BF16)
    total_far = from_row(total)
    keep, send = call(
        output_kernel, (tall, tall_low), hidden, w_down, w_down_far,
    )
    got = from_col(send)
    total_far, got = hold(total_far, got)

    grad_middle, datt, mid_sums = call(
        second_back_kernel,
        (shape((own_rows, half), F32), tall_low, pair_sums),
        seq_lengths, total, total_far, unit_mlp, inverse_mlp, w_kept, w_got, out_grad, top_far,
        smem=(0,),
    )
    datt_col = from_col(datt)
    raised_keep, raised_got = keep, got
    (datt_col,) = arrived([feed], datt_col)
    feed.step()

    split_pair = shape((2, half // 2, 2 * third), BF16)
    first_keep, first_send, second_keep, second_send, keep, send, attn_sums = call(
        lambda *refs: backward_kernel(bits[0], turned[0], *refs),
        (split_pair,) * 4 + (tall, tall_low, shape((8, width), F32)),
        seq_lengths, datt, datt_col, w_out, w_out_far, query, key, value, mixed, lse,
        normed_all, w_kept, w_got,
        scratch=[
            pltpu.VMEM((rows, width), BF16),
            pltpu.VMEM((rows, 3 * third), BF16),
            pltpu.VMEM((rows, third), F32),
            pltpu.VMEM((rows, third), F32),
        ]
        + [pltpu.VMEM((rows, third), BF16)] * 4
        + [pltpu.VMEM((rows, width), BF16), pltpu.SemaphoreType.DMA((4,))],
        smem=(0,),
        hbm=(5, 6, 7, 10),
    )
    keep, send = arrived([feed], keep, send)
    got = from_col(send)
    attention = Pair(first_keep, first_send, second_keep, second_send, bits, turned, False)
    pairs = [feed, attention]
    feed.step()
    (got,) = arrived(pairs, got)

    mine, raised, out, stats, unit_attn, inverse_attn = call(
        first_back_kernel,
        (
            shape((own_rows, half), F32),
            shape((own_rows, half), F32),
            shape((rows + EXTRA, half), BF16),
            shape((8, own_rows), F32),
            shape((own_rows, half), F32),
            column,
        ),
        keep, got, raised_keep, raised_got, tokens, tokens_far, w_kept, w_got,
    )
    got = from_row(out)
    feed.step()
    attention.step()
    (got,) = arrived(pairs, got)

    output, input_grad, halves = call(
        last_kernel,
        (shape((own_rows, half), BF16), shape((own_rows, half), BF16), pair_sums),
        mine, raised, got, stats, unit_attn, inverse_attn, w_kept, middle, grad_middle, mid_sums,
    )
    halves_col = from_col(halves)
    feed.step()
    attention.step()
    (halves_col,) = arrived(pairs, halves_col)
    attention.vectors = (halves, halves_col, mlp_sums, attn_sums)
    while not attention.on_last:
        moving = [pair for pair in pairs if not pair.on_last]
        for pair in moving:
            pair.step()
        arrived(moving)

    wide = w_query.shape[1]
    outs = (shape((half, wide), F32),) * 2
    mine_a, got_a, mine_b, got_b = attention.state
    grad_query, grad_key, small = call(
        lambda *refs: first_end_kernel(bits[0], *refs),
        outs + (shape((EXTRA, half), F32),),
        mine_a,
        got_a,
    )
    grad_value, grad_out = call(
        lambda *refs: second_end_kernel(turned[0], *refs), outs, mine_b, got_b
    )
    a_0, got_a_0, b_0, got_b_0, a_1, got_a_1, b_1, got_b_1 = feed.state
    grad_down = end_call(
        lambda *refs: feed_end_kernel(bits[0], *refs),
        (2, 2),
        shape((2 * units, half), F32),
        (units // 2, half),
        lambda i, j: (2 * i + j, 0),
        a_0,
        got_a_0,
        a_1,
        got_a_1,
    )
    grad_up = end_call(
        lambda *refs: feed_end_kernel(turned[0], *refs),
        (2, 2),
        shape((half, 2 * units), F32),
        (half, units // 2),
        lambda i, j: (0, 2 * i + j),
        b_0,
        got_b_0,
        b_1,
        got_b_1,
    )
    return (
        output,
        input_grad,
        grad_query,
        grad_key,
        grad_value,
        grad_out,
        grad_up,
        grad_down,
        small[4, :third],
        small[4, third:],
        small[5],
        small[6:8].reshape(-1),
        small[8],
        small[0],
        small[1],
        small[2],
        small[3],
    )


def solution(mesh):
    return jax.shard_map(
        body,
        mesh=mesh,
        in_specs=(
            P(("dp", "col"), "row"),
            P(("dp", "col"), "row"),
            P("dp", None),
            P("row", "col"),
            P("row", "col"),
            P("row", "col"),
            P("col", "row"),
            P("row", "col"),
            P("col", "row"),
            P(("col", "row")),
            P(("col", "row")),
            P("row"),
            P(("col", "row")),
            P("row"),
            P("row"),
            P("row"),
            P("row"),
            P("row"),
        ),
        out_specs=(
            P(("dp", "col"), "row"),
            P(("dp", "col"), "row"),
            P("row", "col"),
            P("row", "col"),
            P("row", "col"),
            P("col", "row"),
            P("row", "col"),
            P("col", "row"),
            P(("col", "row")),
            P(("col", "row")),
            P("row"),
            P(("col", "row")),
            P("row"),
            P("row"),
            P("row"),
            P("row"),
            P("row"),
        ),
        check_vma=False,
    )
```

time: 183 us -> 174 us (0.951)
  starting transfers between devices: 60.8 us -> 49.3 us
  waiting for transfers between devices: 83.9 us -> 88.2 us
    ppermute x31 -> x25, starting transfers between devices: 41.5 us -> 28.6 us  [from_dp(): return lax.ppermute(values, 'dp', dp_pairs(bit))]
    ppermute x0 -> x2, waiting for transfers between devices: none -> 9.49 us  [from_both(): return lax.ppermute(values, ('dp', 'row'), pairs)]
    ppermute x31 -> x25, waiting for transfers between devices: 54 us -> 48.6 us  [from_dp(): return lax.ppermute(values, 'dp', dp_pairs(bit))]
    ppermute x0 -> x2, starting transfers between devices: none -> 4 us  [from_both(): return lax.ppermute(values, ('dp', 'row'), pairs)]
    ppermute x16 -> x11, starting transfers between devices: 17.7 us -> 14.9 us  [from_row(): return lax.ppermute(values, 'row', SWAP)]
    ppermute x16 -> x11, waiting for transfers between devices: 27 us -> 29.4 us  [from_row(): return lax.ppermute(values, 'row', SWAP)]
    ppermute x10, waiting for transfers between devices: 2.99 us -> 0.83 us  [from_col(): return lax.ppermute(values, 'col', SWAP)]
    pallas_call x39 -> x23, Pallas kernels: 29.7 us -> 28.2 us  [call(): pl.pallas_call(kernel, out_shape=out_shape, in_specs=[pl.BlockSpec(memory...]
  transfers between devices with their start and end apart: 57 -> 48, of which waited for: 28 -> 26; matrix products, arithmetic and copies ran while one was open for 2% -> 0% of each run, Pallas kernels for 14% -> 14%
where the time goes in v4:
time: 174 us
  waiting for transfers between devices  88.2 us (51%)
  starting transfers between devices  49.3 us (28%)
  Pallas kernels  32.2 us (19%)
  local copies, waits for them, and re-layouts  3.42 us (2%)
    ppermute x25, waiting for transfers between devices, from_dp(): return lax.ppermute(values, 'dp', dp_pairs(bit))  48.6 us
    ppermute x11, waiting for transfers between devices, from_row(): return lax.ppermute(values, 'row', SWAP)  29.4 us
    ppermute x25, starting transfers between devices, from_dp(): return lax.ppermute(values, 'dp', dp_pairs(bit))  28.6 us
    pallas_call x23, Pallas kernels, call(): pl.pallas_call(kernel, out_shape=out_shape, in_specs=[pl.BlockSpec(memory...  28.2 us
    ppermute x11, starting transfers between devices, from_row(): return lax.ppermute(values, 'row', SWAP)  14.9 us
    ppermute x2, waiting for transfers between devices, from_both(): return lax.ppermute(values, ('dp', 'row'), pairs)  9.49 us
    pallas_call x2, Pallas kernels, end_call(): pl.pallas_call(kernel, grid=grid, out_shape=out_shape, in_specs=[whole] *...  4.01 us
    ppermute x2, starting transfers between devices, from_both(): return lax.ppermute(values, ('dp', 'row'), pairs)  4 us
  transfers between devices with their start and end apart: 48, of which 26 were waited for; matrix products, arithmetic and copies ran while one was open for 0% of the time, Pallas kernels for 14%

profile of v4, /device:TPU:0, one launch (start us, length us, event | category | flops | bytes accessed | tf_op | source)
XLA Modules:
  0.0 174.1 jit_solution(10838649801019768097)
XLA Ops:
  0.7 3.0 %collective-permute-start = (bf16[256,384]{1,0:T(8,128)(2,1)}, bf16[256,384]{1,0:T(8,128)(2,1)S(1)}, u32[]{:S(2)}, u32[]{:S(2)}) collective-permute-start(bf16[256,384]{1,0:T(8,128)(2,1)} %own.5), channel_id=1, source_target_pairs={{0,2},{2,0},{1,3},{3,1},{4,6},{6,4},{5,7},{7,5},{8,10},{10,8},{9,1... | collective-permute-start | bytes 589832 | tf_op jit(solution)/shard_map/ppermute | solution.py:34
  3.7 3.0 %shard_map.305 = (bf16[400,576]{1,0:T(8,128)(2,1)}, bf16[400,576]{1,0:T(8,128)(2,1)}, bf16[192,384]{1,0:T(8,128)(2,1)}, bf16[192,768]{1,0:T(8,128)(2,1)}, bf16[384,384]{1,0:T(8,128)(2,1)}) custom-call(bf16[384]{0:T(512)(128)(2,1)} %refs_0_.3, bf16[384]{0:T(512)(128)(2,1)} %refs_1_.2, bf16[384]{0:T(512)(128)(2,1)} %refs_2_.1, bf16[384]{0:T(512)(128)(2,1)} %refs_3_.2, ...), custom_call_target="tpu_custom_call" | custom-call | tf_op jit(solution)/shard_map/pallas_call | solution.py:69
  6.8 2.1 %collective-permute-done.own_far = bf16[256,384]{1,0:T(8,128)(2,1)S(1)} collective-permute-done((bf16[256,384]{1,0:T(8,128)(2,1)}, bf16[256,384]{1,0:T(8,128)(2,1)S(1)}, u32[]{:S(2)}, u32[]{:S(2)}) %collective-permute-start) | collective-permute-done | bytes 196640 | tf_op jit(solution)/shard_map/ppermute | solution.py:34
  8.8 1.7 collective-permute-start.3
  12.0 13.0 %collective-permute-done.4.got = bf16[192,384]{1,0:T(8,128)(2,1)S(1)} collective-permute-done((bf16[192,384]{1,0:T(8,128)(2,1)}, bf16[192,384]{1,0:T(8,128)(2,1)S(1)}, u32[]{:S(2)}, u32[]{:S(2)}) %collective-permute-start.4) | collective-permute-done | bytes 147488 | tf_op jit(solution)/shard_map/ppermute | solution.py:34
  28.1 4.4 %shard_map.306 = (bf16[512,768]{1,0:T(8,128)(2,1)S(1)}, bf16[512,192]{1,0:T(8,128)(2,1)S(1)}, bf16[512,192]{1,0:T(8,128)(2,1)S(1)}, bf16[512,192]{1,0:T(8,128)(2...) custom-call(s32[1,2]{1,0:T(1,128)S(1)} %copy-done.7, bf16[256,384]{1,0:T(8,128)(2,1)S(1)} %copy-done.5, ...), custom_call_target="tpu_custom_call" | custom-call | tf_op jit(solution)/shard_map/pallas_call | solution.py:69
  32.5 2.7 %collective-permute-done.5.got = bf16[192,768]{1,0:T(8,128)(2,1)S(1)} collective-permute-done((bf16[192,768]{1,0:T(8,128)(2,1)}, bf16[192,768]{1,0:T(8,128)(2,1)S(1)}, u32[]{:S(2)}, u32[]{:S(2)}) %collective-permute-start.5) | collective-permute-done | bytes 294944 | tf_op jit(solution)/shard_map/ppermute | solution.py:34
  38.7 4.9 %collective-permute-done.7.got_side = bf16[192,384]{1,0:T(8,128)(2,1)S(1)} collective-permute-done((bf16[192,384]{1,0:T(8,128)(2,1)S(1)}, bf16[192,384]{1,0:T(8,128)(2,1)S(1)}, u32[]{:S(2)}, u32[]{:S(2)}) %collective-permute-start.7) | collective-permute-done | bytes 147488 | tf_op jit(solution)/shard_map/ppermute | solution.py:47
  50.8 1.8 %collective-permute-done.11.refs_2_.top_far = bf16[256,384]{1,0:T(8,128)(2,1)S(1)} collective-permute-done((bf16[256,384]{1,0:T(8,128)(2,1)S(1)}, bf16[256,384]{1,0:T(8,128)(2,1)S(1)}, u32[]{:S(2)}, u32[]{:S(2)}) %collective-permute-start.11) | collective-permute-done | bytes 196640 | tf_op jit(solution)/shard_map/ppermute | solution.py:34
  53.1 2.4 %collective-permute-done.14.refs_10_ = bf16[384,384]{1,0:T(8,128)(2,1)S(1)} collective-permute-done((bf16[384,384]{1,0:T(8,128)(2,1)S(1)}, bf16[384,384]{1,0:T(8,128)(2,1)S(1)}, u32[]{:S(2)}, u32[]{:S(2)}) %collective-permute-start.14) | collective-permute-done | bytes 294944 | tf_op jit(solution)/shard_map/ppermute | solution.py:47
  55.6 4.2 %shard_map.310 = (bf16[2,384,384]{2,1,0:T(8,128)(2,1)S(1)}, bf16[2,384,384]{2,1,0:T(8,128)(2,1)S(1)}, bf16[2,384,384]{2,1,0:T(8,128)(2,1)S(1)}, bf16[2,384,384]{...) custom-call(s32[1,2]{1,0:T(1,128)S(1)} %copy-done.7, ...), custom_call_target="tpu_custom_call" | custom-call | tf_op jit(solution)/shard_map/pallas_call | solution.py:69
  65.3 7.6 %collective-permute-done.18.total_far = bf16[256,768]{1,0:T(8,128)(2,1)S(1)} collective-permute-done((bf16[256,768]{1,0:T(8,128)(2,1)S(1)}, bf16[256,768]{1,0:T(8,128)(2,1)S(1)}, u32[]{:S(2)}, u32[]{:S(2)}) %collective-permute-start.18) | collective-permute-done | bytes 393248 | tf_op jit(solution)/shard_map/ppermute | solution.py:34
  74.1 3.6 %collective-permute-done.15.refs_1_ = bf16[2,384,384]{2,1,0:T(8,128)(2,1)S(1)} collective-permute-done((bf16[2,384,384]{2,1,0:T(8,128)(2,1)S(1)}, bf16[2,384,384]{2,1,0:T(8,128)(2,1)S(1)}, u32[]{:S(2)}, u32[]{:S(2)}) %collective-permute-start.15) | collective-permute-done | bytes 589856 | tf_op jit(solution)/shard_map/ppermute | solution.py:47
  81.1 6.0 %shard_map.314 = (bf16[2,192,384]{2,1,0:T(8,128)(2,1)S(1)}, bf16[2,192,384]{2,1,0:T(8,128)(2,1)S(1)}, bf16[2,192,384]{2,1,0:T(8,128)(2,1)S(1)}, bf16[2,192,384]{...) custom-call(s32[1,2]{1,0:T(1,128)S(1)} %copy-done.7, ...), custom_call_target="tpu_custom_call" | custom-call | tf_op jit(solution)/shard_map/pallas_call | solution.py:69
  89.4 2.7 %collective-permute-start.23 = (bf16[2,96,384]{2,1,0:T(8,128)(2,1)S(1)}, bf16[2,96,384]{2,1,0:T(8,128)(2,1)S(1)}, u32[]{:S(2)}, u32[]{:S(2)}) collective-permute-start(bf16[2,96,384]{2,1,0:T(8,128)(2,1)S(1)} %get-tuple-element.249), channel_id=1, source_target_pairs={{0,16},{4,20},{8,24},{12,28},{16,0},{20,4},{24,8},{28,12},{1,17},{... | collective-permute-start | bytes 442376 | tf_op jit(solution)/shard_map/ppermute | solution.py:47
  94.3 3.6 %collective-permute-start.25 = (bf16[2,96,384]{2,1,0:T(8,128)(2,1)S(1)}, bf16[2,96,384]{2,1,0:T(8,128)(2,1)S(1)}, u32[]{:S(2)}, u32[]{:S(2)}) collective-permute-start(bf16[2,96,384]{2,1,0:T(8,128)(2,1)S(1)} %get-tuple-element.251), channel_id=1, source_target_pairs={{0,18},{2,16},{4,22},{6,20},{8,26},{10,24},{12,30},{14,28},{16,2},... | collective-permute-start | bytes 442376 | tf_op jit(solution)/shard_map/ppermute | solution.py:567
  97.9 5.6 %collective-permute-done.27.refs_3_ = bf16[2,192,384]{2,1,0:T(8,128)(2,1)S(1)} collective-permute-done((bf16[2,192,384]{2,1,0:T(8,128)(2,1)S(1)}, bf16[2,192,384]{2,1,0:T(8,128)(2,1)S(1)}, u32[]{:S(2)}, u32[]{:S(2)}) %collective-permute-start.27) | collective-permute-done | bytes 294944 | tf_op jit(solution)/shard_map/ppermute | solution.py:47
  103.4 4.2 %collective-permute-done.25.from_both_ref = bf16[2,96,384]{2,1,0:T(8,128)(2,1)S(1)} collective-permute-done((bf16[2,96,384]{2,1,0:T(8,128)(2,1)S(1)}, bf16[2,96,384]{2,1,0:T(8,128)(2,1)S(1)}, u32[]{:S(2)}, u32[]{:S(2)}) %collective-permute-start.25) | collective-permute-done | bytes 147488 | tf_op jit(solution)/shard_map/ppermute | solution.py:567
  110.1 2.4 %collective-permute-start.30 = (bf16[2,96,384]{2,1,0:T(8,128)(2,1)S(1)}, bf16[2,96,384]{2,1,0:T(8,128)(2,1)S(1)}, u32[]{:S(2)}, u32[]{:S(2)}) collective-permute-start(bf16[2,96,384]{2,1,0:T(8,128)(2,1)S(1)} %get-tuple-element.271), channel_id=1, source_target_pairs={{0,8},{4,12},{8,0},{12,4},{16,24},{20,28},{24,16},{28,20},{1,9},{5... | collective-permute-start | bytes 442376 | tf_op jit(solution)/shard_map/ppermute | solution.py:47
  113.1 4.2 %collective-permute-done.30.refs_1_ = bf16[2,96,384]{2,1,0:T(8,128)(2,1)S(1)} collective-permute-done((bf16[2,96,384]{2,1,0:T(8,128)(2,1)S(1)}, bf16[2,96,384]{2,1,0:T(8,128)(2,1)S(1)}, u32[]{:S(2)}, u32[]{:S(2)}) %collective-permute-start.30) | collective-permute-done | bytes 147488 | tf_op jit(solution)/shard_map/ppermute | solution.py:47
  117.7 4.6 %collective-permute-done.29.refs_1_ = bf16[2,2,96,384]{3,2,1,0:T(8,128)(2,1)S(1)} collective-permute-done((bf16[2,2,96,384]{3,2,1,0:T(8,128)(2,1)S(1)}, bf16[2,2,96,384]{3,2,1,0:T(8,128)(2,1)S(1)}, u32[]{:S(2)}, u32[]{:S(2)}) %collective-permute-start.29) | collective-permute-done | bytes 294944 | tf_op jit(solution)/shard_map/ppermute | solution.py:47
  124.1 3.4 %collective-permute-start.35 = (bf16[2,48,384]{2,1,0:T(8,128)(2,1)S(1)}, bf16[2,48,384]{2,1,0:T(8,128)(2,1)S(1)}, u32[]{:S(2)}, u32[]{:S(2)}) collective-permute-start(bf16[2,48,384]{2,1,0:T(8,128)(2,1)S(1)} %get-tuple-element.293), channel_id=1, source_target_pairs={{0,16},{4,20},{8,24},{12,28},{16,0},{20,4},{24,8},{28,12},{1,17},{... | collective-permute-start | bytes 221192 | tf_op jit(solution)/shard_map/ppermute | solution.py:47
  129.1 1.7 collective-permute-done.35.from_dp_ref
  131.9 5.3 %collective-permute-done.37.from_both_ref = bf16[2,48,384]{2,1,0:T(8,128)(2,1)S(1)} collective-permute-done((bf16[2,48,384]{2,1,0:T(8,128)(2,1)S(1)}, bf16[2,48,384]{2,1,0:T(8,128)(2,1)S(1)}, u32[]{:S(2)}, u32[]{:S(2)}) %collective-permute-start.37) | collective-permute-done | bytes 73760 | tf_op jit(solution)/shard_map/ppermute | solution.py:567
  138.0 2.4 %collective-permute-start.41 = (bf16[208,384]{1,0:T(8,128)(2,1)S(1)}, bf16[208,384]{1,0:T(8,128)(2,1)S(1)}, u32[]{:S(2)}, u32[]{:S(2)}) collective-permute-start(bf16[208,384]{1,0:T(8,128)(2,1)S(1)} %shard_map.323.refs_0_), channel_id=1, source_target_pairs={{0,16},{4,20},{8,24},{12,28},{16,0},{20,4},{24,8},{28,12},{1,17},{... | collective-permute-start | bytes 479240 | tf_op jit(solution)/shard_map/ppermute | solution.py:47
  140.4 7.4 %collective-permute-done.41.refs_1_ = bf16[208,384]{1,0:T(8,128)(2,1)S(1)} collective-permute-done((bf16[208,384]{1,0:T(8,128)(2,1)S(1)}, bf16[208,384]{1,0:T(8,128)(2,1)S(1)}, u32[]{:S(2)}, u32[]{:S(2)}) %collective-permute-start.41) | collective-permute-done | bytes 159776 | tf_op jit(solution)/shard_map/ppermute | solution.py:47
  147.8 2.2 %collective-permute-done.40.refs_1_ = bf16[384,384]{1,0:T(8,128)(2,1)S(1)} collective-permute-done((bf16[384,384]{1,0:T(8,128)(2,1)S(1)}, bf16[384,384]{1,0:T(8,128)(2,1)S(1)}, u32[]{:S(2)}, u32[]{:S(2)}) %collective-permute-start.40) | collective-permute-done | bytes 294944 | tf_op jit(solution)/shard_map/ppermute | solution.py:47
  151.4 2.1 %collective-permute-start.44 = (bf16[208,384]{1,0:T(8,128)(2,1)S(1)}, bf16[208,384]{1,0:T(8,128)(2,1)S(1)}, u32[]{:S(2)}, u32[]{:S(2)}) collective-permute-start(bf16[208,384]{1,0:T(8,128)(2,1)S(1)} %get-tuple-element.322.refs_0_), channel_id=1, source_target_pairs={{0,8},{4,12},{8,0},{12,4},{16,24},{20,28},{24,16},{28,20},{1,9},{5... | collective-permute-start | bytes 479240 | tf_op jit(solution)/shard_map/ppermute | solution.py:47
  154.1 6.9 %collective-permute-done.45.refs_3_ = bf16[192,384]{1,0:T(8,128)(2,1)S(1)} collective-permute-done((bf16[192,384]{1,0:T(8,128)(2,1)S(1)}, bf16[192,384]{1,0:T(8,128)(2,1)S(1)}, u32[]{:S(2)}, u32[]{:S(2)}) %collective-permute-start.45) | collective-permute-done | bytes 147488 | tf_op jit(solution)/shard_map/ppermute | solution.py:47
  164.0 2.0 %shard_map.328 = f32[384,1536]{1,0:T(8,128)} custom-call(bf16[384,384]{1,0:T(8,128)(2,1)S(1)} %get-tuple-element.336.refs_0_, bf16[384,384]{1,0:T(8,128)(2,1)S(1)} %collective-permute-done.40.refs_1_, bf16[384,384]{1,0:T(8,128)(2,1)S(1)} %get-tuple-element.338.refs_2_, bf16[384,384]{1,0:T(8,128)(2,1)S(1)} %collective-permute-done.43.refs_3_), custom_call_target="tpu_custom_call" | custom-call | tf_op jit(solution)/shard_map/pallas_call | solution.py:720
  166.1 2.0 %shard_map.329 = f32[1536,384]{1,0:T(8,128)} custom-call(bf16[384,384]{1,0:T(8,128)(2,1)S(1)} %get-tuple-element.340.refs_0_, bf16[384,384]{1,0:T(8,128)(2,1)S(1)} %collective-permute-done.39.refs_1_, bf16[384,384]{1,0:T(8,128)(2,1)S(1)} %get-tuple-element.342.refs_2_, bf16[384,384]{1,0:T(8,128)(2,1)S(1)} %collective-permute-done.42.refs_3_), custom_call_target="tpu_custom_call" | custom-call | tf_op jit(solution)/shard_map/pallas_call | solution.py:720
  168.0 1.9 %collective-permute-done.47.refs_1_ = bf16[384,384]{1,0:T(8,128)(2,1)S(1)} collective-permute-done((bf16[384,384]{1,0:T(8,128)(2,1)S(1)}, bf16[384,384]{1,0:T(8,128)(2,1)S(1)}, u32[]{:S(2)}, u32[]{:S(2)}) %collective-permute-start.47) | collective-permute-done | bytes 294944 | tf_op jit(solution)/shard_map/ppermute | solution.py:47
  (110 shorter events, 48.1 us)
Async XLA Ops:
  0.7 8.1 %collective-permute-start = (bf16[256,384]{1,0:T(8,128)(2,1)}, bf16[256,384]{1,0:T(8,128)(2,1)S(1)}, u32[]{:S(2)}, u32[]{:S(2)}) collective-permute-start(bf16[256,384]{1,0:T(8,128)(2,1)} %own.5), channel_id=1, source_target_pairs={{0,2},{2,0},{1,3},{3,1},{4,6},{6,4},{5,7},{7,5},{8,10},{10,8},{9,1... | collective-permute-start | bytes 589832 | tf_op jit(solution)/shard_map/ppermute | solution.py:34
  8.8 16.2 %collective-permute-start.3 = (bf16[400,576]{1,0:T(8,128)(2,1)}, bf16[400,576]{1,0:T(8,128)(2,1)S(1)}, u32[]{:S(2)}, u32[]{:S(2)}) collective-permute-start(bf16[400,576]{1,0:T(8,128)(2,1)} %get-tuple-element.184), channel_id=1, source_target_pairs={{0,2},{2,0},{1,3},{3,1},{4,6},{6,4},{5,7},{7,5},{8,10},{10,8},{9,1... | collective-permute-start | bytes 1382408 | tf_op jit(solution)/shard_map/ppermute | solution.py:34
  10.6 14.5 %collective-permute-start.2 = (bf16[256,384]{1,0:T(8,128)(2,1)S(1)}, bf16[256,384]{1,0:T(8,128)(2,1)S(1)}, u32[]{:S(2)}, u32[]{:S(2)}) collective-permute-start(bf16[256,384]{1,0:T(8,128)(2,1)S(1)} %collective-permute-done.own_far), channel_id=1, source_target_pairs={{0,1},{1,0},{2,3},{3,2},{4,5},{5,4},{6,7},{7,6},{8,9},{9,8},{10,11... | collective-permute-start | bytes 589832 | tf_op jit(solution)/shard_map/ppermute | solution.py:38
  11.1 14.0 %collective-permute-start.4 = (bf16[192,384]{1,0:T(8,128)(2,1)}, bf16[192,384]{1,0:T(8,128)(2,1)S(1)}, u32[]{:S(2)}, u32[]{:S(2)}) collective-permute-start(bf16[192,384]{1,0:T(8,128)(2,1)} %get-tuple-element.185), channel_id=1, source_target_pairs={{0,2},{2,0},{1,3},{3,1},{4,6},{6,4},{5,7},{7,5},{8,10},{10,8},{9,1... | collective-permute-start | bytes 442376 | tf_op jit(solution)/shard_map/ppermute | solution.py:34
  25.0 10.2 %collective-permute-start.5 = (bf16[192,768]{1,0:T(8,128)(2,1)}, bf16[192,768]{1,0:T(8,128)(2,1)S(1)}, u32[]{:S(2)}, u32[]{:S(2)}) collective-permute-start(bf16[192,768]{1,0:T(8,128)(2,1)} %get-tuple-element.194), channel_id=1, source_target_pairs={{0,2},{2,0},{1,3},{3,1},{4,6},{6,4},{5,7},{7,5},{8,10},{10,8},{9,1... | collective-permute-start | bytes 884744 | tf_op jit(solution)/shard_map/ppermute | solution.py:34
  26.5 18.0 %collective-permute-start.9 = (bf16[384,384]{1,0:T(8,128)(2,1)}, bf16[384,384]{1,0:T(8,128)(2,1)S(1)}, u32[]{:S(2)}, u32[]{:S(2)}) collective-permute-start(bf16[384,384]{1,0:T(8,128)(2,1)} %get-tuple-element.198), channel_id=1, source_target_pairs={{0,2},{2,0},{1,3},{3,1},{4,6},{6,4},{5,7},{7,5},{8,10},{10,8},{9,1... | collective-permute-start | bytes 884744 | tf_op jit(solution)/shard_map/ppermute | solution.py:34
  35.2 9.3 %collective-permute-start.8 = (bf16[192,768]{1,0:T(8,128)(2,1)S(1)}, bf16[192,768]{1,0:T(8,128)(2,1)S(1)}, u32[]{:S(2)}, u32[]{:S(2)}) collective-permute-start(bf16[192,768]{1,0:T(8,128)(2,1)S(1)} %collective-permute-done.5.got), channel_id=1, source_target_pairs={{0,4},{4,0},{8,12},{12,8},{16,20},{20,16},{24,28},{28,24},{1,5},{5... | collective-permute-start | bytes 884744 | tf_op jit(solution)/shard_map/ppermute | solution.py:47
  36.6 7.9 %collective-permute-start.6 = (bf16[512,192]{1,0:T(8,128)(2,1)S(1)}, bf16[512,192]{1,0:T(8,128)(2,1)S(1)}, u32[]{:S(2)}, u32[]{:S(2)}) collective-permute-start(bf16[512,192]{1,0:T(8,128)(2,1)S(1)} %get-tuple-element.195.mixed.refs_8_), channel_id=1, source_target_pairs={{0,2},{2,0},{1,3},{3,1},{4,6},{6,4},{5,7},{7,5},{8,10},{10,8},{9,1... | collective-permute-start | bytes 589832 | tf_op jit(solution)/shard_map/ppermute | solution.py:34
  46.5 9.1 %collective-permute-start.14 = (bf16[384,384]{1,0:T(8,128)(2,1)S(1)}, bf16[384,384]{1,0:T(8,128)(2,1)S(1)}, u32[]{:S(2)}, u32[]{:S(2)}) collective-permute-start(bf16[384,384]{1,0:T(8,128)(2,1)S(1)} %collective-permute-done.9.refs_9_), channel_id=1, source_target_pairs={{0,8},{4,12},{8,0},{12,4},{16,24},{20,28},{24,16},{28,20},{1,9},{5... | collective-permute-start | bytes 884744 | tf_op jit(solution)/shard_map/ppermute | solution.py:47
  61.7 11.2 %collective-permute-start.18 = (bf16[256,768]{1,0:T(8,128)(2,1)S(1)}, bf16[256,768]{1,0:T(8,128)(2,1)S(1)}, u32[]{:S(2)}, u32[]{:S(2)}) collective-permute-start(bf16[256,768]{1,0:T(8,128)(2,1)S(1)} %add_convert_fusion.total), channel_id=1, source_target_pairs={{0,2},{2,0},{1,3},{3,1},{4,6},{6,4},{5,7},{7,5},{8,10},{10,8},{9,1... | collective-permute-start | bytes 1179656 | tf_op jit(solution)/shard_map/ppermute | solution.py:34
  62.7 15.1 %collective-permute-start.15 = (bf16[2,384,384]{2,1,0:T(8,128)(2,1)S(1)}, bf16[2,384,384]{2,1,0:T(8,128)(2,1)S(1)}, u32[]{:S(2)}, u32[]{:S(2)}) collective-permute-start(bf16[2,384,384]{2,1,0:T(8,128)(2,1)S(1)} %get-tuple-element.215), channel_id=1, source_target_pairs={{0,4},{4,0},{8,12},{12,8},{16,20},{20,16},{24,28},{28,24},{1,5},{5... | collective-permute-start | bytes 1769480 | tf_op jit(solution)/shard_map/ppermute | solution.py:47
  63.7 14.8 %collective-permute-start.16 = (bf16[2,384,384]{2,1,0:T(8,128)(2,1)S(1)}, bf16[2,384,384]{2,1,0:T(8,128)(2,1)S(1)}, u32[]{:S(2)}, u32[]{:S(2)}) collective-permute-start(bf16[2,384,384]{2,1,0:T(8,128)(2,1)S(1)} %get-tuple-element.217), channel_id=1, source_target_pairs={{0,8},{4,12},{8,0},{12,4},{16,24},{20,28},{24,16},{28,20},{1,9},{5... | collective-permute-start | bytes 1769480 | tf_op jit(solution)/shard_map/ppermute | solution.py:47
  78.9 9.8 %collective-permute-start.21 = (bf16[2,192,384]{2,1,0:T(8,128)(2,1)S(1)}, bf16[2,192,384]{2,1,0:T(8,128)(2,1)S(1)}, u32[]{:S(2)}, u32[]{:S(2)}) collective-permute-start(bf16[2,192,384]{2,1,0:T(8,128)(2,1)S(1)} %get-tuple-element.231), channel_id=1, source_target_pairs={{0,8},{4,12},{8,0},{12,4},{16,24},{20,28},{24,16},{28,20},{1,9},{5... | collective-permute-start | bytes 884744 | tf_op jit(solution)/shard_map/ppermute | solution.py:47
  80.6 8.1 %collective-permute-start.22 = (bf16[2,192,384]{2,1,0:T(8,128)(2,1)S(1)}, bf16[2,192,384]{2,1,0:T(8,128)(2,1)S(1)}, u32[]{:S(2)}, u32[]{:S(2)}) collective-permute-start(bf16[2,192,384]{2,1,0:T(8,128)(2,1)S(1)} %get-tuple-element.233), channel_id=1, source_target_pairs={{0,4},{4,0},{8,12},{12,8},{16,20},{20,16},{24,28},{28,24},{1,5},{5... | collective-permute-start | bytes 884744 | tf_op jit(solution)/shard_map/ppermute | solution.py:47
  88.7 19.0 %collective-permute-start.28 = (bf16[256,768]{1,0:T(8,128)(2,1)S(1)}, bf16[256,768]{1,0:T(8,128)(2,1)S(1)}, u32[]{:S(2)}, u32[]{:S(2)}) collective-permute-start(bf16[256,768]{1,0:T(8,128)(2,1)S(1)} %get-tuple-element.256), channel_id=1, source_target_pairs={{0,1},{1,0},{2,3},{3,2},{4,5},{5,4},{6,7},{7,6},{8,9},{9,8},{10,11... | collective-permute-start | bytes 1179656 | tf_op jit(solution)/shard_map/ppermute | solution.py:38
  88.7 14.7 %collective-permute-start.27 = (bf16[2,192,384]{2,1,0:T(8,128)(2,1)S(1)}, bf16[2,192,384]{2,1,0:T(8,128)(2,1)S(1)}, u32[]{:S(2)}, u32[]{:S(2)}) collective-permute-start(bf16[2,192,384]{2,1,0:T(8,128)(2,1)S(1)} %get-tuple-element.255), channel_id=1, source_target_pairs={{0,8},{4,12},{8,0},{12,4},{16,24},{20,28},{24,16},{28,20},{1,9},{5... | collective-permute-start | bytes 884744 | tf_op jit(solution)/shard_map/ppermute | solution.py:47
  89.4 14.0 %collective-permute-start.23 = (bf16[2,96,384]{2,1,0:T(8,128)(2,1)S(1)}, bf16[2,96,384]{2,1,0:T(8,128)(2,1)S(1)}, u32[]{:S(2)}, u32[]{:S(2)}) collective-permute-start(bf16[2,96,384]{2,1,0:T(8,128)(2,1)S(1)} %get-tuple-element.249), channel_id=1, source_target_pairs={{0,16},{4,20},{8,24},{12,28},{16,0},{20,4},{24,8},{28,12},{1,17},{... | collective-permute-start | bytes 442376 | tf_op jit(solution)/shard_map/ppermute | solution.py:47
  92.1 11.4 %collective-permute-start.24 = (bf16[2,96,384]{2,1,0:T(8,128)(2,1)S(1)}, bf16[2,96,384]{2,1,0:T(8,128)(2,1)S(1)}, u32[]{:S(2)}, u32[]{:S(2)}) collective-permute-start(bf16[2,96,384]{2,1,0:T(8,128)(2,1)S(1)} %get-tuple-element.250), channel_id=1, source_target_pairs={{0,2},{2,0},{1,3},{3,1},{4,6},{6,4},{5,7},{7,5},{8,10},{10,8},{9,1... | collective-permute-start | bytes 442376 | tf_op jit(solution)/shard_map/ppermute | solution.py:34
  94.3 13.4 %collective-permute-start.25 = (bf16[2,96,384]{2,1,0:T(8,128)(2,1)S(1)}, bf16[2,96,384]{2,1,0:T(8,128)(2,1)S(1)}, u32[]{:S(2)}, u32[]{:S(2)}) collective-permute-start(bf16[2,96,384]{2,1,0:T(8,128)(2,1)S(1)} %get-tuple-element.251), channel_id=1, source_target_pairs={{0,18},{2,16},{4,22},{6,20},{8,26},{10,24},{12,30},{14,28},{16,2},... | collective-permute-start | bytes 442376 | tf_op jit(solution)/shard_map/ppermute | solution.py:567
  108.3 14.0 %collective-permute-start.32 = (bf16[528,384]{1,0:T(8,128)(2,1)S(1)}, bf16[528,384]{1,0:T(8,128)(2,1)S(1)}, u32[]{:S(2)}, u32[]{:S(2)}) collective-permute-start(bf16[528,384]{1,0:T(8,128)(2,1)S(1)} %get-tuple-element.274), channel_id=1, source_target_pairs={{0,2},{2,0},{1,3},{3,1},{4,6},{6,4},{5,7},{7,5},{8,10},{10,8},{9,1... | collective-permute-start | bytes 1216520 | tf_op jit(solution)/shard_map/ppermute | solution.py:34
  109.8 12.5 %collective-permute-start.29 = (bf16[2,2,96,384]{3,2,1,0:T(8,128)(2,1)S(1)}, bf16[2,2,96,384]{3,2,1,0:T(8,128)(2,1)S(1)}, u32[]{:S(2)}, u32[]{:S(2)}) collective-permute-start(bf16[2,2,96,384]{3,2,1,0:T(8,128)(2,1)S(1)} %shard_map.317.refs_0_), channel_id=1, source_target_pairs={{0,16},{4,20},{8,24},{12,28},{16,0},{20,4},{24,8},{28,12},{1,17},{... | collective-permute-start | bytes 884744 | tf_op jit(solution)/shard_map/ppermute | solution.py:47
  122.4 14.8 %collective-permute-start.33 = (bf16[2,192,384]{2,1,0:T(8,128)(2,1)S(1)}, bf16[2,192,384]{2,1,0:T(8,128)(2,1)S(1)}, u32[]{:S(2)}, u32[]{:S(2)}) collective-permute-start(bf16[2,192,384]{2,1,0:T(8,128)(2,1)S(1)} %get-tuple-element.297.refs_0_), channel_id=1, source_target_pairs={{0,8},{4,12},{8,0},{12,4},{16,24},{20,28},{24,16},{28,20},{1,9},{5... | collective-permute-start | bytes 884744 | tf_op jit(solution)/shard_map/ppermute | solution.py:47
  122.5 14.7 %collective-permute-start.34 = (bf16[2,192,384]{2,1,0:T(8,128)(2,1)S(1)}, bf16[2,192,384]{2,1,0:T(8,128)(2,1)S(1)}, u32[]{:S(2)}, u32[]{:S(2)}) collective-permute-start(bf16[2,192,384]{2,1,0:T(8,128)(2,1)S(1)} %get-tuple-element.299.refs_2_), channel_id=1, source_target_pairs={{0,4},{4,0},{8,12},{12,8},{16,20},{20,16},{24,28},{28,24},{1,5},{5... | collective-permute-start | bytes 884744 | tf_op jit(solution)/shard_map/ppermute | solution.py:47
  128.7 8.6 %collective-permute-start.37 = (bf16[2,48,384]{2,1,0:T(8,128)(2,1)S(1)}, bf16[2,48,384]{2,1,0:T(8,128)(2,1)S(1)}, u32[]{:S(2)}, u32[]{:S(2)}) collective-permute-start(bf16[2,48,384]{2,1,0:T(8,128)(2,1)S(1)} %get-tuple-element.295), channel_id=1, source_target_pairs={{0,18},{2,16},{4,22},{6,20},{8,26},{10,24},{12,30},{14,28},{16,2},... | collective-permute-start | bytes 221192 | tf_op jit(solution)/shard_map/ppermute | solution.py:567
  137.4 10.4 %collective-permute-start.39 = (bf16[384,384]{1,0:T(8,128)(2,1)S(1)}, bf16[384,384]{1,0:T(8,128)(2,1)S(1)}, u32[]{:S(2)}, u32[]{:S(2)}) collective-permute-start(bf16[384,384]{1,0:T(8,128)(2,1)S(1)} %get-tuple-element.340.refs_0_), channel_id=1, source_target_pairs={{0,4},{4,0},{8,12},{12,8},{16,20},{20,16},{24,28},{28,24},{1,5},{5... | collective-permute-start | bytes 884744 | tf_op jit(solution)/shard_map/ppermute | solution.py:47
  137.9 12.1 %collective-permute-start.40 = (bf16[384,384]{1,0:T(8,128)(2,1)S(1)}, bf16[384,384]{1,0:T(8,128)(2,1)S(1)}, u32[]{:S(2)}, u32[]{:S(2)}) collective-permute-start(bf16[384,384]{1,0:T(8,128)(2,1)S(1)} %get-tuple-element.336.refs_0_), channel_id=1, source_target_pairs={{0,8},{4,12},{8,0},{12,4},{16,24},{20,28},{24,16},{28,20},{1,9},{5... | collective-permute-start | bytes 884744 | tf_op jit(solution)/shard_map/ppermute | solution.py:47
  138.0 9.8 %collective-permute-start.41 = (bf16[208,384]{1,0:T(8,128)(2,1)S(1)}, bf16[208,384]{1,0:T(8,128)(2,1)S(1)}, u32[]{:S(2)}, u32[]{:S(2)}) collective-permute-start(bf16[208,384]{1,0:T(8,128)(2,1)S(1)} %shard_map.323.refs_0_), channel_id=1, source_target_pairs={{0,16},{4,20},{8,24},{12,28},{16,0},{20,4},{24,8},{28,12},{1,17},{... | collective-permute-start | bytes 479240 | tf_op jit(solution)/shard_map/ppermute | solution.py:47
  150.0 12.3 %collective-permute-start.42 = (bf16[384,384]{1,0:T(8,128)(2,1)S(1)}, bf16[384,384]{1,0:T(8,128)(2,1)S(1)}, u32[]{:S(2)}, u32[]{:S(2)}) collective-permute-start(bf16[384,384]{1,0:T(8,128)(2,1)S(1)} %get-tuple-element.342.refs_2_), channel_id=1, source_target_pairs={{0,4},{4,0},{8,12},{12,8},{16,20},{20,16},{24,28},{28,24},{1,5},{5... | collective-permute-start | bytes 884744 | tf_op jit(solution)/shard_map/ppermute | solution.py:47
  151.3 11.0 %collective-permute-start.43 = (bf16[384,384]{1,0:T(8,128)(2,1)S(1)}, bf16[384,384]{1,0:T(8,128)(2,1)S(1)}, u32[]{:S(2)}, u32[]{:S(2)}) collective-permute-start(bf16[384,384]{1,0:T(8,128)(2,1)S(1)} %get-tuple-element.338.refs_2_), channel_id=1, source_target_pairs={{0,8},{4,12},{8,0},{12,4},{16,24},{20,28},{24,16},{28,20},{1,9},{5... | collective-permute-start | bytes 884744 | tf_op jit(solution)/shard_map/ppermute | solution.py:47
  151.4 10.9 %collective-permute-start.44 = (bf16[208,384]{1,0:T(8,128)(2,1)S(1)}, bf16[208,384]{1,0:T(8,128)(2,1)S(1)}, u32[]{:S(2)}, u32[]{:S(2)}) collective-permute-start(bf16[208,384]{1,0:T(8,128)(2,1)S(1)} %get-tuple-element.322.refs_0_), channel_id=1, source_target_pairs={{0,8},{4,12},{8,0},{12,4},{16,24},{20,28},{24,16},{28,20},{1,9},{5... | collective-permute-start | bytes 479240 | tf_op jit(solution)/shard_map/ppermute | solution.py:47
  153.5 7.6 %collective-permute-start.45 = (bf16[192,384]{1,0:T(8,128)(2,1)S(1)}, bf16[192,384]{1,0:T(8,128)(2,1)S(1)}, u32[]{:S(2)}, u32[]{:S(2)}) collective-permute-start(bf16[192,384]{1,0:T(8,128)(2,1)S(1)} %get-tuple-element.324.refs_2_), channel_id=1, source_target_pairs={{0,4},{4,0},{8,12},{12,8},{16,20},{20,16},{24,28},{28,24},{1,5},{5... | collective-permute-start | bytes 442376 | tf_op jit(solution)/shard_map/ppermute | solution.py:47
  162.4 7.5 %collective-permute-start.46 = (bf16[400,384]{1,0:T(8,128)(2,1)S(1)}, bf16[400,384]{1,0:T(8,128)(2,1)S(1)}, u32[]{:S(2)}, u32[]{:S(2)}) collective-permute-start(bf16[400,384]{1,0:T(8,128)(2,1)S(1)} %get-tuple-element.328.refs_0_), channel_id=1, source_target_pairs={{0,4},{4,0},{8,12},{12,8},{16,20},{20,16},{24,28},{28,24},{1,5},{5... | collective-permute-start | bytes 921608 | tf_op jit(solution)/shard_map/ppermute | solution.py:47
  (24 other events, 223.2 us)

commit v5 on v4

--- a/solution.py
+++ b/solution.py
@@ -112,14 +112,16 @@
     )
     first = row == 0
     half, third = w_q.shape[0], w_q.shape[1] // 2
+    part = half // 2
     keeps, sends = [], []
     for ref, copy in zip(held_w, copies):
         copy.wait()
         low, high = ref[:, :third], ref[:, third:]
         keeps.append(jnp.where(first, low, high))
-        sends.append(jnp.where(first, high, low))
+        away = jnp.where(first, high, low)
+        sends.append(jnp.where(side == 0, away[:part], away[part:]))
     kept[:half] = jnp.concatenate(keeps, axis=1)
-    sent[:half] = jnp.concatenate(sends, axis=1)
+    sent[:part] = jnp.concatenate(sends, axis=1)
     for copy in copies[3:]:
         copy.wait()
     extra[...] = jnp.zeros_like(extra)
@@ -133,7 +135,7 @@
         extra[BIAS_UP + i : BIAS_UP + i + 1, :half] = b_u[:, i * half : (i + 1) * half]
     extra[BIAS_DOWN : BIAS_DOWN + 1, :half] = b_d
     kept[half:] = extra[...].astype(BF16)
-    sent[half:] = extra[...].astype(BF16)
+    sent[part:] = extra[...].astype(BF16)
 
 
 def normed_parts(values):
@@ -149,8 +151,7 @@
 
 
 def vector_of(kept, i):
-    half = kept.shape[0] - EXTRA
-    return kept[half:].astype(F32)[i : i + 1, :half]
+    return kept[kept.shape[0] - EXTRA :].astype(F32)[i : i + 1, : 2 * kept.shape[1] // 3]
 
 
 def wide_vector(kept, got, i):
@@ -170,19 +171,27 @@
     return (key >= begin) & (key <= query)
 
 
-def forward_kernel(lengths, own, own_far, col_own, col_far, w_kept, w_got, norm_hbm, q_hbm, k_hbm, v_hbm, o_out, lse,
+def weights_got(got, got_side):
+    part = got.shape[0] - EXTRA
+    first = lax.axis_index("dp") % 2 == 0
+    here, there = got[:part], got_side[:part]
+    return jnp.concatenate([jnp.where(first, here, there), jnp.where(first, there, here)], axis=0)
+
+
+def forward_kernel(lengths, own, own_far, col_own, col_far, w_kept, got, got_side, norm_hbm, q_hbm, k_hbm, v_hbm, o_out, lse,
                    norm_out, q_out, k_out, v_out, sems):
     own_rows, half = own.shape
+    w_got = weights_got(got, got_side)
     third = q_out.shape[1]
     col = lax.axis_index("col")
-    gain, shift = wide_vector(w_kept, w_got, GAIN_A), wide_vector(w_kept, w_got, SHIFT_A)
+    gain, shift = wide_vector(w_kept, got, GAIN_A), wide_vector(w_kept, got, SHIFT_A)
     bias = w_kept[half:].astype(F32)[BIAS_QKV : BIAS_QKV + 1]
     for ref, far, at in ((own, own_far, col), (col_own, col_far, 1 - col)):
         where = half_rows(at, own_rows)
         unit, _ = normed_parts(both_halves(ref, far))
         values = (unit * gain + shift).astype(BF16)
         norm_out[where] = values
-        total = dot(values[:, :half], w_kept[:half]) + dot(values[:, half:], w_got[:half])
+        total = dot(values[:, :half], w_kept[:half]) + dot(values[:, half:], w_got)
         total = (total + bias).astype(BF16)
         q_out[where] = total[:, :third]
         k_out[where] = total[:, third : 2 * third]
@@ -353,7 +362,7 @@
     sums[1:2] = jnp.sum(grads[:, :half], axis=0, keepdims=True)
 
 
-def backward_kernel(bit_first, bit_second, lengths, own, other, w_mine, w_other, q_hbm, k_hbm, v_hbm, o_ref, lse, normed_hbm, w_kept, w_got,
+def backward_kernel(bit_first, bit_second, lengths, own, other, w_mine, w_other, q_hbm, k_hbm, v_hbm, o_ref, lse, normed_hbm, w_kept, got, got_side,
                     first_keep, first_send, second_keep, second_send, keep, send, sums, datt, out, acc_k, acc_v, do_ref,
                     q_ref, k_ref, v_ref, normed, sems):
     copies = start_copies(
@@ -406,9 +415,11 @@
     last = jnp.concatenate([weights[:, 2 * third :], grad_out], axis=1)
     split_rows(last.reshape(2, half, 2 * third), second_keep, second_send, bit_second)
 
+    w_got = weights_got(got, got_side)
+
     def total_of(rows):
         values = out[rows]
-        return jnp.concatenate([dot_nt(values, w_kept[:half]), dot_nt(values, w_got[:half])], axis=1)
+        return jnp.concatenate([dot_nt(values, w_kept[:half]), dot_nt(values, w_got)], axis=1)
 
     split_tokens(total_of, keep, send, own_rows, col)
     sums[...] = jnp.zeros_like(sums)
@@ -706,9 +717,24 @@
     right[...] = last.T if flip else last
 
 
-def first_end_kernel(bit, mine, got, left, right, small):
+def first_end_kernel(bit, mine, got, left, right, *refs):
+    outs, held, sems = refs[:9], refs[9:18], refs[18]
+    small = extra_sum(mine, got)
+    half = small.shape[1]
+    third = half // 2
+    lines = [
+        small[4:5, :third],
+        small[4:5, third:],
+        small[5:6],
+        jnp.concatenate([small[6:7], small[7:8]], axis=1),
+        small[8:9],
+    ] + [small[i : i + 1] for i in range(4)]
+    for ref, line in zip(held, lines):
+        ref[...] = line.reshape(line.shape[1])
+    copies = start_copies(list(zip(held, outs)), sems)
     attention_end(bit, False, mine, got, left, right)
-    small[...] = extra_sum(mine, got)
+    for copy in copies:
+        copy.wait()
 
 
 def second_end_kernel(bit, mine, got, left, right):
@@ -769,7 +795,7 @@
         start_kernel,
         (
             shape((half + EXTRA, 3 * third), BF16),
-            shape((half + EXTRA, 3 * third), BF16),
+            shape((half // 2 + EXTRA, 3 * third), BF16),
             shape((w_out.shape[0] // 2, half), BF16),
             shape((half // 2, units), BF16),
             shape((units // 2, half), BF16),
@@ -780,18 +806,22 @@
         + [block, block, block, pltpu.VMEM((EXTRA, 3 * third), F32), pltpu.SemaphoreType.DMA((15,))],
         vmem=VMEM_START,
     )
-    tokens_far, sent, sent_out = hold(tokens_far, sent, sent_out)
+    tokens_col = from_col(tokens)
+    tokens_far, tokens_col, sent, sent_out, sent_up = hold(
+        tokens_far, tokens_col, sent, sent_out, sent_up
+    )
     w_got = from_row(sent)
+    w_side = from_dp(w_got, 0)
     out_got = from_row(sent_out)
-    tokens_col = from_col(tokens)
+    up_got = from_row(sent_up)
     tokens_far_col = from_col(tokens_far)
-    top_col = from_col(out_grad)
-    tokens_far, tokens_col, tokens_far_col, w_got, out_got, sent_up, sent_down = hold(
-        tokens_far, tokens_col, tokens_far_col, w_got, out_got, sent_up, sent_down
-    )
-    up_got = from_row(sent_up)
+    tokens_far, tokens_far_col, w_got, w_side, out_got, up_got, sent_down, out_grad_col = hold(
+        tokens_far, tokens_far_col, w_got, w_side, out_got, up_got, sent_down, out_grad
+    )
+    top_col = from_col(out_grad_col)
     down_got = from_row(sent_down)
     out_side = from_dp(out_got, 0)
+    up_side = from_dp(up_got, 0)
     every_token = (tokens, tokens_far, tokens_col, tokens_far_col)
 
     like = shape((rows, third), BF16)
@@ -802,6 +832,7 @@
         *every_token,
         w_kept,
         w_got,
+        w_side,
         smem=(0,),
         hbm_out=range(4),
         scratch=[pltpu.VMEM((rows, width), BF16)]
@@ -809,8 +840,7 @@
         + [pltpu.SemaphoreType.DMA((4,))],
     )
     mixed_far = from_row(mixed)
-    mixed_gate, up_got = hold(mixed, up_got)
-    up_side = from_dp(up_got, 0)
+    mixed_gate = mixed
     mixed_far, out_side, up_side, down_got, out_grad_send = hold(
         mixed_far, out_side, up_side, down_got, out_grad
     )
@@ -880,7 +910,7 @@
         lambda *refs: backward_kernel(bits[0], turned[0], *refs),
         (split_pair,) * 4 + (tall, tall_low, shape((8, width), F32)),
         seq_lengths, datt, datt_col, w_out, w_out_far, query, key, value, mixed, lse,
-        normed_all, w_kept, w_got,
+        normed_all, w_kept, w_got, w_side,
         scratch=[
             pltpu.VMEM((rows, width), BF16),
             pltpu.VMEM((rows, 3 * third), BF16),
@@ -897,8 +927,6 @@
     attention = Pair(first_keep, first_send, second_keep, second_send, bits, turned, False)
     pairs = [feed, attention]
     feed.step()
-    (got,) = arrived(pairs, got)
-
     mine, raised, out, stats, unit_attn, inverse_attn = call(
         first_back_kernel,
         (
@@ -911,16 +939,17 @@
         ),
         keep, got, raised_keep, raised_got, tokens, tokens_far, w_kept, w_got,
     )
+    (out,) = arrived(pairs, out)
     got = from_row(out)
     feed.step()
     attention.step()
-    (got,) = arrived(pairs, got)
 
     output, input_grad, halves = call(
         last_kernel,
         (shape((own_rows, half), BF16), shape((own_rows, half), BF16), pair_sums),
         mine, raised, got, stats, unit_attn, inverse_attn, w_kept, middle, grad_middle, mid_sums,
     )
+    (halves,) = arrived(pairs, halves)
     halves_col = from_col(halves)
     feed.step()
     attention.step()
@@ -935,11 +964,14 @@
     wide = w_query.shape[1]
     outs = (shape((half, wide), F32),) * 2
     mine_a, got_a, mine_b, got_b = attention.state
-    grad_query, grad_key, small = call(
+    sizes = (third, third, half, 2 * half, half, half, half, half, half)
+    grad_query, grad_key, *vector_grads = call(
         lambda *refs: first_end_kernel(bits[0], *refs),
-        outs + (shape((EXTRA, half), F32),),
+        outs + tuple(shape((size,), F32) for size in sizes),
         mine_a,
         got_a,
+        hbm_out=range(2, 11),
+        scratch=[pltpu.VMEM((size,), F32) for size in sizes] + [pltpu.SemaphoreType.DMA((9,))],
     )
     grad_value, grad_out = call(
         lambda *refs: second_end_kernel(turned[0], *refs), outs, mine_b, got_b
@@ -976,15 +1008,7 @@
         grad_out,
         grad_up,
         grad_down,
-        small[4, :third],
-        small[4, third:],
-        small[5],
-        small[6:8].reshape(-1),
-        small[8],
-        small[0],
-        small[1],
-        small[2],
-        small[3],
+        *vector_grads,
     )
 
 

time: 174 us -> 169 us (0.971)
  waiting for transfers between devices: 88.2 us -> 82.4 us
  starting transfers between devices: 49.3 us -> 51.4 us
  local copies, waits for them, and re-layouts: 3.42 us -> 1.56 us
    ppermute x25 -> x26, starting transfers between devices: 28.6 us -> 35 us  [from_dp(): return lax.ppermute(values, 'dp', dp_pairs(bit))]
    ppermute x2, waiting for transfers between devices: 9.49 us -> 5.06 us  [from_both(): return lax.ppermute(values, ('dp', 'row'), pairs)]
    ppermute x11, starting transfers between devices: 14.9 us -> 12.3 us  [from_row(): return lax.ppermute(values, 'row', SWAP)]
    ppermute x25 -> x26, waiting for transfers between devices: 48.6 us -> 49 us  [from_dp(): return lax.ppermute(values, 'dp', dp_pairs(bit))]
  transfers between devices with their start and end apart: 48 -> 49, of which waited for: 26 -> 25; matrix products, arithmetic and copies ran while one was open for 0% -> 0% of each run, Pallas kernels for 14% -> 14%
where the time goes in v5:
time: 169 us
  waiting for transfers between devices  82.4 us (49%)
  starting transfers between devices  51.4 us (30%)
  Pallas kernels  32.7 us (19%)
    ppermute x26, waiting for transfers between devices, from_dp(): return lax.ppermute(values, 'dp', dp_pairs(bit))  49 us
    ppermute x26, starting transfers between devices, from_dp(): return lax.ppermute(values, 'dp', dp_pairs(bit))  35 us
    pallas_call x23, Pallas kernels, call(): pl.pallas_call(kernel, out_shape=out_shape, in_specs=[pl.BlockSpec(memory...  28.7 us
    ppermute x11, waiting for transfers between devices, from_row(): return lax.ppermute(values, 'row', SWAP)  28.1 us
    ppermute x11, starting transfers between devices, from_row(): return lax.ppermute(values, 'row', SWAP)  12.3 us
    ppermute x2, waiting for transfers between devices, from_both(): return lax.ppermute(values, ('dp', 'row'), pairs)  5.06 us
    pallas_call x2, Pallas kernels, end_call(): pl.pallas_call(kernel, grid=grid, out_shape=out_shape, in_specs=[whole] *...  4.01 us
  transfers between devices with their start and end apart: 49, of which 25 were waited for; matrix products, arithmetic and copies ran while one was open for 0% of the time, Pallas kernels for 14%

profile of v5, /device:TPU:0, one launch (start us, length us, event | category | flops | bytes accessed | tf_op | source)
XLA Modules:
  0.0 169.1 jit_solution(16910216028295399343)
XLA Ops:
  1.2 2.6 %collective-permute-start = (bf16[256,384]{1,0:T(8,128)(2,1)}, bf16[256,384]{1,0:T(8,128)(2,1)S(1)}, u32[]{:S(2)}, u32[]{:S(2)}) collective-permute-start(bf16[256,384]{1,0:T(8,128)(2,1)} %own.5), channel_id=1, source_target_pairs={{0,2},{2,0},{1,3},{3,1},{4,6},{6,4},{5,7},{7,5},{8,10},{10,8},{9,1... | collective-permute-start | bytes 589832 | tf_op jit(solution)/shard_map/ppermute | solution.py:34
  3.8 2.9 %shard_map.305 = (bf16[400,576]{1,0:T(8,128)(2,1)}, bf16[208,576]{1,0:T(8,128)(2,1)}, bf16[192,384]{1,0:T(8,128)(2,1)}, bf16[192,768]{1,0:T(8,128)(2,1)}, bf16[384,384]{1,0:T(8,128)(2,1)}) custom-call(bf16[384]{0:T(512)(128)(2,1)} %refs_0_.3, bf16[384]{0:T(512)(128)(2,1)} %refs_1_.2, bf16[384]{0:T(512)(128)(2,1)} %refs_2_.1, bf16[384]{0:T(512)(128)(2,1)} %refs_3_.2, ...), custom_call_target="tpu_custom_call" | custom-call | tf_op jit(solution)/shard_map/pallas_call | solution.py:69
  6.7 2.8 %collective-permute-done.own_far = bf16[256,384]{1,0:T(8,128)(2,1)S(1)} collective-permute-done((bf16[256,384]{1,0:T(8,128)(2,1)}, bf16[256,384]{1,0:T(8,128)(2,1)S(1)}, u32[]{:S(2)}, u32[]{:S(2)}) %collective-permute-start) | collective-permute-done | bytes 196640 | tf_op jit(solution)/shard_map/ppermute | solution.py:34
  9.5 1.8 %collective-permute-start.3 = (bf16[208,576]{1,0:T(8,128)(2,1)}, bf16[208,576]{1,0:T(8,128)(2,1)S(1)}, u32[]{:S(2)}, u32[]{:S(2)}) collective-permute-start(bf16[208,576]{1,0:T(8,128)(2,1)} %get-tuple-element.194), channel_id=1, source_target_pairs={{0,2},{2,0},{1,3},{3,1},{4,6},{6,4},{5,7},{7,5},{8,10},{10,8},{9,1... | collective-permute-start | bytes 718856 | tf_op jit(solution)/shard_map/ppermute | solution.py:34
  11.5 7.5 %collective-permute-done.3.got.sent.refs_12_ = bf16[208,576]{1,0:T(8,128)(2,1)S(1)} collective-permute-done((bf16[208,576]{1,0:T(8,128)(2,1)}, bf16[208,576]{1,0:T(8,128)(2,1)S(1)}, u32[]{:S(2)}, u32[]{:S(2)}) %collective-permute-start.3) | collective-permute-done | bytes 239648 | tf_op jit(solution)/shard_map/ppermute | solution.py:34
  22.3 5.1 %collective-permute-done.5.got = bf16[192,384]{1,0:T(8,128)(2,1)S(1)} collective-permute-done((bf16[192,384]{1,0:T(8,128)(2,1)}, bf16[192,384]{1,0:T(8,128)(2,1)S(1)}, u32[]{:S(2)}, u32[]{:S(2)}) %collective-permute-start.5) | collective-permute-done | bytes 147488 | tf_op jit(solution)/shard_map/ppermute | solution.py:34
  31.5 4.4 %shard_map.306 = (bf16[512,768]{1,0:T(8,128)(2,1)S(1)}, bf16[512,192]{1,0:T(8,128)(2,1)S(1)}, bf16[512,192]{1,0:T(8,128)(2,1)S(1)}, bf16[512,192]{1,0:T(8,128)(2...) custom-call(s32[1,2]{1,0:T(1,128)S(1)} %copy-done.7, bf16[256,384]{1,0:T(8,128)(2,1)S(1)} %copy-done.5, ...), custom_call_target="tpu_custom_call" | custom-call | tf_op jit(solution)/shard_map/pallas_call | solution.py:69
  37.0 4.7 %collective-permute-done.8.got_side = bf16[192,384]{1,0:T(8,128)(2,1)S(1)} collective-permute-done((bf16[192,384]{1,0:T(8,128)(2,1)S(1)}, bf16[192,384]{1,0:T(8,128)(2,1)S(1)}, u32[]{:S(2)}, u32[]{:S(2)}) %collective-permute-start.8) | collective-permute-done | bytes 147488 | tf_op jit(solution)/shard_map/ppermute | solution.py:47
  48.7 2.1 %collective-permute-done.12.refs_2_.top_far = bf16[256,384]{1,0:T(8,128)(2,1)S(1)} collective-permute-done((bf16[256,384]{1,0:T(8,128)(2,1)S(1)}, bf16[256,384]{1,0:T(8,128)(2,1)S(1)}, u32[]{:S(2)}, u32[]{:S(2)}) %collective-permute-start.12) | collective-permute-done | bytes 196640 | tf_op jit(solution)/shard_map/ppermute | solution.py:34
  51.3 2.2 %collective-permute-done.15.refs_10_ = bf16[384,384]{1,0:T(8,128)(2,1)S(1)} collective-permute-done((bf16[384,384]{1,0:T(8,128)(2,1)S(1)}, bf16[384,384]{1,0:T(8,128)(2,1)S(1)}, u32[]{:S(2)}, u32[]{:S(2)}) %collective-permute-start.15) | collective-permute-done | bytes 294944 | tf_op jit(solution)/shard_map/ppermute | solution.py:47
  53.5 4.2 %shard_map.310 = (bf16[2,384,384]{2,1,0:T(8,128)(2,1)S(1)}, bf16[2,384,384]{2,1,0:T(8,128)(2,1)S(1)}, bf16[2,384,384]{2,1,0:T(8,128)(2,1)S(1)}, bf16[2,384,384]{...) custom-call(s32[1,2]{1,0:T(1,128)S(1)} %copy-done.7, ...), custom_call_target="tpu_custom_call" | custom-call | tf_op jit(solution)/shard_map/pallas_call | solution.py:69
  63.7 7.1 %collective-permute-done.19.total_far = bf16[256,768]{1,0:T(8,128)(2,1)S(1)} collective-permute-done((bf16[256,768]{1,0:T(8,128)(2,1)S(1)}, bf16[256,768]{1,0:T(8,128)(2,1)S(1)}, u32[]{:S(2)}, u32[]{:S(2)}) %collective-permute-start.19) | collective-permute-done | bytes 393248 | tf_op jit(solution)/shard_map/ppermute | solution.py:34
  72.1 3.9 %collective-permute-done.16.refs_1_ = bf16[2,384,384]{2,1,0:T(8,128)(2,1)S(1)} collective-permute-done((bf16[2,384,384]{2,1,0:T(8,128)(2,1)S(1)}, bf16[2,384,384]{2,1,0:T(8,128)(2,1)S(1)}, u32[]{:S(2)}, u32[]{:S(2)}) %collective-permute-start.16) | collective-permute-done | bytes 589856 | tf_op jit(solution)/shard_map/ppermute | solution.py:47
  79.7 6.1 %shard_map.314 = (bf16[2,192,384]{2,1,0:T(8,128)(2,1)S(1)}, bf16[2,192,384]{2,1,0:T(8,128)(2,1)S(1)}, bf16[2,192,384]{2,1,0:T(8,128)(2,1)S(1)}, bf16[2,192,384]{...) custom-call(s32[1,2]{1,0:T(1,128)S(1)} %copy-done.7, ...), custom_call_target="tpu_custom_call" | custom-call | tf_op jit(solution)/shard_map/pallas_call | solution.py:69
  87.9 2.7 %collective-permute-start.25 = (bf16[2,96,384]{2,1,0:T(8,128)(2,1)S(1)}, bf16[2,96,384]{2,1,0:T(8,128)(2,1)S(1)}, u32[]{:S(2)}, u32[]{:S(2)}) collective-permute-start(bf16[2,96,384]{2,1,0:T(8,128)(2,1)S(1)} %get-tuple-element.264), channel_id=1, source_target_pairs={{0,16},{4,20},{8,24},{12,28},{16,0},{20,4},{24,8},{28,12},{1,17},{... | collective-permute-start | bytes 442376 | tf_op jit(solution)/shard_map/ppermute | solution.py:47
  92.9 2.8 %collective-permute-done.28.refs_1_ = bf16[2,192,384]{2,1,0:T(8,128)(2,1)S(1)} collective-permute-done((bf16[2,192,384]{2,1,0:T(8,128)(2,1)S(1)}, bf16[2,192,384]{2,1,0:T(8,128)(2,1)S(1)}, u32[]{:S(2)}, u32[]{:S(2)}) %collective-permute-start.28) | collective-permute-done | bytes 294944 | tf_op jit(solution)/shard_map/ppermute | solution.py:47
  95.7 6.9 %collective-permute-done.29.refs_3_ = bf16[2,192,384]{2,1,0:T(8,128)(2,1)S(1)} collective-permute-done((bf16[2,192,384]{2,1,0:T(8,128)(2,1)S(1)}, bf16[2,192,384]{2,1,0:T(8,128)(2,1)S(1)}, u32[]{:S(2)}, u32[]{:S(2)}) %collective-permute-start.29) | collective-permute-done | bytes 294944 | tf_op jit(solution)/shard_map/ppermute | solution.py:47
  103.5 2.2 %collective-permute-start.31 = (bf16[2,2,96,384]{3,2,1,0:T(8,128)(2,1)S(1)}, bf16[2,2,96,384]{3,2,1,0:T(8,128)(2,1)S(1)}, u32[]{:S(2)}, u32[]{:S(2)}) collective-permute-start(bf16[2,2,96,384]{3,2,1,0:T(8,128)(2,1)S(1)} %shard_map.318.refs_0_), channel_id=1, source_target_pairs={{0,16},{4,20},{8,24},{12,28},{16,0},{20,4},{24,8},{28,12},{1,17},{... | collective-permute-start | bytes 884744 | tf_op jit(solution)/shard_map/ppermute | solution.py:47
  105.9 4.1 %collective-permute-start.32 = (bf16[2,96,384]{2,1,0:T(8,128)(2,1)S(1)}, bf16[2,96,384]{2,1,0:T(8,128)(2,1)S(1)}, u32[]{:S(2)}, u32[]{:S(2)}) collective-permute-start(bf16[2,96,384]{2,1,0:T(8,128)(2,1)S(1)} %get-tuple-element.290), channel_id=1, source_target_pairs={{0,8},{4,12},{8,0},{12,4},{16,24},{20,28},{24,16},{28,20},{1,9},{5... | collective-permute-start | bytes 442376 | tf_op jit(solution)/shard_map/ppermute | solution.py:47
  111.2 2.2 %collective-permute-done.30.got = bf16[528,384]{1,0:T(8,128)(2,1)S(1)} collective-permute-done((bf16[528,384]{1,0:T(8,128)(2,1)S(1)}, bf16[528,384]{1,0:T(8,128)(2,1)S(1)}, u32[]{:S(2)}, u32[]{:S(2)}) %collective-permute-start.30) | collective-permute-done | bytes 405536 | tf_op jit(solution)/shard_map/ppermute | solution.py:34
  115.2 3.6 %collective-permute-done.31.refs_1_ = bf16[2,2,96,384]{3,2,1,0:T(8,128)(2,1)S(1)} collective-permute-done((bf16[2,2,96,384]{3,2,1,0:T(8,128)(2,1)S(1)}, bf16[2,2,96,384]{3,2,1,0:T(8,128)(2,1)S(1)}, u32[]{:S(2)}, u32[]{:S(2)}) %collective-permute-start.31) | collective-permute-done | bytes 294944 | tf_op jit(solution)/shard_map/ppermute | solution.py:47
  120.4 3.4 %collective-permute-start.36 = (bf16[2,48,384]{2,1,0:T(8,128)(2,1)S(1)}, bf16[2,48,384]{2,1,0:T(8,128)(2,1)S(1)}, u32[]{:S(2)}, u32[]{:S(2)}) collective-permute-start(bf16[2,48,384]{2,1,0:T(8,128)(2,1)S(1)} %get-tuple-element.303), channel_id=1, source_target_pairs={{0,16},{4,20},{8,24},{12,28},{16,0},{20,4},{24,8},{28,12},{1,17},{... | collective-permute-start | bytes 221192 | tf_op jit(solution)/shard_map/ppermute | solution.py:47
  125.4 2.5 %collective-permute-done.36.from_dp_ref = bf16[2,48,384]{2,1,0:T(8,128)(2,1)S(1)} collective-permute-done((bf16[2,48,384]{2,1,0:T(8,128)(2,1)S(1)}, bf16[2,48,384]{2,1,0:T(8,128)(2,1)S(1)}, u32[]{:S(2)}, u32[]{:S(2)}) %collective-permute-start.36) | collective-permute-done | bytes 73760 | tf_op jit(solution)/shard_map/ppermute | solution.py:47
  128.2 5.1 %collective-permute-done.38.from_both_ref = bf16[2,48,384]{2,1,0:T(8,128)(2,1)S(1)} collective-permute-done((bf16[2,48,384]{2,1,0:T(8,128)(2,1)S(1)}, bf16[2,48,384]{2,1,0:T(8,128)(2,1)S(1)}, u32[]{:S(2)}, u32[]{:S(2)}) %collective-permute-start.38) | collective-permute-done | bytes 73760 | tf_op jit(solution)/shard_map/ppermute | solution.py:578
  136.2 7.8 %collective-permute-done.42.refs_1_ = bf16[208,384]{1,0:T(8,128)(2,1)S(1)} collective-permute-done((bf16[208,384]{1,0:T(8,128)(2,1)S(1)}, bf16[208,384]{1,0:T(8,128)(2,1)S(1)}, u32[]{:S(2)}, u32[]{:S(2)}) %collective-permute-start.42) | collective-permute-done | bytes 159776 | tf_op jit(solution)/shard_map/ppermute | solution.py:47
  144.0 2.2 %collective-permute-done.41.refs_1_ = bf16[384,384]{1,0:T(8,128)(2,1)S(1)} collective-permute-done((bf16[384,384]{1,0:T(8,128)(2,1)S(1)}, bf16[384,384]{1,0:T(8,128)(2,1)S(1)}, u32[]{:S(2)}, u32[]{:S(2)}) %collective-permute-start.41) | collective-permute-done | bytes 294944 | tf_op jit(solution)/shard_map/ppermute | solution.py:47
  147.2 2.1 %collective-permute-start.45 = (bf16[208,384]{1,0:T(8,128)(2,1)S(1)}, bf16[208,384]{1,0:T(8,128)(2,1)S(1)}, u32[]{:S(2)}, u32[]{:S(2)}) collective-permute-start(bf16[208,384]{1,0:T(8,128)(2,1)S(1)} %get-tuple-element.332.refs_0_), channel_id=1, source_target_pairs={{0,8},{4,12},{8,0},{12,4},{16,24},{20,28},{24,16},{28,20},{1,9},{5... | collective-permute-start | bytes 479240 | tf_op jit(solution)/shard_map/ppermute | solution.py:47
  150.3 6.8 %collective-permute-done.46.refs_3_ = bf16[192,384]{1,0:T(8,128)(2,1)S(1)} collective-permute-done((bf16[192,384]{1,0:T(8,128)(2,1)S(1)}, bf16[192,384]{1,0:T(8,128)(2,1)S(1)}, u32[]{:S(2)}, u32[]{:S(2)}) %collective-permute-start.46) | collective-permute-done | bytes 147488 | tf_op jit(solution)/shard_map/ppermute | solution.py:47
  159.6 2.0 %shard_map.328 = f32[384,1536]{1,0:T(8,128)} custom-call(bf16[384,384]{1,0:T(8,128)(2,1)S(1)} %get-tuple-element.346.refs_0_, bf16[384,384]{1,0:T(8,128)(2,1)S(1)} %collective-permute-done.41.refs_1_, bf16[384,384]{1,0:T(8,128)(2,1)S(1)} %get-tuple-element.348.refs_2_, bf16[384,384]{1,0:T(8,128)(2,1)S(1)} %collective-permute-done.44.refs_3_), custom_call_target="tpu_custom_call" | custom-call | tf_op jit(solution)/shard_map/pallas_call | solution.py:746
  161.6 2.0 %shard_map.329 = f32[1536,384]{1,0:T(8,128)} custom-call(bf16[384,384]{1,0:T(8,128)(2,1)S(1)} %get-tuple-element.350.refs_0_, bf16[384,384]{1,0:T(8,128)(2,1)S(1)} %collective-permute-done.40.refs_1_, bf16[384,384]{1,0:T(8,128)(2,1)S(1)} %get-tuple-element.352.refs_2_, bf16[384,384]{1,0:T(8,128)(2,1)S(1)} %collective-permute-done.43.refs_3_), custom_call_target="tpu_custom_call" | custom-call | tf_op jit(solution)/shard_map/pallas_call | solution.py:746
  163.6 2.4 %collective-permute-done.48.refs_1_ = bf16[384,384]{1,0:T(8,128)(2,1)S(1)} collective-permute-done((bf16[384,384]{1,0:T(8,128)(2,1)S(1)}, bf16[384,384]{1,0:T(8,128)(2,1)S(1)}, u32[]{:S(2)}, u32[]{:S(2)}) %collective-permute-start.48) | collective-permute-done | bytes 294944 | tf_op jit(solution)/shard_map/ppermute | solution.py:47
  166.1 1.8 %shard_map.326 = (f32[384,384]{1,0:T(8,128)}, f32[384,384]{1,0:T(8,128)}, f32[192]{0:T(256)}, f32[192]{0:T(256)}, f32[384]{0:T(512)}, /*index=5*/f32[768]{0:T(10...) custom-call(bf16[400,384]{1,0:T(8,128)(2,1)S(1)} %get-tuple-element.338.refs_0_, ...), custom_call_target="tpu_custom_call" | custom-call | tf_op jit(solution)/shard_map/pallas_call | solution.py:69
  (108 shorter events, 48.3 us)
Async XLA Ops:
  1.2 8.3 %collective-permute-start = (bf16[256,384]{1,0:T(8,128)(2,1)}, bf16[256,384]{1,0:T(8,128)(2,1)S(1)}, u32[]{:S(2)}, u32[]{:S(2)}) collective-permute-start(bf16[256,384]{1,0:T(8,128)(2,1)} %own.5), channel_id=1, source_target_pairs={{0,2},{2,0},{1,3},{3,1},{4,6},{6,4},{5,7},{7,5},{8,10},{10,8},{9,1... | collective-permute-start | bytes 589832 | tf_op jit(solution)/shard_map/ppermute | solution.py:34
  9.5 9.5 %collective-permute-start.3 = (bf16[208,576]{1,0:T(8,128)(2,1)}, bf16[208,576]{1,0:T(8,128)(2,1)S(1)}, u32[]{:S(2)}, u32[]{:S(2)}) collective-permute-start(bf16[208,576]{1,0:T(8,128)(2,1)} %get-tuple-element.194), channel_id=1, source_target_pairs={{0,2},{2,0},{1,3},{3,1},{4,6},{6,4},{5,7},{7,5},{8,10},{10,8},{9,1... | collective-permute-start | bytes 718856 | tf_op jit(solution)/shard_map/ppermute | solution.py:34
  11.3 16.1 %collective-permute-start.6 = (bf16[192,768]{1,0:T(8,128)(2,1)}, bf16[192,768]{1,0:T(8,128)(2,1)S(1)}, u32[]{:S(2)}, u32[]{:S(2)}) collective-permute-start(bf16[192,768]{1,0:T(8,128)(2,1)} %get-tuple-element.196), channel_id=1, source_target_pairs={{0,2},{2,0},{1,3},{3,1},{4,6},{6,4},{5,7},{7,5},{8,10},{10,8},{9,1... | collective-permute-start | bytes 884744 | tf_op jit(solution)/shard_map/ppermute | solution.py:34
  19.0 8.4 %collective-permute-start.4 = (bf16[208,576]{1,0:T(8,128)(2,1)S(1)}, bf16[208,576]{1,0:T(8,128)(2,1)S(1)}, u32[]{:S(2)}, u32[]{:S(2)}) collective-permute-start(bf16[208,576]{1,0:T(8,128)(2,1)S(1)} %collective-permute-done.3.got.sent.refs_12_), channel_id=1, source_target_pairs={{0,4},{4,0},{8,12},{12,8},{16,20},{20,16},{24,28},{28,24},{1,5},{5... | collective-permute-start | bytes 718856 | tf_op jit(solution)/shard_map/ppermute | solution.py:47
  27.4 15.3 %collective-permute-start.10 = (bf16[384,384]{1,0:T(8,128)(2,1)}, bf16[384,384]{1,0:T(8,128)(2,1)S(1)}, u32[]{:S(2)}, u32[]{:S(2)}) collective-permute-start(bf16[384,384]{1,0:T(8,128)(2,1)} %get-tuple-element.207), channel_id=1, source_target_pairs={{0,2},{2,0},{1,3},{3,1},{4,6},{6,4},{5,7},{7,5},{8,10},{10,8},{9,1... | collective-permute-start | bytes 884744 | tf_op jit(solution)/shard_map/ppermute | solution.py:34
  29.0 13.7 %collective-permute-start.9 = (bf16[192,768]{1,0:T(8,128)(2,1)S(1)}, bf16[192,768]{1,0:T(8,128)(2,1)S(1)}, u32[]{:S(2)}, u32[]{:S(2)}) collective-permute-start(bf16[192,768]{1,0:T(8,128)(2,1)S(1)} %collective-permute-done.6.got), channel_id=1, source_target_pairs={{0,4},{4,0},{8,12},{12,8},{16,20},{20,16},{24,28},{28,24},{1,5},{5... | collective-permute-start | bytes 884744 | tf_op jit(solution)/shard_map/ppermute | solution.py:47
  43.5 7.3 %collective-permute-start.12 = (bf16[256,384]{1,0:T(8,128)(2,1)S(1)}, bf16[256,384]{1,0:T(8,128)(2,1)S(1)}, u32[]{:S(2)}, u32[]{:S(2)}) collective-permute-start(bf16[256,384]{1,0:T(8,128)(2,1)S(1)} %copy-done.6), channel_id=1, source_target_pairs={{0,2},{2,0},{1,3},{3,1},{4,6},{6,4},{5,7},{7,5},{8,10},{10,8},{9,1... | collective-permute-start | bytes 589832 | tf_op jit(solution)/shard_map/ppermute | solution.py:34
  44.4 9.1 %collective-permute-start.15 = (bf16[384,384]{1,0:T(8,128)(2,1)S(1)}, bf16[384,384]{1,0:T(8,128)(2,1)S(1)}, u32[]{:S(2)}, u32[]{:S(2)}) collective-permute-start(bf16[384,384]{1,0:T(8,128)(2,1)S(1)} %collective-permute-done.10.refs_9_), channel_id=1, source_target_pairs={{0,8},{4,12},{8,0},{12,4},{16,24},{20,28},{24,16},{28,20},{1,9},{5... | collective-permute-start | bytes 884744 | tf_op jit(solution)/shard_map/ppermute | solution.py:47
  59.6 11.2 %collective-permute-start.19 = (bf16[256,768]{1,0:T(8,128)(2,1)S(1)}, bf16[256,768]{1,0:T(8,128)(2,1)S(1)}, u32[]{:S(2)}, u32[]{:S(2)}) collective-permute-start(bf16[256,768]{1,0:T(8,128)(2,1)S(1)} %add_convert_fusion.total), channel_id=1, source_target_pairs={{0,2},{2,0},{1,3},{3,1},{4,6},{6,4},{5,7},{7,5},{8,10},{10,8},{9,1... | collective-permute-start | bytes 1179656 | tf_op jit(solution)/shard_map/ppermute | solution.py:34
  60.9 15.1 %collective-permute-start.16 = (bf16[2,384,384]{2,1,0:T(8,128)(2,1)S(1)}, bf16[2,384,384]{2,1,0:T(8,128)(2,1)S(1)}, u32[]{:S(2)}, u32[]{:S(2)}) collective-permute-start(bf16[2,384,384]{2,1,0:T(8,128)(2,1)S(1)} %get-tuple-element.225), channel_id=1, source_target_pairs={{0,4},{4,0},{8,12},{12,8},{16,20},{20,16},{24,28},{28,24},{1,5},{5... | collective-permute-start | bytes 1769480 | tf_op jit(solution)/shard_map/ppermute | solution.py:47
  62.2 14.8 %collective-permute-start.17 = (bf16[2,384,384]{2,1,0:T(8,128)(2,1)S(1)}, bf16[2,384,384]{2,1,0:T(8,128)(2,1)S(1)}, u32[]{:S(2)}, u32[]{:S(2)}) collective-permute-start(bf16[2,384,384]{2,1,0:T(8,128)(2,1)S(1)} %get-tuple-element.227), channel_id=1, source_target_pairs={{0,8},{4,12},{8,0},{12,4},{16,24},{20,28},{24,16},{28,20},{1,9},{5... | collective-permute-start | bytes 1769480 | tf_op jit(solution)/shard_map/ppermute | solution.py:47
  77.4 8.4 %collective-permute-start.22 = (bf16[2,192,384]{2,1,0:T(8,128)(2,1)S(1)}, bf16[2,192,384]{2,1,0:T(8,128)(2,1)S(1)}, u32[]{:S(2)}, u32[]{:S(2)}) collective-permute-start(bf16[2,192,384]{2,1,0:T(8,128)(2,1)S(1)} %get-tuple-element.241), channel_id=1, source_target_pairs={{0,8},{4,12},{8,0},{12,4},{16,24},{20,28},{24,16},{28,20},{1,9},{5... | collective-permute-start | bytes 884744 | tf_op jit(solution)/shard_map/ppermute | solution.py:47
  86.3 9.4 %collective-permute-start.28 = (bf16[2,192,384]{2,1,0:T(8,128)(2,1)S(1)}, bf16[2,192,384]{2,1,0:T(8,128)(2,1)S(1)}, u32[]{:S(2)}, u32[]{:S(2)}) collective-permute-start(bf16[2,192,384]{2,1,0:T(8,128)(2,1)S(1)} %get-tuple-element.268), channel_id=1, source_target_pairs={{0,4},{4,0},{8,12},{12,8},{16,20},{20,16},{24,28},{28,24},{1,5},{5... | collective-permute-start | bytes 884744 | tf_op jit(solution)/shard_map/ppermute | solution.py:47
  87.3 15.4 %collective-permute-start.29 = (bf16[2,192,384]{2,1,0:T(8,128)(2,1)S(1)}, bf16[2,192,384]{2,1,0:T(8,128)(2,1)S(1)}, u32[]{:S(2)}, u32[]{:S(2)}) collective-permute-start(bf16[2,192,384]{2,1,0:T(8,128)(2,1)S(1)} %get-tuple-element.270), channel_id=1, source_target_pairs={{0,8},{4,12},{8,0},{12,4},{16,24},{20,28},{24,16},{28,20},{1,9},{5... | collective-permute-start | bytes 884744 | tf_op jit(solution)/shard_map/ppermute | solution.py:47
  87.9 14.8 %collective-permute-start.25 = (bf16[2,96,384]{2,1,0:T(8,128)(2,1)S(1)}, bf16[2,96,384]{2,1,0:T(8,128)(2,1)S(1)}, u32[]{:S(2)}, u32[]{:S(2)}) collective-permute-start(bf16[2,96,384]{2,1,0:T(8,128)(2,1)S(1)} %get-tuple-element.264), channel_id=1, source_target_pairs={{0,16},{4,20},{8,24},{12,28},{16,0},{20,4},{24,8},{28,12},{1,17},{... | collective-permute-start | bytes 442376 | tf_op jit(solution)/shard_map/ppermute | solution.py:47
  90.5 12.1 %collective-permute-start.26 = (bf16[2,96,384]{2,1,0:T(8,128)(2,1)S(1)}, bf16[2,96,384]{2,1,0:T(8,128)(2,1)S(1)}, u32[]{:S(2)}, u32[]{:S(2)}) collective-permute-start(bf16[2,96,384]{2,1,0:T(8,128)(2,1)S(1)} %get-tuple-element.265), channel_id=1, source_target_pairs={{0,2},{2,0},{1,3},{3,1},{4,6},{6,4},{5,7},{7,5},{8,10},{10,8},{9,1... | collective-permute-start | bytes 442376 | tf_op jit(solution)/shard_map/ppermute | solution.py:34
  91.2 11.5 %collective-permute-start.27 = (bf16[2,96,384]{2,1,0:T(8,128)(2,1)S(1)}, bf16[2,96,384]{2,1,0:T(8,128)(2,1)S(1)}, u32[]{:S(2)}, u32[]{:S(2)}) collective-permute-start(bf16[2,96,384]{2,1,0:T(8,128)(2,1)S(1)} %get-tuple-element.266), channel_id=1, source_target_pairs={{0,18},{2,16},{4,22},{6,20},{8,26},{10,24},{12,30},{14,28},{16,2},... | collective-permute-start | bytes 442376 | tf_op jit(solution)/shard_map/ppermute | solution.py:578
  102.7 10.7 %collective-permute-start.30 = (bf16[528,384]{1,0:T(8,128)(2,1)S(1)}, bf16[528,384]{1,0:T(8,128)(2,1)S(1)}, u32[]{:S(2)}, u32[]{:S(2)}) collective-permute-start(bf16[528,384]{1,0:T(8,128)(2,1)S(1)} %get-tuple-element.272), channel_id=1, source_target_pairs={{0,2},{2,0},{1,3},{3,1},{4,6},{6,4},{5,7},{7,5},{8,10},{10,8},{9,1... | collective-permute-start | bytes 1216520 | tf_op jit(solution)/shard_map/ppermute | solution.py:34
  103.5 15.3 %collective-permute-start.31 = (bf16[2,2,96,384]{3,2,1,0:T(8,128)(2,1)S(1)}, bf16[2,2,96,384]{3,2,1,0:T(8,128)(2,1)S(1)}, u32[]{:S(2)}, u32[]{:S(2)}) collective-permute-start(bf16[2,2,96,384]{3,2,1,0:T(8,128)(2,1)S(1)} %shard_map.318.refs_0_), channel_id=1, source_target_pairs={{0,16},{4,20},{8,24},{12,28},{16,0},{20,4},{24,8},{28,12},{1,17},{... | collective-permute-start | bytes 884744 | tf_op jit(solution)/shard_map/ppermute | solution.py:47
  105.9 8.6 %collective-permute-start.32 = (bf16[2,96,384]{2,1,0:T(8,128)(2,1)S(1)}, bf16[2,96,384]{2,1,0:T(8,128)(2,1)S(1)}, u32[]{:S(2)}, u32[]{:S(2)}) collective-permute-start(bf16[2,96,384]{2,1,0:T(8,128)(2,1)S(1)} %get-tuple-element.290), channel_id=1, source_target_pairs={{0,8},{4,12},{8,0},{12,4},{16,24},{20,28},{24,16},{28,20},{1,9},{5... | collective-permute-start | bytes 442376 | tf_op jit(solution)/shard_map/ppermute | solution.py:47
  118.9 14.4 %collective-permute-start.34 = (bf16[2,192,384]{2,1,0:T(8,128)(2,1)S(1)}, bf16[2,192,384]{2,1,0:T(8,128)(2,1)S(1)}, u32[]{:S(2)}, u32[]{:S(2)}) collective-permute-start(bf16[2,192,384]{2,1,0:T(8,128)(2,1)S(1)} %get-tuple-element.307.refs_0_), channel_id=1, source_target_pairs={{0,8},{4,12},{8,0},{12,4},{16,24},{20,28},{24,16},{28,20},{1,9},{5... | collective-permute-start | bytes 884744 | tf_op jit(solution)/shard_map/ppermute | solution.py:47
  119.1 14.2 %collective-permute-start.35 = (bf16[2,192,384]{2,1,0:T(8,128)(2,1)S(1)}, bf16[2,192,384]{2,1,0:T(8,128)(2,1)S(1)}, u32[]{:S(2)}, u32[]{:S(2)}) collective-permute-start(bf16[2,192,384]{2,1,0:T(8,128)(2,1)S(1)} %get-tuple-element.309.refs_2_), channel_id=1, source_target_pairs={{0,4},{4,0},{8,12},{12,8},{16,20},{20,16},{24,28},{28,24},{1,5},{5... | collective-permute-start | bytes 884744 | tf_op jit(solution)/shard_map/ppermute | solution.py:47
  120.4 7.5 %collective-permute-start.36 = (bf16[2,48,384]{2,1,0:T(8,128)(2,1)S(1)}, bf16[2,48,384]{2,1,0:T(8,128)(2,1)S(1)}, u32[]{:S(2)}, u32[]{:S(2)}) collective-permute-start(bf16[2,48,384]{2,1,0:T(8,128)(2,1)S(1)} %get-tuple-element.303), channel_id=1, source_target_pairs={{0,16},{4,20},{8,24},{12,28},{16,0},{20,4},{24,8},{28,12},{1,17},{... | collective-permute-start | bytes 221192 | tf_op jit(solution)/shard_map/ppermute | solution.py:47
  124.2 9.1 %collective-permute-start.38 = (bf16[2,48,384]{2,1,0:T(8,128)(2,1)S(1)}, bf16[2,48,384]{2,1,0:T(8,128)(2,1)S(1)}, u32[]{:S(2)}, u32[]{:S(2)}) collective-permute-start(bf16[2,48,384]{2,1,0:T(8,128)(2,1)S(1)} %get-tuple-element.305), channel_id=1, source_target_pairs={{0,18},{2,16},{4,22},{6,20},{8,26},{10,24},{12,30},{14,28},{16,2},... | collective-permute-start | bytes 221192 | tf_op jit(solution)/shard_map/ppermute | solution.py:578
  133.5 10.5 %collective-permute-start.40 = (bf16[384,384]{1,0:T(8,128)(2,1)S(1)}, bf16[384,384]{1,0:T(8,128)(2,1)S(1)}, u32[]{:S(2)}, u32[]{:S(2)}) collective-permute-start(bf16[384,384]{1,0:T(8,128)(2,1)S(1)} %get-tuple-element.350.refs_0_), channel_id=1, source_target_pairs={{0,4},{4,0},{8,12},{12,8},{16,20},{20,16},{24,28},{28,24},{1,5},{5... | collective-permute-start | bytes 884744 | tf_op jit(solution)/shard_map/ppermute | solution.py:47
  134.5 11.7 %collective-permute-start.41 = (bf16[384,384]{1,0:T(8,128)(2,1)S(1)}, bf16[384,384]{1,0:T(8,128)(2,1)S(1)}, u32[]{:S(2)}, u32[]{:S(2)}) collective-permute-start(bf16[384,384]{1,0:T(8,128)(2,1)S(1)} %get-tuple-element.346.refs_0_), channel_id=1, source_target_pairs={{0,8},{4,12},{8,0},{12,4},{16,24},{20,28},{24,16},{28,20},{1,9},{5... | collective-permute-start | bytes 884744 | tf_op jit(solution)/shard_map/ppermute | solution.py:47
  134.6 9.4 %collective-permute-start.42 = (bf16[208,384]{1,0:T(8,128)(2,1)S(1)}, bf16[208,384]{1,0:T(8,128)(2,1)S(1)}, u32[]{:S(2)}, u32[]{:S(2)}) collective-permute-start(bf16[208,384]{1,0:T(8,128)(2,1)S(1)} %shard_map.323.refs_0_), channel_id=1, source_target_pairs={{0,16},{4,20},{8,24},{12,28},{16,0},{20,4},{24,8},{28,12},{1,17},{... | collective-permute-start | bytes 479240 | tf_op jit(solution)/shard_map/ppermute | solution.py:47
  146.2 12.0 %collective-permute-start.43 = (bf16[384,384]{1,0:T(8,128)(2,1)S(1)}, bf16[384,384]{1,0:T(8,128)(2,1)S(1)}, u32[]{:S(2)}, u32[]{:S(2)}) collective-permute-start(bf16[384,384]{1,0:T(8,128)(2,1)S(1)} %get-tuple-element.352.refs_2_), channel_id=1, source_target_pairs={{0,4},{4,0},{8,12},{12,8},{16,20},{20,16},{24,28},{28,24},{1,5},{5... | collective-permute-start | bytes 884744 | tf_op jit(solution)/shard_map/ppermute | solution.py:47
  147.2 11.0 %collective-permute-start.44 = (bf16[384,384]{1,0:T(8,128)(2,1)S(1)}, bf16[384,384]{1,0:T(8,128)(2,1)S(1)}, u32[]{:S(2)}, u32[]{:S(2)}) collective-permute-start(bf16[384,384]{1,0:T(8,128)(2,1)S(1)} %get-tuple-element.348.refs_2_), channel_id=1, source_target_pairs={{0,8},{4,12},{8,0},{12,4},{16,24},{20,28},{24,16},{28,20},{1,9},{5... | collective-permute-start | bytes 884744 | tf_op jit(solution)/shard_map/ppermute | solution.py:47
  147.2 10.9 %collective-permute-start.45 = (bf16[208,384]{1,0:T(8,128)(2,1)S(1)}, bf16[208,384]{1,0:T(8,128)(2,1)S(1)}, u32[]{:S(2)}, u32[]{:S(2)}) collective-permute-start(bf16[208,384]{1,0:T(8,128)(2,1)S(1)} %get-tuple-element.332.refs_0_), channel_id=1, source_target_pairs={{0,8},{4,12},{8,0},{12,4},{16,24},{20,28},{24,16},{28,20},{1,9},{5... | collective-permute-start | bytes 479240 | tf_op jit(solution)/shard_map/ppermute | solution.py:47
  149.3 7.8 %collective-permute-start.46 = (bf16[192,384]{1,0:T(8,128)(2,1)S(1)}, bf16[192,384]{1,0:T(8,128)(2,1)S(1)}, u32[]{:S(2)}, u32[]{:S(2)}) collective-permute-start(bf16[192,384]{1,0:T(8,128)(2,1)S(1)} %get-tuple-element.334.refs_2_), channel_id=1, source_target_pairs={{0,4},{4,0},{8,12},{12,8},{16,20},{20,16},{24,28},{28,24},{1,5},{5... | collective-permute-start | bytes 442376 | tf_op jit(solution)/shard_map/ppermute | solution.py:47
  158.3 7.8 %collective-permute-start.47 = (bf16[400,384]{1,0:T(8,128)(2,1)S(1)}, bf16[400,384]{1,0:T(8,128)(2,1)S(1)}, u32[]{:S(2)}, u32[]{:S(2)}) collective-permute-start(bf16[400,384]{1,0:T(8,128)(2,1)S(1)} %get-tuple-element.338.refs_0_), channel_id=1, source_target_pairs={{0,4},{4,0},{8,12},{12,8},{16,20},{20,16},{24,28},{28,24},{1,5},{5... | collective-permute-start | bytes 921608 | tf_op jit(solution)/shard_map/ppermute | solution.py:47
  (25 other events, 245.0 us)

commit v6 on v5

--- a/solution.py
+++ b/solution.py
@@ -807,18 +807,17 @@
         vmem=VMEM_START,
     )
     tokens_col = from_col(tokens)
-    tokens_far, tokens_col, sent, sent_out, sent_up = hold(
-        tokens_far, tokens_col, sent, sent_out, sent_up
-    )
     w_got = from_row(sent)
     w_side = from_dp(w_got, 0)
-    out_got = from_row(sent_out)
     up_got = from_row(sent_up)
     tokens_far_col = from_col(tokens_far)
-    tokens_far, tokens_far_col, w_got, w_side, out_got, up_got, sent_down, out_grad_col = hold(
-        tokens_far, tokens_far_col, w_got, w_side, out_got, up_got, sent_down, out_grad
+    (
+        tokens_far, tokens_col, tokens_far_col, w_got, w_side, up_got, sent_out, sent_down, out_grad_col
+    ) = hold(
+        tokens_far, tokens_col, tokens_far_col, w_got, w_side, up_got, sent_out, sent_down, out_grad
     )
     top_col = from_col(out_grad_col)
+    out_got = from_row(sent_out)
     down_got = from_row(sent_down)
     out_side = from_dp(out_got, 0)
     up_side = from_dp(up_got, 0)
@@ -939,7 +938,7 @@
         ),
         keep, got, raised_keep, raised_got, tokens, tokens_far, w_kept, w_got,
     )
-    (out,) = arrived(pairs, out)
+    (out,) = arrived([attention], out)
     got = from_row(out)
     feed.step()
     attention.step()

time: 169 us -> 167 us (0.988)
    ppermute x26, waiting for transfers between devices: 49 us -> 45.2 us  [from_dp(): return lax.ppermute(values, 'dp', dp_pairs(bit))]
    ppermute x11, waiting for transfers between devices: 28.1 us -> 30.9 us  [from_row(): return lax.ppermute(values, 'row', SWAP)]
    ppermute x11, starting transfers between devices: 12.3 us -> 14.4 us  [from_row(): return lax.ppermute(values, 'row', SWAP)]
    ppermute x26, starting transfers between devices: 35 us -> 33.2 us  [from_dp(): return lax.ppermute(values, 'dp', dp_pairs(bit))]
  transfers between devices with their start and end apart: 49 -> 49, of which waited for: 25 -> 23; matrix products, arithmetic and copies ran while one was open for 0% -> 0% of each run, Pallas kernels for 14% -> 13%
where the time goes in v6:
time: 167 us
  waiting for transfers between devices  81.3 us (49%)
  starting transfers between devices  50.6 us (30%)
  Pallas kernels  32.8 us (20%)
    ppermute x26, waiting for transfers between devices, from_dp(): return lax.ppermute(values, 'dp', dp_pairs(bit))  45.2 us
    ppermute x26, starting transfers between devices, from_dp(): return lax.ppermute(values, 'dp', dp_pairs(bit))  33.2 us
    ppermute x11, waiting for transfers between devices, from_row(): return lax.ppermute(values, 'row', SWAP)  30.9 us
    pallas_call x23, Pallas kernels, call(): pl.pallas_call(kernel, out_shape=out_shape, in_specs=[pl.BlockSpec(memory...  28.7 us
    ppermute x11, starting transfers between devices, from_row(): return lax.ppermute(values, 'row', SWAP)  14.4 us
    ppermute x2, waiting for transfers between devices, from_both(): return lax.ppermute(values, ('dp', 'row'), pairs)  5.07 us
    pallas_call x2, Pallas kernels, end_call(): pl.pallas_call(kernel, grid=grid, out_shape=out_shape, in_specs=[whole] *...  4.01 us
  transfers between devices with their start and end apart: 49, of which 23 were waited for; matrix products, arithmetic and copies ran while one was open for 0% of the time, Pallas kernels for 13%

profile of v6, /device:TPU:0, one launch (start us, length us, event | category | flops | bytes accessed | tf_op | source)
XLA Modules:
  0.0 167.2 jit_solution(2504968995784239681)
XLA Ops:
  0.7 2.9 %shard_map.305 = (bf16[400,576]{1,0:T(8,128)(2,1)}, bf16[208,576]{1,0:T(8,128)(2,1)}, bf16[192,384]{1,0:T(8,128)(2,1)}, bf16[192,768]{1,0:T(8,128)(2,1)}, bf16[384,384]{1,0:T(8,128)(2,1)}) custom-call(bf16[384]{0:T(512)(128)(2,1)} %refs_0_.3, bf16[384]{0:T(512)(128)(2,1)} %refs_1_.2, bf16[384]{0:T(512)(128)(2,1)} %refs_2_.1, bf16[384]{0:T(512)(128)(2,1)} %refs_3_.2, ...), custom_call_target="tpu_custom_call" | custom-call | tf_op jit(solution)/shard_map/pallas_call | solution.py:69
  3.6 3.0 %collective-permute-start.3 = (bf16[208,576]{1,0:T(8,128)(2,1)}, bf16[208,576]{1,0:T(8,128)(2,1)S(1)}, u32[]{:S(2)}, u32[]{:S(2)}) collective-permute-start(bf16[208,576]{1,0:T(8,128)(2,1)} %get-tuple-element.182), channel_id=1, source_target_pairs={{0,2},{2,0},{1,3},{3,1},{4,6},{6,4},{5,7},{7,5},{8,10},{10,8},{9,1... | collective-permute-start | bytes 718856 | tf_op jit(solution)/shard_map/ppermute | solution.py:34
  6.8 1.9 %collective-permute-start.5 = (bf16[192,768]{1,0:T(8,128)(2,1)}, bf16[192,768]{1,0:T(8,128)(2,1)S(1)}, u32[]{:S(2)}, u32[]{:S(2)}) collective-permute-start(bf16[192,768]{1,0:T(8,128)(2,1)} %get-tuple-element.183), channel_id=1, source_target_pairs={{0,2},{2,0},{1,3},{3,1},{4,6},{6,4},{5,7},{7,5},{8,10},{10,8},{9,1... | collective-permute-start | bytes 884744 | tf_op jit(solution)/shard_map/ppermute | solution.py:34
  8.7 5.4 %collective-permute-done.3.got.sent.refs_12_ = bf16[208,576]{1,0:T(8,128)(2,1)S(1)} collective-permute-done((bf16[208,576]{1,0:T(8,128)(2,1)}, bf16[208,576]{1,0:T(8,128)(2,1)S(1)}, u32[]{:S(2)}, u32[]{:S(2)}) %collective-permute-start.3) | collective-permute-done | bytes 239648 | tf_op jit(solution)/shard_map/ppermute | solution.py:34
  14.1 2.0 %collective-permute-start.4 = (bf16[208,576]{1,0:T(8,128)(2,1)S(1)}, bf16[208,576]{1,0:T(8,128)(2,1)S(1)}, u32[]{:S(2)}, u32[]{:S(2)}) collective-permute-start(bf16[208,576]{1,0:T(8,128)(2,1)S(1)} %collective-permute-done.3.got.sent.refs_12_), channel_id=1, source_target_pairs={{0,4},{4,0},{8,12},{12,8},{16,20},{20,16},{24,28},{28,24},{1,5},{5... | collective-permute-start | bytes 718856 | tf_op jit(solution)/shard_map/ppermute | solution.py:47
  16.1 2.2 %collective-permute-done.own_far = bf16[256,384]{1,0:T(8,128)(2,1)S(1)} collective-permute-done((bf16[256,384]{1,0:T(8,128)(2,1)S(1)}, bf16[256,384]{1,0:T(8,128)(2,1)S(1)}, u32[]{:S(2)}, u32[]{:S(2)}) %collective-permute-start) | collective-permute-done | bytes 196640 | tf_op jit(solution)/shard_map/ppermute | solution.py:34
  18.3 5.5 %collective-permute-done.5.got = bf16[192,768]{1,0:T(8,128)(2,1)S(1)} collective-permute-done((bf16[192,768]{1,0:T(8,128)(2,1)}, bf16[192,768]{1,0:T(8,128)(2,1)S(1)}, u32[]{:S(2)}, u32[]{:S(2)}) %collective-permute-start.5) | collective-permute-done | bytes 294944 | tf_op jit(solution)/shard_map/ppermute | solution.py:34
  23.8 1.7 %collective-permute-start.7 = (bf16[192,384]{1,0:T(8,128)(2,1)}, bf16[192,384]{1,0:T(8,128)(2,1)S(1)}, u32[]{:S(2)}, u32[]{:S(2)}) collective-permute-start(bf16[192,384]{1,0:T(8,128)(2,1)} %get-tuple-element.193), channel_id=1, source_target_pairs={{0,2},{2,0},{1,3},{3,1},{4,6},{6,4},{5,7},{7,5},{8,10},{10,8},{9,1... | collective-permute-start | bytes 442376 | tf_op jit(solution)/shard_map/ppermute | solution.py:34
  28.6 4.4 %shard_map.306 = (bf16[512,768]{1,0:T(8,128)(2,1)S(1)}, bf16[512,192]{1,0:T(8,128)(2,1)S(1)}, bf16[512,192]{1,0:T(8,128)(2,1)S(1)}, bf16[512,192]{1,0:T(8,128)(2...) custom-call(s32[1,2]{1,0:T(1,128)S(1)} %copy-done.7, bf16[256,384]{1,0:T(8,128)(2,1)S(1)} %copy-done.5, ...), custom_call_target="tpu_custom_call" | custom-call | tf_op jit(solution)/shard_map/pallas_call | solution.py:69
  35.1 5.9 %collective-permute-done.6.mixed_other = bf16[512,192]{1,0:T(8,128)(2,1)S(1)} collective-permute-done((bf16[512,192]{1,0:T(8,128)(2,1)S(1)}, bf16[512,192]{1,0:T(8,128)(2,1)S(1)}, u32[]{:S(2)}, u32[]{:S(2)}) %collective-permute-start.6) | collective-permute-done | bytes 196640 | tf_op jit(solution)/shard_map/ppermute | solution.py:34
  49.6 2.7 %collective-permute-done.15.refs_10_ = bf16[384,384]{1,0:T(8,128)(2,1)S(1)} collective-permute-done((bf16[384,384]{1,0:T(8,128)(2,1)S(1)}, bf16[384,384]{1,0:T(8,128)(2,1)S(1)}, u32[]{:S(2)}, u32[]{:S(2)}) %collective-permute-start.15) | collective-permute-done | bytes 294944 | tf_op jit(solution)/shard_map/ppermute | solution.py:47
  52.4 4.2 %shard_map.310 = (bf16[2,384,384]{2,1,0:T(8,128)(2,1)S(1)}, bf16[2,384,384]{2,1,0:T(8,128)(2,1)S(1)}, bf16[2,384,384]{2,1,0:T(8,128)(2,1)S(1)}, bf16[2,384,384]{...) custom-call(s32[1,2]{1,0:T(1,128)S(1)} %copy-done.7, ...), custom_call_target="tpu_custom_call" | custom-call | tf_op jit(solution)/shard_map/pallas_call | solution.py:69
  62.2 7.6 %collective-permute-done.19.total_far = bf16[256,768]{1,0:T(8,128)(2,1)S(1)} collective-permute-done((bf16[256,768]{1,0:T(8,128)(2,1)S(1)}, bf16[256,768]{1,0:T(8,128)(2,1)S(1)}, u32[]{:S(2)}, u32[]{:S(2)}) %collective-permute-start.19) | collective-permute-done | bytes 393248 | tf_op jit(solution)/shard_map/ppermute | solution.py:34
  70.9 3.3 %collective-permute-done.16.refs_1_ = bf16[2,384,384]{2,1,0:T(8,128)(2,1)S(1)} collective-permute-done((bf16[2,384,384]{2,1,0:T(8,128)(2,1)S(1)}, bf16[2,384,384]{2,1,0:T(8,128)(2,1)S(1)}, u32[]{:S(2)}, u32[]{:S(2)}) %collective-permute-start.16) | collective-permute-done | bytes 589856 | tf_op jit(solution)/shard_map/ppermute | solution.py:47
  77.9 6.1 %shard_map.314 = (bf16[2,192,384]{2,1,0:T(8,128)(2,1)S(1)}, bf16[2,192,384]{2,1,0:T(8,128)(2,1)S(1)}, bf16[2,192,384]{2,1,0:T(8,128)(2,1)S(1)}, bf16[2,192,384]{...) custom-call(s32[1,2]{1,0:T(1,128)S(1)} %copy-done.7, ...), custom_call_target="tpu_custom_call" | custom-call | tf_op jit(solution)/shard_map/pallas_call | solution.py:69
  86.3 2.7 %collective-permute-start.28 = (bf16[2,96,384]{2,1,0:T(8,128)(2,1)S(1)}, bf16[2,96,384]{2,1,0:T(8,128)(2,1)S(1)}, u32[]{:S(2)}, u32[]{:S(2)}) collective-permute-start(bf16[2,96,384]{2,1,0:T(8,128)(2,1)S(1)} %get-tuple-element.266), channel_id=1, source_target_pairs={{0,16},{4,20},{8,24},{12,28},{16,0},{20,4},{24,8},{28,12},{1,17},{... | collective-permute-start | bytes 442376 | tf_op jit(solution)/shard_map/ppermute | solution.py:47
  91.4 2.8 %collective-permute-done.25.refs_1_ = bf16[2,192,384]{2,1,0:T(8,128)(2,1)S(1)} collective-permute-done((bf16[2,192,384]{2,1,0:T(8,128)(2,1)S(1)}, bf16[2,192,384]{2,1,0:T(8,128)(2,1)S(1)}, u32[]{:S(2)}, u32[]{:S(2)}) %collective-permute-start.25) | collective-permute-done | bytes 294944 | tf_op jit(solution)/shard_map/ppermute | solution.py:47
  94.1 6.9 %collective-permute-done.26.refs_3_ = bf16[2,192,384]{2,1,0:T(8,128)(2,1)S(1)} collective-permute-done((bf16[2,192,384]{2,1,0:T(8,128)(2,1)S(1)}, bf16[2,192,384]{2,1,0:T(8,128)(2,1)S(1)}, u32[]{:S(2)}, u32[]{:S(2)}) %collective-permute-start.26) | collective-permute-done | bytes 294944 | tf_op jit(solution)/shard_map/ppermute | solution.py:47
  103.9 4.2 %collective-permute-start.32 = (bf16[2,96,384]{2,1,0:T(8,128)(2,1)S(1)}, bf16[2,96,384]{2,1,0:T(8,128)(2,1)S(1)}, u32[]{:S(2)}, u32[]{:S(2)}) collective-permute-start(bf16[2,96,384]{2,1,0:T(8,128)(2,1)S(1)} %get-tuple-element.274), channel_id=1, source_target_pairs={{0,8},{4,12},{8,0},{12,4},{16,24},{20,28},{24,16},{28,20},{1,9},{5... | collective-permute-start | bytes 442376 | tf_op jit(solution)/shard_map/ppermute | solution.py:47
  109.2 2.5 %collective-permute-done.27.got = bf16[528,384]{1,0:T(8,128)(2,1)S(1)} collective-permute-done((bf16[528,384]{1,0:T(8,128)(2,1)S(1)}, bf16[528,384]{1,0:T(8,128)(2,1)S(1)}, u32[]{:S(2)}, u32[]{:S(2)}) %collective-permute-start.27) | collective-permute-done | bytes 405536 | tf_op jit(solution)/shard_map/ppermute | solution.py:34
  112.9 5.1 %collective-permute-done.31.refs_1_ = bf16[2,2,96,384]{3,2,1,0:T(8,128)(2,1)S(1)} collective-permute-done((bf16[2,2,96,384]{3,2,1,0:T(8,128)(2,1)S(1)}, bf16[2,2,96,384]{3,2,1,0:T(8,128)(2,1)S(1)}, u32[]{:S(2)}, u32[]{:S(2)}) %collective-permute-start.31) | collective-permute-done | bytes 294944 | tf_op jit(solution)/shard_map/ppermute | solution.py:47
  119.5 2.5 %collective-permute-start.36 = (bf16[2,48,384]{2,1,0:T(8,128)(2,1)S(1)}, bf16[2,48,384]{2,1,0:T(8,128)(2,1)S(1)}, u32[]{:S(2)}, u32[]{:S(2)}) collective-permute-start(bf16[2,48,384]{2,1,0:T(8,128)(2,1)S(1)} %get-tuple-element.287), channel_id=1, source_target_pairs={{0,16},{4,20},{8,24},{12,28},{16,0},{20,4},{24,8},{28,12},{1,17},{... | collective-permute-start | bytes 221192 | tf_op jit(solution)/shard_map/ppermute | solution.py:47
  123.9 2.2 %collective-permute-done.36.from_dp_ref = bf16[2,48,384]{2,1,0:T(8,128)(2,1)S(1)} collective-permute-done((bf16[2,48,384]{2,1,0:T(8,128)(2,1)S(1)}, bf16[2,48,384]{2,1,0:T(8,128)(2,1)S(1)}, u32[]{:S(2)}, u32[]{:S(2)}) %collective-permute-start.36) | collective-permute-done | bytes 73760 | tf_op jit(solution)/shard_map/ppermute | solution.py:47
  126.4 5.1 %collective-permute-done.38.from_both_ref = bf16[2,48,384]{2,1,0:T(8,128)(2,1)S(1)} collective-permute-done((bf16[2,48,384]{2,1,0:T(8,128)(2,1)S(1)}, bf16[2,48,384]{2,1,0:T(8,128)(2,1)S(1)}, u32[]{:S(2)}, u32[]{:S(2)}) %collective-permute-start.38) | collective-permute-done | bytes 73760 | tf_op jit(solution)/shard_map/ppermute | solution.py:578
  134.3 7.8 %collective-permute-done.42.refs_1_ = bf16[208,384]{1,0:T(8,128)(2,1)S(1)} collective-permute-done((bf16[208,384]{1,0:T(8,128)(2,1)S(1)}, bf16[208,384]{1,0:T(8,128)(2,1)S(1)}, u32[]{:S(2)}, u32[]{:S(2)}) %collective-permute-start.42) | collective-permute-done | bytes 159776 | tf_op jit(solution)/shard_map/ppermute | solution.py:47
  142.1 2.2 %collective-permute-done.41.refs_1_ = bf16[384,384]{1,0:T(8,128)(2,1)S(1)} collective-permute-done((bf16[384,384]{1,0:T(8,128)(2,1)S(1)}, bf16[384,384]{1,0:T(8,128)(2,1)S(1)}, u32[]{:S(2)}, u32[]{:S(2)}) %collective-permute-start.41) | collective-permute-done | bytes 294944 | tf_op jit(solution)/shard_map/ppermute | solution.py:47
  145.7 1.9 %collective-permute-start.45 = (bf16[208,384]{1,0:T(8,128)(2,1)S(1)}, bf16[208,384]{1,0:T(8,128)(2,1)S(1)}, u32[]{:S(2)}, u32[]{:S(2)}) collective-permute-start(bf16[208,384]{1,0:T(8,128)(2,1)S(1)} %get-tuple-element.316.refs_0_), channel_id=1, source_target_pairs={{0,8},{4,12},{8,0},{12,4},{16,24},{20,28},{24,16},{28,20},{1,9},{5... | collective-permute-start | bytes 479240 | tf_op jit(solution)/shard_map/ppermute | solution.py:47
  148.5 6.8 %collective-permute-done.46.refs_3_ = bf16[192,384]{1,0:T(8,128)(2,1)S(1)} collective-permute-done((bf16[192,384]{1,0:T(8,128)(2,1)S(1)}, bf16[192,384]{1,0:T(8,128)(2,1)S(1)}, u32[]{:S(2)}, u32[]{:S(2)}) %collective-permute-start.46) | collective-permute-done | bytes 147488 | tf_op jit(solution)/shard_map/ppermute | solution.py:47
  157.7 2.0 %shard_map.328 = f32[384,1536]{1,0:T(8,128)} custom-call(bf16[384,384]{1,0:T(8,128)(2,1)S(1)} %get-tuple-element.330.refs_0_, bf16[384,384]{1,0:T(8,128)(2,1)S(1)} %collective-permute-done.41.refs_1_, bf16[384,384]{1,0:T(8,128)(2,1)S(1)} %get-tuple-element.332.refs_2_, bf16[384,384]{1,0:T(8,128)(2,1)S(1)} %collective-permute-done.44.refs_3_), custom_call_target="tpu_custom_call" | custom-call | tf_op jit(solution)/shard_map/pallas_call | solution.py:746
  159.8 2.0 %shard_map.329 = f32[1536,384]{1,0:T(8,128)} custom-call(bf16[384,384]{1,0:T(8,128)(2,1)S(1)} %get-tuple-element.334.refs_0_, bf16[384,384]{1,0:T(8,128)(2,1)S(1)} %collective-permute-done.40.refs_1_, bf16[384,384]{1,0:T(8,128)(2,1)S(1)} %get-tuple-element.336.refs_2_, bf16[384,384]{1,0:T(8,128)(2,1)S(1)} %collective-permute-done.43.refs_3_), custom_call_target="tpu_custom_call" | custom-call | tf_op jit(solution)/shard_map/pallas_call | solution.py:746
  161.8 2.4 %collective-permute-done.48.refs_1_ = bf16[384,384]{1,0:T(8,128)(2,1)S(1)} collective-permute-done((bf16[384,384]{1,0:T(8,128)(2,1)S(1)}, bf16[384,384]{1,0:T(8,128)(2,1)S(1)}, u32[]{:S(2)}, u32[]{:S(2)}) %collective-permute-start.48) | collective-permute-done | bytes 294944 | tf_op jit(solution)/shard_map/ppermute | solution.py:47
  164.2 1.8 %shard_map.326 = (f32[384,384]{1,0:T(8,128)}, f32[384,384]{1,0:T(8,128)}, f32[192]{0:T(256)}, f32[192]{0:T(256)}, f32[384]{0:T(512)}, /*index=5*/f32[768]{0:T(10...) custom-call(bf16[400,384]{1,0:T(8,128)(2,1)S(1)} %get-tuple-element.322.refs_0_, ...), custom_call_target="tpu_custom_call" | custom-call | tf_op jit(solution)/shard_map/pallas_call | solution.py:69
  (108 shorter events, 46.5 us)
Async XLA Ops:
  3.6 10.5 %collective-permute-start.3 = (bf16[208,576]{1,0:T(8,128)(2,1)}, bf16[208,576]{1,0:T(8,128)(2,1)S(1)}, u32[]{:S(2)}, u32[]{:S(2)}) collective-permute-start(bf16[208,576]{1,0:T(8,128)(2,1)} %get-tuple-element.182), channel_id=1, source_target_pairs={{0,2},{2,0},{1,3},{3,1},{4,6},{6,4},{5,7},{7,5},{8,10},{10,8},{9,1... | collective-permute-start | bytes 718856 | tf_op jit(solution)/shard_map/ppermute | solution.py:34
  6.7 11.6 %collective-permute-start = (bf16[256,384]{1,0:T(8,128)(2,1)S(1)}, bf16[256,384]{1,0:T(8,128)(2,1)S(1)}, u32[]{:S(2)}, u32[]{:S(2)}) collective-permute-start(bf16[256,384]{1,0:T(8,128)(2,1)S(1)} %copy-done.5), channel_id=1, source_target_pairs={{0,2},{2,0},{1,3},{3,1},{4,6},{6,4},{5,7},{7,5},{8,10},{10,8},{9,1... | collective-permute-start | bytes 589832 | tf_op jit(solution)/shard_map/ppermute | solution.py:34
  6.8 17.0 %collective-permute-start.5 = (bf16[192,768]{1,0:T(8,128)(2,1)}, bf16[192,768]{1,0:T(8,128)(2,1)S(1)}, u32[]{:S(2)}, u32[]{:S(2)}) collective-permute-start(bf16[192,768]{1,0:T(8,128)(2,1)} %get-tuple-element.183), channel_id=1, source_target_pairs={{0,2},{2,0},{1,3},{3,1},{4,6},{6,4},{5,7},{7,5},{8,10},{10,8},{9,1... | collective-permute-start | bytes 884744 | tf_op jit(solution)/shard_map/ppermute | solution.py:34
  14.1 9.7 %collective-permute-start.4 = (bf16[208,576]{1,0:T(8,128)(2,1)S(1)}, bf16[208,576]{1,0:T(8,128)(2,1)S(1)}, u32[]{:S(2)}, u32[]{:S(2)}) collective-permute-start(bf16[208,576]{1,0:T(8,128)(2,1)S(1)} %collective-permute-done.3.got.sent.refs_12_), channel_id=1, source_target_pairs={{0,4},{4,0},{8,12},{12,8},{16,20},{20,16},{24,28},{28,24},{1,5},{5... | collective-permute-start | bytes 718856 | tf_op jit(solution)/shard_map/ppermute | solution.py:47
  23.8 10.8 %collective-permute-start.7 = (bf16[192,384]{1,0:T(8,128)(2,1)}, bf16[192,384]{1,0:T(8,128)(2,1)S(1)}, u32[]{:S(2)}, u32[]{:S(2)}) collective-permute-start(bf16[192,384]{1,0:T(8,128)(2,1)} %get-tuple-element.193), channel_id=1, source_target_pairs={{0,2},{2,0},{1,3},{3,1},{4,6},{6,4},{5,7},{7,5},{8,10},{10,8},{9,1... | collective-permute-start | bytes 442376 | tf_op jit(solution)/shard_map/ppermute | solution.py:34
  25.5 15.4 %collective-permute-start.10 = (bf16[384,384]{1,0:T(8,128)(2,1)}, bf16[384,384]{1,0:T(8,128)(2,1)S(1)}, u32[]{:S(2)}, u32[]{:S(2)}) collective-permute-start(bf16[384,384]{1,0:T(8,128)(2,1)} %get-tuple-element.195), channel_id=1, source_target_pairs={{0,2},{2,0},{1,3},{3,1},{4,6},{6,4},{5,7},{7,5},{8,10},{10,8},{9,1... | collective-permute-start | bytes 884744 | tf_op jit(solution)/shard_map/ppermute | solution.py:34
  25.8 15.2 %collective-permute-start.9 = (bf16[192,768]{1,0:T(8,128)(2,1)S(1)}, bf16[192,768]{1,0:T(8,128)(2,1)S(1)}, u32[]{:S(2)}, u32[]{:S(2)}) collective-permute-start(bf16[192,768]{1,0:T(8,128)(2,1)S(1)} %collective-permute-done.5.got), channel_id=1, source_target_pairs={{0,4},{4,0},{8,12},{12,8},{16,20},{20,16},{24,28},{28,24},{1,5},{5... | collective-permute-start | bytes 884744 | tf_op jit(solution)/shard_map/ppermute | solution.py:47
  33.0 8.0 %collective-permute-start.6 = (bf16[512,192]{1,0:T(8,128)(2,1)S(1)}, bf16[512,192]{1,0:T(8,128)(2,1)S(1)}, u32[]{:S(2)}, u32[]{:S(2)}) collective-permute-start(bf16[512,192]{1,0:T(8,128)(2,1)S(1)} %get-tuple-element.192.mixed.refs_8_), channel_id=1, source_target_pairs={{0,2},{2,0},{1,3},{3,1},{4,6},{6,4},{5,7},{7,5},{8,10},{10,8},{9,1... | collective-permute-start | bytes 589832 | tf_op jit(solution)/shard_map/ppermute | solution.py:34
  43.3 9.1 %collective-permute-start.15 = (bf16[384,384]{1,0:T(8,128)(2,1)S(1)}, bf16[384,384]{1,0:T(8,128)(2,1)S(1)}, u32[]{:S(2)}, u32[]{:S(2)}) collective-permute-start(bf16[384,384]{1,0:T(8,128)(2,1)S(1)} %collective-permute-done.10.refs_9_), channel_id=1, source_target_pairs={{0,8},{4,12},{8,0},{12,4},{16,24},{20,28},{24,16},{28,20},{1,9},{5... | collective-permute-start | bytes 884744 | tf_op jit(solution)/shard_map/ppermute | solution.py:47
  58.5 11.2 %collective-permute-start.19 = (bf16[256,768]{1,0:T(8,128)(2,1)S(1)}, bf16[256,768]{1,0:T(8,128)(2,1)S(1)}, u32[]{:S(2)}, u32[]{:S(2)}) collective-permute-start(bf16[256,768]{1,0:T(8,128)(2,1)S(1)} %add_convert_fusion.total), channel_id=1, source_target_pairs={{0,2},{2,0},{1,3},{3,1},{4,6},{6,4},{5,7},{7,5},{8,10},{10,8},{9,1... | collective-permute-start | bytes 1179656 | tf_op jit(solution)/shard_map/ppermute | solution.py:34
  59.2 15.1 %collective-permute-start.16 = (bf16[2,384,384]{2,1,0:T(8,128)(2,1)S(1)}, bf16[2,384,384]{2,1,0:T(8,128)(2,1)S(1)}, u32[]{:S(2)}, u32[]{:S(2)}) collective-permute-start(bf16[2,384,384]{2,1,0:T(8,128)(2,1)S(1)} %get-tuple-element.213), channel_id=1, source_target_pairs={{0,4},{4,0},{8,12},{12,8},{16,20},{20,16},{24,28},{28,24},{1,5},{5... | collective-permute-start | bytes 1769480 | tf_op jit(solution)/shard_map/ppermute | solution.py:47
  60.6 14.8 %collective-permute-start.17 = (bf16[2,384,384]{2,1,0:T(8,128)(2,1)S(1)}, bf16[2,384,384]{2,1,0:T(8,128)(2,1)S(1)}, u32[]{:S(2)}, u32[]{:S(2)}) collective-permute-start(bf16[2,384,384]{2,1,0:T(8,128)(2,1)S(1)} %get-tuple-element.215), channel_id=1, source_target_pairs={{0,8},{4,12},{8,0},{12,4},{16,24},{20,28},{24,16},{28,20},{1,9},{5... | collective-permute-start | bytes 1769480 | tf_op jit(solution)/shard_map/ppermute | solution.py:47
  75.8 8.2 %collective-permute-start.22 = (bf16[2,192,384]{2,1,0:T(8,128)(2,1)S(1)}, bf16[2,192,384]{2,1,0:T(8,128)(2,1)S(1)}, u32[]{:S(2)}, u32[]{:S(2)}) collective-permute-start(bf16[2,192,384]{2,1,0:T(8,128)(2,1)S(1)} %get-tuple-element.229), channel_id=1, source_target_pairs={{0,8},{4,12},{8,0},{12,4},{16,24},{20,28},{24,16},{28,20},{1,9},{5... | collective-permute-start | bytes 884744 | tf_op jit(solution)/shard_map/ppermute | solution.py:47
  84.7 9.4 %collective-permute-start.25 = (bf16[2,192,384]{2,1,0:T(8,128)(2,1)S(1)}, bf16[2,192,384]{2,1,0:T(8,128)(2,1)S(1)}, u32[]{:S(2)}, u32[]{:S(2)}) collective-permute-start(bf16[2,192,384]{2,1,0:T(8,128)(2,1)S(1)} %get-tuple-element.248), channel_id=1, source_target_pairs={{0,4},{4,0},{8,12},{12,8},{16,20},{20,16},{24,28},{28,24},{1,5},{5... | collective-permute-start | bytes 884744 | tf_op jit(solution)/shard_map/ppermute | solution.py:47
  85.7 15.4 %collective-permute-start.26 = (bf16[2,192,384]{2,1,0:T(8,128)(2,1)S(1)}, bf16[2,192,384]{2,1,0:T(8,128)(2,1)S(1)}, u32[]{:S(2)}, u32[]{:S(2)}) collective-permute-start(bf16[2,192,384]{2,1,0:T(8,128)(2,1)S(1)} %get-tuple-element.250), channel_id=1, source_target_pairs={{0,8},{4,12},{8,0},{12,4},{16,24},{20,28},{24,16},{28,20},{1,9},{5... | collective-permute-start | bytes 884744 | tf_op jit(solution)/shard_map/ppermute | solution.py:47
  86.3 16.3 %collective-permute-start.28 = (bf16[2,96,384]{2,1,0:T(8,128)(2,1)S(1)}, bf16[2,96,384]{2,1,0:T(8,128)(2,1)S(1)}, u32[]{:S(2)}, u32[]{:S(2)}) collective-permute-start(bf16[2,96,384]{2,1,0:T(8,128)(2,1)S(1)} %get-tuple-element.266), channel_id=1, source_target_pairs={{0,16},{4,20},{8,24},{12,28},{16,0},{20,4},{24,8},{28,12},{1,17},{... | collective-permute-start | bytes 442376 | tf_op jit(solution)/shard_map/ppermute | solution.py:47
  89.0 13.6 %collective-permute-start.29 = (bf16[2,96,384]{2,1,0:T(8,128)(2,1)S(1)}, bf16[2,96,384]{2,1,0:T(8,128)(2,1)S(1)}, u32[]{:S(2)}, u32[]{:S(2)}) collective-permute-start(bf16[2,96,384]{2,1,0:T(8,128)(2,1)S(1)} %get-tuple-element.267), channel_id=1, source_target_pairs={{0,2},{2,0},{1,3},{3,1},{4,6},{6,4},{5,7},{7,5},{8,10},{10,8},{9,1... | collective-permute-start | bytes 442376 | tf_op jit(solution)/shard_map/ppermute | solution.py:34
  90.5 12.1 %collective-permute-start.30 = (bf16[2,96,384]{2,1,0:T(8,128)(2,1)S(1)}, bf16[2,96,384]{2,1,0:T(8,128)(2,1)S(1)}, u32[]{:S(2)}, u32[]{:S(2)}) collective-permute-start(bf16[2,96,384]{2,1,0:T(8,128)(2,1)S(1)} %get-tuple-element.268), channel_id=1, source_target_pairs={{0,18},{2,16},{4,22},{6,20},{8,26},{10,24},{12,30},{14,28},{16,2},... | collective-permute-start | bytes 442376 | tf_op jit(solution)/shard_map/ppermute | solution.py:578
  101.1 10.6 %collective-permute-start.27 = (bf16[528,384]{1,0:T(8,128)(2,1)S(1)}, bf16[528,384]{1,0:T(8,128)(2,1)S(1)}, u32[]{:S(2)}, u32[]{:S(2)}) collective-permute-start(bf16[528,384]{1,0:T(8,128)(2,1)S(1)} %get-tuple-element.252), channel_id=1, source_target_pairs={{0,2},{2,0},{1,3},{3,1},{4,6},{6,4},{5,7},{7,5},{8,10},{10,8},{9,1... | collective-permute-start | bytes 1216520 | tf_op jit(solution)/shard_map/ppermute | solution.py:34
  102.7 15.3 %collective-permute-start.31 = (bf16[2,2,96,384]{3,2,1,0:T(8,128)(2,1)S(1)}, bf16[2,2,96,384]{3,2,1,0:T(8,128)(2,1)S(1)}, u32[]{:S(2)}, u32[]{:S(2)}) collective-permute-start(bf16[2,2,96,384]{3,2,1,0:T(8,128)(2,1)S(1)} %shard_map.318.refs_0_), channel_id=1, source_target_pairs={{0,16},{4,20},{8,24},{12,28},{16,0},{20,4},{24,8},{28,12},{1,17},{... | collective-permute-start | bytes 884744 | tf_op jit(solution)/shard_map/ppermute | solution.py:47
  103.9 14.0 %collective-permute-start.32 = (bf16[2,96,384]{2,1,0:T(8,128)(2,1)S(1)}, bf16[2,96,384]{2,1,0:T(8,128)(2,1)S(1)}, u32[]{:S(2)}, u32[]{:S(2)}) collective-permute-start(bf16[2,96,384]{2,1,0:T(8,128)(2,1)S(1)} %get-tuple-element.274), channel_id=1, source_target_pairs={{0,8},{4,12},{8,0},{12,4},{16,24},{20,28},{24,16},{28,20},{1,9},{5... | collective-permute-start | bytes 442376 | tf_op jit(solution)/shard_map/ppermute | solution.py:47
  108.1 9.9 %collective-permute-start.33 = (bf16[2,96,384]{2,1,0:T(8,128)(2,1)S(1)}, bf16[2,96,384]{2,1,0:T(8,128)(2,1)S(1)}, u32[]{:S(2)}, u32[]{:S(2)}) collective-permute-start(bf16[2,96,384]{2,1,0:T(8,128)(2,1)S(1)} %get-tuple-element.276), channel_id=1, source_target_pairs={{0,4},{4,0},{8,12},{12,8},{16,20},{20,16},{24,28},{28,24},{1,5},{5... | collective-permute-start | bytes 442376 | tf_op jit(solution)/shard_map/ppermute | solution.py:47
  118.0 13.5 %collective-permute-start.34 = (bf16[2,192,384]{2,1,0:T(8,128)(2,1)S(1)}, bf16[2,192,384]{2,1,0:T(8,128)(2,1)S(1)}, u32[]{:S(2)}, u32[]{:S(2)}) collective-permute-start(bf16[2,192,384]{2,1,0:T(8,128)(2,1)S(1)} %get-tuple-element.291.refs_0_), channel_id=1, source_target_pairs={{0,8},{4,12},{8,0},{12,4},{16,24},{20,28},{24,16},{28,20},{1,9},{5... | collective-permute-start | bytes 884744 | tf_op jit(solution)/shard_map/ppermute | solution.py:47
  118.1 13.4 %collective-permute-start.35 = (bf16[2,192,384]{2,1,0:T(8,128)(2,1)S(1)}, bf16[2,192,384]{2,1,0:T(8,128)(2,1)S(1)}, u32[]{:S(2)}, u32[]{:S(2)}) collective-permute-start(bf16[2,192,384]{2,1,0:T(8,128)(2,1)S(1)} %get-tuple-element.293.refs_2_), channel_id=1, source_target_pairs={{0,4},{4,0},{8,12},{12,8},{16,20},{20,16},{24,28},{28,24},{1,5},{5... | collective-permute-start | bytes 884744 | tf_op jit(solution)/shard_map/ppermute | solution.py:47
  122.5 8.9 %collective-permute-start.38 = (bf16[2,48,384]{2,1,0:T(8,128)(2,1)S(1)}, bf16[2,48,384]{2,1,0:T(8,128)(2,1)S(1)}, u32[]{:S(2)}, u32[]{:S(2)}) collective-permute-start(bf16[2,48,384]{2,1,0:T(8,128)(2,1)S(1)} %get-tuple-element.289), channel_id=1, source_target_pairs={{0,18},{2,16},{4,22},{6,20},{8,26},{10,24},{12,30},{14,28},{16,2},... | collective-permute-start | bytes 221192 | tf_op jit(solution)/shard_map/ppermute | solution.py:578
  131.7 10.4 %collective-permute-start.40 = (bf16[384,384]{1,0:T(8,128)(2,1)S(1)}, bf16[384,384]{1,0:T(8,128)(2,1)S(1)}, u32[]{:S(2)}, u32[]{:S(2)}) collective-permute-start(bf16[384,384]{1,0:T(8,128)(2,1)S(1)} %get-tuple-element.334.refs_0_), channel_id=1, source_target_pairs={{0,4},{4,0},{8,12},{12,8},{16,20},{20,16},{24,28},{28,24},{1,5},{5... | collective-permute-start | bytes 884744 | tf_op jit(solution)/shard_map/ppermute | solution.py:47
  132.7 11.6 %collective-permute-start.41 = (bf16[384,384]{1,0:T(8,128)(2,1)S(1)}, bf16[384,384]{1,0:T(8,128)(2,1)S(1)}, u32[]{:S(2)}, u32[]{:S(2)}) collective-permute-start(bf16[384,384]{1,0:T(8,128)(2,1)S(1)} %get-tuple-element.330.refs_0_), channel_id=1, source_target_pairs={{0,8},{4,12},{8,0},{12,4},{16,24},{20,28},{24,16},{28,20},{1,9},{5... | collective-permute-start | bytes 884744 | tf_op jit(solution)/shard_map/ppermute | solution.py:47
  132.8 9.3 %collective-permute-start.42 = (bf16[208,384]{1,0:T(8,128)(2,1)S(1)}, bf16[208,384]{1,0:T(8,128)(2,1)S(1)}, u32[]{:S(2)}, u32[]{:S(2)}) collective-permute-start(bf16[208,384]{1,0:T(8,128)(2,1)S(1)} %shard_map.323.refs_0_), channel_id=1, source_target_pairs={{0,16},{4,20},{8,24},{12,28},{16,0},{20,4},{24,8},{28,12},{1,17},{... | collective-permute-start | bytes 479240 | tf_op jit(solution)/shard_map/ppermute | solution.py:47
  144.3 12.1 %collective-permute-start.43 = (bf16[384,384]{1,0:T(8,128)(2,1)S(1)}, bf16[384,384]{1,0:T(8,128)(2,1)S(1)}, u32[]{:S(2)}, u32[]{:S(2)}) collective-permute-start(bf16[384,384]{1,0:T(8,128)(2,1)S(1)} %get-tuple-element.336.refs_2_), channel_id=1, source_target_pairs={{0,4},{4,0},{8,12},{12,8},{16,20},{20,16},{24,28},{28,24},{1,5},{5... | collective-permute-start | bytes 884744 | tf_op jit(solution)/shard_map/ppermute | solution.py:47
  145.4 11.0 %collective-permute-start.44 = (bf16[384,384]{1,0:T(8,128)(2,1)S(1)}, bf16[384,384]{1,0:T(8,128)(2,1)S(1)}, u32[]{:S(2)}, u32[]{:S(2)}) collective-permute-start(bf16[384,384]{1,0:T(8,128)(2,1)S(1)} %get-tuple-element.332.refs_2_), channel_id=1, source_target_pairs={{0,8},{4,12},{8,0},{12,4},{16,24},{20,28},{24,16},{28,20},{1,9},{5... | collective-permute-start | bytes 884744 | tf_op jit(solution)/shard_map/ppermute | solution.py:47
  145.7 10.7 %collective-permute-start.45 = (bf16[208,384]{1,0:T(8,128)(2,1)S(1)}, bf16[208,384]{1,0:T(8,128)(2,1)S(1)}, u32[]{:S(2)}, u32[]{:S(2)}) collective-permute-start(bf16[208,384]{1,0:T(8,128)(2,1)S(1)} %get-tuple-element.316.refs_0_), channel_id=1, source_target_pairs={{0,8},{4,12},{8,0},{12,4},{16,24},{20,28},{24,16},{28,20},{1,9},{5... | collective-permute-start | bytes 479240 | tf_op jit(solution)/shard_map/ppermute | solution.py:47
  147.5 7.8 %collective-permute-start.46 = (bf16[192,384]{1,0:T(8,128)(2,1)S(1)}, bf16[192,384]{1,0:T(8,128)(2,1)S(1)}, u32[]{:S(2)}, u32[]{:S(2)}) collective-permute-start(bf16[192,384]{1,0:T(8,128)(2,1)S(1)} %get-tuple-element.318.refs_2_), channel_id=1, source_target_pairs={{0,4},{4,0},{8,12},{12,8},{16,20},{20,16},{24,28},{28,24},{1,5},{5... | collective-permute-start | bytes 442376 | tf_op jit(solution)/shard_map/ppermute | solution.py:47
  (25 other events, 223.3 us)

commit v7 on v6

--- a/solution.py
+++ b/solution.py
@@ -717,7 +717,7 @@
     right[...] = last.T if flip else last
 
 
-def first_end_kernel(bit, mine, got, left, right, *refs):
+def end_kernel(bit_a, bit_b, mine, got, mine_b, got_b, left, right, left_b, right_b, *refs):
     outs, held, sems = refs[:9], refs[9:18], refs[18]
     small = extra_sum(mine, got)
     half = small.shape[1]
@@ -732,13 +732,10 @@
     for ref, line in zip(held, lines):
         ref[...] = line.reshape(line.shape[1])
     copies = start_copies(list(zip(held, outs)), sems)
-    attention_end(bit, False, mine, got, left, right)
+    attention_end(bit_a, False, mine, got, left, right)
+    attention_end(bit_b, True, mine_b, got_b, left_b, right_b)
     for copy in copies:
         copy.wait()
-
-
-def second_end_kernel(bit, mine, got, left, right):
-    attention_end(bit, True, mine, got, left, right)
 
 
 def end_call(kernel, grid, out_shape, block, index, *operands):
@@ -964,16 +961,15 @@
     outs = (shape((half, wide), F32),) * 2
     mine_a, got_a, mine_b, got_b = attention.state
     sizes = (third, third, half, 2 * half, half, half, half, half, half)
-    grad_query, grad_key, *vector_grads = call(
-        lambda *refs: first_end_kernel(bits[0], *refs),
-        outs + tuple(shape((size,), F32) for size in sizes),
+    grad_query, grad_key, grad_value, grad_out, *vector_grads = call(
+        lambda *refs: end_kernel(bits[0], turned[0], *refs),
+        outs + outs + tuple(shape((size,), F32) for size in sizes),
         mine_a,
         got_a,
-        hbm_out=range(2, 11),
+        mine_b,
+        got_b,
+        hbm_out=range(4, 13),
         scratch=[pltpu.VMEM((size,), F32) for size in sizes] + [pltpu.SemaphoreType.DMA((9,))],
-    )
-    grad_value, grad_out = call(
-        lambda *refs: second_end_kernel(turned[0], *refs), outs, mine_b, got_b
     )
     a_0, got_a_0, b_0, got_b_0, a_1, got_a_1, b_1, got_b_1 = feed.state
     grad_down = end_call(

time: 167 us -> 167 us (level)
    pallas_call x23 -> x22, Pallas kernels: 28.7 us -> 28.2 us  [call(): pl.pallas_call(kernel, out_shape=out_shape, in_specs=[pl.BlockSpec(memory...]
where the time goes in v7:
time: 167 us
  waiting for transfers between devices  81.3 us (49%)
  starting transfers between devices  50.6 us (30%)
  Pallas kernels  32.2 us (19%)
    ppermute x26, waiting for transfers between devices, from_dp(): return lax.ppermute(values, 'dp', dp_pairs(bit))  45.2 us
    ppermute x26, starting transfers between devices, from_dp(): return lax.ppermute(values, 'dp', dp_pairs(bit))  33.2 us
    ppermute x11, waiting for transfers between devices, from_row(): return lax.ppermute(values, 'row', SWAP)  30.9 us
    pallas_call x22, Pallas kernels, call(): pl.pallas_call(kernel, out_shape=out_shape, in_specs=[pl.BlockSpec(memory...  28.2 us
    ppermute x11, starting transfers between devices, from_row(): return lax.ppermute(values, 'row', SWAP)  14.4 us
    ppermute x2, waiting for transfers between devices, from_both(): return lax.ppermute(values, ('dp', 'row'), pairs)  5.07 us
    pallas_call x2, Pallas kernels, end_call(): pl.pallas_call(kernel, grid=grid, out_shape=out_shape, in_specs=[whole] *...  4.01 us
  transfers between devices with their start and end apart: 49, of which 23 were waited for; matrix products, arithmetic and copies ran while one was open for 0% of the time, Pallas kernels for 13%

profile of v7, /device:TPU:0, one launch (start us, length us, event | category | flops | bytes accessed | tf_op | source)
XLA Modules:
  0.0 166.9 jit_solution(13505870169857133438)
XLA Ops:
  0.7 2.9 %shard_map.305 = (bf16[400,576]{1,0:T(8,128)(2,1)}, bf16[208,576]{1,0:T(8,128)(2,1)}, bf16[192,384]{1,0:T(8,128)(2,1)}, bf16[192,768]{1,0:T(8,128)(2,1)}, bf16[384,384]{1,0:T(8,128)(2,1)}) custom-call(bf16[384]{0:T(512)(128)(2,1)} %refs_0_.3, bf16[384]{0:T(512)(128)(2,1)} %refs_1_.2, bf16[384]{0:T(512)(128)(2,1)} %refs_2_.1, bf16[384]{0:T(512)(128)(2,1)} %refs_3_.2, ...), custom_call_target="tpu_custom_call" | custom-call | tf_op jit(solution)/shard_map/pallas_call | solution.py:69
  3.6 3.0 %collective-permute-start.3 = (bf16[208,576]{1,0:T(8,128)(2,1)}, bf16[208,576]{1,0:T(8,128)(2,1)S(1)}, u32[]{:S(2)}, u32[]{:S(2)}) collective-permute-start(bf16[208,576]{1,0:T(8,128)(2,1)} %get-tuple-element.182), channel_id=1, source_target_pairs={{0,2},{2,0},{1,3},{3,1},{4,6},{6,4},{5,7},{7,5},{8,10},{10,8},{9,1... | collective-permute-start | bytes 718856 | tf_op jit(solution)/shard_map/ppermute | solution.py:34
  6.8 1.9 %collective-permute-start.5 = (bf16[192,768]{1,0:T(8,128)(2,1)}, bf16[192,768]{1,0:T(8,128)(2,1)S(1)}, u32[]{:S(2)}, u32[]{:S(2)}) collective-permute-start(bf16[192,768]{1,0:T(8,128)(2,1)} %get-tuple-element.183), channel_id=1, source_target_pairs={{0,2},{2,0},{1,3},{3,1},{4,6},{6,4},{5,7},{7,5},{8,10},{10,8},{9,1... | collective-permute-start | bytes 884744 | tf_op jit(solution)/shard_map/ppermute | solution.py:34
  8.7 5.4 %collective-permute-done.3.got.sent.refs_12_ = bf16[208,576]{1,0:T(8,128)(2,1)S(1)} collective-permute-done((bf16[208,576]{1,0:T(8,128)(2,1)}, bf16[208,576]{1,0:T(8,128)(2,1)S(1)}, u32[]{:S(2)}, u32[]{:S(2)}) %collective-permute-start.3) | collective-permute-done | bytes 239648 | tf_op jit(solution)/shard_map/ppermute | solution.py:34
  14.1 2.0 %collective-permute-start.4 = (bf16[208,576]{1,0:T(8,128)(2,1)S(1)}, bf16[208,576]{1,0:T(8,128)(2,1)S(1)}, u32[]{:S(2)}, u32[]{:S(2)}) collective-permute-start(bf16[208,576]{1,0:T(8,128)(2,1)S(1)} %collective-permute-done.3.got.sent.refs_12_), channel_id=1, source_target_pairs={{0,4},{4,0},{8,12},{12,8},{16,20},{20,16},{24,28},{28,24},{1,5},{5... | collective-permute-start | bytes 718856 | tf_op jit(solution)/shard_map/ppermute | solution.py:47
  16.1 2.2 %collective-permute-done.own_far = bf16[256,384]{1,0:T(8,128)(2,1)S(1)} collective-permute-done((bf16[256,384]{1,0:T(8,128)(2,1)S(1)}, bf16[256,384]{1,0:T(8,128)(2,1)S(1)}, u32[]{:S(2)}, u32[]{:S(2)}) %collective-permute-start) | collective-permute-done | bytes 196640 | tf_op jit(solution)/shard_map/ppermute | solution.py:34
  18.3 5.5 %collective-permute-done.5.got = bf16[192,768]{1,0:T(8,128)(2,1)S(1)} collective-permute-done((bf16[192,768]{1,0:T(8,128)(2,1)}, bf16[192,768]{1,0:T(8,128)(2,1)S(1)}, u32[]{:S(2)}, u32[]{:S(2)}) %collective-permute-start.5) | collective-permute-done | bytes 294944 | tf_op jit(solution)/shard_map/ppermute | solution.py:34
  23.8 1.7 %collective-permute-start.7 = (bf16[192,384]{1,0:T(8,128)(2,1)}, bf16[192,384]{1,0:T(8,128)(2,1)S(1)}, u32[]{:S(2)}, u32[]{:S(2)}) collective-permute-start(bf16[192,384]{1,0:T(8,128)(2,1)} %get-tuple-element.193), channel_id=1, source_target_pairs={{0,2},{2,0},{1,3},{3,1},{4,6},{6,4},{5,7},{7,5},{8,10},{10,8},{9,1... | collective-permute-start | bytes 442376 | tf_op jit(solution)/shard_map/ppermute | solution.py:34
  28.6 4.4 %shard_map.306 = (bf16[512,768]{1,0:T(8,128)(2,1)S(1)}, bf16[512,192]{1,0:T(8,128)(2,1)S(1)}, bf16[512,192]{1,0:T(8,128)(2,1)S(1)}, bf16[512,192]{1,0:T(8,128)(2...) custom-call(s32[1,2]{1,0:T(1,128)S(1)} %copy-done.7, bf16[256,384]{1,0:T(8,128)(2,1)S(1)} %copy-done.5, ...), custom_call_target="tpu_custom_call" | custom-call | tf_op jit(solution)/shard_map/pallas_call | solution.py:69
  35.1 5.9 %collective-permute-done.6.mixed_other = bf16[512,192]{1,0:T(8,128)(2,1)S(1)} collective-permute-done((bf16[512,192]{1,0:T(8,128)(2,1)S(1)}, bf16[512,192]{1,0:T(8,128)(2,1)S(1)}, u32[]{:S(2)}, u32[]{:S(2)}) %collective-permute-start.6) | collective-permute-done | bytes 196640 | tf_op jit(solution)/shard_map/ppermute | solution.py:34
  49.6 2.7 %collective-permute-done.15.refs_10_ = bf16[384,384]{1,0:T(8,128)(2,1)S(1)} collective-permute-done((bf16[384,384]{1,0:T(8,128)(2,1)S(1)}, bf16[384,384]{1,0:T(8,128)(2,1)S(1)}, u32[]{:S(2)}, u32[]{:S(2)}) %collective-permute-start.15) | collective-permute-done | bytes 294944 | tf_op jit(solution)/shard_map/ppermute | solution.py:47
  52.4 4.2 %shard_map.310 = (bf16[2,384,384]{2,1,0:T(8,128)(2,1)S(1)}, bf16[2,384,384]{2,1,0:T(8,128)(2,1)S(1)}, bf16[2,384,384]{2,1,0:T(8,128)(2,1)S(1)}, bf16[2,384,384]{...) custom-call(s32[1,2]{1,0:T(1,128)S(1)} %copy-done.7, ...), custom_call_target="tpu_custom_call" | custom-call | tf_op jit(solution)/shard_map/pallas_call | solution.py:69
  62.2 7.6 %collective-permute-done.19.total_far = bf16[256,768]{1,0:T(8,128)(2,1)S(1)} collective-permute-done((bf16[256,768]{1,0:T(8,128)(2,1)S(1)}, bf16[256,768]{1,0:T(8,128)(2,1)S(1)}, u32[]{:S(2)}, u32[]{:S(2)}) %collective-permute-start.19) | collective-permute-done | bytes 393248 | tf_op jit(solution)/shard_map/ppermute | solution.py:34
  70.9 3.3 %collective-permute-done.16.refs_1_ = bf16[2,384,384]{2,1,0:T(8,128)(2,1)S(1)} collective-permute-done((bf16[2,384,384]{2,1,0:T(8,128)(2,1)S(1)}, bf16[2,384,384]{2,1,0:T(8,128)(2,1)S(1)}, u32[]{:S(2)}, u32[]{:S(2)}) %collective-permute-start.16) | collective-permute-done | bytes 589856 | tf_op jit(solution)/shard_map/ppermute | solution.py:47
  77.9 6.1 %shard_map.314 = (bf16[2,192,384]{2,1,0:T(8,128)(2,1)S(1)}, bf16[2,192,384]{2,1,0:T(8,128)(2,1)S(1)}, bf16[2,192,384]{2,1,0:T(8,128)(2,1)S(1)}, bf16[2,192,384]{...) custom-call(s32[1,2]{1,0:T(1,128)S(1)} %copy-done.7, ...), custom_call_target="tpu_custom_call" | custom-call | tf_op jit(solution)/shard_map/pallas_call | solution.py:69
  86.3 2.7 %collective-permute-start.28 = (bf16[2,96,384]{2,1,0:T(8,128)(2,1)S(1)}, bf16[2,96,384]{2,1,0:T(8,128)(2,1)S(1)}, u32[]{:S(2)}, u32[]{:S(2)}) collective-permute-start(bf16[2,96,384]{2,1,0:T(8,128)(2,1)S(1)} %get-tuple-element.266), channel_id=1, source_target_pairs={{0,16},{4,20},{8,24},{12,28},{16,0},{20,4},{24,8},{28,12},{1,17},{... | collective-permute-start | bytes 442376 | tf_op jit(solution)/shard_map/ppermute | solution.py:47
  91.4 2.8 %collective-permute-done.25.refs_1_ = bf16[2,192,384]{2,1,0:T(8,128)(2,1)S(1)} collective-permute-done((bf16[2,192,384]{2,1,0:T(8,128)(2,1)S(1)}, bf16[2,192,384]{2,1,0:T(8,128)(2,1)S(1)}, u32[]{:S(2)}, u32[]{:S(2)}) %collective-permute-start.25) | collective-permute-done | bytes 294944 | tf_op jit(solution)/shard_map/ppermute | solution.py:47
  94.1 6.9 %collective-permute-done.26.refs_3_ = bf16[2,192,384]{2,1,0:T(8,128)(2,1)S(1)} collective-permute-done((bf16[2,192,384]{2,1,0:T(8,128)(2,1)S(1)}, bf16[2,192,384]{2,1,0:T(8,128)(2,1)S(1)}, u32[]{:S(2)}, u32[]{:S(2)}) %collective-permute-start.26) | collective-permute-done | bytes 294944 | tf_op jit(solution)/shard_map/ppermute | solution.py:47
  103.9 4.2 %collective-permute-start.32 = (bf16[2,96,384]{2,1,0:T(8,128)(2,1)S(1)}, bf16[2,96,384]{2,1,0:T(8,128)(2,1)S(1)}, u32[]{:S(2)}, u32[]{:S(2)}) collective-permute-start(bf16[2,96,384]{2,1,0:T(8,128)(2,1)S(1)} %get-tuple-element.274), channel_id=1, source_target_pairs={{0,8},{4,12},{8,0},{12,4},{16,24},{20,28},{24,16},{28,20},{1,9},{5... | collective-permute-start | bytes 442376 | tf_op jit(solution)/shard_map/ppermute | solution.py:47
  109.2 2.5 %collective-permute-done.27.got = bf16[528,384]{1,0:T(8,128)(2,1)S(1)} collective-permute-done((bf16[528,384]{1,0:T(8,128)(2,1)S(1)}, bf16[528,384]{1,0:T(8,128)(2,1)S(1)}, u32[]{:S(2)}, u32[]{:S(2)}) %collective-permute-start.27) | collective-permute-done | bytes 405536 | tf_op jit(solution)/shard_map/ppermute | solution.py:34
  112.9 5.1 %collective-permute-done.31.refs_1_ = bf16[2,2,96,384]{3,2,1,0:T(8,128)(2,1)S(1)} collective-permute-done((bf16[2,2,96,384]{3,2,1,0:T(8,128)(2,1)S(1)}, bf16[2,2,96,384]{3,2,1,0:T(8,128)(2,1)S(1)}, u32[]{:S(2)}, u32[]{:S(2)}) %collective-permute-start.31) | collective-permute-done | bytes 294944 | tf_op jit(solution)/shard_map/ppermute | solution.py:47
  119.5 2.5 %collective-permute-start.36 = (bf16[2,48,384]{2,1,0:T(8,128)(2,1)S(1)}, bf16[2,48,384]{2,1,0:T(8,128)(2,1)S(1)}, u32[]{:S(2)}, u32[]{:S(2)}) collective-permute-start(bf16[2,48,384]{2,1,0:T(8,128)(2,1)S(1)} %get-tuple-element.287), channel_id=1, source_target_pairs={{0,16},{4,20},{8,24},{12,28},{16,0},{20,4},{24,8},{28,12},{1,17},{... | collective-permute-start | bytes 221192 | tf_op jit(solution)/shard_map/ppermute | solution.py:47
  123.9 2.2 %collective-permute-done.36.from_dp_ref = bf16[2,48,384]{2,1,0:T(8,128)(2,1)S(1)} collective-permute-done((bf16[2,48,384]{2,1,0:T(8,128)(2,1)S(1)}, bf16[2,48,384]{2,1,0:T(8,128)(2,1)S(1)}, u32[]{:S(2)}, u32[]{:S(2)}) %collective-permute-start.36) | collective-permute-done | bytes 73760 | tf_op jit(solution)/shard_map/ppermute | solution.py:47
  126.4 5.1 %collective-permute-done.38.from_both_ref = bf16[2,48,384]{2,1,0:T(8,128)(2,1)S(1)} collective-permute-done((bf16[2,48,384]{2,1,0:T(8,128)(2,1)S(1)}, bf16[2,48,384]{2,1,0:T(8,128)(2,1)S(1)}, u32[]{:S(2)}, u32[]{:S(2)}) %collective-permute-start.38) | collective-permute-done | bytes 73760 | tf_op jit(solution)/shard_map/ppermute | solution.py:578
  134.3 7.8 %collective-permute-done.42.refs_1_ = bf16[208,384]{1,0:T(8,128)(2,1)S(1)} collective-permute-done((bf16[208,384]{1,0:T(8,128)(2,1)S(1)}, bf16[208,384]{1,0:T(8,128)(2,1)S(1)}, u32[]{:S(2)}, u32[]{:S(2)}) %collective-permute-start.42) | collective-permute-done | bytes 159776 | tf_op jit(solution)/shard_map/ppermute | solution.py:47
  142.1 2.2 %collective-permute-done.41.refs_1_ = bf16[384,384]{1,0:T(8,128)(2,1)S(1)} collective-permute-done((bf16[384,384]{1,0:T(8,128)(2,1)S(1)}, bf16[384,384]{1,0:T(8,128)(2,1)S(1)}, u32[]{:S(2)}, u32[]{:S(2)}) %collective-permute-start.41) | collective-permute-done | bytes 294944 | tf_op jit(solution)/shard_map/ppermute | solution.py:47
  145.7 1.9 %collective-permute-start.45 = (bf16[208,384]{1,0:T(8,128)(2,1)S(1)}, bf16[208,384]{1,0:T(8,128)(2,1)S(1)}, u32[]{:S(2)}, u32[]{:S(2)}) collective-permute-start(bf16[208,384]{1,0:T(8,128)(2,1)S(1)} %get-tuple-element.316.refs_0_), channel_id=1, source_target_pairs={{0,8},{4,12},{8,0},{12,4},{16,24},{20,28},{24,16},{28,20},{1,9},{5... | collective-permute-start | bytes 479240 | tf_op jit(solution)/shard_map/ppermute | solution.py:47
  148.5 6.8 %collective-permute-done.46.refs_3_ = bf16[192,384]{1,0:T(8,128)(2,1)S(1)} collective-permute-done((bf16[192,384]{1,0:T(8,128)(2,1)S(1)}, bf16[192,384]{1,0:T(8,128)(2,1)S(1)}, u32[]{:S(2)}, u32[]{:S(2)}) %collective-permute-start.46) | collective-permute-done | bytes 147488 | tf_op jit(solution)/shard_map/ppermute | solution.py:47
  157.7 2.0 %shard_map.327 = f32[384,1536]{1,0:T(8,128)} custom-call(bf16[384,384]{1,0:T(8,128)(2,1)S(1)} %get-tuple-element.330.refs_0_, bf16[384,384]{1,0:T(8,128)(2,1)S(1)} %collective-permute-done.41.refs_1_, bf16[384,384]{1,0:T(8,128)(2,1)S(1)} %get-tuple-element.332.refs_2_, bf16[384,384]{1,0:T(8,128)(2,1)S(1)} %collective-permute-done.44.refs_3_), custom_call_target="tpu_custom_call" | custom-call | tf_op jit(solution)/shard_map/pallas_call | solution.py:743
  159.8 2.0 %shard_map.328 = f32[1536,384]{1,0:T(8,128)} custom-call(bf16[384,384]{1,0:T(8,128)(2,1)S(1)} %get-tuple-element.334.refs_0_, bf16[384,384]{1,0:T(8,128)(2,1)S(1)} %collective-permute-done.40.refs_1_, bf16[384,384]{1,0:T(8,128)(2,1)S(1)} %get-tuple-element.336.refs_2_, bf16[384,384]{1,0:T(8,128)(2,1)S(1)} %collective-permute-done.43.refs_3_), custom_call_target="tpu_custom_call" | custom-call | tf_op jit(solution)/shard_map/pallas_call | solution.py:743
  161.8 2.4 %collective-permute-done.48.refs_3_ = bf16[384,384]{1,0:T(8,128)(2,1)S(1)} collective-permute-done((bf16[384,384]{1,0:T(8,128)(2,1)S(1)}, bf16[384,384]{1,0:T(8,128)(2,1)S(1)}, u32[]{:S(2)}, u32[]{:S(2)}) %collective-permute-start.48) | collective-permute-done | bytes 294944 | tf_op jit(solution)/shard_map/ppermute | solution.py:47
  164.2 2.5 %shard_map.326 = (f32[384,384]{1,0:T(8,128)}, f32[384,384]{1,0:T(8,128)}, f32[384,384]{1,0:T(8,128)}, f32[384,384]{1,0:T(8,128)}, f32[192]{0:T(256)}, /*index=5*...) custom-call(bf16[400,384]{1,0:T(8,128)(2,1)S(1)} %get-tuple-element., ...), custom_call_target="tpu_custom_call" | custom-call | tf_op jit(solution)/shard_map/pallas_call | solution.py:69
  (107 shorter events, 45.3 us)
Async XLA Ops:
  3.6 10.5 %collective-permute-start.3 = (bf16[208,576]{1,0:T(8,128)(2,1)}, bf16[208,576]{1,0:T(8,128)(2,1)S(1)}, u32[]{:S(2)}, u32[]{:S(2)}) collective-permute-start(bf16[208,576]{1,0:T(8,128)(2,1)} %get-tuple-element.182), channel_id=1, source_target_pairs={{0,2},{2,0},{1,3},{3,1},{4,6},{6,4},{5,7},{7,5},{8,10},{10,8},{9,1... | collective-permute-start | bytes 718856 | tf_op jit(solution)/shard_map/ppermute | solution.py:34
  6.7 11.6 %collective-permute-start = (bf16[256,384]{1,0:T(8,128)(2,1)S(1)}, bf16[256,384]{1,0:T(8,128)(2,1)S(1)}, u32[]{:S(2)}, u32[]{:S(2)}) collective-permute-start(bf16[256,384]{1,0:T(8,128)(2,1)S(1)} %copy-done.5), channel_id=1, source_target_pairs={{0,2},{2,0},{1,3},{3,1},{4,6},{6,4},{5,7},{7,5},{8,10},{10,8},{9,1... | collective-permute-start | bytes 589832 | tf_op jit(solution)/shard_map/ppermute | solution.py:34
  6.8 17.0 %collective-permute-start.5 = (bf16[192,768]{1,0:T(8,128)(2,1)}, bf16[192,768]{1,0:T(8,128)(2,1)S(1)}, u32[]{:S(2)}, u32[]{:S(2)}) collective-permute-start(bf16[192,768]{1,0:T(8,128)(2,1)} %get-tuple-element.183), channel_id=1, source_target_pairs={{0,2},{2,0},{1,3},{3,1},{4,6},{6,4},{5,7},{7,5},{8,10},{10,8},{9,1... | collective-permute-start | bytes 884744 | tf_op jit(solution)/shard_map/ppermute | solution.py:34
  14.1 9.7 %collective-permute-start.4 = (bf16[208,576]{1,0:T(8,128)(2,1)S(1)}, bf16[208,576]{1,0:T(8,128)(2,1)S(1)}, u32[]{:S(2)}, u32[]{:S(2)}) collective-permute-start(bf16[208,576]{1,0:T(8,128)(2,1)S(1)} %collective-permute-done.3.got.sent.refs_12_), channel_id=1, source_target_pairs={{0,4},{4,0},{8,12},{12,8},{16,20},{20,16},{24,28},{28,24},{1,5},{5... | collective-permute-start | bytes 718856 | tf_op jit(solution)/shard_map/ppermute | solution.py:47
  23.8 10.8 %collective-permute-start.7 = (bf16[192,384]{1,0:T(8,128)(2,1)}, bf16[192,384]{1,0:T(8,128)(2,1)S(1)}, u32[]{:S(2)}, u32[]{:S(2)}) collective-permute-start(bf16[192,384]{1,0:T(8,128)(2,1)} %get-tuple-element.193), channel_id=1, source_target_pairs={{0,2},{2,0},{1,3},{3,1},{4,6},{6,4},{5,7},{7,5},{8,10},{10,8},{9,1... | collective-permute-start | bytes 442376 | tf_op jit(solution)/shard_map/ppermute | solution.py:34
  25.5 15.4 %collective-permute-start.10 = (bf16[384,384]{1,0:T(8,128)(2,1)}, bf16[384,384]{1,0:T(8,128)(2,1)S(1)}, u32[]{:S(2)}, u32[]{:S(2)}) collective-permute-start(bf16[384,384]{1,0:T(8,128)(2,1)} %get-tuple-element.195), channel_id=1, source_target_pairs={{0,2},{2,0},{1,3},{3,1},{4,6},{6,4},{5,7},{7,5},{8,10},{10,8},{9,1... | collective-permute-start | bytes 884744 | tf_op jit(solution)/shard_map/ppermute | solution.py:34
  25.8 15.2 %collective-permute-start.9 = (bf16[192,768]{1,0:T(8,128)(2,1)S(1)}, bf16[192,768]{1,0:T(8,128)(2,1)S(1)}, u32[]{:S(2)}, u32[]{:S(2)}) collective-permute-start(bf16[192,768]{1,0:T(8,128)(2,1)S(1)} %collective-permute-done.5.got), channel_id=1, source_target_pairs={{0,4},{4,0},{8,12},{12,8},{16,20},{20,16},{24,28},{28,24},{1,5},{5... | collective-permute-start | bytes 884744 | tf_op jit(solution)/shard_map/ppermute | solution.py:47
  33.0 8.0 %collective-permute-start.6 = (bf16[512,192]{1,0:T(8,128)(2,1)S(1)}, bf16[512,192]{1,0:T(8,128)(2,1)S(1)}, u32[]{:S(2)}, u32[]{:S(2)}) collective-permute-start(bf16[512,192]{1,0:T(8,128)(2,1)S(1)} %get-tuple-element.192.mixed.refs_8_), channel_id=1, source_target_pairs={{0,2},{2,0},{1,3},{3,1},{4,6},{6,4},{5,7},{7,5},{8,10},{10,8},{9,1... | collective-permute-start | bytes 589832 | tf_op jit(solution)/shard_map/ppermute | solution.py:34
  43.3 9.1 %collective-permute-start.15 = (bf16[384,384]{1,0:T(8,128)(2,1)S(1)}, bf16[384,384]{1,0:T(8,128)(2,1)S(1)}, u32[]{:S(2)}, u32[]{:S(2)}) collective-permute-start(bf16[384,384]{1,0:T(8,128)(2,1)S(1)} %collective-permute-done.10.refs_9_), channel_id=1, source_target_pairs={{0,8},{4,12},{8,0},{12,4},{16,24},{20,28},{24,16},{28,20},{1,9},{5... | collective-permute-start | bytes 884744 | tf_op jit(solution)/shard_map/ppermute | solution.py:47
  58.5 11.2 %collective-permute-start.19 = (bf16[256,768]{1,0:T(8,128)(2,1)S(1)}, bf16[256,768]{1,0:T(8,128)(2,1)S(1)}, u32[]{:S(2)}, u32[]{:S(2)}) collective-permute-start(bf16[256,768]{1,0:T(8,128)(2,1)S(1)} %add_convert_fusion.total), channel_id=1, source_target_pairs={{0,2},{2,0},{1,3},{3,1},{4,6},{6,4},{5,7},{7,5},{8,10},{10,8},{9,1... | collective-permute-start | bytes 1179656 | tf_op jit(solution)/shard_map/ppermute | solution.py:34
  59.2 15.1 %collective-permute-start.16 = (bf16[2,384,384]{2,1,0:T(8,128)(2,1)S(1)}, bf16[2,384,384]{2,1,0:T(8,128)(2,1)S(1)}, u32[]{:S(2)}, u32[]{:S(2)}) collective-permute-start(bf16[2,384,384]{2,1,0:T(8,128)(2,1)S(1)} %get-tuple-element.213), channel_id=1, source_target_pairs={{0,4},{4,0},{8,12},{12,8},{16,20},{20,16},{24,28},{28,24},{1,5},{5... | collective-permute-start | bytes 1769480 | tf_op jit(solution)/shard_map/ppermute | solution.py:47
  60.6 14.8 %collective-permute-start.17 = (bf16[2,384,384]{2,1,0:T(8,128)(2,1)S(1)}, bf16[2,384,384]{2,1,0:T(8,128)(2,1)S(1)}, u32[]{:S(2)}, u32[]{:S(2)}) collective-permute-start(bf16[2,384,384]{2,1,0:T(8,128)(2,1)S(1)} %get-tuple-element.215), channel_id=1, source_target_pairs={{0,8},{4,12},{8,0},{12,4},{16,24},{20,28},{24,16},{28,20},{1,9},{5... | collective-permute-start | bytes 1769480 | tf_op jit(solution)/shard_map/ppermute | solution.py:47
  75.8 8.2 %collective-permute-start.22 = (bf16[2,192,384]{2,1,0:T(8,128)(2,1)S(1)}, bf16[2,192,384]{2,1,0:T(8,128)(2,1)S(1)}, u32[]{:S(2)}, u32[]{:S(2)}) collective-permute-start(bf16[2,192,384]{2,1,0:T(8,128)(2,1)S(1)} %get-tuple-element.229), channel_id=1, source_target_pairs={{0,8},{4,12},{8,0},{12,4},{16,24},{20,28},{24,16},{28,20},{1,9},{5... | collective-permute-start | bytes 884744 | tf_op jit(solution)/shard_map/ppermute | solution.py:47
  84.7 9.4 %collective-permute-start.25 = (bf16[2,192,384]{2,1,0:T(8,128)(2,1)S(1)}, bf16[2,192,384]{2,1,0:T(8,128)(2,1)S(1)}, u32[]{:S(2)}, u32[]{:S(2)}) collective-permute-start(bf16[2,192,384]{2,1,0:T(8,128)(2,1)S(1)} %get-tuple-element.248), channel_id=1, source_target_pairs={{0,4},{4,0},{8,12},{12,8},{16,20},{20,16},{24,28},{28,24},{1,5},{5... | collective-permute-start | bytes 884744 | tf_op jit(solution)/shard_map/ppermute | solution.py:47
  85.7 15.4 %collective-permute-start.26 = (bf16[2,192,384]{2,1,0:T(8,128)(2,1)S(1)}, bf16[2,192,384]{2,1,0:T(8,128)(2,1)S(1)}, u32[]{:S(2)}, u32[]{:S(2)}) collective-permute-start(bf16[2,192,384]{2,1,0:T(8,128)(2,1)S(1)} %get-tuple-element.250), channel_id=1, source_target_pairs={{0,8},{4,12},{8,0},{12,4},{16,24},{20,28},{24,16},{28,20},{1,9},{5... | collective-permute-start | bytes 884744 | tf_op jit(solution)/shard_map/ppermute | solution.py:47
  86.3 16.3 %collective-permute-start.28 = (bf16[2,96,384]{2,1,0:T(8,128)(2,1)S(1)}, bf16[2,96,384]{2,1,0:T(8,128)(2,1)S(1)}, u32[]{:S(2)}, u32[]{:S(2)}) collective-permute-start(bf16[2,96,384]{2,1,0:T(8,128)(2,1)S(1)} %get-tuple-element.266), channel_id=1, source_target_pairs={{0,16},{4,20},{8,24},{12,28},{16,0},{20,4},{24,8},{28,12},{1,17},{... | collective-permute-start | bytes 442376 | tf_op jit(solution)/shard_map/ppermute | solution.py:47
  89.0 13.6 %collective-permute-start.29 = (bf16[2,96,384]{2,1,0:T(8,128)(2,1)S(1)}, bf16[2,96,384]{2,1,0:T(8,128)(2,1)S(1)}, u32[]{:S(2)}, u32[]{:S(2)}) collective-permute-start(bf16[2,96,384]{2,1,0:T(8,128)(2,1)S(1)} %get-tuple-element.267), channel_id=1, source_target_pairs={{0,2},{2,0},{1,3},{3,1},{4,6},{6,4},{5,7},{7,5},{8,10},{10,8},{9,1... | collective-permute-start | bytes 442376 | tf_op jit(solution)/shard_map/ppermute | solution.py:34
  90.5 12.1 %collective-permute-start.30 = (bf16[2,96,384]{2,1,0:T(8,128)(2,1)S(1)}, bf16[2,96,384]{2,1,0:T(8,128)(2,1)S(1)}, u32[]{:S(2)}, u32[]{:S(2)}) collective-permute-start(bf16[2,96,384]{2,1,0:T(8,128)(2,1)S(1)} %get-tuple-element.268), channel_id=1, source_target_pairs={{0,18},{2,16},{4,22},{6,20},{8,26},{10,24},{12,30},{14,28},{16,2},... | collective-permute-start | bytes 442376 | tf_op jit(solution)/shard_map/ppermute | solution.py:578
  101.1 10.6 %collective-permute-start.27 = (bf16[528,384]{1,0:T(8,128)(2,1)S(1)}, bf16[528,384]{1,0:T(8,128)(2,1)S(1)}, u32[]{:S(2)}, u32[]{:S(2)}) collective-permute-start(bf16[528,384]{1,0:T(8,128)(2,1)S(1)} %get-tuple-element.252), channel_id=1, source_target_pairs={{0,2},{2,0},{1,3},{3,1},{4,6},{6,4},{5,7},{7,5},{8,10},{10,8},{9,1... | collective-permute-start | bytes 1216520 | tf_op jit(solution)/shard_map/ppermute | solution.py:34
  102.7 15.3 %collective-permute-start.31 = (bf16[2,2,96,384]{3,2,1,0:T(8,128)(2,1)S(1)}, bf16[2,2,96,384]{3,2,1,0:T(8,128)(2,1)S(1)}, u32[]{:S(2)}, u32[]{:S(2)}) collective-permute-start(bf16[2,2,96,384]{3,2,1,0:T(8,128)(2,1)S(1)} %shard_map.318.refs_0_), channel_id=1, source_target_pairs={{0,16},{4,20},{8,24},{12,28},{16,0},{20,4},{24,8},{28,12},{1,17},{... | collective-permute-start | bytes 884744 | tf_op jit(solution)/shard_map/ppermute | solution.py:47
  103.9 14.0 %collective-permute-start.32 = (bf16[2,96,384]{2,1,0:T(8,128)(2,1)S(1)}, bf16[2,96,384]{2,1,0:T(8,128)(2,1)S(1)}, u32[]{:S(2)}, u32[]{:S(2)}) collective-permute-start(bf16[2,96,384]{2,1,0:T(8,128)(2,1)S(1)} %get-tuple-element.274), channel_id=1, source_target_pairs={{0,8},{4,12},{8,0},{12,4},{16,24},{20,28},{24,16},{28,20},{1,9},{5... | collective-permute-start | bytes 442376 | tf_op jit(solution)/shard_map/ppermute | solution.py:47
  108.1 9.9 %collective-permute-start.33 = (bf16[2,96,384]{2,1,0:T(8,128)(2,1)S(1)}, bf16[2,96,384]{2,1,0:T(8,128)(2,1)S(1)}, u32[]{:S(2)}, u32[]{:S(2)}) collective-permute-start(bf16[2,96,384]{2,1,0:T(8,128)(2,1)S(1)} %get-tuple-element.276), channel_id=1, source_target_pairs={{0,4},{4,0},{8,12},{12,8},{16,20},{20,16},{24,28},{28,24},{1,5},{5... | collective-permute-start | bytes 442376 | tf_op jit(solution)/shard_map/ppermute | solution.py:47
  118.0 13.5 %collective-permute-start.34 = (bf16[2,192,384]{2,1,0:T(8,128)(2,1)S(1)}, bf16[2,192,384]{2,1,0:T(8,128)(2,1)S(1)}, u32[]{:S(2)}, u32[]{:S(2)}) collective-permute-start(bf16[2,192,384]{2,1,0:T(8,128)(2,1)S(1)} %get-tuple-element.291.refs_0_), channel_id=1, source_target_pairs={{0,8},{4,12},{8,0},{12,4},{16,24},{20,28},{24,16},{28,20},{1,9},{5... | collective-permute-start | bytes 884744 | tf_op jit(solution)/shard_map/ppermute | solution.py:47
  118.1 13.4 %collective-permute-start.35 = (bf16[2,192,384]{2,1,0:T(8,128)(2,1)S(1)}, bf16[2,192,384]{2,1,0:T(8,128)(2,1)S(1)}, u32[]{:S(2)}, u32[]{:S(2)}) collective-permute-start(bf16[2,192,384]{2,1,0:T(8,128)(2,1)S(1)} %get-tuple-element.293.refs_2_), channel_id=1, source_target_pairs={{0,4},{4,0},{8,12},{12,8},{16,20},{20,16},{24,28},{28,24},{1,5},{5... | collective-permute-start | bytes 884744 | tf_op jit(solution)/shard_map/ppermute | solution.py:47
  122.5 8.9 %collective-permute-start.38 = (bf16[2,48,384]{2,1,0:T(8,128)(2,1)S(1)}, bf16[2,48,384]{2,1,0:T(8,128)(2,1)S(1)}, u32[]{:S(2)}, u32[]{:S(2)}) collective-permute-start(bf16[2,48,384]{2,1,0:T(8,128)(2,1)S(1)} %get-tuple-element.289), channel_id=1, source_target_pairs={{0,18},{2,16},{4,22},{6,20},{8,26},{10,24},{12,30},{14,28},{16,2},... | collective-permute-start | bytes 221192 | tf_op jit(solution)/shard_map/ppermute | solution.py:578
  131.7 10.4 %collective-permute-start.40 = (bf16[384,384]{1,0:T(8,128)(2,1)S(1)}, bf16[384,384]{1,0:T(8,128)(2,1)S(1)}, u32[]{:S(2)}, u32[]{:S(2)}) collective-permute-start(bf16[384,384]{1,0:T(8,128)(2,1)S(1)} %get-tuple-element.334.refs_0_), channel_id=1, source_target_pairs={{0,4},{4,0},{8,12},{12,8},{16,20},{20,16},{24,28},{28,24},{1,5},{5... | collective-permute-start | bytes 884744 | tf_op jit(solution)/shard_map/ppermute | solution.py:47
  132.7 11.6 %collective-permute-start.41 = (bf16[384,384]{1,0:T(8,128)(2,1)S(1)}, bf16[384,384]{1,0:T(8,128)(2,1)S(1)}, u32[]{:S(2)}, u32[]{:S(2)}) collective-permute-start(bf16[384,384]{1,0:T(8,128)(2,1)S(1)} %get-tuple-element.330.refs_0_), channel_id=1, source_target_pairs={{0,8},{4,12},{8,0},{12,4},{16,24},{20,28},{24,16},{28,20},{1,9},{5... | collective-permute-start | bytes 884744 | tf_op jit(solution)/shard_map/ppermute | solution.py:47
  132.8 9.3 %collective-permute-start.42 = (bf16[208,384]{1,0:T(8,128)(2,1)S(1)}, bf16[208,384]{1,0:T(8,128)(2,1)S(1)}, u32[]{:S(2)}, u32[]{:S(2)}) collective-permute-start(bf16[208,384]{1,0:T(8,128)(2,1)S(1)} %shard_map.323.refs_0_), channel_id=1, source_target_pairs={{0,16},{4,20},{8,24},{12,28},{16,0},{20,4},{24,8},{28,12},{1,17},{... | collective-permute-start | bytes 479240 | tf_op jit(solution)/shard_map/ppermute | solution.py:47
  144.3 12.1 %collective-permute-start.43 = (bf16[384,384]{1,0:T(8,128)(2,1)S(1)}, bf16[384,384]{1,0:T(8,128)(2,1)S(1)}, u32[]{:S(2)}, u32[]{:S(2)}) collective-permute-start(bf16[384,384]{1,0:T(8,128)(2,1)S(1)} %get-tuple-element.336.refs_2_), channel_id=1, source_target_pairs={{0,4},{4,0},{8,12},{12,8},{16,20},{20,16},{24,28},{28,24},{1,5},{5... | collective-permute-start | bytes 884744 | tf_op jit(solution)/shard_map/ppermute | solution.py:47
  145.4 11.0 %collective-permute-start.44 = (bf16[384,384]{1,0:T(8,128)(2,1)S(1)}, bf16[384,384]{1,0:T(8,128)(2,1)S(1)}, u32[]{:S(2)}, u32[]{:S(2)}) collective-permute-start(bf16[384,384]{1,0:T(8,128)(2,1)S(1)} %get-tuple-element.332.refs_2_), channel_id=1, source_target_pairs={{0,8},{4,12},{8,0},{12,4},{16,24},{20,28},{24,16},{28,20},{1,9},{5... | collective-permute-start | bytes 884744 | tf_op jit(solution)/shard_map/ppermute | solution.py:47
  145.7 10.7 %collective-permute-start.45 = (bf16[208,384]{1,0:T(8,128)(2,1)S(1)}, bf16[208,384]{1,0:T(8,128)(2,1)S(1)}, u32[]{:S(2)}, u32[]{:S(2)}) collective-permute-start(bf16[208,384]{1,0:T(8,128)(2,1)S(1)} %get-tuple-element.316.refs_0_), channel_id=1, source_target_pairs={{0,8},{4,12},{8,0},{12,4},{16,24},{20,28},{24,16},{28,20},{1,9},{5... | collective-permute-start | bytes 479240 | tf_op jit(solution)/shard_map/ppermute | solution.py:47
  147.5 7.8 %collective-permute-start.46 = (bf16[192,384]{1,0:T(8,128)(2,1)S(1)}, bf16[192,384]{1,0:T(8,128)(2,1)S(1)}, u32[]{:S(2)}, u32[]{:S(2)}) collective-permute-start(bf16[192,384]{1,0:T(8,128)(2,1)S(1)} %get-tuple-element.318.refs_2_), channel_id=1, source_target_pairs={{0,4},{4,0},{8,12},{12,8},{16,20},{20,16},{24,28},{28,24},{1,5},{5... | collective-permute-start | bytes 442376 | tf_op jit(solution)/shard_map/ppermute | solution.py:47
  (25 other events, 223.3 us)

commit v8 on v7

--- a/solution.py
+++ b/solution.py
@@ -919,10 +919,13 @@
         hbm=(5, 6, 7, 10),
     )
     keep, send = arrived([feed], keep, send)
+    feed.step()
+    feed_keep, first_send, second_send, send = hold(feed.state[0], first_send, second_send, send)
+    feed.state = (feed_keep,) + feed.state[1:]
     got = from_col(send)
     attention = Pair(first_keep, first_send, second_keep, second_send, bits, turned, False)
     pairs = [feed, attention]
-    feed.step()
+
     mine, raised, out, stats, unit_attn, inverse_attn = call(
         first_back_kernel,
         (

time: 167 us -> 167 us (level)
  no operation moved by 1% of the time
where the time goes in v8:
time: 167 us
  waiting for transfers between devices  81.7 us (49%)
  starting transfers between devices  50.3 us (30%)
  Pallas kernels  32.2 us (19%)
    ppermute x26, waiting for transfers between devices, from_dp(): return lax.ppermute(values, 'dp', dp_pairs(bit))  45.4 us
    ppermute x26, starting transfers between devices, from_dp(): return lax.ppermute(values, 'dp', dp_pairs(bit))  32.9 us
    ppermute x11, waiting for transfers between devices, from_row(): return lax.ppermute(values, 'row', SWAP)  31 us
    pallas_call x22, Pallas kernels, call(): pl.pallas_call(kernel, out_shape=out_shape, in_specs=[pl.BlockSpec(memory...  28.2 us
    ppermute x11, starting transfers between devices, from_row(): return lax.ppermute(values, 'row', SWAP)  14.3 us
    ppermute x2, waiting for transfers between devices, from_both(): return lax.ppermute(values, ('dp', 'row'), pairs)  5.07 us
    pallas_call x2, Pallas kernels, end_call(): pl.pallas_call(kernel, grid=grid, out_shape=out_shape, in_specs=[whole] *...  4.01 us
  transfers between devices with their start and end apart: 49, of which 23 were waited for; matrix products, arithmetic and copies ran while one was open for 0% of the time, Pallas kernels for 13%

profile of v8, /device:TPU:0, one launch (start us, length us, event | category | flops | bytes accessed | tf_op | source)
XLA Modules:
  0.0 167.1 jit_solution(579882748094081150)
XLA Ops:
  0.7 2.9 %shard_map.305 = (bf16[400,576]{1,0:T(8,128)(2,1)}, bf16[208,576]{1,0:T(8,128)(2,1)}, bf16[192,384]{1,0:T(8,128)(2,1)}, bf16[192,768]{1,0:T(8,128)(2,1)}, bf16[384,384]{1,0:T(8,128)(2,1)}) custom-call(bf16[384]{0:T(512)(128)(2,1)} %refs_0_.3, bf16[384]{0:T(512)(128)(2,1)} %refs_1_.2, bf16[384]{0:T(512)(128)(2,1)} %refs_2_.1, bf16[384]{0:T(512)(128)(2,1)} %refs_3_.2, ...), custom_call_target="tpu_custom_call" | custom-call | tf_op jit(solution)/shard_map/pallas_call | solution.py:69
  3.6 3.0 %collective-permute-start.3 = (bf16[208,576]{1,0:T(8,128)(2,1)}, bf16[208,576]{1,0:T(8,128)(2,1)S(1)}, u32[]{:S(2)}, u32[]{:S(2)}) collective-permute-start(bf16[208,576]{1,0:T(8,128)(2,1)} %get-tuple-element.186), channel_id=1, source_target_pairs={{0,2},{2,0},{1,3},{3,1},{4,6},{6,4},{5,7},{7,5},{8,10},{10,8},{9,1... | collective-permute-start | bytes 718856 | tf_op jit(solution)/shard_map/ppermute | solution.py:34
  6.8 1.9 %collective-permute-start.5 = (bf16[192,768]{1,0:T(8,128)(2,1)}, bf16[192,768]{1,0:T(8,128)(2,1)S(1)}, u32[]{:S(2)}, u32[]{:S(2)}) collective-permute-start(bf16[192,768]{1,0:T(8,128)(2,1)} %get-tuple-element.187), channel_id=1, source_target_pairs={{0,2},{2,0},{1,3},{3,1},{4,6},{6,4},{5,7},{7,5},{8,10},{10,8},{9,1... | collective-permute-start | bytes 884744 | tf_op jit(solution)/shard_map/ppermute | solution.py:34
  8.7 5.4 %collective-permute-done.3.got.sent.refs_12_ = bf16[208,576]{1,0:T(8,128)(2,1)S(1)} collective-permute-done((bf16[208,576]{1,0:T(8,128)(2,1)}, bf16[208,576]{1,0:T(8,128)(2,1)S(1)}, u32[]{:S(2)}, u32[]{:S(2)}) %collective-permute-start.3) | collective-permute-done | bytes 239648 | tf_op jit(solution)/shard_map/ppermute | solution.py:34
  14.1 2.0 %collective-permute-start.4 = (bf16[208,576]{1,0:T(8,128)(2,1)S(1)}, bf16[208,576]{1,0:T(8,128)(2,1)S(1)}, u32[]{:S(2)}, u32[]{:S(2)}) collective-permute-start(bf16[208,576]{1,0:T(8,128)(2,1)S(1)} %collective-permute-done.3.got.sent.refs_12_), channel_id=1, source_target_pairs={{0,4},{4,0},{8,12},{12,8},{16,20},{20,16},{24,28},{28,24},{1,5},{5... | collective-permute-start | bytes 718856 | tf_op jit(solution)/shard_map/ppermute | solution.py:47
  16.1 2.2 %collective-permute-done.own_far = bf16[256,384]{1,0:T(8,128)(2,1)S(1)} collective-permute-done((bf16[256,384]{1,0:T(8,128)(2,1)S(1)}, bf16[256,384]{1,0:T(8,128)(2,1)S(1)}, u32[]{:S(2)}, u32[]{:S(2)}) %collective-permute-start) | collective-permute-done | bytes 196640 | tf_op jit(solution)/shard_map/ppermute | solution.py:34
  18.3 5.5 %collective-permute-done.5.got = bf16[192,768]{1,0:T(8,128)(2,1)S(1)} collective-permute-done((bf16[192,768]{1,0:T(8,128)(2,1)}, bf16[192,768]{1,0:T(8,128)(2,1)S(1)}, u32[]{:S(2)}, u32[]{:S(2)}) %collective-permute-start.5) | collective-permute-done | bytes 294944 | tf_op jit(solution)/shard_map/ppermute | solution.py:34
  23.8 1.7 %collective-permute-start.7 = (bf16[192,384]{1,0:T(8,128)(2,1)}, bf16[192,384]{1,0:T(8,128)(2,1)S(1)}, u32[]{:S(2)}, u32[]{:S(2)}) collective-permute-start(bf16[192,384]{1,0:T(8,128)(2,1)} %get-tuple-element.197), channel_id=1, source_target_pairs={{0,2},{2,0},{1,3},{3,1},{4,6},{6,4},{5,7},{7,5},{8,10},{10,8},{9,1... | collective-permute-start | bytes 442376 | tf_op jit(solution)/shard_map/ppermute | solution.py:34
  28.6 4.4 %shard_map.306 = (bf16[512,768]{1,0:T(8,128)(2,1)S(1)}, bf16[512,192]{1,0:T(8,128)(2,1)S(1)}, bf16[512,192]{1,0:T(8,128)(2,1)S(1)}, bf16[512,192]{1,0:T(8,128)(2...) custom-call(s32[1,2]{1,0:T(1,128)S(1)} %copy-done.7, bf16[256,384]{1,0:T(8,128)(2,1)S(1)} %copy-done.5, ...), custom_call_target="tpu_custom_call" | custom-call | tf_op jit(solution)/shard_map/pallas_call | solution.py:69
  35.1 5.9 %collective-permute-done.6.mixed_other = bf16[512,192]{1,0:T(8,128)(2,1)S(1)} collective-permute-done((bf16[512,192]{1,0:T(8,128)(2,1)S(1)}, bf16[512,192]{1,0:T(8,128)(2,1)S(1)}, u32[]{:S(2)}, u32[]{:S(2)}) %collective-permute-start.6) | collective-permute-done | bytes 196640 | tf_op jit(solution)/shard_map/ppermute | solution.py:34
  49.6 2.7 %collective-permute-done.15.refs_10_ = bf16[384,384]{1,0:T(8,128)(2,1)S(1)} collective-permute-done((bf16[384,384]{1,0:T(8,128)(2,1)S(1)}, bf16[384,384]{1,0:T(8,128)(2,1)S(1)}, u32[]{:S(2)}, u32[]{:S(2)}) %collective-permute-start.15) | collective-permute-done | bytes 294944 | tf_op jit(solution)/shard_map/ppermute | solution.py:47
  52.4 4.2 %shard_map.310 = (bf16[2,384,384]{2,1,0:T(8,128)(2,1)S(1)}, bf16[2,384,384]{2,1,0:T(8,128)(2,1)S(1)}, bf16[2,384,384]{2,1,0:T(8,128)(2,1)S(1)}, bf16[2,384,384]{...) custom-call(s32[1,2]{1,0:T(1,128)S(1)} %copy-done.7, ...), custom_call_target="tpu_custom_call" | custom-call | tf_op jit(solution)/shard_map/pallas_call | solution.py:69
  62.2 7.6 %collective-permute-done.19.total_far = bf16[256,768]{1,0:T(8,128)(2,1)S(1)} collective-permute-done((bf16[256,768]{1,0:T(8,128)(2,1)S(1)}, bf16[256,768]{1,0:T(8,128)(2,1)S(1)}, u32[]{:S(2)}, u32[]{:S(2)}) %collective-permute-start.19) | collective-permute-done | bytes 393248 | tf_op jit(solution)/shard_map/ppermute | solution.py:34
  71.0 3.3 %collective-permute-done.16.refs_1_ = bf16[2,384,384]{2,1,0:T(8,128)(2,1)S(1)} collective-permute-done((bf16[2,384,384]{2,1,0:T(8,128)(2,1)S(1)}, bf16[2,384,384]{2,1,0:T(8,128)(2,1)S(1)}, u32[]{:S(2)}, u32[]{:S(2)}) %collective-permute-start.16) | collective-permute-done | bytes 589856 | tf_op jit(solution)/shard_map/ppermute | solution.py:47
  78.0 6.1 %shard_map.314 = (bf16[2,192,384]{2,1,0:T(8,128)(2,1)S(1)}, bf16[2,192,384]{2,1,0:T(8,128)(2,1)S(1)}, bf16[2,192,384]{2,1,0:T(8,128)(2,1)S(1)}, bf16[2,192,384]{...) custom-call(s32[1,2]{1,0:T(1,128)S(1)} %copy-done.7, ...), custom_call_target="tpu_custom_call" | custom-call | tf_op jit(solution)/shard_map/pallas_call | solution.py:69
  86.3 2.6 %collective-permute-start.28 = (bf16[2,96,384]{2,1,0:T(8,128)(2,1)S(1)}, bf16[2,96,384]{2,1,0:T(8,128)(2,1)S(1)}, u32[]{:S(2)}, u32[]{:S(2)}) collective-permute-start(bf16[2,96,384]{2,1,0:T(8,128)(2,1)S(1)} %get-tuple-element.274), channel_id=1, source_target_pairs={{0,16},{4,20},{8,24},{12,28},{16,0},{20,4},{24,8},{28,12},{1,17},{... | collective-permute-start | bytes 442376 | tf_op jit(solution)/shard_map/ppermute | solution.py:47
  91.3 3.1 %collective-permute-done.25.refs_1_ = bf16[2,192,384]{2,1,0:T(8,128)(2,1)S(1)} collective-permute-done((bf16[2,192,384]{2,1,0:T(8,128)(2,1)S(1)}, bf16[2,192,384]{2,1,0:T(8,128)(2,1)S(1)}, u32[]{:S(2)}, u32[]{:S(2)}) %collective-permute-start.25) | collective-permute-done | bytes 294944 | tf_op jit(solution)/shard_map/ppermute | solution.py:47
  94.4 6.9 %collective-permute-done.26.refs_3_ = bf16[2,192,384]{2,1,0:T(8,128)(2,1)S(1)} collective-permute-done((bf16[2,192,384]{2,1,0:T(8,128)(2,1)S(1)}, bf16[2,192,384]{2,1,0:T(8,128)(2,1)S(1)}, u32[]{:S(2)}, u32[]{:S(2)}) %collective-permute-start.26) | collective-permute-done | bytes 294944 | tf_op jit(solution)/shard_map/ppermute | solution.py:47
  104.1 3.9 %collective-permute-start.32 = (bf16[2,96,384]{2,1,0:T(8,128)(2,1)S(1)}, bf16[2,96,384]{2,1,0:T(8,128)(2,1)S(1)}, u32[]{:S(2)}, u32[]{:S(2)}) collective-permute-start(bf16[2,96,384]{2,1,0:T(8,128)(2,1)S(1)} %get-tuple-element.282), channel_id=1, source_target_pairs={{0,8},{4,12},{8,0},{12,4},{16,24},{20,28},{24,16},{28,20},{1,9},{5... | collective-permute-start | bytes 442376 | tf_op jit(solution)/shard_map/ppermute | solution.py:47
  109.2 2.7 %collective-permute-done.27.got = bf16[528,384]{1,0:T(8,128)(2,1)S(1)} collective-permute-done((bf16[528,384]{1,0:T(8,128)(2,1)S(1)}, bf16[528,384]{1,0:T(8,128)(2,1)S(1)}, u32[]{:S(2)}, u32[]{:S(2)}) %collective-permute-start.27) | collective-permute-done | bytes 405536 | tf_op jit(solution)/shard_map/ppermute | solution.py:34
  113.1 5.0 %collective-permute-done.31.refs_1_ = bf16[2,2,96,384]{3,2,1,0:T(8,128)(2,1)S(1)} collective-permute-done((bf16[2,2,96,384]{3,2,1,0:T(8,128)(2,1)S(1)}, bf16[2,2,96,384]{3,2,1,0:T(8,128)(2,1)S(1)}, u32[]{:S(2)}, u32[]{:S(2)}) %collective-permute-start.31) | collective-permute-done | bytes 294944 | tf_op jit(solution)/shard_map/ppermute | solution.py:47
  119.7 2.5 %collective-permute-start.36 = (bf16[2,48,384]{2,1,0:T(8,128)(2,1)S(1)}, bf16[2,48,384]{2,1,0:T(8,128)(2,1)S(1)}, u32[]{:S(2)}, u32[]{:S(2)}) collective-permute-start(bf16[2,48,384]{2,1,0:T(8,128)(2,1)S(1)} %get-tuple-element.295), channel_id=1, source_target_pairs={{0,16},{4,20},{8,24},{12,28},{16,0},{20,4},{24,8},{28,12},{1,17},{... | collective-permute-start | bytes 221192 | tf_op jit(solution)/shard_map/ppermute | solution.py:47
  124.1 2.2 %collective-permute-done.36.from_dp_ref = bf16[2,48,384]{2,1,0:T(8,128)(2,1)S(1)} collective-permute-done((bf16[2,48,384]{2,1,0:T(8,128)(2,1)S(1)}, bf16[2,48,384]{2,1,0:T(8,128)(2,1)S(1)}, u32[]{:S(2)}, u32[]{:S(2)}) %collective-permute-start.36) | collective-permute-done | bytes 73760 | tf_op jit(solution)/shard_map/ppermute | solution.py:47
  126.6 5.1 %collective-permute-done.38.from_both_ref = bf16[2,48,384]{2,1,0:T(8,128)(2,1)S(1)} collective-permute-done((bf16[2,48,384]{2,1,0:T(8,128)(2,1)S(1)}, bf16[2,48,384]{2,1,0:T(8,128)(2,1)S(1)}, u32[]{:S(2)}, u32[]{:S(2)}) %collective-permute-start.38) | collective-permute-done | bytes 73760 | tf_op jit(solution)/shard_map/ppermute | solution.py:578
  134.5 7.8 %collective-permute-done.42.refs_1_ = bf16[208,384]{1,0:T(8,128)(2,1)S(1)} collective-permute-done((bf16[208,384]{1,0:T(8,128)(2,1)S(1)}, bf16[208,384]{1,0:T(8,128)(2,1)S(1)}, u32[]{:S(2)}, u32[]{:S(2)}) %collective-permute-start.42) | collective-permute-done | bytes 159776 | tf_op jit(solution)/shard_map/ppermute | solution.py:47
  142.3 2.2 %collective-permute-done.41.refs_1_ = bf16[384,384]{1,0:T(8,128)(2,1)S(1)} collective-permute-done((bf16[384,384]{1,0:T(8,128)(2,1)S(1)}, bf16[384,384]{1,0:T(8,128)(2,1)S(1)}, u32[]{:S(2)}, u32[]{:S(2)}) %collective-permute-start.41) | collective-permute-done | bytes 294944 | tf_op jit(solution)/shard_map/ppermute | solution.py:47
  145.9 1.9 %collective-permute-start.45 = (bf16[208,384]{1,0:T(8,128)(2,1)S(1)}, bf16[208,384]{1,0:T(8,128)(2,1)S(1)}, u32[]{:S(2)}, u32[]{:S(2)}) collective-permute-start(bf16[208,384]{1,0:T(8,128)(2,1)S(1)} %get-tuple-element.324.refs_0_), channel_id=1, source_target_pairs={{0,8},{4,12},{8,0},{12,4},{16,24},{20,28},{24,16},{28,20},{1,9},{5... | collective-permute-start | bytes 479240 | tf_op jit(solution)/shard_map/ppermute | solution.py:47
  148.7 6.8 %collective-permute-done.46.refs_3_ = bf16[192,384]{1,0:T(8,128)(2,1)S(1)} collective-permute-done((bf16[192,384]{1,0:T(8,128)(2,1)S(1)}, bf16[192,384]{1,0:T(8,128)(2,1)S(1)}, u32[]{:S(2)}, u32[]{:S(2)}) %collective-permute-start.46) | collective-permute-done | bytes 147488 | tf_op jit(solution)/shard_map/ppermute | solution.py:47
  157.9 2.0 %shard_map.327 = f32[384,1536]{1,0:T(8,128)} custom-call(bf16[384,384]{1,0:T(8,128)(2,1)S(1)} %get-tuple-element.338.refs_0_, bf16[384,384]{1,0:T(8,128)(2,1)S(1)} %collective-permute-done.41.refs_1_, bf16[384,384]{1,0:T(8,128)(2,1)S(1)} %get-tuple-element.340.refs_2_, bf16[384,384]{1,0:T(8,128)(2,1)S(1)} %collective-permute-done.44.refs_3_), custom_call_target="tpu_custom_call" | custom-call | tf_op jit(solution)/shard_map/pallas_call | solution.py:743
  160.0 2.0 %shard_map.328 = f32[1536,384]{1,0:T(8,128)} custom-call(bf16[384,384]{1,0:T(8,128)(2,1)S(1)} %get-tuple-element.342.refs_0_, bf16[384,384]{1,0:T(8,128)(2,1)S(1)} %collective-permute-done.40.refs_1_, bf16[384,384]{1,0:T(8,128)(2,1)S(1)} %get-tuple-element.344.refs_2_, bf16[384,384]{1,0:T(8,128)(2,1)S(1)} %collective-permute-done.43.refs_3_), custom_call_target="tpu_custom_call" | custom-call | tf_op jit(solution)/shard_map/pallas_call | solution.py:743
  162.0 2.4 %collective-permute-done.48.refs_3_ = bf16[384,384]{1,0:T(8,128)(2,1)S(1)} collective-permute-done((bf16[384,384]{1,0:T(8,128)(2,1)S(1)}, bf16[384,384]{1,0:T(8,128)(2,1)S(1)}, u32[]{:S(2)}, u32[]{:S(2)}) %collective-permute-start.48) | collective-permute-done | bytes 294944 | tf_op jit(solution)/shard_map/ppermute | solution.py:47
  164.4 2.5 %shard_map.326 = (f32[384,384]{1,0:T(8,128)}, f32[384,384]{1,0:T(8,128)}, f32[384,384]{1,0:T(8,128)}, f32[384,384]{1,0:T(8,128)}, f32[192]{0:T(256)}, /*index=5*...) custom-call(bf16[400,384]{1,0:T(8,128)(2,1)S(1)} %get-tuple-element., ...), custom_call_target="tpu_custom_call" | custom-call | tf_op jit(solution)/shard_map/pallas_call | solution.py:69
  (107 shorter events, 45.4 us)
Async XLA Ops:
  3.6 10.5 %collective-permute-start.3 = (bf16[208,576]{1,0:T(8,128)(2,1)}, bf16[208,576]{1,0:T(8,128)(2,1)S(1)}, u32[]{:S(2)}, u32[]{:S(2)}) collective-permute-start(bf16[208,576]{1,0:T(8,128)(2,1)} %get-tuple-element.186), channel_id=1, source_target_pairs={{0,2},{2,0},{1,3},{3,1},{4,6},{6,4},{5,7},{7,5},{8,10},{10,8},{9,1... | collective-permute-start | bytes 718856 | tf_op jit(solution)/shard_map/ppermute | solution.py:34
  6.7 11.6 %collective-permute-start = (bf16[256,384]{1,0:T(8,128)(2,1)S(1)}, bf16[256,384]{1,0:T(8,128)(2,1)S(1)}, u32[]{:S(2)}, u32[]{:S(2)}) collective-permute-start(bf16[256,384]{1,0:T(8,128)(2,1)S(1)} %copy-done.5), channel_id=1, source_target_pairs={{0,2},{2,0},{1,3},{3,1},{4,6},{6,4},{5,7},{7,5},{8,10},{10,8},{9,1... | collective-permute-start | bytes 589832 | tf_op jit(solution)/shard_map/ppermute | solution.py:34
  6.8 17.0 %collective-permute-start.5 = (bf16[192,768]{1,0:T(8,128)(2,1)}, bf16[192,768]{1,0:T(8,128)(2,1)S(1)}, u32[]{:S(2)}, u32[]{:S(2)}) collective-permute-start(bf16[192,768]{1,0:T(8,128)(2,1)} %get-tuple-element.187), channel_id=1, source_target_pairs={{0,2},{2,0},{1,3},{3,1},{4,6},{6,4},{5,7},{7,5},{8,10},{10,8},{9,1... | collective-permute-start | bytes 884744 | tf_op jit(solution)/shard_map/ppermute | solution.py:34
  14.1 9.7 %collective-permute-start.4 = (bf16[208,576]{1,0:T(8,128)(2,1)S(1)}, bf16[208,576]{1,0:T(8,128)(2,1)S(1)}, u32[]{:S(2)}, u32[]{:S(2)}) collective-permute-start(bf16[208,576]{1,0:T(8,128)(2,1)S(1)} %collective-permute-done.3.got.sent.refs_12_), channel_id=1, source_target_pairs={{0,4},{4,0},{8,12},{12,8},{16,20},{20,16},{24,28},{28,24},{1,5},{5... | collective-permute-start | bytes 718856 | tf_op jit(solution)/shard_map/ppermute | solution.py:47
  23.8 10.8 %collective-permute-start.7 = (bf16[192,384]{1,0:T(8,128)(2,1)}, bf16[192,384]{1,0:T(8,128)(2,1)S(1)}, u32[]{:S(2)}, u32[]{:S(2)}) collective-permute-start(bf16[192,384]{1,0:T(8,128)(2,1)} %get-tuple-element.197), channel_id=1, source_target_pairs={{0,2},{2,0},{1,3},{3,1},{4,6},{6,4},{5,7},{7,5},{8,10},{10,8},{9,1... | collective-permute-start | bytes 442376 | tf_op jit(solution)/shard_map/ppermute | solution.py:34
  25.5 15.4 %collective-permute-start.10 = (bf16[384,384]{1,0:T(8,128)(2,1)}, bf16[384,384]{1,0:T(8,128)(2,1)S(1)}, u32[]{:S(2)}, u32[]{:S(2)}) collective-permute-start(bf16[384,384]{1,0:T(8,128)(2,1)} %get-tuple-element.199), channel_id=1, source_target_pairs={{0,2},{2,0},{1,3},{3,1},{4,6},{6,4},{5,7},{7,5},{8,10},{10,8},{9,1... | collective-permute-start | bytes 884744 | tf_op jit(solution)/shard_map/ppermute | solution.py:34
  25.8 15.2 %collective-permute-start.9 = (bf16[192,768]{1,0:T(8,128)(2,1)S(1)}, bf16[192,768]{1,0:T(8,128)(2,1)S(1)}, u32[]{:S(2)}, u32[]{:S(2)}) collective-permute-start(bf16[192,768]{1,0:T(8,128)(2,1)S(1)} %collective-permute-done.5.got), channel_id=1, source_target_pairs={{0,4},{4,0},{8,12},{12,8},{16,20},{20,16},{24,28},{28,24},{1,5},{5... | collective-permute-start | bytes 884744 | tf_op jit(solution)/shard_map/ppermute | solution.py:47
  33.0 8.0 %collective-permute-start.6 = (bf16[512,192]{1,0:T(8,128)(2,1)S(1)}, bf16[512,192]{1,0:T(8,128)(2,1)S(1)}, u32[]{:S(2)}, u32[]{:S(2)}) collective-permute-start(bf16[512,192]{1,0:T(8,128)(2,1)S(1)} %get-tuple-element.196.mixed.refs_8_), channel_id=1, source_target_pairs={{0,2},{2,0},{1,3},{3,1},{4,6},{6,4},{5,7},{7,5},{8,10},{10,8},{9,1... | collective-permute-start | bytes 589832 | tf_op jit(solution)/shard_map/ppermute | solution.py:34
  43.3 9.1 %collective-permute-start.15 = (bf16[384,384]{1,0:T(8,128)(2,1)S(1)}, bf16[384,384]{1,0:T(8,128)(2,1)S(1)}, u32[]{:S(2)}, u32[]{:S(2)}) collective-permute-start(bf16[384,384]{1,0:T(8,128)(2,1)S(1)} %collective-permute-done.10.refs_9_), channel_id=1, source_target_pairs={{0,8},{4,12},{8,0},{12,4},{16,24},{20,28},{24,16},{28,20},{1,9},{5... | collective-permute-start | bytes 884744 | tf_op jit(solution)/shard_map/ppermute | solution.py:47
  58.5 11.2 %collective-permute-start.19 = (bf16[256,768]{1,0:T(8,128)(2,1)S(1)}, bf16[256,768]{1,0:T(8,128)(2,1)S(1)}, u32[]{:S(2)}, u32[]{:S(2)}) collective-permute-start(bf16[256,768]{1,0:T(8,128)(2,1)S(1)} %add_convert_fusion.total), channel_id=1, source_target_pairs={{0,2},{2,0},{1,3},{3,1},{4,6},{6,4},{5,7},{7,5},{8,10},{10,8},{9,1... | collective-permute-start | bytes 1179656 | tf_op jit(solution)/shard_map/ppermute | solution.py:34
  59.2 15.1 %collective-permute-start.16 = (bf16[2,384,384]{2,1,0:T(8,128)(2,1)S(1)}, bf16[2,384,384]{2,1,0:T(8,128)(2,1)S(1)}, u32[]{:S(2)}, u32[]{:S(2)}) collective-permute-start(bf16[2,384,384]{2,1,0:T(8,128)(2,1)S(1)} %get-tuple-element.217), channel_id=1, source_target_pairs={{0,4},{4,0},{8,12},{12,8},{16,20},{20,16},{24,28},{28,24},{1,5},{5... | collective-permute-start | bytes 1769480 | tf_op jit(solution)/shard_map/ppermute | solution.py:47
  60.6 14.8 %collective-permute-start.17 = (bf16[2,384,384]{2,1,0:T(8,128)(2,1)S(1)}, bf16[2,384,384]{2,1,0:T(8,128)(2,1)S(1)}, u32[]{:S(2)}, u32[]{:S(2)}) collective-permute-start(bf16[2,384,384]{2,1,0:T(8,128)(2,1)S(1)} %get-tuple-element.219), channel_id=1, source_target_pairs={{0,8},{4,12},{8,0},{12,4},{16,24},{20,28},{24,16},{28,20},{1,9},{5... | collective-permute-start | bytes 1769480 | tf_op jit(solution)/shard_map/ppermute | solution.py:47
  75.8 8.2 %collective-permute-start.22 = (bf16[2,192,384]{2,1,0:T(8,128)(2,1)S(1)}, bf16[2,192,384]{2,1,0:T(8,128)(2,1)S(1)}, u32[]{:S(2)}, u32[]{:S(2)}) collective-permute-start(bf16[2,192,384]{2,1,0:T(8,128)(2,1)S(1)} %get-tuple-element.233), channel_id=1, source_target_pairs={{0,8},{4,12},{8,0},{12,4},{16,24},{20,28},{24,16},{28,20},{1,9},{5... | collective-permute-start | bytes 884744 | tf_op jit(solution)/shard_map/ppermute | solution.py:47
  85.0 9.4 %collective-permute-start.25 = (bf16[2,192,384]{2,1,0:T(8,128)(2,1)S(1)}, bf16[2,192,384]{2,1,0:T(8,128)(2,1)S(1)}, u32[]{:S(2)}, u32[]{:S(2)}) collective-permute-start(bf16[2,192,384]{2,1,0:T(8,128)(2,1)S(1)} %get-tuple-element.260), channel_id=1, source_target_pairs={{0,4},{4,0},{8,12},{12,8},{16,20},{20,16},{24,28},{28,24},{1,5},{5... | collective-permute-start | bytes 884744 | tf_op jit(solution)/shard_map/ppermute | solution.py:47
  85.9 15.4 %collective-permute-start.26 = (bf16[2,192,384]{2,1,0:T(8,128)(2,1)S(1)}, bf16[2,192,384]{2,1,0:T(8,128)(2,1)S(1)}, u32[]{:S(2)}, u32[]{:S(2)}) collective-permute-start(bf16[2,192,384]{2,1,0:T(8,128)(2,1)S(1)} %get-tuple-element.262), channel_id=1, source_target_pairs={{0,8},{4,12},{8,0},{12,4},{16,24},{20,28},{24,16},{28,20},{1,9},{5... | collective-permute-start | bytes 884744 | tf_op jit(solution)/shard_map/ppermute | solution.py:47
  86.3 16.4 %collective-permute-start.28 = (bf16[2,96,384]{2,1,0:T(8,128)(2,1)S(1)}, bf16[2,96,384]{2,1,0:T(8,128)(2,1)S(1)}, u32[]{:S(2)}, u32[]{:S(2)}) collective-permute-start(bf16[2,96,384]{2,1,0:T(8,128)(2,1)S(1)} %get-tuple-element.274), channel_id=1, source_target_pairs={{0,16},{4,20},{8,24},{12,28},{16,0},{20,4},{24,8},{28,12},{1,17},{... | collective-permute-start | bytes 442376 | tf_op jit(solution)/shard_map/ppermute | solution.py:47
  88.9 13.9 %collective-permute-start.29 = (bf16[2,96,384]{2,1,0:T(8,128)(2,1)S(1)}, bf16[2,96,384]{2,1,0:T(8,128)(2,1)S(1)}, u32[]{:S(2)}, u32[]{:S(2)}) collective-permute-start(bf16[2,96,384]{2,1,0:T(8,128)(2,1)S(1)} %get-tuple-element.275), channel_id=1, source_target_pairs={{0,2},{2,0},{1,3},{3,1},{4,6},{6,4},{5,7},{7,5},{8,10},{10,8},{9,1... | collective-permute-start | bytes 442376 | tf_op jit(solution)/shard_map/ppermute | solution.py:34
  90.4 12.4 %collective-permute-start.30 = (bf16[2,96,384]{2,1,0:T(8,128)(2,1)S(1)}, bf16[2,96,384]{2,1,0:T(8,128)(2,1)S(1)}, u32[]{:S(2)}, u32[]{:S(2)}) collective-permute-start(bf16[2,96,384]{2,1,0:T(8,128)(2,1)S(1)} %get-tuple-element.276), channel_id=1, source_target_pairs={{0,18},{2,16},{4,22},{6,20},{8,26},{10,24},{12,30},{14,28},{16,2},... | collective-permute-start | bytes 442376 | tf_op jit(solution)/shard_map/ppermute | solution.py:578
  101.3 10.6 %collective-permute-start.27 = (bf16[528,384]{1,0:T(8,128)(2,1)S(1)}, bf16[528,384]{1,0:T(8,128)(2,1)S(1)}, u32[]{:S(2)}, u32[]{:S(2)}) collective-permute-start(bf16[528,384]{1,0:T(8,128)(2,1)S(1)} %get-tuple-element.264), channel_id=1, source_target_pairs={{0,2},{2,0},{1,3},{3,1},{4,6},{6,4},{5,7},{7,5},{8,10},{10,8},{9,1... | collective-permute-start | bytes 1216520 | tf_op jit(solution)/shard_map/ppermute | solution.py:34
  102.9 15.3 %collective-permute-start.31 = (bf16[2,2,96,384]{3,2,1,0:T(8,128)(2,1)S(1)}, bf16[2,2,96,384]{3,2,1,0:T(8,128)(2,1)S(1)}, u32[]{:S(2)}, u32[]{:S(2)}) collective-permute-start(bf16[2,2,96,384]{3,2,1,0:T(8,128)(2,1)S(1)} %shard_map.318.refs_0_), channel_id=1, source_target_pairs={{0,16},{4,20},{8,24},{12,28},{16,0},{20,4},{24,8},{28,12},{1,17},{... | collective-permute-start | bytes 884744 | tf_op jit(solution)/shard_map/ppermute | solution.py:47
  104.1 14.0 %collective-permute-start.32 = (bf16[2,96,384]{2,1,0:T(8,128)(2,1)S(1)}, bf16[2,96,384]{2,1,0:T(8,128)(2,1)S(1)}, u32[]{:S(2)}, u32[]{:S(2)}) collective-permute-start(bf16[2,96,384]{2,1,0:T(8,128)(2,1)S(1)} %get-tuple-element.282), channel_id=1, source_target_pairs={{0,8},{4,12},{8,0},{12,4},{16,24},{20,28},{24,16},{28,20},{1,9},{5... | collective-permute-start | bytes 442376 | tf_op jit(solution)/shard_map/ppermute | solution.py:47
  108.0 10.1 %collective-permute-start.33 = (bf16[2,96,384]{2,1,0:T(8,128)(2,1)S(1)}, bf16[2,96,384]{2,1,0:T(8,128)(2,1)S(1)}, u32[]{:S(2)}, u32[]{:S(2)}) collective-permute-start(bf16[2,96,384]{2,1,0:T(8,128)(2,1)S(1)} %get-tuple-element.284), channel_id=1, source_target_pairs={{0,4},{4,0},{8,12},{12,8},{16,20},{20,16},{24,28},{28,24},{1,5},{5... | collective-permute-start | bytes 442376 | tf_op jit(solution)/shard_map/ppermute | solution.py:47
  118.2 13.5 %collective-permute-start.34 = (bf16[2,192,384]{2,1,0:T(8,128)(2,1)S(1)}, bf16[2,192,384]{2,1,0:T(8,128)(2,1)S(1)}, u32[]{:S(2)}, u32[]{:S(2)}) collective-permute-start(bf16[2,192,384]{2,1,0:T(8,128)(2,1)S(1)} %get-tuple-element.299.refs_0_), channel_id=1, source_target_pairs={{0,8},{4,12},{8,0},{12,4},{16,24},{20,28},{24,16},{28,20},{1,9},{5... | collective-permute-start | bytes 884744 | tf_op jit(solution)/shard_map/ppermute | solution.py:47
  118.3 13.4 %collective-permute-start.35 = (bf16[2,192,384]{2,1,0:T(8,128)(2,1)S(1)}, bf16[2,192,384]{2,1,0:T(8,128)(2,1)S(1)}, u32[]{:S(2)}, u32[]{:S(2)}) collective-permute-start(bf16[2,192,384]{2,1,0:T(8,128)(2,1)S(1)} %get-tuple-element.301.refs_2_), channel_id=1, source_target_pairs={{0,4},{4,0},{8,12},{12,8},{16,20},{20,16},{24,28},{28,24},{1,5},{5... | collective-permute-start | bytes 884744 | tf_op jit(solution)/shard_map/ppermute | solution.py:47
  122.7 8.9 %collective-permute-start.38 = (bf16[2,48,384]{2,1,0:T(8,128)(2,1)S(1)}, bf16[2,48,384]{2,1,0:T(8,128)(2,1)S(1)}, u32[]{:S(2)}, u32[]{:S(2)}) collective-permute-start(bf16[2,48,384]{2,1,0:T(8,128)(2,1)S(1)} %get-tuple-element.297), channel_id=1, source_target_pairs={{0,18},{2,16},{4,22},{6,20},{8,26},{10,24},{12,30},{14,28},{16,2},... | collective-permute-start | bytes 221192 | tf_op jit(solution)/shard_map/ppermute | solution.py:578
  131.9 10.4 %collective-permute-start.40 = (bf16[384,384]{1,0:T(8,128)(2,1)S(1)}, bf16[384,384]{1,0:T(8,128)(2,1)S(1)}, u32[]{:S(2)}, u32[]{:S(2)}) collective-permute-start(bf16[384,384]{1,0:T(8,128)(2,1)S(1)} %get-tuple-element.342.refs_0_), channel_id=1, source_target_pairs={{0,4},{4,0},{8,12},{12,8},{16,20},{20,16},{24,28},{28,24},{1,5},{5... | collective-permute-start | bytes 884744 | tf_op jit(solution)/shard_map/ppermute | solution.py:47
  132.9 11.6 %collective-permute-start.41 = (bf16[384,384]{1,0:T(8,128)(2,1)S(1)}, bf16[384,384]{1,0:T(8,128)(2,1)S(1)}, u32[]{:S(2)}, u32[]{:S(2)}) collective-permute-start(bf16[384,384]{1,0:T(8,128)(2,1)S(1)} %get-tuple-element.338.refs_0_), channel_id=1, source_target_pairs={{0,8},{4,12},{8,0},{12,4},{16,24},{20,28},{24,16},{28,20},{1,9},{5... | collective-permute-start | bytes 884744 | tf_op jit(solution)/shard_map/ppermute | solution.py:47
  133.0 9.3 %collective-permute-start.42 = (bf16[208,384]{1,0:T(8,128)(2,1)S(1)}, bf16[208,384]{1,0:T(8,128)(2,1)S(1)}, u32[]{:S(2)}, u32[]{:S(2)}) collective-permute-start(bf16[208,384]{1,0:T(8,128)(2,1)S(1)} %shard_map.323.refs_0_), channel_id=1, source_target_pairs={{0,16},{4,20},{8,24},{12,28},{16,0},{20,4},{24,8},{28,12},{1,17},{... | collective-permute-start | bytes 479240 | tf_op jit(solution)/shard_map/ppermute | solution.py:47
  144.5 12.1 %collective-permute-start.43 = (bf16[384,384]{1,0:T(8,128)(2,1)S(1)}, bf16[384,384]{1,0:T(8,128)(2,1)S(1)}, u32[]{:S(2)}, u32[]{:S(2)}) collective-permute-start(bf16[384,384]{1,0:T(8,128)(2,1)S(1)} %get-tuple-element.344.refs_2_), channel_id=1, source_target_pairs={{0,4},{4,0},{8,12},{12,8},{16,20},{20,16},{24,28},{28,24},{1,5},{5... | collective-permute-start | bytes 884744 | tf_op jit(solution)/shard_map/ppermute | solution.py:47
  145.6 11.0 %collective-permute-start.44 = (bf16[384,384]{1,0:T(8,128)(2,1)S(1)}, bf16[384,384]{1,0:T(8,128)(2,1)S(1)}, u32[]{:S(2)}, u32[]{:S(2)}) collective-permute-start(bf16[384,384]{1,0:T(8,128)(2,1)S(1)} %get-tuple-element.340.refs_2_), channel_id=1, source_target_pairs={{0,8},{4,12},{8,0},{12,4},{16,24},{20,28},{24,16},{28,20},{1,9},{5... | collective-permute-start | bytes 884744 | tf_op jit(solution)/shard_map/ppermute | solution.py:47
  145.9 10.7 %collective-permute-start.45 = (bf16[208,384]{1,0:T(8,128)(2,1)S(1)}, bf16[208,384]{1,0:T(8,128)(2,1)S(1)}, u32[]{:S(2)}, u32[]{:S(2)}) collective-permute-start(bf16[208,384]{1,0:T(8,128)(2,1)S(1)} %get-tuple-element.324.refs_0_), channel_id=1, source_target_pairs={{0,8},{4,12},{8,0},{12,4},{16,24},{20,28},{24,16},{28,20},{1,9},{5... | collective-permute-start | bytes 479240 | tf_op jit(solution)/shard_map/ppermute | solution.py:47
  147.7 7.8 %collective-permute-start.46 = (bf16[192,384]{1,0:T(8,128)(2,1)S(1)}, bf16[192,384]{1,0:T(8,128)(2,1)S(1)}, u32[]{:S(2)}, u32[]{:S(2)}) collective-permute-start(bf16[192,384]{1,0:T(8,128)(2,1)S(1)} %get-tuple-element.326.refs_2_), channel_id=1, source_target_pairs={{0,4},{4,0},{8,12},{12,8},{16,20},{20,16},{24,28},{28,24},{1,5},{5... | collective-permute-start | bytes 442376 | tf_op jit(solution)/shard_map/ppermute | solution.py:47
  (25 other events, 223.0 us)
